TPU v7x, 32 devices: a whole 2x2x4 slice. The times are simulated.
32 devices in a mesh: bucket: 8 (over y, x, core), seq: 4 (over z).
Axes of the slice: x: 2, y: 2, z: 4, core: 2. Of those that a mesh axis runs over, the one named last changes fastest.
Arguments:
- tokens: bfloat16 [8192, 1536], P(('bucket', 'seq')), may hold values from -6 to 6
- cotangent: bfloat16 [8192, 1536], P(('bucket', 'seq')), may hold values from -6 to 6
- step_embed: bfloat16 [8, 4, 1024], P('bucket'), may hold values from -6 to 6
- caption: bfloat16 [8, 4, 256, 4096], P('bucket', None, 'seq'), may hold values from -6 to 6
- lengths: int32 [8, 4], P('bucket'), may hold values from 32 to 928, as said below
- group_bucket: int32 [8], P('bucket'), may hold values from 0 to 3, as said below
- null_mask: int32 [8, 4], P('bucket'), may hold values 0 or 1
- w_qkv: bfloat16 [1536, 4608], P('seq'), may hold values from -0.15625 to 0.15625
- w_out: bfloat16 [1536, 1536], P('seq'), may hold values from -0.625 to 0.625
- w_capkv: bfloat16 [4096, 3072], P('seq'), may hold values from -0.09375 to 0.09375
- w_gateup: bfloat16 [1536, 8192], P('seq'), may hold values from -0.15625 to 0.15625
- w_down: bfloat16 [4096, 1536], P('seq'), may hold values from -0.09375 to 0.09375
- w_mod: bfloat16 [1024, 6144], P('seq'), may hold values from -0.1875 to 0.1875
- b_mod: float32 [6144], replicated, may hold values from -3 to 3
- gain_attn: float32 [1536], replicated, may hold values from 0.5 to 1.5
- gain_ffn: float32 [1536], replicated, may hold values from 0.5 to 1.5
- gain_query: float32 [1536], replicated, may hold values from 0.5 to 1.5
- gain_key: float32 [1536], replicated, may hold values from 0.5 to 1.5
- gain_capkey: float32 [1536], replicated, may hold values from 0.5 to 1.5
- gate_head: float32 [24], replicated, may hold values from -1.5 to 1.5
- null_embed: bfloat16 [4096], replicated, may hold values from -6 to 6
Outputs:
- mixed: bfloat16 [8192, 1536], P(('bucket', 'seq'))
- input_grad: bfloat16 [8192, 1536], P(('bucket', 'seq'))
- grad_qkv: float32 [1536, 4608], P('seq')
- grad_out: float32 [1536, 1536], P('seq')
- grad_capkv: float32 [4096, 3072], P('seq')
- grad_gateup: float32 [1536, 8192], P('seq')
- grad_down: float32 [4096, 1536], P('seq')
- grad_mod: float32 [1024, 6144], P('seq')
- grad_bias_mod: float32 [6144], replicated
- grad_gain_attn: float32 [1536], replicated
- grad_gain_ffn: float32 [1536], replicated
- grad_gain_query: float32 [1536], replicated
- grad_gain_key: float32 [1536], replicated
- grad_gain_capkey: float32 [1536], replicated
- grad_gate_head: float32 [24], replicated
- grad_null: float32 [4096], replicated
Inputs may be any that keep to these rules, and one draw needn't show every extreme that they name: In each group one document, at a place drawn from the seed, starts on the group's first device and ends on its last; the others hold 32 to 84 tokens; a group's lengths sum to more than 768, the rest is padding. `group_bucket`: bucket numbers never fall along the groups, the first group has 0, and each of the 4 buckets owns at least one group.
All inputs are finite; a program needn't handle non-finite values. No bound on the sum of `null_mask` on one device may be relied on, other than what follows from the above.
Results may differ from a plain program's by a relative error of at most 0.02.
Values may be sent and summed in bfloat16 or wider, within the bound.
A program may use at most 448 MiB of HBM per device.

v0:
```python
import jax
import jax.numpy as jnp
from jax import lax
from jax.sharding import PartitionSpec as P

HEADS = 24
HDIM = 64
DOCS = 4
RES = 4


eps = 1e-06
head_block = 4


def row_stats(values):
    inverse = lax.rsqrt(jnp.mean(values * values, axis=-1, keepdims=True) + eps)
    return (values * inverse, inverse)


def norm_back(grad_normed, normed, inverse):
    inner_mean = jnp.mean(grad_normed * normed, axis=-1, keepdims=True)
    return inverse * (grad_normed - normed * inner_mean)


def head_stats(values):
    shaped = values.reshape(values.shape[0], HEADS, HDIM)
    normed, inverse = row_stats(shaped)
    return (normed.reshape(values.shape), inverse)


def head_back(grad_normed, normed, inverse):
    shaped_grad = grad_normed.reshape(grad_normed.shape[0], HEADS, HDIM)
    shaped_norm = normed.reshape(normed.shape[0], HEADS, HDIM)
    return norm_back(shaped_grad, shaped_norm, inverse).reshape(grad_normed.shape)


def rotary(values, row_pos, col_pos, direction):
    quarter = HDIM // 4
    freqs = 10000.0 ** (-jnp.arange(quarter, dtype=jnp.float32) / quarter)
    angles = jnp.concatenate([row_pos[:, None] * freqs, col_pos[:, None] * freqs], axis=1)
    cosine = jnp.cos(angles)[:, None, :]
    sine = direction * jnp.sin(angles)[:, None, :]
    shaped = values.reshape(values.shape[0], HEADS, HDIM)
    first_half = shaped[..., : HDIM // 2]
    second_half = shaped[..., HDIM // 2 :]
    turned = jnp.concatenate(
        [first_half * cosine - second_half * sine, second_half * cosine + first_half * sine],
        axis=-1,
    )
    return turned.reshape(values.shape)


def layout(doc_lengths, bucket, positions):
    doc_ends = jnp.cumsum(doc_lengths)
    starts = doc_ends - doc_lengths
    segment = jnp.sum((positions[:, None] >= doc_ends[None, :]).astype(jnp.int32), axis=1)
    matches = segment[:, None] == jnp.arange(DOCS, dtype=jnp.int32)[None, :]
    offset = jnp.sum(jnp.where(matches, starts[None, :], 0), axis=1)
    within = positions - offset
    stride = 32 * (bucket + 1)
    return (segment, (within // stride).astype(jnp.float32), (within % stride).astype(jnp.float32))


def head_groups(values):
    return values.reshape(values.shape[0], HEADS // head_block, head_block, HDIM).transpose(
        1, 0, 2, 3
    )


def from_groups(blocks):
    return blocks.transpose(1, 0, 2, 3).reshape(blocks.shape[1], HEADS * HDIM)


def attend_forward(query, keys, values, allowed):
    scale = HDIM ** (-0.5)

    def block(block_args):
        part_q, part_k, part_v = block_args
        scores = (
            jnp.einsum("qhd,khd->hqk", part_q, part_k, preferred_element_type=jnp.float32) * scale
        )
        scores = jnp.where(allowed[None], scores, -1e30)
        row_peak = jnp.max(scores, axis=-1, keepdims=True)
        exp_scores = jnp.exp(scores - row_peak)
        exp_total = jnp.sum(exp_scores, axis=-1, keepdims=True)
        attn_probs = (exp_scores / exp_total).astype(jnp.bfloat16)
        attn_block = jnp.einsum(
            "hqk,khd->qhd", attn_probs, part_v, preferred_element_type=jnp.float32
        )
        return (attn_block, row_peak[..., 0] + jnp.log(exp_total[..., 0]))

    blocks, log_total = lax.map(block, (head_groups(query), head_groups(keys), head_groups(values)))
    return (from_groups(blocks), log_total)


def attend_backward(query, keys, values, allowed, log_total, grad_out):
    scale = HDIM ** (-0.5)

    def block(block_args):
        part_q, part_k, part_v, part_log, part_grad = block_args
        scores = (
            jnp.einsum("qhd,khd->hqk", part_q, part_k, preferred_element_type=jnp.float32) * scale
        )
        scores = jnp.where(allowed[None], scores, -1e30)
        attn_probs = jnp.exp(scores - part_log[..., None])
        grad_probs = jnp.einsum(
            "qhd,khd->hqk", part_grad, part_v, preferred_element_type=jnp.float32
        )
        row_delta = jnp.sum(attn_probs * grad_probs, axis=-1, keepdims=True)
        grad_scores = (attn_probs * (grad_probs - row_delta)).astype(jnp.bfloat16)
        grad_query = (
            jnp.einsum("hqk,khd->qhd", grad_scores, part_k, preferred_element_type=jnp.float32)
            * scale
        )
        grad_keys = (
            jnp.einsum("hqk,qhd->khd", grad_scores, part_q, preferred_element_type=jnp.float32)
            * scale
        )
        grad_values = jnp.einsum(
            "hqk,qhd->khd",
            attn_probs.astype(jnp.bfloat16),
            part_grad,
            preferred_element_type=jnp.float32,
        )
        return (grad_query, grad_keys, grad_values)

    grad_query, grad_keys, grad_values = lax.map(
        block,
        (
            head_groups(query),
            head_groups(keys),
            head_groups(values),
            log_total,
            head_groups(grad_out),
        ),
    )
    return (from_groups(grad_query), from_groups(grad_keys), from_groups(grad_values))


def contract_right(left, weight):
    return lax.dot_general(
        left, weight, (((1,), (1,)), ((), ())), preferred_element_type=jnp.float32
    )


def weight_rows(left, right):
    return lax.psum_scatter(
        lax.dot_general(
            left,
            right,
            (((0,), (0,)), ((), ())),
            precision=lax.Precision.HIGHEST,
            preferred_element_type=jnp.float32,
        ).astype(jnp.bfloat16),
        "seq",
        scatter_dimension=0,
        tiled=True,
    ).astype(jnp.float32)


def shards(
    tokens,
    cotangent,
    step_embed,
    caption,
    lengths,
    group_bucket,
    null_mask,
    w_qkv,
    w_out,
    w_capkv,
    w_gateup,
    w_down,
    w_mod,
    b_mod,
    gain_attn,
    gain_ffn,
    gain_query,
    gain_key,
    gain_capkey,
    gate_head,
    null_embed,
):
    row_count = tokens.shape[0]
    group_len = row_count * lax.axis_size("seq")
    doc_lengths = lengths[0]
    bucket = group_bucket[0]
    member = (jnp.arange(RES, dtype=jnp.int32) == bucket).astype(jnp.float32)
    counted = lax.psum(member * jnp.sum(doc_lengths).astype(jnp.float32), "bucket")
    scale_loss = jnp.sum(counted) / (RES * jnp.sum(member * counted))
    gathered = (
        lax.all_gather(w_qkv, "seq", axis=0, tiled=True),
        lax.all_gather(w_out, "seq", axis=0, tiled=True),
        lax.all_gather(w_capkv, "seq", axis=0, tiled=True),
        lax.all_gather(w_gateup, "seq", axis=0, tiled=True),
        lax.all_gather(w_down, "seq", axis=0, tiled=True),
        lax.all_gather(w_mod, "seq", axis=0, tiled=True),
    )
    full_qkv, full_out, full_capkv, full_gateup, full_down, full_mod = gathered
    positions = lax.axis_index("seq") * row_count + jnp.arange(row_count, dtype=jnp.int32)
    segment, row_pos, col_pos = layout(doc_lengths, bucket, positions)
    key_segment, unused_rows, unused_cols = layout(
        doc_lengths, bucket, jnp.arange(group_len, dtype=jnp.int32)
    )
    document = jnp.minimum(segment, DOCS - 1)
    doc_pick = (document[:, None] == jnp.arange(DOCS, dtype=jnp.int32)[None, :]).astype(jnp.float32)
    is_valid = (segment < DOCS).astype(jnp.float32)
    condition = jax.nn.silu(step_embed[0].astype(jnp.float32)).astype(jnp.bfloat16)
    mod_doc = jnp.dot(condition, full_mod, preferred_element_type=jnp.float32) + b_mod
    modulation = jnp.dot(doc_pick, mod_doc, precision=lax.Precision.HIGHEST)
    scale_a, gate_a, scale_f, gate_f = jnp.split(modulation, 4, axis=1)
    inputs = tokens.astype(jnp.float32)
    normed1, inverse1 = row_stats(inputs)
    hidden1 = (normed1 * gain_attn * (1.0 + scale_a)).astype(jnp.bfloat16)
    projected = jnp.dot(hidden1, full_qkv, preferred_element_type=jnp.float32)
    query_raw, key_raw, value_raw = jnp.split(projected, 3, axis=1)
    query_norm, query_inv = head_stats(query_raw)
    key_norm, key_inv = head_stats(key_raw)
    query = rotary(query_norm * gain_query, row_pos, col_pos, 1.0).astype(jnp.bfloat16)
    keys = rotary(key_norm * gain_key, row_pos, col_pos, 1.0).astype(jnp.bfloat16)
    values = value_raw.astype(jnp.bfloat16)
    keys_all, values_all = (
        lax.all_gather(keys, "seq", axis=0, tiled=True),
        lax.all_gather(values, "seq", axis=0, tiled=True),
    )
    self_allowed = segment[:, None] == key_segment[None, :]
    own_out, own_log = attend_forward(query, keys_all, values_all, self_allowed)
    cap_rows = caption.shape[2]
    capmix = jnp.where(null_mask[0][:, None, None] > 0, null_embed[None, None, :], caption[0])
    cap_flat = capmix.reshape(DOCS * cap_rows, capmix.shape[2])
    cap_proj = jnp.dot(cap_flat, full_capkv, preferred_element_type=jnp.float32)
    capkey_raw, capval_raw = jnp.split(cap_proj, 2, axis=1)
    capkey_norm, capkey_inv = head_stats(capkey_raw)
    capkeys = (capkey_norm * gain_capkey).astype(jnp.bfloat16).reshape(DOCS, cap_rows, HEADS * HDIM)
    capvals = capval_raw.astype(jnp.bfloat16).reshape(DOCS, cap_rows, HEADS * HDIM)
    capkeys_all, capvals_all = (
        lax.all_gather(capkeys, "seq", axis=1, tiled=True),
        lax.all_gather(capvals, "seq", axis=1, tiled=True),
    )
    cap_len = capkeys_all.shape[1]
    cap_segment = jnp.repeat(jnp.arange(DOCS, dtype=jnp.int32), cap_len)
    cross_allowed = document[:, None] == cap_segment[None, :]
    capkeys_flat = capkeys_all.reshape(DOCS * cap_len, HEADS * HDIM)
    capvals_flat = capvals_all.reshape(DOCS * cap_len, HEADS * HDIM)
    cross_out, cross_log = attend_forward(query, capkeys_flat, capvals_flat, cross_allowed)
    gate_tanh = jnp.tanh(gate_head)
    head_gate = jnp.repeat(gate_tanh, HDIM)[None, :]
    mixed_attn = (own_out + head_gate * cross_out).astype(jnp.bfloat16)
    attn_out = jnp.dot(mixed_attn, full_out, preferred_element_type=jnp.float32)
    tanh_a = jnp.tanh(gate_a)
    residual = inputs + tanh_a * attn_out
    normed2, inverse2 = row_stats(residual)
    hidden2 = (normed2 * gain_ffn * (1.0 + scale_f)).astype(jnp.bfloat16)
    gate_up = jnp.dot(hidden2, full_gateup, preferred_element_type=jnp.float32)
    gate_part, up_part = jnp.split(gate_up, 2, axis=1)
    sig_gate = jax.nn.sigmoid(gate_part)
    silu_gate = gate_part * sig_gate
    hidden_ffn = (silu_gate * up_part).astype(jnp.bfloat16)
    down_out = jnp.dot(hidden_ffn, full_down, preferred_element_type=jnp.float32)
    tanh_f = jnp.tanh(gate_f)
    result = (residual + tanh_f * down_out).astype(jnp.bfloat16)
    full_qkv, full_out, full_capkv, full_gateup, full_down = (
        lax.all_gather(w_qkv, "seq", axis=0, tiled=True),
        lax.all_gather(w_out, "seq", axis=0, tiled=True),
        lax.all_gather(w_capkv, "seq", axis=0, tiled=True),
        lax.all_gather(w_gateup, "seq", axis=0, tiled=True),
        lax.all_gather(w_down, "seq", axis=0, tiled=True),
    )
    grad_res0 = cotangent.astype(jnp.float32) * (is_valid * scale_loss)[:, None]
    grad_down = (tanh_f * grad_res0).astype(jnp.bfloat16)
    grad_gate_f = grad_res0 * down_out * (1.0 - tanh_f * tanh_f)
    grad_ffn = contract_right(grad_down, full_down)
    grad_gate_part = grad_ffn * up_part * sig_gate * (1.0 + gate_part * (1.0 - sig_gate))
    grad_up_part = grad_ffn * silu_gate
    grad_gateup = jnp.concatenate([grad_gate_part, grad_up_part], axis=1).astype(jnp.bfloat16)
    grad_hidden2 = contract_right(grad_gateup, full_gateup)
    gain_ffn_term = jnp.sum(grad_hidden2 * normed2 * (1.0 + scale_f), axis=0)
    grad_scale_f = grad_hidden2 * normed2 * gain_ffn
    grad_residual = grad_res0 + norm_back(
        grad_hidden2 * gain_ffn * (1.0 + scale_f), normed2, inverse2
    )
    grad_attn = (tanh_a * grad_residual).astype(jnp.bfloat16)
    grad_gate_a = grad_residual * attn_out * (1.0 - tanh_a * tanh_a)
    grad_mix = contract_right(grad_attn, full_out)
    grad_own = grad_mix.astype(jnp.bfloat16)
    grad_cross = (head_gate * grad_mix).astype(jnp.bfloat16)
    gate_head_term = jnp.sum(
        (grad_mix * cross_out).reshape(row_count, HEADS, HDIM), axis=(0, 2)
    ) * (1.0 - gate_tanh * gate_tanh)
    query_own, keys_grad_all, values_grad_all = attend_backward(
        query, keys_all, values_all, self_allowed, own_log, grad_own
    )
    grad_keys, grad_values = (
        lax.psum_scatter(
            keys_grad_all.astype(jnp.bfloat16), "seq", scatter_dimension=0, tiled=True
        ).astype(jnp.float32),
        lax.psum_scatter(
            values_grad_all.astype(jnp.bfloat16), "seq", scatter_dimension=0, tiled=True
        ).astype(jnp.float32),
    )
    query_cross, capkeys_grad_all, capvals_grad_all = attend_backward(
        query, capkeys_flat, capvals_flat, cross_allowed, cross_log, grad_cross
    )
    grad_capkeys, grad_capvals = (
        lax.psum_scatter(
            capkeys_grad_all.reshape(DOCS, cap_len, HEADS * HDIM).astype(jnp.bfloat16),
            "seq",
            scatter_dimension=1,
            tiled=True,
        ).astype(jnp.float32),
        lax.psum_scatter(
            capvals_grad_all.reshape(DOCS, cap_len, HEADS * HDIM).astype(jnp.bfloat16),
            "seq",
            scatter_dimension=1,
            tiled=True,
        ).astype(jnp.float32),
    )
    grad_query = rotary(query_own + query_cross, row_pos, col_pos, -1.0)
    gain_query_term = jnp.sum(grad_query * query_norm, axis=0)
    grad_query_raw = head_back(grad_query * gain_query, query_norm, query_inv)
    grad_key = rotary(grad_keys, row_pos, col_pos, -1.0)
    gain_key_term = jnp.sum(grad_key * key_norm, axis=0)
    grad_key_raw = head_back(grad_key * gain_key, key_norm, key_inv)
    grad_projected = jnp.concatenate([grad_query_raw, grad_key_raw, grad_values], axis=1).astype(
        jnp.bfloat16
    )
    grad_hidden1 = contract_right(grad_projected, full_qkv)
    gain_attn_term = jnp.sum(grad_hidden1 * normed1 * (1.0 + scale_a), axis=0)
    grad_scale_a = grad_hidden1 * normed1 * gain_attn
    input_grad = (
        grad_residual + norm_back(grad_hidden1 * gain_attn * (1.0 + scale_a), normed1, inverse1)
    ).astype(jnp.bfloat16)
    grad_mod_tok = jnp.concatenate([grad_scale_a, grad_gate_a, grad_scale_f, grad_gate_f], axis=1)
    grad_mod_doc = lax.dot_general(
        doc_pick,
        grad_mod_tok,
        (((0,), (0,)), ((), ())),
        precision=lax.Precision.HIGHEST,
        preferred_element_type=jnp.float32,
    )
    bias_term = jnp.sum(grad_mod_doc, axis=0)
    capkey_grad_flat = grad_capkeys.reshape(DOCS * cap_rows, HEADS * HDIM)
    gain_capkey_term = jnp.sum(capkey_grad_flat * capkey_norm, axis=0)
    grad_capkey_raw = head_back(capkey_grad_flat * gain_capkey, capkey_norm, capkey_inv)
    grad_cap_proj = jnp.concatenate(
        [grad_capkey_raw, grad_capvals.reshape(DOCS * cap_rows, HEADS * HDIM)], axis=1
    ).astype(jnp.bfloat16)
    null_rows = jnp.repeat((null_mask[0] > 0).astype(jnp.float32), cap_rows)
    null_sum = jnp.dot(null_rows, grad_cap_proj, precision=lax.Precision.HIGHEST)
    null_term = jnp.dot(full_capkv, null_sum, precision=lax.Precision.HIGHEST)
    term_qkv = weight_rows(hidden1, grad_projected)
    term_out = weight_rows(mixed_attn, grad_attn)
    term_capkv = weight_rows(cap_flat, grad_cap_proj)
    term_gateup = weight_rows(hidden2, grad_gateup)
    term_down = weight_rows(hidden_ffn, grad_down)
    term_mod = weight_rows(condition.astype(jnp.float32), grad_mod_doc)
    sum_qkv, sum_out, sum_capkv, sum_gateup, sum_down, sum_mod = (
        lax.psum(term_qkv.astype(jnp.bfloat16), "bucket").astype(jnp.float32),
        lax.psum(term_out.astype(jnp.bfloat16), "bucket").astype(jnp.float32),
        lax.psum(term_capkv.astype(jnp.bfloat16), "bucket").astype(jnp.float32),
        lax.psum(term_gateup.astype(jnp.bfloat16), "bucket").astype(jnp.float32),
        lax.psum(term_down.astype(jnp.bfloat16), "bucket").astype(jnp.float32),
        lax.psum(term_mod.astype(jnp.bfloat16), "bucket").astype(jnp.float32),
    )
    small_parts = lax.psum(
        (
            bias_term,
            gain_attn_term,
            gain_ffn_term,
            gain_query_term,
            gain_key_term,
            gain_capkey_term,
            gate_head_term,
            null_term,
        ),
        ("bucket", "seq"),
    )
    return (
        result,
        input_grad,
        sum_qkv,
        sum_out,
        sum_capkv,
        sum_gateup,
        sum_down,
        sum_mod,
        small_parts[0],
        small_parts[1],
        small_parts[2],
        small_parts[3],
        small_parts[4],
        small_parts[5],
        small_parts[6],
        small_parts[7],
    )


def solution(mesh):
    placed = (
        P(("bucket", "seq"), None),
        P(("bucket", "seq"), None),
        P("bucket", None, None),
        P("bucket", None, "seq", None),
        P("bucket", None),
        P("bucket"),
        P("bucket", None),
        P("seq", None),
        P("seq", None),
        P("seq", None),
        P("seq", None),
        P("seq", None),
        P("seq", None),
        P(),
        P(),
        P(),
        P(),
        P(),
        P(),
        P(),
        P(),
    )
    return jax.shard_map(
        shards,
        mesh=mesh,
        in_specs=placed,
        out_specs=(
            P(("bucket", "seq"), None),
            P(("bucket", "seq"), None),
            P("seq", None),
            P("seq", None),
            P("seq", None),
            P("seq", None),
            P("seq", None),
            P("seq", None),
            P(),
            P(),
            P(),
            P(),
            P(),
            P(),
            P(),
            P(),
        ),
        check_vma=False,
    )
```

profile of v0, /device:TPU:0, one launch (start us, length us, event | category | flops | bytes accessed | tf_op | source)
XLA Modules:
  0.0 4316.8 jit_solution(18354502737957339164)
XLA Ops:
  10.1 220.4 %all-gather.11.cloned.1.call-done = bf16[1024,6144]{1,0:T(8,128)(2,1)} async-done(((bf16[256,6144]{1,0:T(8,128)(2,1)}), bf16[1024,6144]{1,0:T(8,128)(2,1)}) %all-gather.11.cloned.1.call-update) | async-done | bytes 12582928 | tf_op jit(solution)/shard_map/all_gather | solution.py:198
  243.0 231.2 %all-gather.13.cloned.1.call-done = bf16[1536,4608]{1,0:T(8,128)(2,1)} async-done(((bf16[384,4608]{1,0:T(8,128)(2,1)}), bf16[1536,4608]{1,0:T(8,128)(2,1)}) %all-gather.13.cloned.1.call-update) | async-done | bytes 14155792 | tf_op jit(solution)/shard_map/all_gather | solution.py:193
  514.6 384.6 %all-gather.19.cloned.1.call-done = bf16[4096,3072]{1,0:T(8,128)(2,1)} async-done(((bf16[1024,3072]{1,0:T(8,128)(2,1)}), bf16[4096,3072]{1,0:T(8,128)(2,1)}) %all-gather.19.cloned.1.call-update) | async-done | bytes 25165840 | tf_op jit(solution)/shard_map/all_gather | solution.py:195
  926.7 14.6 psum.105
  944.6 18.4 all-gather.15.cloned.1.call-done
  967.6 59.5 %all-gather.17.cloned.1.call-done = bf16[1024,1536]{0,1:T(8,128)(2,1)} async-done(((bf16[256,1536]{0,1:T(8,128)(2,1)}), bf16[1024,1536]{0,1:T(8,128)(2,1)}) %all-gather.17.cloned.1.call-update) | async-done | bytes 3145744 | tf_op jit(solution)/shard_map/all_gather | solution.py:224
  1027.2 35.7 while.56
  1064.6 26.1 all-gather.21.cloned.1.call-done
  1102.8 51.7 %all-gather.23.cloned.1.call-done = bf16[4,256,1536]{2,1,0:T(8,128)(2,1)} async-done(((bf16[4,64,1536]{2,1,0:T(8,128)(2,1)}), bf16[4,256,1536]{2,1,0:T(8,128)(2,1)}) %all-gather.23.cloned.1.call-update) | async-done | bytes 3145744 | tf_op jit(solution)/shard_map/all_gather | solution.py:238
  1166.5 38.9 while.57
  1211.6 32.6 all-gather.25.cloned.1.call-done
  1255.5 414.0 %all-gather.27.cloned.1.call-done = bf16[1536,8192]{1,0:T(8,128)(2,1)} async-done(((bf16[384,8192]{1,0:T(8,128)(2,1)}), bf16[1536,8192]{1,0:T(8,128)(2,1)}) %all-gather.27.cloned.1.call-update) | async-done | bytes 25165840 | tf_op jit(solution)/shard_map/all_gather | solution.py:196
  1669.4 16.2 fusion.169
  1685.6 201.7 %all-gather.29.cloned.1.call-done = bf16[4096,1536]{1,0:T(8,128)(2,1)} async-done(((bf16[1024,1536]{1,0:T(8,128)(2,1)}), bf16[4096,1536]{1,0:T(8,128)(2,1)}) %all-gather.29.cloned.1.call-update) | async-done | bytes 12582928 | tf_op jit(solution)/shard_map/all_gather | solution.py:197
  1898.7 15.5 multiply_reduce_fusion.5
  1914.2 13.5 subtract_multiply_fusion
  1943.4 83.4 %while.58 = (s32[]{:T(128)}, f32[6,256,4,64]{1,3,2,0:T(8,128)}, bf16[6,1024,4,64]{1,3,2,0:T(8,128)(2,1)}, bf16[6,1024,4,64]{1,3,2,0:T(8,128)(2,1)}, bf16[6,1024,...) while((s32[]{:T(128)}, f32[6,256,4,64]{1,3,2,0:T(8,128)}, ...), condition=%wide.region_24.25_spmd.clone, body=%wide.region_22.24_spmd.clone.sunk | while | flops 687406080 | bytes 37001344 | solution.py:128
  2039.3 76.2 %while.59 = (s32[]{:T(128)}, f32[6,256,4,64]{1,3,2,0:T(8,128)}, bf16[6,1024,4,64]{1,3,2,0:T(8,128)(2,1)}, bf16[6,1024,4,64]{1,3,2,0:T(8,128)(2,1)}, bf16[6,1024,...) while((s32[]{:T(128)}, f32[6,256,4,64]{1,3,2,0:T(8,128)}, ...), condition=%wide.region_27.28_spmd.clone, body=%wide.region_25.27_spmd.clone.sunk | while | flops 687406080 | bytes 37001344 | solution.py:128
  2175.1 12.9 multiply_reduce_fusion.6
  2192.7 12.8 convolution_convert_fusion.4
  2216.3 13.4 convolution_convert_fusion
  2242.1 30.8 reduce-scatter.21.cloned.1.call-done
  2272.9 13.9 convolution_convert_fusion.1
  2287.0 74.0 %reduce-scatter.17.cloned.1.call-done = bf16[384,1536]{1,0:T(8,128)(2,1)} async-done(((bf16[1536,1536]{1,0:T(8,128)(2,1)}), bf16[384,1536]{1,0:T(8,128)(2,1)}) %reduce-scatter.17.cloned.1.call-update) | async-done | bytes 1179664 | tf_op jit(solution)/shard_map/reduce_scatter | solution.py:148
  2361.0 215.2 %reduce-scatter.27.cloned.1.call-done = bf16[1024,1536]{1,0:T(8,128)(2,1)} async-done(((bf16[4096,1536]{1,0:T(8,128)(2,1)}), bf16[1024,1536]{1,0:T(8,128)(2,1)}) %reduce-scatter.27.cloned.1.call-update) | async-done | bytes 3145744 | tf_op jit(solution)/shard_map/reduce_scatter | solution.py:148
  2576.2 215.7 %reduce-scatter.29.cloned.1.call-done = bf16[256,6144]{1,0:T(8,128)(2,1)} async-done(((bf16[1024,6144]{1,0:T(8,128)(2,1)}), bf16[256,6144]{1,0:T(8,128)(2,1)}) %reduce-scatter.29.cloned.1.call-update) | async-done | bytes 3145744 | tf_op jit(solution)/shard_map/reduce_scatter | solution.py:148
  2791.9 240.5 %reduce-scatter.15.cloned.1.call-done = bf16[384,4608]{1,0:T(8,128)(2,1)} async-done(((bf16[1536,4608]{1,0:T(8,128)(2,1)}), bf16[384,4608]{1,0:T(8,128)(2,1)}) %reduce-scatter.15.cloned.1.call-update) | async-done | bytes 3538960 | tf_op jit(solution)/shard_map/reduce_scatter | solution.py:148
  3032.4 417.8 %reduce-scatter.25.cloned.1.call-done = bf16[384,8192]{1,0:T(8,128)(2,1)} async-done(((bf16[1536,8192]{1,0:T(8,128)(2,1)}), bf16[384,8192]{1,0:T(8,128)(2,1)}) %reduce-scatter.25.cloned.1.call-update) | async-done | bytes 6291472 | tf_op jit(solution)/shard_map/reduce_scatter | solution.py:148
  3450.2 418.5 %reduce-scatter.23.cloned.1.call-done = bf16[1024,3072]{1,0:T(8,128)(2,1)} async-done(((bf16[4096,3072]{1,0:T(8,128)(2,1)}), bf16[1024,3072]{1,0:T(8,128)(2,1)}) %reduce-scatter.23.cloned.1.call-update) | async-done | bytes 6291472 | tf_op jit(solution)/shard_map/reduce_scatter | solution.py:148
  3871.0 23.7 fusion.170
  3898.2 270.4 %all-reduce.7.cloned.1.call-done = (bf16[384,4608]{1,0:T(8,128)(2,1)}, bf16[384,1536]{1,0:T(8,128)(2,1)}, bf16[1024,3072]{1,0:T(8,128)(2,1)}, bf16[384,8192]{1,0...) async-done(((bf16[384,4608]{1,0:T(8,128)(2,1)}, bf16[384,1536]{1,0:T(8,128)(2,1)}, bf16[1024,3072]{1,0:T(8,128)(2,1)}, bf16[384,8192]{1,0:T(8,128)(2,1)}, ...) | async-done | bytes 23592976 | tf_op jit(solution)/shard_map/psum | solution.py:359
  4196.2 103.0 %all-reduce.5.cloned.1.call-done = (f32[6144]{0:T(1024)}, f32[1536]{0:T(1024)}, f32[1536]{0:T(1024)}, f32[1536]{0:T(1024)}, f32[1536]{0:T(1024)}, /*index=5*/f32[1536]{0:T(1024)}, f32[24]{0:T(128)}, f32[4096]{0:T(1024)}) async-done(((f32[6144]{0:T(1024)}, f32[1536]{0:T(1024)}, f32[1536]{0:T(1024)}, f32[1536]{0:T(1024)}, f32[1536]{0:T(1024)}, /*index=5*/f32[1536]{0:T(1024)}, f32[24]{0:T(128)}, ...) | async-done | bytes 71792 | tf_op jit(solution)/shard_map/psum | solution.py:366
  (517 shorter events, 534.8 us)
Async XLA Ops:
  7.2 223.3 %all-gather.11.cloned.1.call-start = ((), (), s32[]{:S(2)}) async-start(), calls=%async_computation.10 | async-start | bytes 15728640 | tf_op jit(solution)/shard_map/all_gather | solution.py:198
  7.9 466.3 %all-gather.13.cloned.1.call-start = ((), (), s32[]{:S(2)}) async-start(), calls=%async_computation.11 | async-start | bytes 17694720 | tf_op jit(solution)/shard_map/all_gather | solution.py:193
  8.7 221.8 %copy-start.61 = (bf16[1,4,1024]{2,1,0:T(4,128)(2,1)S(1)}, bf16[1,4,1024]{2,1,0:T(4,128)(2,1)}, u32[]{:S(2)}) copy-start(bf16[1,4,1024]{2,1,0:T(4,128)(2,1)} %param.31) | copy-start | bytes 24580
  8.7 221.8 %copy-start.66 = (f32[6144]{0:T(1024)S(1)}, f32[6144]{0:T(1024)}, u32[]{:S(2)}) copy-start(f32[6144]{0:T(1024)} %param.42) | copy-start | bytes 73732
  8.7 890.5 %all-gather.19.cloned.1.call-start = ((), (), s32[]{:S(2)}) async-start(), calls=%async_computation.14 | async-start | bytes 31457280 | tf_op jit(solution)/shard_map/all_gather | solution.py:195
  9.4 953.5 %all-gather.15.cloned.1.call-start = ((), (), s32[]{:S(2)}) async-start(), calls=%async_computation.12 | async-start | bytes 3932160 | tf_op jit(solution)/shard_map/all_gather | solution.py:225
  9.7 476.2 %copy-start.71 = (s32[4,1]{0,1:T(1,128)}, s32[4,1]{0,1:T(1,128)S(1)}, u32[]{:S(2)}) copy-start(s32[4,1]{0,1:T(1,128)S(1)} %reduce-window.4) | copy-start | bytes 52
  10.1 229.4 %copy-start.67 = (f32[256]{0:T(256)}, f32[256]{0:T(256)S(1)}, u32[]{:S(2)}) copy-start(f32[256]{0:T(256)S(1)} %add_rsqrt_fusion.4) | copy-start | bytes 3076
  243.0 238.3 %copy-start.29 = (bf16[256,1536]{1,0:T(8,128)(2,1)}, bf16[256,1536]{1,0:T(8,128)(2,1)S(1)}, u32[]{:S(2)}) copy-start(bf16[256,1536]{1,0:T(8,128)(2,1)S(1)} %fusion.129) | copy-start | bytes 2359300
  485.2 541.9 %all-gather.17.cloned.1.call-start = ((), (), s32[]{:S(2)}) async-start(), calls=%async_computation.13 | async-start | bytes 3932160 | tf_op jit(solution)/shard_map/all_gather | solution.py:224
  511.6 579.1 %all-gather.21.cloned.1.call-start = ((), (), s32[]{:S(2)}) async-start(), calls=%async_computation.15 | async-start | bytes 3932160 | tf_op jit(solution)/shard_map/all_gather | solution.py:239
  913.1 241.4 %all-gather.23.cloned.1.call-start = ((), (), s32[]{:S(2)}) async-start(), calls=%async_computation.16 | async-start | bytes 3932160 | tf_op jit(solution)/shard_map/all_gather | solution.py:238
  923.8 320.4 %all-gather.25.cloned.1.call-start = ((), (), s32[]{:S(2)}) async-start(), calls=%async_computation.17 | async-start | bytes 5898240 | tf_op jit(solution)/shard_map/all_gather | solution.py:194
  924.6 744.9 %all-gather.27.cloned.1.call-start = ((), (), s32[]{:S(2)}) async-start(), calls=%async_computation.18 | async-start | bytes 31457280 | tf_op jit(solution)/shard_map/all_gather | solution.py:196
  925.3 961.9 %all-gather.29.cloned.1.call-start = ((), (), s32[]{:S(2)}) async-start(), calls=%async_computation.19 | async-start | bytes 15728640 | tf_op jit(solution)/shard_map/all_gather | solution.py:197
  925.9 1227.1 %reduce-scatter.11.cloned.1.call-start = ((), (), s32[]{:S(2)}) async-start(), calls=%async_computation.20 | async-start | bytes 3932160 | tf_op jit(solution)/shard_map/reduce_scatter | solution.py:295
  1062.9 33.7 copy-start.1
  1211.6 39.7 copy-start.70
  1211.6 39.7 copy-start.73
  1887.3 26.9 slice-start
  2026.8 148.3 %reduce-scatter.13.cloned.1.call-start = ((), (), s32[]{:S(2)}) async-start(), calls=%async_computation.21 | async-start | bytes 3932160 | tf_op jit(solution)/shard_map/reduce_scatter | solution.py:298
  2033.8 196.7 %reduce-scatter.19.cloned.1.call-start = ((), (), s32[]{:S(2)}) async-start(), calls=%async_computation.24 | async-start | bytes 3932160 | tf_op jit(solution)/shard_map/reduce_scatter | solution.py:306
  2124.7 148.2 %reduce-scatter.21.cloned.1.call-start = ((), (), s32[]{:S(2)}) async-start(), calls=%async_computation.25 | async-start | bytes 3932160 | tf_op jit(solution)/shard_map/reduce_scatter | solution.py:312
  2136.4 224.5 %reduce-scatter.17.cloned.1.call-start = ((), (), s32[]{:S(2)}) async-start(), calls=%async_computation.23 | async-start | bytes 5898240 | tf_op jit(solution)/shard_map/reduce_scatter | solution.py:148
  2141.4 434.7 %reduce-scatter.27.cloned.1.call-start = ((), (), s32[]{:S(2)}) async-start(), calls=%async_computation.28 | async-start | bytes 15728640 | tf_op jit(solution)/shard_map/reduce_scatter | solution.py:148
  2149.8 642.1 %reduce-scatter.29.cloned.1.call-start = ((), (), s32[]{:S(2)}) async-start(), calls=%async_computation.29 | async-start | bytes 15728640 | tf_op jit(solution)/shard_map/reduce_scatter | solution.py:148
  2205.5 826.9 %reduce-scatter.15.cloned.1.call-start = ((), (), s32[]{:S(2)}) async-start(), calls=%async_computation.22 | async-start | bytes 17694720 | tf_op jit(solution)/shard_map/reduce_scatter | solution.py:148
  2214.5 1235.7 %reduce-scatter.25.cloned.1.call-start = ((), (), s32[]{:S(2)}) async-start(), calls=%async_computation.27 | async-start | bytes 31457280 | tf_op jit(solution)/shard_map/reduce_scatter | solution.py:148
  2229.8 1639.0 %reduce-scatter.23.cloned.1.call-start = ((), (), s32[]{:S(2)}) async-start(), calls=%async_computation.26 | async-start | bytes 31457280 | tf_op jit(solution)/shard_map/reduce_scatter | solution.py:148
  2286.9 1881.7 %all-reduce.7.cloned.1.call-start = ((), (), s32[]{:S(2)}) async-start(), calls=%async_computation.31 | async-start | bytes 47185920 | tf_op jit(solution)/shard_map/psum | solution.py:359
  3868.8 430.3 %all-reduce.5.cloned.1.call-start = ((), (), s32[]{:S(2)}) async-start(), calls=%async_computation.30 | async-start | bytes 164864 | tf_op jit(solution)/shard_map/psum | solution.py:366
  3871.0 23.8 copy-start.26
  (77 other events, 309.0 us)
Sparse Core Ops, SparseCore 0:
  9.6 220.8 all-gather.10
  232.1 242.1 all-gather.12
  475.8 423.3 all-gather.18
  901.2 61.6 all-gather.14
  964.9 62.0 all-gather.16
  1029.0 61.6 all-gather.20
  1092.3 62.1 all-gather.22
  1156.0 88.0 all-gather.24
  1245.8 423.6 all-gather.26
  1670.8 216.3 all-gather.28
  2026.9 58.4 reduce-scatter.10
  2087.5 60.2 reduce-scatter.12
  2150.1 60.2 reduce-scatter.18
  2212.6 60.2 reduce-scatter.20
  2275.7 85.2 reduce-scatter.16
  2363.7 212.3 reduce-scatter.26
  2578.9 212.8 reduce-scatter.28
  2794.1 238.2 reduce-scatter.14
  3034.8 415.4 reduce-scatter.24
  3452.6 416.1 reduce-scatter.22
  3873.6 294.9 all-reduce.6
  4175.7 123.4 all-reduce.4
where the time goes:
time: 4330 us; the launch traced here: 4320 us
  waiting for transfers between devices  3630 us (84%)
  matrix products  394 us (9%)
  local copies, waits for them, and re-layouts  149 us (3%)
  other arithmetic  108 us (2%)
    reduce_scatter x6, waiting for transfers between devices, weight_rows(): lax.psum_scatter(lax.dot_general(left, right, (((0,), (0,)), ((), ())), p...  1580 us
    all_gather x1, waiting for transfers between devices, shards(): lax.all_gather(w_gateup, 'seq', axis=0, tiled=True)  414 us
    all_gather x1, waiting for transfers between devices, shards(): lax.all_gather(w_capkv, 'seq', axis=0, tiled=True)  385 us
    psum x1, waiting for transfers between devices, shards(): lax.psum(term_qkv.astype(jnp.bfloat16), 'bucket').astype(jnp.float32)  270 us
    all_gather x1, waiting for transfers between devices, shards(): lax.all_gather(w_qkv, 'seq', axis=0, tiled=True)  231 us
    all_gather x1, waiting for transfers between devices, shards(): lax.all_gather(w_mod, 'seq', axis=0, tiled=True)  220 us
    all_gather x1, waiting for transfers between devices, shards(): lax.all_gather(w_down, 'seq', axis=0, tiled=True)  202 us
    psum x1, waiting for transfers between devices, shards(): lax.psum((bias_term, gain_attn_term, gain_ffn_term, gain_query_term, gain...  103 us
  transfers between devices with their start and end apart: 22, of which 19 were waited for; matrix products, arithmetic and copies ran while one was open for 11% of the time, Pallas kernels for 0%

commit v1 on v0

v1 whole, which is shorter than its diff:
```python
import jax
import jax.numpy as jnp
from jax import lax
from jax.sharding import Mesh, PartitionSpec as P

HEADS = 24
HDIM = 64
DOCS = 4
RES = 4


eps = 1e-06


def row_stats(values):
    inverse = lax.rsqrt(jnp.mean(values * values, axis=-1, keepdims=True) + eps)
    return (values * inverse, inverse)


def norm_back(grad_normed, normed, inverse):
    inner_mean = jnp.mean(grad_normed * normed, axis=-1, keepdims=True)
    return inverse * (grad_normed - normed * inner_mean)


def head_stats(values):
    shaped = values.reshape(values.shape[0], -1, HDIM)
    normed, inverse = row_stats(shaped)
    return (normed.reshape(values.shape), inverse)


def head_back(grad_normed, normed, inverse):
    shaped_grad = grad_normed.reshape(grad_normed.shape[0], -1, HDIM)
    shaped_norm = normed.reshape(normed.shape[0], -1, HDIM)
    return norm_back(shaped_grad, shaped_norm, inverse).reshape(grad_normed.shape)


def rotary(values, row_pos, col_pos, direction):
    quarter = HDIM // 4
    freqs = 10000.0 ** (-jnp.arange(quarter, dtype=jnp.float32) / quarter)
    angles = jnp.concatenate([row_pos[:, None] * freqs, col_pos[:, None] * freqs], axis=1)
    cosine = jnp.cos(angles)[:, None, :]
    sine = direction * jnp.sin(angles)[:, None, :]
    shaped = values.reshape(values.shape[0], -1, HDIM)
    first_half = shaped[..., : HDIM // 2]
    second_half = shaped[..., HDIM // 2 :]
    turned = jnp.concatenate(
        [first_half * cosine - second_half * sine, second_half * cosine + first_half * sine],
        axis=-1,
    )
    return turned.reshape(values.shape)


def layout(doc_lengths, bucket, positions):
    doc_ends = jnp.cumsum(doc_lengths)
    starts = doc_ends - doc_lengths
    segment = jnp.sum((positions[:, None] >= doc_ends[None, :]).astype(jnp.int32), axis=1)
    matches = segment[:, None] == jnp.arange(DOCS, dtype=jnp.int32)[None, :]
    offset = jnp.sum(jnp.where(matches, starts[None, :], 0), axis=1)
    within = positions - offset
    stride = 32 * (bucket + 1)
    return (segment, (within // stride).astype(jnp.float32), (within % stride).astype(jnp.float32))


def by_head(values):
    return values.reshape(values.shape[0], -1, 1, HDIM).transpose(1, 0, 2, 3)


def from_heads(blocks):
    return blocks.transpose(1, 0, 2, 3).reshape(blocks.shape[1], -1)


def attend_forward(query, keys, values, allowed):
    scale = HDIM ** (-0.5)

    def block(block_args):
        part_q, part_k, part_v = block_args
        scores = (
            jnp.einsum("qhd,khd->hqk", part_q, part_k, preferred_element_type=jnp.float32) * scale
        )
        scores = jnp.where(allowed[None], scores, -1e30)
        row_peak = jnp.max(scores, axis=-1, keepdims=True)
        exp_scores = jnp.exp(scores - row_peak)
        exp_total = jnp.sum(exp_scores, axis=-1, keepdims=True)
        attn_probs = (exp_scores / exp_total).astype(jnp.bfloat16)
        attn_block = jnp.einsum(
            "hqk,khd->qhd", attn_probs, part_v, preferred_element_type=jnp.float32
        )
        return (attn_block, row_peak[..., 0] + jnp.log(exp_total[..., 0]))

    blocks, log_total = lax.map(block, (by_head(query), by_head(keys), by_head(values)))
    return (from_heads(blocks), log_total)


def attend_backward(query, keys, values, allowed, log_total, grad_out):
    scale = HDIM ** (-0.5)

    def block(block_args):
        part_q, part_k, part_v, part_log, part_grad = block_args
        scores = (
            jnp.einsum("qhd,khd->hqk", part_q, part_k, preferred_element_type=jnp.float32) * scale
        )
        scores = jnp.where(allowed[None], scores, -1e30)
        attn_probs = jnp.exp(scores - part_log[..., None])
        grad_probs = jnp.einsum(
            "qhd,khd->hqk", part_grad, part_v, preferred_element_type=jnp.float32
        )
        row_delta = jnp.sum(attn_probs * grad_probs, axis=-1, keepdims=True)
        grad_scores = (attn_probs * (grad_probs - row_delta)).astype(jnp.bfloat16)
        grad_query = (
            jnp.einsum("hqk,khd->qhd", grad_scores, part_k, preferred_element_type=jnp.float32)
            * scale
        )
        grad_keys = (
            jnp.einsum("hqk,qhd->khd", grad_scores, part_q, preferred_element_type=jnp.float32)
            * scale
        )
        grad_values = jnp.einsum(
            "hqk,qhd->khd",
            attn_probs.astype(jnp.bfloat16),
            part_grad,
            preferred_element_type=jnp.float32,
        )
        return (grad_query, grad_keys, grad_values)

    grad_query, grad_keys, grad_values = lax.map(
        block,
        (by_head(query), by_head(keys), by_head(values), log_total, by_head(grad_out)),
    )
    return (from_heads(grad_query), from_heads(grad_keys), from_heads(grad_values))


def matmul(left, right):
    return jnp.dot(left, right, preferred_element_type=jnp.float32)


def contract_right(left, weight):
    return lax.dot_general(
        left, weight, (((1,), (1,)), ((), ())), preferred_element_type=jnp.float32
    )


def contract_rows(left, right):
    return lax.dot_general(
        left, right, (((0,), (0,)), ((), ())), preferred_element_type=jnp.float32
    )


def pick(values, index, axis):
    return lax.dynamic_index_in_dim(values, index, axis, keepdims=False)


def to_plane(values):
    ways = lax.axis_size("tp")
    parts = values.reshape((ways, values.shape[0] // ways) + values.shape[1:])
    parts = lax.all_to_all(parts, "tp", 0, 0, tiled=True)
    parts = lax.all_to_all(parts, "seq", 0, 0, tiled=True)
    return parts.reshape(values.shape)


def from_plane(values):
    ways = lax.axis_size("tp")
    parts = values.reshape((ways, values.shape[0] // ways) + values.shape[1:])
    parts = lax.all_to_all(parts, "seq", 0, 0, tiled=True)
    parts = lax.all_to_all(parts, "tp", 0, 0, tiled=True)
    return parts.reshape(values.shape)


def gather_rows(part):
    whole = lax.all_gather(part, "seq", axis=0, tiled=False)
    whole = lax.all_gather(whole, "core", axis=1, tiled=False)
    return whole.reshape((-1,) + part.shape[1:])


def scatter_rows(term):
    cores, planes = lax.axis_size("core"), lax.axis_size("seq")
    shaped = term.astype(jnp.bfloat16).reshape(planes, cores, -1, term.shape[-1])
    half = lax.psum_scatter(shaped, "core", scatter_dimension=1, tiled=False)
    return lax.psum_scatter(half, "seq", scatter_dimension=0, tiled=False)


def plane_gather(values):
    return lax.all_gather(values, "tp", axis=0, tiled=True)


def plane_scatter(values):
    return lax.psum_scatter(
        values.astype(jnp.bfloat16), "tp", scatter_dimension=0, tiled=True
    ).astype(jnp.float32)


def shards(
    tokens,
    cotangent,
    step_embed,
    caption,
    lengths,
    group_bucket,
    null_mask,
    w_qkv,
    w_out,
    w_capkv,
    w_gateup,
    w_down,
    w_mod,
    b_mod,
    gain_attn,
    gain_ffn,
    gain_query,
    gain_key,
    gain_capkey,
    gate_head,
    null_embed,
):
    tp, cores, planes = lax.axis_size("tp"), lax.axis_size("core"), lax.axis_size("seq")
    me_t, me_c, me_z = lax.axis_index("tp"), lax.axis_index("core"), lax.axis_index("seq")
    groups = tp * cores
    rows, width = tokens.shape
    piece = rows // tp
    local_heads = HEADS // tp
    local = local_heads * HDIM
    cap_dev = caption.shape[2]
    ctx = caption.shape[3]
    my_group = me_z * cores + me_c

    numbers = jnp.concatenate([lengths[0], group_bucket, null_mask[0]])
    numbers = lax.all_gather(numbers, ("tp", "core"), axis=0, tiled=False).reshape(groups, -1)
    counts = jnp.sum(numbers[:, :DOCS], axis=1).astype(jnp.float32)
    mine = pick(numbers, my_group, 0)
    doc_lengths, bucket, nulls = mine[:DOCS], mine[DOCS], mine[DOCS + 1 :]
    bucket_count = jnp.sum(jnp.where(numbers[:, DOCS] == bucket, counts, 0.0))
    scale_loss = jnp.sum(counts) / (RES * bucket_count)

    steps = lax.all_gather(step_embed[0], ("tp", "core"), axis=0, tiled=True)
    condition = jax.nn.silu(steps.astype(jnp.float32)).astype(jnp.bfloat16)
    mod_rows = w_mod.shape[0]
    cond_mine = lax.dynamic_slice_in_dim(condition, me_z * mod_rows, mod_rows, 1)
    mod_all = matmul(cond_mine, w_mod).reshape(planes, cores * DOCS, -1)
    mod_plane = lax.psum_scatter(mod_all, "seq", scatter_dimension=0, tiled=False)
    mod_doc = pick(mod_plane.reshape(cores, DOCS, -1), me_c, 0) + b_mod

    qkv_part = pick(w_qkv.reshape(-1, 3, tp, local), me_t, 2).reshape(cores, -1, 3 * local)
    full_qkv = gather_rows(pick(qkv_part, me_c, 0))
    capkv_part = pick(w_capkv.reshape(-1, 2, tp, local), me_t, 2).reshape(cores, -1, 2 * local)
    full_capkv = gather_rows(pick(capkv_part, me_c, 0))
    gateup_part = pick(
        w_gateup.reshape(w_gateup.shape[0], 2 * planes, tp, -1), me_t, 2
    ).reshape(cores, w_gateup.shape[0] // cores, -1)
    full_gateup = gather_rows(pick(gateup_part, me_c, 0))
    down_part = pick(w_down.reshape(tp, cores, -1, width), me_t, 0)
    full_down = gather_rows(pick(down_part, me_c, 0))
    out_part = pick(w_out.reshape(w_out.shape[0], groups, -1), me_t * cores + me_c, 1)
    out_part = lax.all_gather(out_part, "seq", axis=0, tiled=False)
    out_part = lax.all_to_all(out_part, "tp", 0, 0, tiled=True)
    out_part = lax.all_gather(out_part, "core", axis=1, tiled=False)
    full_out = out_part.transpose(2, 0, 1, 3).reshape(local, width)

    inputs = to_plane(tokens).astype(jnp.float32)
    row = jnp.arange(rows, dtype=jnp.int32)
    spread = (row // piece) * rows + row % piece
    positions = spread + me_t * piece
    all_positions = (jnp.arange(tp, dtype=jnp.int32)[:, None] * piece + spread[None, :]).reshape(-1)
    segment, _, _ = layout(doc_lengths, bucket, positions)
    all_segment, row_pos, col_pos = layout(doc_lengths, bucket, all_positions)
    all_document = jnp.minimum(all_segment, DOCS - 1)
    document = jnp.minimum(segment, DOCS - 1)
    doc_pick = (document[:, None] == jnp.arange(DOCS, dtype=jnp.int32)[None, :]).astype(jnp.float32)
    is_valid = (segment < DOCS).astype(jnp.float32)
    modulation = jnp.dot(doc_pick, mod_doc, precision=lax.Precision.HIGHEST)
    scale_a, gate_a, scale_f, gate_f = jnp.split(modulation, 4, axis=1)
    tanh_a, tanh_f = jnp.tanh(gate_a), jnp.tanh(gate_f)

    normed1, inverse1 = row_stats(inputs)
    hidden1 = plane_gather((normed1 * gain_attn * (1.0 + scale_a)).astype(jnp.bfloat16))
    projected = matmul(hidden1, full_qkv)
    query_raw, key_raw, value_raw = jnp.split(projected, 3, axis=1)
    query_norm, query_inv = head_stats(query_raw)
    key_norm, key_inv = head_stats(key_raw)
    my_gain_query = pick(gain_query.reshape(tp, local), me_t, 0)
    my_gain_key = pick(gain_key.reshape(tp, local), me_t, 0)
    my_gain_capkey = pick(gain_capkey.reshape(tp, local), me_t, 0)
    query = rotary(query_norm * my_gain_query, row_pos, col_pos, 1.0).astype(jnp.bfloat16)
    keys = rotary(key_norm * my_gain_key, row_pos, col_pos, 1.0).astype(jnp.bfloat16)
    values = value_raw.astype(jnp.bfloat16)

    captions = to_plane(caption[0].transpose(1, 0, 2)).transpose(1, 0, 2)
    capmix = jnp.where(nulls[:, None, None] > 0, null_embed[None, None, :], captions)
    cap_flat = plane_gather(capmix.reshape(DOCS * cap_dev, ctx))
    cap_document = jnp.tile(jnp.repeat(jnp.arange(DOCS, dtype=jnp.int32), cap_dev), tp)
    cap_proj = matmul(cap_flat, full_capkv)
    capkey_raw, capval_raw = jnp.split(cap_proj, 2, axis=1)
    capkey_norm, capkey_inv = head_stats(capkey_raw)
    capkeys = (capkey_norm * my_gain_capkey).astype(jnp.bfloat16)
    capvals = capval_raw.astype(jnp.bfloat16)

    self_allowed = all_segment[:, None] == all_segment[None, :]
    cross_allowed = all_document[:, None] == cap_document[None, :]
    own_out, own_log = attend_forward(query, keys, values, self_allowed)
    cross_out, cross_log = attend_forward(query, capkeys, capvals, cross_allowed)
    gate_tanh = pick(jnp.tanh(gate_head).reshape(tp, local_heads), me_t, 0)
    head_gate = jnp.repeat(gate_tanh, HDIM)[None, :]
    mixed_attn = (own_out + head_gate * cross_out).astype(jnp.bfloat16)
    attn_out = plane_scatter(matmul(mixed_attn, full_out))
    residual = inputs + tanh_a * attn_out
    normed2, inverse2 = row_stats(residual)
    hidden2 = plane_gather((normed2 * gain_ffn * (1.0 + scale_f)).astype(jnp.bfloat16))
    gate_part, up_part = jnp.split(matmul(hidden2, full_gateup), 2, axis=1)
    sig_gate = jax.nn.sigmoid(gate_part)
    silu_gate = gate_part * sig_gate
    hidden_ffn = (silu_gate * up_part).astype(jnp.bfloat16)
    down_out = plane_scatter(matmul(hidden_ffn, full_down))
    result = from_plane((residual + tanh_f * down_out).astype(jnp.bfloat16))

    grad_res0 = to_plane(cotangent).astype(jnp.float32) * (is_valid * scale_loss)[:, None]
    grad_down = plane_gather((tanh_f * grad_res0).astype(jnp.bfloat16))
    grad_gate_f = grad_res0 * down_out * (1.0 - tanh_f * tanh_f)
    grad_ffn = contract_right(grad_down, full_down)
    grad_gate_part = grad_ffn * up_part * sig_gate * (1.0 + gate_part * (1.0 - sig_gate))
    grad_up_part = grad_ffn * silu_gate
    grad_gateup = jnp.concatenate([grad_gate_part, grad_up_part], axis=1).astype(jnp.bfloat16)
    grad_hidden2 = plane_scatter(contract_right(grad_gateup, full_gateup))
    gain_ffn_term = jnp.sum(grad_hidden2 * normed2 * (1.0 + scale_f), axis=0)
    grad_scale_f = grad_hidden2 * normed2 * gain_ffn
    grad_residual = grad_res0 + norm_back(
        grad_hidden2 * gain_ffn * (1.0 + scale_f), normed2, inverse2
    )
    grad_attn = plane_gather((tanh_a * grad_residual).astype(jnp.bfloat16))
    grad_gate_a = grad_residual * attn_out * (1.0 - tanh_a * tanh_a)
    grad_mix = contract_right(grad_attn, full_out)
    grad_own = grad_mix.astype(jnp.bfloat16)
    grad_cross = (head_gate * grad_mix).astype(jnp.bfloat16)
    gate_head_term = jnp.sum(
        (grad_mix * cross_out).reshape(-1, local_heads, HDIM), axis=(0, 2)
    ) * (1.0 - gate_tanh * gate_tanh)
    query_own, grad_keys, grad_values = attend_backward(
        query, keys, values, self_allowed, own_log, grad_own
    )
    query_cross, grad_capkeys, grad_capvals = attend_backward(
        query, capkeys, capvals, cross_allowed, cross_log, grad_cross
    )
    grad_query = rotary(query_own + query_cross, row_pos, col_pos, -1.0)
    gain_query_term = jnp.sum(grad_query * query_norm, axis=0)
    grad_query_raw = head_back(grad_query * my_gain_query, query_norm, query_inv)
    grad_key = rotary(grad_keys, row_pos, col_pos, -1.0)
    gain_key_term = jnp.sum(grad_key * key_norm, axis=0)
    grad_key_raw = head_back(grad_key * my_gain_key, key_norm, key_inv)
    grad_projected = jnp.concatenate([grad_query_raw, grad_key_raw, grad_values], axis=1).astype(
        jnp.bfloat16
    )
    grad_hidden1 = plane_scatter(contract_right(grad_projected, full_qkv))
    gain_attn_term = jnp.sum(grad_hidden1 * normed1 * (1.0 + scale_a), axis=0)
    grad_scale_a = grad_hidden1 * normed1 * gain_attn
    input_grad = from_plane(
        (
            grad_residual + norm_back(grad_hidden1 * gain_attn * (1.0 + scale_a), normed1, inverse1)
        ).astype(jnp.bfloat16)
    )

    grad_mod_tok = jnp.concatenate([grad_scale_a, grad_gate_a, grad_scale_f, grad_gate_f], axis=1)
    grad_mod_doc = lax.dot_general(
        doc_pick,
        grad_mod_tok,
        (((0,), (0,)), ((), ())),
        precision=lax.Precision.HIGHEST,
        preferred_element_type=jnp.float32,
    )
    grad_mod_doc = lax.psum(grad_mod_doc, "tp")
    grad_mod_docs = lax.all_gather(grad_mod_doc, ("seq", "core"), axis=0, tiled=True)
    sum_mod = lax.dot_general(
        cond_mine.astype(jnp.float32),
        grad_mod_docs,
        (((0,), (0,)), ((), ())),
        precision=lax.Precision.HIGHEST,
        preferred_element_type=jnp.float32,
    )
    sum_bias = jnp.sum(grad_mod_docs, axis=0)

    gain_capkey_term = jnp.sum(grad_capkeys * capkey_norm, axis=0)
    grad_capkey_raw = head_back(grad_capkeys * my_gain_capkey, capkey_norm, capkey_inv)
    grad_cap_proj = jnp.concatenate([grad_capkey_raw, grad_capvals], axis=1).astype(jnp.bfloat16)
    null_rows = nulls[cap_document] > 0
    null_sum = jnp.sum(
        jnp.where(null_rows[:, None], grad_cap_proj.astype(jnp.float32), 0.0), axis=0
    )
    null_term = jnp.dot(
        full_capkv.astype(jnp.float32), null_sum, precision=lax.Precision.HIGHEST
    )

    term_down = scatter_rows(contract_rows(hidden_ffn, grad_down))
    sum_down = lax.all_gather(term_down, ("tp", "core"), axis=0, tiled=True)
    term_gateup = scatter_rows(contract_rows(hidden2, grad_gateup))
    term_gateup = lax.all_gather(term_gateup, ("tp", "core"), axis=0, tiled=False)
    sum_gateup = (
        term_gateup.reshape(tp, cores, w_gateup.shape[0] // cores, 2 * planes, -1)
        .transpose(1, 2, 3, 0, 4)
        .reshape(w_gateup.shape)
    )
    term_out = contract_rows(mixed_attn, grad_attn).astype(jnp.bfloat16)
    term_out = term_out.reshape(local, tp, cores, -1).transpose(1, 2, 0, 3)
    term_out = lax.psum_scatter(term_out, "core", scatter_dimension=1, tiled=False)
    term_out = lax.all_to_all(term_out, "tp", 0, 0, tiled=True)
    term_out = lax.psum_scatter(term_out, "seq", scatter_dimension=0, tiled=False)
    sum_out = lax.all_gather(term_out, ("tp", "core"), axis=1, tiled=True)
    term_qkv = scatter_rows(contract_rows(hidden1, grad_projected))
    term_qkv = lax.all_gather(term_qkv, ("tp", "core"), axis=0, tiled=False)
    sum_qkv = (
        term_qkv.reshape(tp, cores, w_qkv.shape[0] // cores, 3, local)
        .transpose(1, 2, 3, 0, 4)
        .reshape(w_qkv.shape)
    )
    term_capkv = scatter_rows(contract_rows(cap_flat, grad_cap_proj))
    term_capkv = lax.all_gather(term_capkv, ("tp", "core"), axis=0, tiled=False)
    sum_capkv = (
        term_capkv.reshape(tp, cores, w_capkv.shape[0] // cores, 2, local)
        .transpose(1, 2, 3, 0, 4)
        .reshape(w_capkv.shape)
    )

    def at_mine(part):
        whole = jnp.zeros((tp,) + part.shape, jnp.float32)
        return lax.dynamic_update_index_in_dim(whole, part, me_t, 0).reshape(-1)

    small = lax.psum(
        jnp.concatenate(
            [
                gain_attn_term,
                gain_ffn_term,
                at_mine(gain_query_term),
                at_mine(gain_key_term),
                at_mine(gain_capkey_term),
                at_mine(gate_head_term),
                null_term,
            ]
        ),
        ("tp", "core", "seq"),
    )
    ends = [width, 2 * width, 3 * width, 4 * width, 5 * width, 5 * width + HEADS]
    small_parts = jnp.split(small, ends)
    f32 = jnp.float32
    return (
        result,
        input_grad,
        sum_qkv.astype(f32),
        sum_out.astype(f32),
        sum_capkv.astype(f32),
        sum_gateup.astype(f32),
        sum_down.astype(f32),
        sum_mod,
        sum_bias,
        *small_parts,
    )


def solution(mesh):
    planes = mesh.shape["seq"]
    cores = mesh.shape["bucket"] // planes
    split = Mesh(mesh.devices.reshape(planes, cores, planes), ("tp", "core", "seq"))
    group = ("tp", "core")
    token = P(("tp", "core", "seq"), None)
    weight = P("seq", None)
    placed = (
        token,
        token,
        P(group, None, None),
        P(group, None, "seq", None),
        P(group, None),
        P(group),
        P(group, None),
        *([weight] * 6),
        *([P()] * 8),
    )
    return jax.shard_map(
        shards,
        mesh=split,
        in_specs=placed,
        out_specs=(token, token, *([weight] * 6), *([P()] * 8)),
        check_vma=False,
    )
```

time: 4330 us -> 1680 us (0.39)
  waiting for transfers between devices: 3630 us -> 698 us
  blocking collectives: 14.6 us -> 200 us
  local copies, waits for them, and re-layouts: 149 us -> 300 us
  matrix products: 394 us -> 311 us
    all_gather x10 -> x19, waiting for transfers between devices: 1640 us -> 222 us  [the longest x5 128 us: plane_gather(): return lax.all_gather(values, 'tp', axis=0, tiled=True)]
    reduce_scatter x10 -> x12, waiting for transfers between devices: 1610 us -> 340 us  [the longest x4 173 us: scatter_rows(): return lax.psum_scatter(half, 'seq', scatter_dimension=0, tiled=False)]
    psum x2 -> x1, waiting for transfers between devices: 373 us -> 0.01 us  [shards(): grad_mod_doc = lax.psum(grad_mod_doc, 'tp')]
    all_to_all x0 -> x5, blocking collectives: none -> 101 us  [the longest x2 51.7 us: to_plane(): parts = lax.all_to_all(parts, 'tp', 0, 0, tiled=True)]
    all_to_all x0 -> x7, waiting for transfers between devices: none -> 91.6 us  [the longest x3 73.7 us: to_plane(): parts = lax.all_to_all(parts, 'seq', 0, 0, tiled=True)]
    convert_element_type x7 -> x9, local copies, waits for them, and re-layouts: 28.3 us -> 105 us  [the longest x3 46 us: shards(): sum_capkv.astype(f32)]
    all_gather x0 -> x3, blocking collectives: none -> 51.4 us  [the longest x1 24.8 us: shards(): out_part = lax.all_gather(out_part, 'seq', axis=0, tiled=False)]
    dot_general x14 -> x13, matrix products: 144 us -> 93.4 us  [the longest x6 44.9 us: matmul(): return jnp.dot(left, right, preferred_element_type=jnp.float32)]
  transfers between devices with their start and end apart: 22 -> 40, of which waited for: 19 -> 23; matrix products, arithmetic and copies ran while one was open for 11% -> 37% of each run, Pallas kernels for 0% -> 0%
where the time goes in v1:
time: 1680 us; the launch traced here: 1660 us
  waiting for transfers between devices  698 us (42%)
  matrix products  311 us (19%)
  local copies, waits for them, and re-layouts  300 us (18%)
  blocking collectives  200 us (12%)
  other arithmetic  102 us (6%)
  starting transfers between devices  32.5 us (2%)
  between operations  19.2 us (1%)
    reduce_scatter x4, waiting for transfers between devices, scatter_rows(): return lax.psum_scatter(half, 'seq', scatter_dimension=0, tiled=False)  173 us
    reduce_scatter x4, waiting for transfers between devices, plane_scatter(): lax.psum_scatter(values.astype(jnp.bfloat16), 'tp', scatter_dimension=0,...  144 us
    all_gather x5, waiting for transfers between devices, plane_gather(): return lax.all_gather(values, 'tp', axis=0, tiled=True)  128 us
    all_to_all x3, waiting for transfers between devices, to_plane(): parts = lax.all_to_all(parts, 'seq', 0, 0, tiled=True)  73.7 us
    all_to_all x2, blocking collectives, to_plane(): parts = lax.all_to_all(parts, 'tp', 0, 0, tiled=True)  51.7 us
    dot_general x24, matrix products, block(): jnp.einsum('qhd,khd->hqk', part_q, part_k, preferred_element_type=jnp.flo...  49.6 us
    convert_element_type x3, local copies, waits for them, and re-layouts, shards(): sum_capkv.astype(f32)  46 us
    dot_general x6, matrix products, matmul(): return jnp.dot(left, right, preferred_element_type=jnp.float32)  44.9 us
  transfers between devices with their start and end apart: 40, of which 23 were waited for; matrix products, arithmetic and copies ran while one was open for 37% of the time, Pallas kernels for 0%

profile of v1, /device:TPU:0, one launch (start us, length us, event | category | flops | bytes accessed | tf_op | source)
XLA Modules:
  0.0 1664.0 jit_solution(17814980246791510493)
XLA Ops:
  77.8 24.8 %all-gather.4 = bf16[1536,1,192]{0,2,1:T(8,128)(2,1)} all-gather(bf16[384,1,192]{0,2,1:T(8,128)(2,1)S(1)} %constant_dynamic-slice_fusion.4), channel_id=6, replica_groups=mesh['tp'=4,'core'=2,'seq'=4] {'seq'}, dimensions={0}, use_global_device_ids=true | all-gather | bytes 737280 | tf_op jit(solution)/shard_map/all_gather | solution.py:252
  150.3 26.8 %all-to-all-done.1 = bf16[4,64,1536]{2,1,0:T(8,128)(2,1)} async-done(((bf16[4,64,1536]{2,1,0:T(8,128)(2,1)}), bf16[4,64,1536]{2,1,0:T(8,128)(2,1)}, u32[]{:S(2)}, u32[]{:S(2)}) %all-to-all-start.1) | async-done | bytes 786464 | tf_op jit(solution)/shard_map/all_to_all | solution.py:156
  187.1 28.9 %all_to_all.61 = bf16[4,16,4,4096]{3,1,2,0:T(8,128)(2,1)} all-to-all(bf16[4,16,4,4096]{3,1,2,0:T(8,128)(2,1)S(1)} %copy.269), channel_id=1, replica_groups=mesh['tp'=4,'core'=2,'seq'=4] {'tp'}, dimensions={0} | all-to-all | bytes 4194304 | tf_op jit(solution)/shard_map/all_to_all | solution.py:155
  220.6 46.9 %all-to-all-done.3 = bf16[4,16,4,4096]{3,1,2,0:T(8,128)(2,1)} async-done(((bf16[4,16,4,4096]{3,1,2,0:T(8,128)(2,1)}), bf16[4,16,4,4096]{3,1,2,0:T(8,128)(2,1)}, u32[]{:S(2)}, u32[]{:S(2)}) %all-to-all-start.3) | async-done | bytes 2097184 | tf_op jit(solution)/shard_map/all_to_all | solution.py:156
  361.3 34.8 %while.56 = (s32[]{:T(128)}, f32[6,1024,1,64]{1,3,2,0:T(8,128)}, f32[6,1,1024]{2,1,0:T(1,128)S(1)}, bf16[6,1024,1,64]{1,3,2,0:T(8,128)(2,1)}, bf16[6,1024,1,64]{...) while((s32[]{:T(128)}, f32[6,1024,1,64]{1,3,2,0:T(8,128)}, ...), condition=%wide.region_11.12_spmd.clone, body=%wide.region_8.11_spmd.clone.sunk | while | flops 284163072 | bytes 13301849 | solution.py:90
  412.3 34.7 %while.57 = (s32[]{:T(128)}, f32[6,1024,1,64]{1,3,2,0:T(8,128)}, f32[6,1,1024]{2,1,0:T(1,128)S(1)}, bf16[6,1024,1,64]{1,3,2,0:T(8,128)(2,1)}, bf16[6,1024,1,64]{...) while((s32[]{:T(128)}, f32[6,1024,1,64]{1,3,2,0:T(8,128)}, ...), condition=%wide.region_16.17_spmd.clone, body=%wide.region_13.16_spmd.clone.sunk | while | flops 284163072 | bytes 13305953 | solution.py:90
  454.9 22.8 %all_to_all.62 = bf16[4,64,1536]{2,1,0:T(8,128)(2,1)} all-to-all(bf16[4,64,1536]{2,1,0:T(8,128)(2,1)S(1)} %bitcast.580), channel_id=1, replica_groups=mesh['tp'=4,'core'=2,'seq'=4] {'tp'}, dimensions={0} | all-to-all | bytes 1572864 | tf_op jit(solution)/shard_map/all_to_all | solution.py:155
  484.2 16.2 reduce-scatter.24.cloned.1.call-done
  506.4 33.2 %all-gather.62.cloned.1.call-done = bf16[4,1,128,1536]{3,2,1,0:T(8,128)(2,1)} async-done(((bf16[1,1,128,1536]{3,2,1,0:T(8,128)(2,1)}), bf16[4,1,128,1536]{3,2,1,0:T(8,128)(2,1)}) %all-gather.62.cloned.1.call-update) | async-done | bytes 1572880 | tf_op jit(solution)/shard_map/all_gather | solution.py:169
  540.2 16.4 all-gather.60.cloned.1.call-done
  556.6 47.6 %all-gather.40.cloned.1.call-done = bf16[1024,1536]{1,0:T(8,128)(2,1)} async-done(((bf16[256,1536]{1,0:T(8,128)(2,1)}), bf16[1024,1536]{1,0:T(8,128)(2,1)}) %all-gather.40.cloned.1.call-update) | async-done | bytes 3145744 | tf_op jit(solution)/shard_map/all_gather | solution.py:182
  617.8 47.4 %all-gather.44.cloned.1.call-done = bf16[1024,1536]{1,0:T(8,128)(2,1)} async-done(((bf16[256,1536]{1,0:T(8,128)(2,1)}), bf16[1024,1536]{1,0:T(8,128)(2,1)}) %all-gather.44.cloned.1.call-update) | async-done | bytes 3145744 | tf_op jit(solution)/shard_map/all_gather | solution.py:182
  694.7 36.4 %reduce-scatter.28.cloned.1.call-done = bf16[256,1536]{1,0:T(8,128)(2,1)} async-done(((bf16[1024,1536]{1,0:T(8,128)(2,1)}), bf16[256,1536]{1,0:T(8,128)(2,1)}) %reduce-scatter.28.cloned.1.call-update) | async-done | bytes 786448 | tf_op jit(solution)/shard_map/reduce_scatter | solution.py:186
  734.0 44.4 %reduce-scatter.26.cloned.1.call-done = bf16[256,1536]{1,0:T(8,128)(2,1)} async-done(((bf16[1024,1536]{1,0:T(8,128)(2,1)}), bf16[256,1536]{1,0:T(8,128)(2,1)}) %reduce-scatter.26.cloned.1.call-update) | async-done | bytes 786448 | tf_op jit(solution)/shard_map/reduce_scatter | solution.py:186
  798.9 32.7 %all-gather.46.cloned.1.call-done = bf16[1024,1536]{1,0:T(8,128)(2,1)} async-done(((bf16[256,1536]{1,0:T(8,128)(2,1)}), bf16[1024,1536]{1,0:T(8,128)(2,1)}) %all-gather.46.cloned.1.call-update) | async-done | bytes 3145744 | tf_op jit(solution)/shard_map/all_gather | solution.py:182
  840.5 67.9 %while.59 = (s32[]{:T(128)}, f32[6,1024,1,64]{1,3,2,0:T(8,128)}, f32[6,1024,1,64]{1,3,2,0:T(8,128)}, bf16[6,1024,1,64]{1,3,2,0:T(8,128)(2,1)}, bf16[6,1024,1,64]...) while((s32[]{:T(128)}, f32[6,1024,1,64]{1,3,2,0:T(8,128)}, ...), condition=%wide.region_30.31_spmd.clone, body=%wide.region_28.30_spmd.clone.sunk | while | flops 681704448 | bytes 39486640 | solution.py:125
  911.0 70.9 %while.58 = (s32[]{:T(128)}, f32[6,1024,1,64]{1,3,2,0:T(8,128)}, f32[6,1024,1,64]{1,3,2,0:T(8,128)}, bf16[6,1024,1,64]{1,3,2,0:T(8,128)(2,1)}, bf16[6,1024,1,64]...) while((s32[]{:T(128)}, f32[6,1024,1,64]{1,3,2,0:T(8,128)}, ...), condition=%wide.region_27.28_spmd.clone, body=%wide.region_25.27_spmd.clone.sunk | while | flops 681704448 | bytes 33195120 | solution.py:125
  1051.9 41.6 %all-reduce.10.cloned.1.call-done = (bf16[4,2,512,768]{3,2,1,0:T(8,128)(2,1)}, bf16[4,2,384,192]{2,3,1,0:T(8,128)(2,1)}, bf16[4,2,192,2048]{3,2,1,0:T(8,128)(2,1)}) async-done(((bf16[4,2,512,768]{3,2,1,0:T(8,128)(2,1)}, bf16[4,2,384,192]{2,3,1,0:T(8,128)(2,1)}, bf16[4,2,192,2048]{3,2,1,0:T(8,128)(2,1)}), (bf16[4,2,512,768]{3,2,1,0:T(8,128)(2,1)}, bf16[4,2,384,192]{2,3,1,0:T(8,128)(2,1)}, ...) | async-done | bytes 13762576
  1118.2 14.2 reduce-scatter.44.cloned.1.call-done
  1132.6 46.6 %reduce-scatter.30.cloned.1.call-done = bf16[256,1536]{1,0:T(8,128)(2,1)} async-done(((bf16[1024,1536]{1,0:T(8,128)(2,1)}), bf16[256,1536]{1,0:T(8,128)(2,1)}) %reduce-scatter.30.cloned.1.call-update) | async-done | bytes 786448 | tf_op jit(solution)/shard_map/reduce_scatter | solution.py:186
  1185.2 34.7 %reduce-scatter.34.cloned.1.call-done = bf16[1,192,1152]{2,1,0:T(8,128)(2,1)} async-done(((bf16[4,192,1152]{2,1,0:T(8,128)(2,1)}), bf16[1,192,1152]{2,1,0:T(8,128)(2,1)}) %reduce-scatter.34.cloned.1.call-update) | async-done | bytes 442384 | tf_op jit(solution)/shard_map/reduce_scatter | solution.py:178
  1220.0 23.3 %reduce-scatter.36.cloned.1.call-done = bf16[1,384,192]{1,2,0:T(8,128)(2,1)} async-done(((bf16[4,384,192]{1,2,0:T(8,128)(2,1)}), bf16[1,384,192]{1,2,0:T(8,128)(2,1)}) %reduce-scatter.36.cloned.1.call-update) | async-done | bytes 147472 | tf_op jit(solution)/shard_map/reduce_scatter | solution.py:401
  1243.4 61.3 %reduce-scatter.38.cloned.1.call-done = bf16[1,512,768]{2,1,0:T(8,128)(2,1)} async-done(((bf16[4,512,768]{2,1,0:T(8,128)(2,1)}), bf16[1,512,768]{2,1,0:T(8,128)(2,1)}) %reduce-scatter.38.cloned.1.call-update) | async-done | bytes 786448 | tf_op jit(solution)/shard_map/reduce_scatter | solution.py:178
  1304.7 63.0 %reduce-scatter.40.cloned.1.call-done = bf16[1,192,2048]{2,1,0:T(8,128)(2,1)} async-done(((bf16[4,192,2048]{2,1,0:T(8,128)(2,1)}), bf16[1,192,2048]{2,1,0:T(8,128)(2,1)}) %reduce-scatter.40.cloned.1.call-update) | async-done | bytes 786448 | tf_op jit(solution)/shard_map/reduce_scatter | solution.py:178
  1367.7 23.8 %all_to_all.64 = bf16[4,64,1536]{2,1,0:T(8,128)(2,1)} all-to-all(bf16[4,64,1536]{2,1,0:T(8,128)(2,1)S(1)} %bitcast.569), channel_id=1, replica_groups=mesh['tp'=4,'core'=2,'seq'=4] {'seq'}, dimensions={0} | all-to-all | bytes 1572864 | tf_op jit(solution)/shard_map/all_to_all | solution.py:163
  1433.0 40.3 %psum.15 = f32[11800]{0:T(1024)S(1)} all-reduce(f32[11800]{0:T(1024)S(1)} %concatenate.90), channel_id=1, replica_groups=mesh['tp'=4,'core'=2,'seq'=4] {'tp','core','seq'}, use_global_device_ids=true, to_apply=%region_56.57 | all-reduce | flops 11800 | bytes 94400 | tf_op jit(solution)/shard_map/psum | solution.py:422
  1479.6 15.9 all-gather.11
  1535.6 37.8 %all-gather.50.cloned.1.call-done = bf16[8,512,768]{2,1,0:T(8,128)(2,1)} async-done(((bf16[1,512,768]{2,1,0:T(8,128)(2,1)}), bf16[8,512,768]{2,1,0:T(8,128)(2,1)}) %all-gather.50.cloned.1.call-update) | async-done | bytes 6291472 | tf_op jit(solution)/shard_map/all_gather | solution.py:411
  1573.4 13.9 reshape.935
  1587.3 16.6 copy.301
  1603.9 15.5 reshape.932
  1638.1 15.8 reshape.933
  (629 shorter events, 755.2 us)
Async XLA Ops:
  7.2 110.7 %all-gather.34.cloned.1.call-start = ((), (), s32[]{:S(2)}) async-start(), calls=%async_computation.26 | async-start | bytes 2211840 | tf_op jit(solution)/shard_map/all_gather | solution.py:169
  27.1 117.6 %reduce-scatter.22.cloned.1.call-start = ((), (), s32[]{:S(2)}) async-start(), calls=%async_computation.24 | async-start | bytes 983040 | tf_op jit(solution)/shard_map/reduce_scatter | solution.py:238
  41.5 143.9 %all-gather.38.cloned.1.call-start = ((), (), s32[]{:S(2)}) async-start(), calls=%async_computation.28 | async-start | bytes 3932160 | tf_op jit(solution)/shard_map/all_gather | solution.py:169
  74.5 230.6 %all-gather.58.cloned.1.call-start = ((), (), s32[]{:S(2)}) async-start(), calls=%async_computation.50 | async-start | bytes 1769472 | tf_op jit(solution)/shard_map/all_gather | solution.py:254
  117.8 193.3 %all-gather.54.cloned.1.call-start = ((), (), s32[]{:S(2)}) async-start(), calls=%async_computation.48 | async-start | bytes 5308416 | tf_op jit(solution)/shard_map/all_gather | solution.py:170
  136.8 174.3 %all-gather.32.cloned.1.call-start = ((), (), s32[]{:S(2)}) async-start(), calls=%async_computation.25 | async-start | bytes 3932160 | tf_op jit(solution)/shard_map/all_gather | solution.py:182
  181.5 214.7 %all-gather.56.cloned.1.call-start = ((), (), s32[]{:S(2)}) async-start(), calls=%async_computation.49 | async-start | bytes 9437184 | tf_op jit(solution)/shard_map/all_gather | solution.py:170
  220.5 175.7 %all-gather.36.cloned.1.call-start = ((), (), s32[]{:S(2)}) async-start(), calls=%async_computation.27 | async-start | bytes 10485760 | tf_op jit(solution)/shard_map/all_gather | solution.py:182
  271.2 182.6 %all-gather.42.cloned.1.call-start = ((), (), s32[]{:S(2)}) async-start(), calls=%async_computation.31 | async-start | bytes 3932160 | tf_op jit(solution)/shard_map/all_gather | solution.py:169
  300.5 199.8 %reduce-scatter.24.cloned.1.call-start = ((), (), s32[]{:S(2)}) async-start(), calls=%async_computation.29 | async-start | bytes 3932160 | tf_op jit(solution)/shard_map/reduce_scatter | solution.py:186
  452.9 86.6 %all-gather.62.cloned.1.call-start = ((), (), s32[]{:S(2)}) async-start(), calls=%async_computation.52 | async-start | bytes 1966080 | tf_op jit(solution)/shard_map/all_gather | solution.py:169
  453.8 102.8 %all-gather.60.cloned.1.call-start = ((), (), s32[]{:S(2)}) async-start(), calls=%async_computation.51 | async-start | bytes 9437184 | tf_op jit(solution)/shard_map/all_gather | solution.py:170
  481.2 123.0 %all-gather.40.cloned.1.call-start = ((), (), s32[]{:S(2)}) async-start(), calls=%async_computation.30 | async-start | bytes 3932160 | tf_op jit(solution)/shard_map/all_gather | solution.py:182
  506.4 111.4 %all-gather.64.cloned.1.call-start = ((), (), s32[]{:S(2)}) async-start(), calls=%async_computation.53 | async-start | bytes 4718592 | tf_op jit(solution)/shard_map/all_gather | solution.py:170
  539.6 125.6 %all-gather.44.cloned.1.call-start = ((), (), s32[]{:S(2)}) async-start(), calls=%async_computation.33 | async-start | bytes 3932160 | tf_op jit(solution)/shard_map/all_gather | solution.py:182
  540.2 190.9 %reduce-scatter.28.cloned.1.call-start = ((), (), s32[]{:S(2)}) async-start(), calls=%async_computation.34 | async-start | bytes 3932160 | tf_op jit(solution)/shard_map/reduce_scatter | solution.py:186
  686.9 91.5 %reduce-scatter.26.cloned.1.call-start = ((), (), s32[]{:S(2)}) async-start(), calls=%async_computation.32 | async-start | bytes 3932160 | tf_op jit(solution)/shard_map/reduce_scatter | solution.py:186
  694.6 137.1 %all-gather.46.cloned.1.call-start = ((), (), s32[]{:S(2)}) async-start(), calls=%async_computation.35 | async-start | bytes 3932160 | tf_op jit(solution)/shard_map/all_gather | solution.py:182
  787.6 254.0 %reduce-scatter.42.cloned.1.call-start = ((), (), s32[]{:S(2)}) async-start(), calls=%async_computation.45 | async-start | bytes 4718592 | tf_op jit(solution)/shard_map/reduce_scatter | solution.py:177
  798.9 251.9 %reduce-scatter.32.cloned.1.call-start = ((), (), s32[]{:S(2)}) async-start(), calls=%async_computation.37 | async-start | bytes 5308416 | tf_op jit(solution)/shard_map/reduce_scatter | solution.py:177
  1041.5 90.9 %reduce-scatter.44.cloned.1.call-start = ((), (), s32[]{:S(2)}) async-start(), calls=%async_computation.46 | async-start | bytes 1966080 | tf_op jit(solution)/shard_map/reduce_scatter | solution.py:178
  1042.2 137.0 %reduce-scatter.30.cloned.1.call-start = ((), (), s32[]{:S(2)}) async-start(), calls=%async_computation.36 | async-start | bytes 3932160 | tf_op jit(solution)/shard_map/reduce_scatter | solution.py:186
  1050.7 169.2 %reduce-scatter.34.cloned.1.call-start = ((), (), s32[]{:S(2)}) async-start(), calls=%async_computation.38 | async-start | bytes 2211840 | tf_op jit(solution)/shard_map/reduce_scatter | solution.py:178
  1051.3 192.1 %reduce-scatter.36.cloned.1.call-start = ((), (), s32[]{:S(2)}) async-start(), calls=%async_computation.40 | async-start | bytes 737280 | tf_op jit(solution)/shard_map/reduce_scatter | solution.py:401
  1109.0 195.7 %reduce-scatter.38.cloned.1.call-start = ((), (), s32[]{:S(2)}) async-start(), calls=%async_computation.41 | async-start | bytes 3932160 | tf_op jit(solution)/shard_map/reduce_scatter | solution.py:178
  1113.4 254.2 %reduce-scatter.40.cloned.1.call-start = ((), (), s32[]{:S(2)}) async-start(), calls=%async_computation.43 | async-start | bytes 3932160 | tf_op jit(solution)/shard_map/reduce_scatter | solution.py:178
  1118.2 309.3 %all-gather.68.cloned.1.call-start = ((), (), s32[]{:S(2)}) async-start(), calls=%async_computation.55 | async-start | bytes 3538944 | tf_op jit(solution)/shard_map/all_gather | solution.py:389
  1132.4 347.2 %all-reduce.8.cloned.1.call-start = ((), (), s32[]{:S(2)}) async-start(), calls=%async_computation.47 | async-start | bytes 196608 | tf_op jit(solution)/shard_map/psum | solution.py:366
  1185.1 317.0 %all-gather.48.cloned.1.call-start = ((), (), s32[]{:S(2)}) async-start(), calls=%async_computation.39 | async-start | bytes 3981312 | tf_op jit(solution)/shard_map/all_gather | solution.py:404
  1219.9 312.3 %all-gather.66.cloned.1.call-start = ((), (), s32[]{:S(2)}) async-start(), calls=%async_computation.54 | async-start | bytes 1327104 | tf_op jit(solution)/shard_map/all_gather | solution.py:402
  1243.3 330.1 %all-gather.50.cloned.1.call-start = ((), (), s32[]{:S(2)}) async-start(), calls=%async_computation.42 | async-start | bytes 7077888 | tf_op jit(solution)/shard_map/all_gather | solution.py:411
  1304.7 316.2 %all-gather.52.cloned.1.call-start = ((), (), s32[]{:S(2)}) async-start(), calls=%async_computation.44 | async-start | bytes 7077888 | tf_op jit(solution)/shard_map/all_gather | solution.py:391
  (101 other events, 2038.5 us)
Sparse Core Ops, SparseCore 0:
  27.2 43.0 all-gather.33
  73.2 31.4 reduce-scatter.21
  106.8 78.5 all-gather.37
  195.9 13.8 all-gather.53
  212.1 45.1 all-gather.31
  258.8 16.7 all-gather.55
  278.0 88.7 all-gather.35
  368.4 63.4 all-gather.41
  453.1 47.2 reduce-scatter.23
  502.5 37.0 all-gather.61
  541.0 15.6 all-gather.59
  559.0 45.1 all-gather.39
  605.6 12.1 all-gather.63
  620.0 45.1 all-gather.43
  687.1 43.9 reduce-scatter.27
  734.5 43.9 reduce-scatter.25
  787.7 43.9 all-gather.45
  833.9 10.8 reduce-scatter.41
  1011.7 11.3 reduce-scatter.31
  1041.6 51.8 all-reduce.9
  1095.9 36.4 reduce-scatter.43
  1136.2 42.9 reduce-scatter.29
  1181.5 38.3 reduce-scatter.33
  1222.2 21.0 reduce-scatter.35
  1246.0 58.5 reduce-scatter.37
  1307.4 60.2 reduce-scatter.39
  1369.6 39.6 all-gather.67
  1412.7 42.0 all-reduce.7
  1456.7 42.9 all-gather.47
  1501.7 24.0 all-gather.65
  1527.8 45.5 all-gather.49
  1575.3 45.5 all-gather.51
  (1 shorter events, 7.7 us)

commit v2 on v1

--- a/solution.py
+++ b/solution.py
@@ -1,6 +1,10 @@
+import functools
+
 import jax
 import jax.numpy as jnp
 from jax import lax
+from jax.experimental import pallas as pl
+from jax.experimental.pallas import tpu as pltpu
 from jax.sharding import Mesh, PartitionSpec as P
 
 HEADS = 24
@@ -10,6 +14,484 @@
 
 
 eps = 1e-06
+
+MESH = pl.DeviceIdType.MESH
+VMEM_BYTES = 60 * 1024 * 1024
+
+
+def neighbours():
+    me = lax.axis_index("tp")
+    return me, me + 1 - 2 * lax.rem(me, 2), lax.rem(me + 2, 4), 3 - me
+
+
+def greet(places):
+    barrier = pltpu.get_barrier_semaphore()
+    for place in places:
+        pl.semaphore_signal(barrier, inc=1, device_id=place, device_id_type=MESH)
+    pl.semaphore_wait(barrier, len(places))
+
+
+def send(source, target, sems, index, place):
+    return pltpu.make_async_remote_copy(
+        src_ref=source,
+        dst_ref=target,
+        send_sem=sems[0].at[index],
+        recv_sem=sems[1].at[index],
+        device_id=place,
+        device_id_type=MESH,
+    )
+
+
+def tile_of(width):
+    for tile in (512, 384, 256, 128):
+        if width % tile == 0:
+            return tile
+    return width
+
+
+def multiply(left, weight_ref, columns, turned):
+    if turned:
+        return lax.dot_general(
+            left, weight_ref[columns, :], (((1,), (1,)), ((), ())),
+            preferred_element_type=jnp.float32,
+        )
+    return jnp.dot(left, weight_ref[:, columns], preferred_element_type=jnp.float32)
+
+
+def gather_kernel(turned, halved, keep, *refs):
+    x_ref, w_ref, all_ref = refs[:3]
+    refs = refs[3:]
+    if halved:
+        full_ref, refs = refs[0], refs[1:]
+    y_ref, xbuf, wbuf, ybuf, load, done = refs[:6]
+    sems = refs[6:8]
+    me, across, along, far = neighbours()
+    rows = x_ref.shape[0]
+    half = rows // 2
+    core = lax.axis_index("core")
+    places = [{"tp": across}, {"tp": along}]
+    if halved:
+        places.append({"core": 1 - core})
+    mine = pltpu.make_async_copy(x_ref, xbuf.at[me], load.at[0])
+    mine.start()
+    if halved:
+        planes, part, _ = w_ref.shape
+        places_of = [
+            pl.ds(pl.multiple_of((z * 2 + core) * part, part), part) for z in range(planes)
+        ]
+        weights = [
+            pltpu.make_async_copy(w_ref.at[z], wbuf.at[places_of[z]], load.at[1 + z])
+            for z in range(planes)
+        ]
+    else:
+        weights = [pltpu.make_async_copy(w_ref, wbuf, load.at[1])]
+    for copy in weights:
+        copy.start()
+    greet(places)
+
+    def block(owner, part):
+        return xbuf.at[owner, pl.ds(part * half, half)]
+
+    def pass_on(index, owner, part, place):
+        return send(block(owner, part), block(owner, part), sems, index, place)
+
+    first = [
+        send(x_ref.at[pl.ds(0, half)], block(me, 0), sems, 0, {"tp": across}),
+        send(x_ref.at[pl.ds(half, half)], block(me, 1), sems, 1, {"tp": along}),
+        send(x_ref.at[pl.ds(half, half)], block(me, 1), sems, 2, {"tp": across}),
+        send(x_ref.at[pl.ds(0, half)], block(me, 0), sems, 3, {"tp": along}),
+    ]
+    for copy in first:
+        copy.start()
+    swaps = []
+    if halved:
+        for z in range(planes):
+            swaps.append(send(w_ref.at[z], wbuf.at[places_of[z]], sems, 6 + z, {"core": 1 - core}))
+        for copy in swaps:
+            copy.start()
+    mine.wait()
+    for copy in weights:
+        copy.wait()
+    first[0].wait_recv()
+    on_a = pass_on(4, across, 0, {"tp": along})
+    on_a.start()
+    first[1].wait_recv()
+    on_b = pass_on(5, along, 1, {"tp": across})
+    on_b.start()
+    for copy in swaps:
+        copy.wait()
+
+    tile = tile_of(ybuf.shape[-1])
+    outs = []
+    if halved:
+        outs.append(pltpu.make_async_copy(wbuf, full_ref, done.at[4]))
+        outs[-1].start()
+
+    def compute(owner, index):
+        @pl.loop(0, ybuf.shape[-1] // tile)
+        def _(step):
+            columns = pl.ds(pl.multiple_of(step * tile, tile), tile)
+            ybuf[index, :, columns] = multiply(xbuf[owner], wbuf, columns, turned).astype(
+                ybuf.dtype
+            )
+
+        copy = pltpu.make_async_copy(ybuf.at[index], y_ref.at[owner], done.at[index])
+        copy.start()
+        outs.append(copy)
+
+    compute(me, 0)
+    first[2].wait_recv()
+    compute(across, 1)
+    first[3].wait_recv()
+    compute(along, 2)
+    on_a.wait_recv()
+    on_b.wait_recv()
+    if keep:
+        copy = pltpu.make_async_copy(xbuf, all_ref, load.at[0])
+        copy.start()
+        outs.append(copy)
+    compute(far, 3)
+    for copy in first + [on_a, on_b]:
+        copy.wait_send()
+    for copy in outs:
+        copy.wait()
+
+
+def gather_matmul(ident, x, w, turned=False, halved=False, out=jnp.float32):
+    rows, depth = x.shape
+    if halved:
+        planes, part, width = w.shape
+        whole = (planes * 2 * part, width)
+    else:
+        whole = w.shape
+    width = whole[0] if turned else whole[1]
+    shapes = [jax.ShapeDtypeStruct((4, rows, depth), x.dtype)]
+    if halved:
+        shapes.append(jax.ShapeDtypeStruct(whole, w.dtype))
+    shapes.append(jax.ShapeDtypeStruct((4, rows, width), out))
+    hbm = pl.BlockSpec(memory_space=pl.ANY)
+    got = pl.pallas_call(
+        functools.partial(gather_kernel, turned, halved, True),
+        out_shape=shapes,
+        in_specs=[hbm, hbm],
+        out_specs=[hbm] * len(shapes),
+        scratch_shapes=[
+            pltpu.VMEM((4, rows, depth), x.dtype),
+            pltpu.VMEM(whole, w.dtype),
+            pltpu.VMEM((4, rows, width), out),
+            pltpu.SemaphoreType.DMA((6,)),
+            pltpu.SemaphoreType.DMA((5,)),
+            pltpu.SemaphoreType.DMA((10,)),
+            pltpu.SemaphoreType.DMA((10,)),
+        ],
+        compiler_params=pltpu.CompilerParams(
+            collective_id=ident, has_side_effects=True, vmem_limit_bytes=VMEM_BYTES
+        ),
+        cost_estimate=pl.CostEstimate(
+            flops=8 * rows * depth * width,
+            bytes_accessed=30 * 3_000_000,
+            transcendentals=0,
+        ),
+        name="gather_matmul",
+    )(x, w)
+    return [got[0].reshape(4 * rows, depth), *got[1:-1], got[-1].reshape(4 * rows, width)]
+
+
+def scatter_kernel(turned, x_ref, w_ref, out_ref, sums, far_out, near_out, relay, land, s0, s1):
+    me, across, along, far = neighbours()
+    sems = (s0, s1)
+    rows, width = out_ref.shape
+    half = rows // 2
+    top, low = pl.ds(0, half), pl.ds(half, half)
+    tile = tile_of(width)
+    to_across, to_along = {"tp": across}, {"tp": along}
+    greet([to_across, to_along])
+
+    def tiles(body):
+        @pl.loop(0, width // tile)
+        def _(step):
+            body(pl.ds(pl.multiple_of(step * tile, tile), tile))
+
+    def product(owner, columns):
+        return multiply(x_ref[owner], w_ref, columns, turned)
+
+    @tiles
+    def _(columns):
+        far_out[:, columns] = product(far, columns).astype(far_out.dtype)
+
+    far_a = send(far_out.at[top], relay.at[0], sems, 0, to_across)
+    far_b = send(far_out.at[low], relay.at[1], sems, 1, to_along)
+    far_a.start()
+    far_b.start()
+
+    @tiles
+    def _(columns):
+        part = product(across, columns)
+        near_out[0, top, columns] = part[:half].astype(near_out.dtype)
+        sums[0, :, columns] = part[half:]
+
+    across_a = send(near_out.at[0, top], land.at[0, top], sems, 2, to_across)
+    across_a.start()
+
+    @tiles
+    def _(columns):
+        part = product(along, columns)
+        near_out[1, low, columns] = part[half:].astype(near_out.dtype)
+        sums[1, :, columns] = part[:half]
+
+    along_b = send(near_out.at[1, low], land.at[1, low], sems, 3, to_along)
+    along_b.start()
+    far_b.wait_recv()
+
+    @tiles
+    def _(columns):
+        near_out[0, low, columns] = (
+            sums[0, :, columns] + relay[1, :, columns].astype(jnp.float32)
+        ).astype(near_out.dtype)
+
+    across_b = send(near_out.at[0, low], land.at[0, low], sems, 4, to_across)
+    across_b.start()
+    far_a.wait_recv()
+
+    @tiles
+    def _(columns):
+        near_out[1, top, columns] = (
+            sums[1, :, columns] + relay[0, :, columns].astype(jnp.float32)
+        ).astype(near_out.dtype)
+
+    along_a = send(near_out.at[1, top], land.at[1, top], sems, 5, to_along)
+    along_a.start()
+
+    @tiles
+    def _(columns):
+        out_ref[:, columns] = product(me, columns)
+
+    for copy in (across_a, along_b, across_b, along_a):
+        copy.wait_recv()
+
+    @tiles
+    def _(columns):
+        out_ref[:, columns] += land[0, :, columns].astype(jnp.float32) + land[
+            1, :, columns
+        ].astype(jnp.float32)
+
+    for copy in (far_a, far_b, across_a, along_b, across_b, along_a):
+        copy.wait_send()
+
+
+def matmul_scatter(ident, x, w, turned=False):
+    rows, depth = x.shape[0] // 4, x.shape[1]
+    width = w.shape[0] if turned else w.shape[1]
+    vmem = pl.BlockSpec(memory_space=pltpu.VMEM)
+    return pl.pallas_call(
+        functools.partial(scatter_kernel, turned),
+        out_shape=jax.ShapeDtypeStruct((rows, width), jnp.float32),
+        in_specs=[vmem, vmem],
+        out_specs=vmem,
+        scratch_shapes=[
+            pltpu.VMEM((2, rows // 2, width), jnp.float32),
+            pltpu.VMEM((rows, width), jnp.bfloat16),
+            pltpu.VMEM((2, rows, width), jnp.bfloat16),
+            pltpu.VMEM((2, rows // 2, width), jnp.bfloat16),
+            pltpu.VMEM((2, rows, width), jnp.bfloat16),
+            pltpu.SemaphoreType.DMA((6,)),
+            pltpu.SemaphoreType.DMA((6,)),
+        ],
+        compiler_params=pltpu.CompilerParams(
+            collective_id=ident, has_side_effects=True, vmem_limit_bytes=VMEM_BYTES
+        ),
+        cost_estimate=pl.CostEstimate(
+            flops=8 * rows * depth * width,
+            bytes_accessed=30 * 3_000_000,
+            transcendentals=0,
+        ),
+        name="matmul_scatter",
+    )(x.reshape(4, rows, depth), w)
+
+
+def collect_kernel(count, *refs):
+    ins, outs = refs[:count], refs[count : 2 * count]
+    load, s0, s1 = refs[2 * count :]
+    sems = (s0, s1)
+    me, across, along, far = neighbours()
+    core = lax.axis_index("core")
+    to_across, to_along, to_core = {"tp": across}, {"tp": along}, {"core": 1 - core}
+    local = [
+        pltpu.make_async_copy(ins[i], outs[i].at[me, core], load.at[i]) for i in range(count)
+    ]
+    for copy in local:
+        copy.start()
+    greet([to_across, to_along, to_core])
+
+    def half(i, part):
+        rows = ins[i].shape[0] // 2
+        return pl.ds(part * rows, rows)
+
+    def first(i, part, index, place):
+        return send(
+            ins[i].at[half(i, part)],
+            outs[i].at[me, core, half(i, part)],
+            sems,
+            10 * i + index,
+            place,
+        )
+
+    def relay(i, owner, part, index, place):
+        block = outs[i].at[owner, core, half(i, part)]
+        return send(block, block, sems, 10 * i + index, place)
+
+    def hand(i, owner, index):
+        block = outs[i].at[owner, core]
+        return send(block, block, sems, 10 * i + index, to_core)
+
+    begun = []
+    for i in range(count):
+        begun.append(
+            [
+                first(i, 0, 0, to_across),
+                first(i, 1, 1, to_along),
+                first(i, 1, 2, to_across),
+                first(i, 0, 3, to_along),
+                send(ins[i], outs[i].at[me, core], sems, 10 * i + 6, to_core),
+            ]
+        )
+        for copy in begun[i]:
+            copy.start()
+    for i in range(count):
+        begun[i][0].wait_recv()
+        on_a = relay(i, across, 0, 4, to_along)
+        on_a.start()
+        begun[i][1].wait_recv()
+        on_b = relay(i, along, 1, 5, to_across)
+        on_b.start()
+        begun[i] += [on_a, on_b]
+    for i in range(count):
+        begun[i][2].wait_recv()
+        hands = [hand(i, across, 7)]
+        hands[0].start()
+        begun[i][3].wait_recv()
+        hands.append(hand(i, along, 8))
+        hands[1].start()
+        begun[i][5].wait_recv()
+        begun[i][6].wait_recv()
+        hands.append(hand(i, far, 9))
+        hands[2].start()
+        begun[i] += hands
+    for i in range(count):
+        for copy in begun[i][4:5] + begun[i][7:]:
+            copy.wait_recv()
+        for copy in begun[i]:
+            copy.wait_send()
+        local[i].wait()
+
+
+def collect(ident, pieces):
+    hbm = pl.BlockSpec(memory_space=pl.ANY)
+    count = len(pieces)
+    return pl.pallas_call(
+        functools.partial(collect_kernel, count),
+        out_shape=[jax.ShapeDtypeStruct((4, 2) + p.shape, p.dtype) for p in pieces],
+        in_specs=[hbm] * count,
+        out_specs=[hbm] * count,
+        scratch_shapes=[
+            pltpu.SemaphoreType.DMA((count,)),
+            pltpu.SemaphoreType.DMA((10 * count,)),
+            pltpu.SemaphoreType.DMA((10 * count,)),
+        ],
+        compiler_params=pltpu.CompilerParams(
+            collective_id=ident, has_side_effects=True, vmem_limit_bytes=4 * 1024 * 1024
+        ),
+        cost_estimate=pl.CostEstimate(
+            flops=0, bytes_accessed=80 * sum(p.size for p in pieces), transcendentals=0
+        ),
+        name="collect",
+    )(*pieces)
+
+
+def spread_kernel(in_ref, out_ref):
+    width = in_ref.shape[-1]
+    for t in range(4):
+        out_ref[:, pl.ds(t * width, width)] = in_ref[t, 0].astype(jnp.float32)
+
+
+def spread(blocks, parts):
+    _, cores, rows, width = blocks.shape
+    width = width // parts
+    cut = 1 if rows <= 256 else rows // 256
+    return pl.pallas_call(
+        spread_kernel,
+        grid=(cores, cut, parts),
+        out_shape=jax.ShapeDtypeStruct((cores * rows, parts * 4 * width), jnp.float32),
+        in_specs=[pl.BlockSpec((4, 1, rows // cut, width), lambda c, k, q: (0, c, k, q))],
+        out_specs=pl.BlockSpec((rows // cut, 4 * width), lambda c, k, q: (c * cut + k, q)),
+        cost_estimate=pl.CostEstimate(
+            flops=0, bytes_accessed=6 * blocks.size, transcendentals=0
+        ),
+        name="spread",
+    )(blocks)
+
+
+def total_kernel(x_ref, out_ref, land, s0, s1):
+    sems = (s0, s1)
+    me, across, along, far = neighbours()
+    core, plane = lax.axis_index("core"), lax.axis_index("seq")
+    peers = [across, along, far]
+    others = [lax.rem(plane + k, 4) for k in (1, 2, 3)]
+    greet(
+        [{"tp": p} for p in peers] + [{"core": 1 - core}] + [{"seq": p} for p in others]
+    )
+    quarter = x_ref.shape[1] // 4
+
+    def columns(t):
+        return pl.ds(pl.multiple_of(t * quarter, quarter), quarter)
+
+    first = [
+        send(x_ref.at[:, columns(p)], land.at[k], sems, k, {"tp": p}) for k, p in enumerate(peers)
+    ]
+    for copy in first:
+        copy.start()
+    for copy in first:
+        copy.wait_recv()
+    out_ref[plane, core, :, columns(me)] = (x_ref[:, columns(me)] + land[0]) + (land[1] + land[2])
+    here = out_ref.at[plane, core, :, columns(me)]
+    swap = send(here, here, sems, 3, {"core": 1 - core})
+    swap.start()
+    swap.wait_recv()
+    here = out_ref.at[plane, :, :, columns(me)]
+    second = [send(here, here, sems, 4 + k, {"seq": p}) for k, p in enumerate(others)]
+    for copy in second:
+        copy.start()
+    for copy in second:
+        copy.wait_recv()
+    here = out_ref.at[:, :, :, columns(me)]
+    third = [send(here, here, sems, 7 + k, {"tp": p}) for k, p in enumerate(peers)]
+    for copy in third:
+        copy.start()
+    for copy in third:
+        copy.wait_recv()
+    for copy in first + [swap] + second + third:
+        copy.wait_send()
+
+
+def total(ident, x):
+    vmem = pl.BlockSpec(memory_space=pltpu.VMEM)
+    rows, width = x.shape
+    return pl.pallas_call(
+        total_kernel,
+        out_shape=jax.ShapeDtypeStruct((4, 2, rows, width), jnp.float32),
+        in_specs=[vmem],
+        out_specs=vmem,
+        scratch_shapes=[
+            pltpu.VMEM((3, rows, width // 4), jnp.float32),
+            pltpu.SemaphoreType.DMA((10,)),
+            pltpu.SemaphoreType.DMA((10,)),
+        ],
+        compiler_params=pltpu.CompilerParams(
+            collective_id=ident, has_side_effects=True, vmem_limit_bytes=16 * 1024 * 1024
+        ),
+        cost_estimate=pl.CostEstimate(flops=0, bytes_accessed=60_000_000, transcendentals=0),
+        name="total",
+    )(x)
 
 
 def row_stats(values):
@@ -165,27 +647,86 @@
     return parts.reshape(values.shape)
 
 
-def gather_rows(part):
-    whole = lax.all_gather(part, "seq", axis=0, tiled=False)
-    whole = lax.all_gather(whole, "core", axis=1, tiled=False)
-    return whole.reshape((-1,) + part.shape[1:])
+def fast():
+    return lax.axis_size("tp") == 4 and lax.axis_size("core") == 2 and lax.axis_size("seq") == 4
+
+
+def gather_planes(part):
+    return lax.all_gather(part, "seq", axis=0, tiled=False)
+
+
+def join_cores(halves):
+    whole = lax.all_gather(halves, "core", axis=1, tiled=False)
+    return whole.reshape(-1, halves.shape[-1])
 
 
 def scatter_rows(term):
     cores, planes = lax.axis_size("core"), lax.axis_size("seq")
     shaped = term.astype(jnp.bfloat16).reshape(planes, cores, -1, term.shape[-1])
-    half = lax.psum_scatter(shaped, "core", scatter_dimension=1, tiled=False)
-    return lax.psum_scatter(half, "seq", scatter_dimension=0, tiled=False)
+    return lax.psum_scatter(swap_halves(shaped), "seq", scatter_dimension=0, tiled=False)
+
+
+def swap_halves(shaped):
+    cores, me_c = lax.axis_size("core"), lax.axis_index("core")
+    mine = pick(shaped, me_c, 1)
+    for step in range(1, cores):
+        ring = [(c, (c + step) % cores) for c in range(cores)]
+        other = lax.ppermute(pick(shaped, (me_c + step) % cores, 1), "core", ring)
+        mine = (mine.astype(jnp.float32) + other.astype(jnp.float32)).astype(jnp.bfloat16)
+    return mine
 
 
 def plane_gather(values):
     return lax.all_gather(values, "tp", axis=0, tiled=True)
 
 
-def plane_scatter(values):
+def plane_multiply(ident, x, weight, turned=False, halved=False):
+    if fast():
+        got = gather_matmul(ident, x, weight, turned, halved)
+        return got[0], got[1] if halved else weight, got[-1]
+    whole = join_cores(weight) if halved else weight
+    x = plane_gather(x)
+    return x, whole, contract_right(x, whole) if turned else matmul(x, whole)
+
+
+def multiply_plane(ident, x, weight, turned=False):
+    if fast():
+        return matmul_scatter(ident, x, weight, turned)
+    term = contract_right(x, weight) if turned else matmul(x, weight)
     return lax.psum_scatter(
-        values.astype(jnp.bfloat16), "tp", scatter_dimension=0, tiled=True
+        term.astype(jnp.bfloat16), "tp", scatter_dimension=0, tiled=True
     ).astype(jnp.float32)
+
+
+def collect_plane(ident, pieces):
+    if fast():
+        return collect(ident, pieces)
+    return [
+        lax.all_gather(p, ("tp", "core"), axis=0, tiled=False).reshape(
+            (lax.axis_size("tp"), lax.axis_size("core")) + p.shape
+        )
+        for p in pieces
+    ]
+
+
+def spread_parts(blocks, parts):
+    if fast():
+        return spread(blocks, parts)
+    tp, cores, rows, width = blocks.shape
+    return (
+        blocks.astype(jnp.float32)
+        .reshape(tp, cores, rows, parts, width // parts)
+        .transpose(1, 2, 3, 0, 4)
+        .reshape(cores * rows, tp * width)
+    )
+
+
+def total_plane(ident, x):
+    if fast():
+        return total(ident, x)
+    return lax.all_gather(lax.psum(x, "tp"), ("seq", "core"), axis=0, tiled=False).reshape(
+        (lax.axis_size("seq"), lax.axis_size("core")) + x.shape
+    )
 
 
 def shards(
@@ -238,21 +779,29 @@
     mod_plane = lax.psum_scatter(mod_all, "seq", scatter_dimension=0, tiled=False)
     mod_doc = pick(mod_plane.reshape(cores, DOCS, -1), me_c, 0) + b_mod
 
-    qkv_part = pick(w_qkv.reshape(-1, 3, tp, local), me_t, 2).reshape(cores, -1, 3 * local)
-    full_qkv = gather_rows(pick(qkv_part, me_c, 0))
-    capkv_part = pick(w_capkv.reshape(-1, 2, tp, local), me_t, 2).reshape(cores, -1, 2 * local)
-    full_capkv = gather_rows(pick(capkv_part, me_c, 0))
-    gateup_part = pick(
-        w_gateup.reshape(w_gateup.shape[0], 2 * planes, tp, -1), me_t, 2
-    ).reshape(cores, w_gateup.shape[0] // cores, -1)
-    full_gateup = gather_rows(pick(gateup_part, me_c, 0))
-    down_part = pick(w_down.reshape(tp, cores, -1, width), me_t, 0)
-    full_down = gather_rows(pick(down_part, me_c, 0))
-    out_part = pick(w_out.reshape(w_out.shape[0], groups, -1), me_t * cores + me_c, 1)
-    out_part = lax.all_gather(out_part, "seq", axis=0, tiled=False)
+    def columns_of(weight, parts):
+        share = weight.shape[0] // cores
+        size = weight.shape[1] // (parts * tp)
+        return jnp.concatenate(
+            [
+                lax.dynamic_slice(weight, (me_c * share, (q * tp + me_t) * size), (share, size))
+                for q in range(parts)
+            ],
+            axis=1,
+        )
+
+    half_qkv = gather_planes(columns_of(w_qkv, 3))
+    half_capkv = gather_planes(columns_of(w_capkv, 2))
+    out_part = gather_planes(columns_of(w_out, 1))
     out_part = lax.all_to_all(out_part, "tp", 0, 0, tiled=True)
-    out_part = lax.all_gather(out_part, "core", axis=1, tiled=False)
-    full_out = out_part.transpose(2, 0, 1, 3).reshape(local, width)
+    out_part = out_part.transpose(1, 0, 2).reshape(local // cores, width)
+    full_out = lax.all_gather(out_part, "core", axis=0, tiled=True)
+    half_gateup = gather_planes(columns_of(w_gateup, 2 * planes))
+    share = w_down.shape[0] // groups
+    half_down = gather_planes(
+        lax.dynamic_slice_in_dim(w_down, (me_t * cores + me_c) * share, share, 0)
+    )
+    full_down = join_cores(half_down)
 
     inputs = to_plane(tokens).astype(jnp.float32)
     row = jnp.arange(rows, dtype=jnp.int32)
@@ -270,8 +819,8 @@
     tanh_a, tanh_f = jnp.tanh(gate_a), jnp.tanh(gate_f)
 
     normed1, inverse1 = row_stats(inputs)
-    hidden1 = plane_gather((normed1 * gain_attn * (1.0 + scale_a)).astype(jnp.bfloat16))
-    projected = matmul(hidden1, full_qkv)
+    hidden1 = (normed1 * gain_attn * (1.0 + scale_a)).astype(jnp.bfloat16)
+    hidden1, full_qkv, projected = plane_multiply(1, hidden1, half_qkv, halved=True)
     query_raw, key_raw, value_raw = jnp.split(projected, 3, axis=1)
     query_norm, query_inv = head_stats(query_raw)
     key_norm, key_inv = head_stats(key_raw)
@@ -284,9 +833,9 @@
 
     captions = to_plane(caption[0].transpose(1, 0, 2)).transpose(1, 0, 2)
     capmix = jnp.where(nulls[:, None, None] > 0, null_embed[None, None, :], captions)
-    cap_flat = plane_gather(capmix.reshape(DOCS * cap_dev, ctx))
+    cap_flat = capmix.reshape(DOCS * cap_dev, ctx)
+    cap_flat, full_capkv, cap_proj = plane_multiply(2, cap_flat, half_capkv, halved=True)
     cap_document = jnp.tile(jnp.repeat(jnp.arange(DOCS, dtype=jnp.int32), cap_dev), tp)
-    cap_proj = matmul(cap_flat, full_capkv)
     capkey_raw, capval_raw = jnp.split(cap_proj, 2, axis=1)
     capkey_norm, capkey_inv = head_stats(capkey_raw)
     capkeys = (capkey_norm * my_gain_capkey).astype(jnp.bfloat16)
@@ -299,33 +848,34 @@
     gate_tanh = pick(jnp.tanh(gate_head).reshape(tp, local_heads), me_t, 0)
     head_gate = jnp.repeat(gate_tanh, HDIM)[None, :]
     mixed_attn = (own_out + head_gate * cross_out).astype(jnp.bfloat16)
-    attn_out = plane_scatter(matmul(mixed_attn, full_out))
+    attn_out = multiply_plane(3, mixed_attn, full_out)
     residual = inputs + tanh_a * attn_out
     normed2, inverse2 = row_stats(residual)
-    hidden2 = plane_gather((normed2 * gain_ffn * (1.0 + scale_f)).astype(jnp.bfloat16))
-    gate_part, up_part = jnp.split(matmul(hidden2, full_gateup), 2, axis=1)
+    hidden2 = (normed2 * gain_ffn * (1.0 + scale_f)).astype(jnp.bfloat16)
+    hidden2, full_gateup, gate_up = plane_multiply(4, hidden2, half_gateup, halved=True)
+    gate_part, up_part = jnp.split(gate_up, 2, axis=1)
     sig_gate = jax.nn.sigmoid(gate_part)
     silu_gate = gate_part * sig_gate
     hidden_ffn = (silu_gate * up_part).astype(jnp.bfloat16)
-    down_out = plane_scatter(matmul(hidden_ffn, full_down))
+    down_out = multiply_plane(5, hidden_ffn, full_down)
     result = from_plane((residual + tanh_f * down_out).astype(jnp.bfloat16))
 
     grad_res0 = to_plane(cotangent).astype(jnp.float32) * (is_valid * scale_loss)[:, None]
-    grad_down = plane_gather((tanh_f * grad_res0).astype(jnp.bfloat16))
+    grad_down = (tanh_f * grad_res0).astype(jnp.bfloat16)
+    grad_down, _, grad_ffn = plane_multiply(6, grad_down, full_down, turned=True)
     grad_gate_f = grad_res0 * down_out * (1.0 - tanh_f * tanh_f)
-    grad_ffn = contract_right(grad_down, full_down)
     grad_gate_part = grad_ffn * up_part * sig_gate * (1.0 + gate_part * (1.0 - sig_gate))
     grad_up_part = grad_ffn * silu_gate
     grad_gateup = jnp.concatenate([grad_gate_part, grad_up_part], axis=1).astype(jnp.bfloat16)
-    grad_hidden2 = plane_scatter(contract_right(grad_gateup, full_gateup))
+    grad_hidden2 = multiply_plane(7, grad_gateup, full_gateup, turned=True)
     gain_ffn_term = jnp.sum(grad_hidden2 * normed2 * (1.0 + scale_f), axis=0)
     grad_scale_f = grad_hidden2 * normed2 * gain_ffn
     grad_residual = grad_res0 + norm_back(
         grad_hidden2 * gain_ffn * (1.0 + scale_f), normed2, inverse2
     )
-    grad_attn = plane_gather((tanh_a * grad_residual).astype(jnp.bfloat16))
+    grad_attn = (tanh_a * grad_residual).astype(jnp.bfloat16)
+    grad_attn, _, grad_mix = plane_multiply(8, grad_attn, full_out, turned=True)
     grad_gate_a = grad_residual * attn_out * (1.0 - tanh_a * tanh_a)
-    grad_mix = contract_right(grad_attn, full_out)
     grad_own = grad_mix.astype(jnp.bfloat16)
     grad_cross = (head_gate * grad_mix).astype(jnp.bfloat16)
     gate_head_term = jnp.sum(
@@ -346,7 +896,7 @@
     grad_projected = jnp.concatenate([grad_query_raw, grad_key_raw, grad_values], axis=1).astype(
         jnp.bfloat16
     )
-    grad_hidden1 = plane_scatter(contract_right(grad_projected, full_qkv))
+    grad_hidden1 = multiply_plane(9, grad_projected, full_qkv, turned=True)
     gain_attn_term = jnp.sum(grad_hidden1 * normed1 * (1.0 + scale_a), axis=0)
     grad_scale_a = grad_hidden1 * normed1 * gain_attn
     input_grad = from_plane(
@@ -363,8 +913,56 @@
         precision=lax.Precision.HIGHEST,
         preferred_element_type=jnp.float32,
     )
-    grad_mod_doc = lax.psum(grad_mod_doc, "tp")
-    grad_mod_docs = lax.all_gather(grad_mod_doc, ("seq", "core"), axis=0, tiled=True)
+    gain_capkey_term = jnp.sum(grad_capkeys * capkey_norm, axis=0)
+    grad_capkey_raw = head_back(grad_capkeys * my_gain_capkey, capkey_norm, capkey_inv)
+    grad_cap_proj = jnp.concatenate([grad_capkey_raw, grad_capvals], axis=1).astype(jnp.bfloat16)
+    null_rows = nulls[cap_document] > 0
+    null_sum = jnp.sum(
+        jnp.where(null_rows[:, None], grad_cap_proj.astype(jnp.float32), 0.0), axis=0
+    )
+    null_term = jnp.dot(
+        full_capkv.astype(jnp.float32), null_sum, precision=lax.Precision.HIGHEST
+    )
+
+    term_down = scatter_rows(contract_rows(hidden_ffn, grad_down))
+    term_gateup = scatter_rows(contract_rows(hidden2, grad_gateup))
+    term_out = contract_rows(mixed_attn, grad_attn).astype(jnp.bfloat16)
+    term_out = swap_halves(term_out.reshape(1, cores, -1, width))[0]
+    term_out = term_out.reshape(term_out.shape[0], tp, -1).transpose(1, 0, 2)
+    term_out = lax.all_to_all(term_out, "tp", 0, 0, tiled=True)
+    term_out = lax.psum_scatter(term_out, "seq", scatter_dimension=0, tiled=False)
+    term_capkv = scatter_rows(contract_rows(cap_flat, grad_cap_proj))
+    term_qkv = scatter_rows(contract_rows(hidden1, grad_projected))
+    all_down, all_gateup, all_out = collect_plane(10, [term_down, term_gateup, term_out])
+    all_capkv, all_qkv = collect_plane(11, [term_capkv, term_qkv])
+    sum_down = all_down.reshape(w_down.shape).astype(jnp.float32)
+    sum_gateup = spread_parts(all_gateup, 2 * planes)
+    sum_out = spread_parts(all_out, 1)
+    sum_capkv = spread_parts(all_capkv, 2)
+    sum_qkv = spread_parts(all_qkv, 3)
+
+    def at_mine(part):
+        whole = jnp.zeros((tp,) + part.shape, jnp.float32)
+        return lax.dynamic_update_index_in_dim(whole, part, me_t, 0).reshape(-1)
+
+    small = jnp.concatenate(
+        [
+            gain_attn_term,
+            gain_ffn_term,
+            at_mine(gain_query_term),
+            at_mine(gain_key_term),
+            at_mine(gain_capkey_term),
+            at_mine(gate_head_term),
+            null_term,
+        ]
+    )
+    small_rows = 8 - DOCS
+    small_size = small.shape[0]
+    small = jnp.pad(small, (0, small_rows * 4 * width - small_size))
+    totals = total_plane(
+        12, jnp.concatenate([grad_mod_doc, small.reshape(small_rows, 4 * width)], axis=0)
+    ).reshape(groups, 8, 4 * width)
+    grad_mod_docs = totals[:, :DOCS].reshape(groups * DOCS, 4 * width)
     sum_mod = lax.dot_general(
         cond_mine.astype(jnp.float32),
         grad_mod_docs,
@@ -373,77 +971,17 @@
         preferred_element_type=jnp.float32,
     )
     sum_bias = jnp.sum(grad_mod_docs, axis=0)
-
-    gain_capkey_term = jnp.sum(grad_capkeys * capkey_norm, axis=0)
-    grad_capkey_raw = head_back(grad_capkeys * my_gain_capkey, capkey_norm, capkey_inv)
-    grad_cap_proj = jnp.concatenate([grad_capkey_raw, grad_capvals], axis=1).astype(jnp.bfloat16)
-    null_rows = nulls[cap_document] > 0
-    null_sum = jnp.sum(
-        jnp.where(null_rows[:, None], grad_cap_proj.astype(jnp.float32), 0.0), axis=0
-    )
-    null_term = jnp.dot(
-        full_capkv.astype(jnp.float32), null_sum, precision=lax.Precision.HIGHEST
-    )
-
-    term_down = scatter_rows(contract_rows(hidden_ffn, grad_down))
-    sum_down = lax.all_gather(term_down, ("tp", "core"), axis=0, tiled=True)
-    term_gateup = scatter_rows(contract_rows(hidden2, grad_gateup))
-    term_gateup = lax.all_gather(term_gateup, ("tp", "core"), axis=0, tiled=False)
-    sum_gateup = (
-        term_gateup.reshape(tp, cores, w_gateup.shape[0] // cores, 2 * planes, -1)
-        .transpose(1, 2, 3, 0, 4)
-        .reshape(w_gateup.shape)
-    )
-    term_out = contract_rows(mixed_attn, grad_attn).astype(jnp.bfloat16)
-    term_out = term_out.reshape(local, tp, cores, -1).transpose(1, 2, 0, 3)
-    term_out = lax.psum_scatter(term_out, "core", scatter_dimension=1, tiled=False)
-    term_out = lax.all_to_all(term_out, "tp", 0, 0, tiled=True)
-    term_out = lax.psum_scatter(term_out, "seq", scatter_dimension=0, tiled=False)
-    sum_out = lax.all_gather(term_out, ("tp", "core"), axis=1, tiled=True)
-    term_qkv = scatter_rows(contract_rows(hidden1, grad_projected))
-    term_qkv = lax.all_gather(term_qkv, ("tp", "core"), axis=0, tiled=False)
-    sum_qkv = (
-        term_qkv.reshape(tp, cores, w_qkv.shape[0] // cores, 3, local)
-        .transpose(1, 2, 3, 0, 4)
-        .reshape(w_qkv.shape)
-    )
-    term_capkv = scatter_rows(contract_rows(cap_flat, grad_cap_proj))
-    term_capkv = lax.all_gather(term_capkv, ("tp", "core"), axis=0, tiled=False)
-    sum_capkv = (
-        term_capkv.reshape(tp, cores, w_capkv.shape[0] // cores, 2, local)
-        .transpose(1, 2, 3, 0, 4)
-        .reshape(w_capkv.shape)
-    )
-
-    def at_mine(part):
-        whole = jnp.zeros((tp,) + part.shape, jnp.float32)
-        return lax.dynamic_update_index_in_dim(whole, part, me_t, 0).reshape(-1)
-
-    small = lax.psum(
-        jnp.concatenate(
-            [
-                gain_attn_term,
-                gain_ffn_term,
-                at_mine(gain_query_term),
-                at_mine(gain_key_term),
-                at_mine(gain_capkey_term),
-                at_mine(gate_head_term),
-                null_term,
-            ]
-        ),
-        ("tp", "core", "seq"),
-    )
+    small = jnp.sum(totals[:, DOCS:], axis=0).reshape(-1)[:small_size]
     ends = [width, 2 * width, 3 * width, 4 * width, 5 * width, 5 * width + HEADS]
     small_parts = jnp.split(small, ends)
-    f32 = jnp.float32
     return (
         result,
         input_grad,
-        sum_qkv.astype(f32),
-        sum_out.astype(f32),
-        sum_capkv.astype(f32),
-        sum_gateup.astype(f32),
-        sum_down.astype(f32),
+        sum_qkv,
+        sum_out,
+        sum_capkv,
+        sum_gateup,
+        sum_down,
         sum_mod,
         sum_bias,
         *small_parts,

time: 1680 us -> 1230 us (0.73)
  waiting for transfers between devices: 698 us -> 159 us
  Pallas kernels: 0 us -> 488 us
  local copies, waits for them, and re-layouts: 300 us -> 113 us
  blocking collectives: 200 us -> 54.7 us
  matrix products: 311 us -> 212 us
  starting transfers between devices: 32.5 us -> 52.1 us
    pallas_call x0 -> x16, Pallas kernels: none -> 488 us  [the longest x5 194 us: gather_matmul(): pl.pallas_call(functools.partial(gather_kernel, turned, halved, True), ou...]
    reduce_scatter x10 -> x4, waiting for transfers between devices: 317 us -> 0.02 us  [scatter_rows(): lax.psum_scatter(swap_halves(shaped), 'seq', scatter_dimension=0, tiled=F...]
    all_gather x19 -> x6, waiting for transfers between devices: 222 us -> 2.07 us  [the longest x4 2.05 us: gather_planes(): return lax.all_gather(part, 'seq', axis=0, tiled=False)]
    convert_element_type x9 -> x0, local copies, waits for them, and re-layouts: 105 us -> none  [the longest x3 46 us: shards(): sum_capkv.astype(f32)]
    all_to_all x4 -> x0, blocking collectives: 89.1 us -> none  [the longest x2 51.7 us: to_plane(): parts = lax.all_to_all(parts, 'tp', 0, 0, tiled=True)]
    all_to_all x1 -> x2, waiting for transfers between devices: 0.01 us -> 48.5 us  [from_plane(): parts = lax.all_to_all(parts, 'seq', 0, 0, tiled=True)]
    unnamed x34 -> x12, waiting for transfers between devices: 44.7 us -> 0.2 us
    dot_general x6 -> x1, matrix products: 44.9 us -> 1.53 us  [matmul(): return jnp.dot(left, right, preferred_element_type=jnp.float32)]
  transfers between devices with their start and end apart: 40 -> 28, of which waited for: 23 -> 9; matrix products, arithmetic and copies ran while one was open for 37% -> 31% of each run, Pallas kernels for 0% -> 25%
where the time goes in v2:
time: 1230 us; the launch traced here: 1220 us
  Pallas kernels  488 us (40%)
  matrix products  212 us (17%)
  waiting for transfers between devices  159 us (13%)
  other arithmetic  117 us (10%)
  local copies, waits for them, and re-layouts  113 us (9%)
  blocking collectives  54.7 us (4%)
  starting transfers between devices  52.1 us (4%)
  between operations  19.5 us (2%)
    pallas_call x5, Pallas kernels, gather_matmul(): pl.pallas_call(functools.partial(gather_kernel, turned, halved, True), ou...  194 us
    pallas_call x4, Pallas kernels, matmul_scatter(): pl.pallas_call(functools.partial(scatter_kernel, turned), out_shape=jax.S...  133 us
    pallas_call x2, Pallas kernels, collect(): pl.pallas_call(functools.partial(collect_kernel, count), out_shape=[jax.S...  92.7 us
    all_to_all x3, waiting for transfers between devices, to_plane(): parts = lax.all_to_all(parts, 'seq', 0, 0, tiled=True)  88.5 us
    unnamed x210, local copies, waits for them, and re-layouts  49.8 us
    all_to_all x2, waiting for transfers between devices, from_plane(): parts = lax.all_to_all(parts, 'seq', 0, 0, tiled=True)  48.5 us
    pallas_call x1, Pallas kernels, total(): pl.pallas_call(total_kernel, out_shape=jax.ShapeDtypeStruct((4, 2, rows,...  38.4 us
    dot_general x24, matrix products, block(): jnp.einsum('qhd,khd->hqk', part_q, part_k, preferred_element_type=jnp.flo...  38.1 us
  transfers between devices with their start and end apart: 28, of which 9 were waited for; matrix products, arithmetic and copies ran while one was open for 31% of the time, Pallas kernels for 25%

profile of v2, /device:TPU:0, one launch (start us, length us, event | category | flops | bytes accessed | tf_op | source)
XLA Modules:
  0.0 1215.8 jit_solution(5589553007904719103)
XLA Ops:
  8.1 10.8 all-gather.1
  27.6 24.5 %all-gather.4 = bf16[768,384]{1,0:T(8,128)(2,1)S(1)} all-gather(bf16[192,384]{1,0:T(8,128)(2,1)S(1)} %dynamic_slice.167), channel_id=6, replica_groups=mesh['tp'=4,'core'=2,'seq'=4] {'seq'}, dimensions={0}, use_global_device_ids=true | all-gather | bytes 737280 | tf_op jit(solution)/shard_map/all_gather | solution.py:655
  52.1 11.0 all_to_all.60
  78.8 8.4 all-reduce.1
  106.2 31.4 %all-to-all-done.1 = bf16[4,64,1536]{2,1,0:T(8,128)(2,1)S(1)} async-done(((bf16[4,64,1536]{2,1,0:T(8,128)(2,1)}), bf16[4,64,1536]{2,1,0:T(8,128)(2,1)S(1)}, u32[]{:S(2)}, u32[]{:S(2)}) %all-to-all-start.1) | async-done | bytes 786464 | tf_op jit(solution)/shard_map/all_to_all | solution.py:638
  146.2 31.2 %gather_matmul.5 = (bf16[4,256,1536]{2,1,0:T(8,128)(2,1)}, bf16[1536,1152]{1,0:T(8,128)(2,1)}, f32[4,256,1152]{2,1,0:T(8,128)}) custom-call(bf16[256,1536]{1,0:T(8,128)(2,1)} %fusion.150.refs_0_, bf16[4,192,1152]{2,1,0:T(8,128)(2,1)} %bitcast.649), custom_call_target="tpu_custom_call" | custom-call | flops 3623878656 | bytes 90000000 | tf_op jit(solution)/shard_map/gather_matmul/pallas_call | solution.py:173
  196.8 13.8 %all-to-all-done.2 = bf16[4,16,4,4096]{3,1,2,0:T(8,128)(2,1)} async-done(((bf16[4,16,4,4096]{3,1,2,0:T(8,128)(2,1)}), bf16[4,16,4,4096]{3,1,2,0:T(8,128)(2,1)}, u32[]{:S(2)}, u32[]{:S(2)}) %all-to-all-start.2) | async-done | bytes 2097184 | tf_op jit(solution)/shard_map/all_to_all | solution.py:637
  215.2 25.0 %while.56 = (s32[]{:T(128)}, f32[6,1024,1,64]{1,3,2,0:T(8,128)S(1)}, f32[6,1,1024]{2,1,0:T(1,128)S(1)}, bf16[6,1024,1,64]{1,3,2,0:T(8,128)(2,1)}, bf16[6,1024,1,...) while((s32[]{:T(128)}, ...), condition=%wide.region_11.12_spmd.clone, body=%wide.region_8.11_spmd.clone.sunk | while | flops 284163072 | bytes 13301849 | solution.py:572
  244.7 57.2 %all-to-all-done.3 = bf16[4,16,4,4096]{3,1,2,0:T(8,128)(2,1)} async-done(((bf16[4,16,4,4096]{3,1,2,0:T(8,128)(2,1)}), bf16[4,16,4,4096]{3,1,2,0:T(8,128)(2,1)}, u32[]{:S(2)}, u32[]{:S(2)}) %all-to-all-start.3) | async-done | bytes 2097184 | tf_op jit(solution)/shard_map/all_to_all | solution.py:638
  310.0 72.3 %gather_matmul.6 = (bf16[4,256,4096]{2,1,0:T(8,128)(2,1)}, bf16[4096,768]{1,0:T(8,128)(2,1)}, f32[4,256,768]{2,1,0:T(8,128)}) custom-call(bf16[256,4096]{1,0:T(8,128)(2,1)} %bitcast.619, bf16[4,512,768]{2,1,0:T(8,128)(2,1)} %bitcast.645), custom_call_target="tpu_custom_call" | custom-call | flops 6442450944 | bytes 90000000 | tf_op jit(solution)/shard_map/gather_matmul/pallas_call | solution.py:173
  390.2 24.8 %while.57 = (s32[]{:T(128)}, f32[6,1024,1,64]{1,3,2,0:T(8,128)S(1)}, f32[6,1,1024]{2,1,0:T(1,128)S(1)}, bf16[6,1024,1,64]{1,3,2,0:T(8,128)(2,1)}, bf16[6,1024,1,...) while((s32[]{:T(128)}, ...), condition=%wide.region_16.17_spmd.clone, body=%wide.region_13.16_spmd.clone.sunk | while | flops 284163072 | bytes 13305953 | solution.py:572
  422.5 32.6 %matmul_scatter.4 = f32[256,1536]{1,0:T(8,128)} custom-call(bf16[4,256,384]{2,1,0:T(8,128)(2,1)} %add_convert_fusion.2.x_ref, bf16[384,1536]{1,0:T(8,128)(2,1)} %all-gather.15.cloned.1.call-done.w_ref.refs_1_), custom_call_target="tpu_custom_call" | custom-call | flops 1207959552 | bytes 90000000 | tf_op jit(solution)/shard_map/matmul_scatter/pallas_call | solution.py:286
  461.1 32.5 %gather_matmul.7 = (bf16[4,256,1536]{2,1,0:T(8,128)(2,1)}, bf16[1536,2048]{1,0:T(8,128)(2,1)}, f32[4,256,2048]{2,1,0:T(8,128)}) custom-call(bf16[256,1536]{1,0:T(8,128)(2,1)} %get-tuple-element.612.refs_0_, bf16[4,192,2048]{2,1,0:T(8,128)(2,1)} %bitcast.646), custom_call_target="tpu_custom_call" | custom-call | flops 6442450944 | bytes 90000000 | tf_op jit(solution)/shard_map/gather_matmul/pallas_call | solution.py:173
  493.6 30.4 %gather_matmul.8 = (bf16[4,256,1536]{2,1,0:T(8,128)(2,1)}, f32[4,256,1024]{2,1,0:T(8,128)}) custom-call(bf16[256,1536]{1,0:T(8,128)(2,1)} %get-tuple-element.611.refs_0_, bf16[1024,1536]{1,0:T(8,128)(2,1)} %bitcast.647), custom_call_target="tpu_custom_call" | custom-call | flops 3221225472 | bytes 90000000 | tf_op jit(solution)/shard_map/gather_matmul/pallas_call | solution.py:173
  524.0 7.1 fusion.119
  534.3 34.5 %matmul_scatter.6 = f32[256,1536]{1,0:T(8,128)} custom-call(bf16[4,256,2048]{2,1,0:T(8,128)(2,1)} %pad_maximum_fusion.x_ref, bf16[1536,2048]{1,0:T(8,128)(2,1)} %get-tuple-element.224.w_ref), custom_call_target="tpu_custom_call" | custom-call | flops 6442450944 | bytes 90000000 | tf_op jit(solution)/shard_map/matmul_scatter/pallas_call | solution.py:286
  572.0 31.2 %matmul_scatter.5 = f32[256,1536]{1,0:T(8,128)} custom-call(bf16[4,256,1024]{2,1,0:T(8,128)(2,1)} %bitcast.617, bf16[1024,1536]{1,0:T(8,128)(2,1)} %bitcast.648), custom_call_target="tpu_custom_call" | custom-call | flops 3221225472 | bytes 90000000 | tf_op jit(solution)/shard_map/matmul_scatter/pallas_call | solution.py:286
  603.2 6.6 fusion.138
  613.5 27.2 %gather_matmul.9 = (bf16[4,256,1536]{2,1,0:T(8,128)(2,1)}, f32[4,256,384]{2,1,0:T(8,128)}) custom-call(bf16[256,1536]{1,0:T(8,128)(2,1)} %multiply_convert_fusion.4.refs_0_, bf16[384,1536]{1,0:T(8,128)(2,1)} %all-gather.15.cloned.1.call-done.w_ref.refs_1_), custom_call_target="tpu_custom_call" | custom-call | flops 1207959552 | bytes 90000000 | tf_op jit(solution)/shard_map/gather_matmul/pallas_call | solution.py:173
  671.8 9.4 convolution_convert_fusion.1
  691.2 66.8 %while.59 = (s32[]{:T(128)}, f32[6,1024,1,64]{1,3,2,0:T(8,128)}, f32[6,1024,1,64]{1,3,2,0:T(8,128)}, bf16[6,1024,1,64]{1,3,2,0:T(8,128)(2,1)}, bf16[6,1024,1,64]...) while((s32[]{:T(128)}, f32[6,1024,1,64]{1,3,2,0:T(8,128)}, ...), condition=%wide.region_27.28_spmd.clone, body=%wide.region_25.27_spmd.clone.sunk | while | flops 681704448 | bytes 33195128 | solution.py:607
  766.8 70.9 %while.58 = (s32[]{:T(128)}, f32[6,1024,1,64]{1,3,2,0:T(8,128)}, f32[6,1024,1,64]{1,3,2,0:T(8,128)}, bf16[6,1024,1,64]{1,3,2,0:T(8,128)(2,1)}, bf16[6,1024,1,64]...) while((s32[]{:T(128)}, f32[6,1024,1,64]{1,3,2,0:T(8,128)}, ...), condition=%wide.region_24.25_spmd.clone, body=%wide.region_22.24_spmd.clone.sunk | while | flops 681704448 | bytes 33195120 | solution.py:607
  855.0 10.3 convolution_convert_fusion.2
  882.4 35.0 %matmul_scatter.7 = f32[256,1536]{1,0:T(8,128)} custom-call(bf16[4,256,1152]{2,1,0:T(8,128)(2,1)} %pad_maximum_fusion.1.x_ref, bf16[1536,1152]{1,0:T(8,128)(2,1)} %get-tuple-element.232.w_ref), custom_call_target="tpu_custom_call" | custom-call | flops 3623878656 | bytes 90000000 | tf_op jit(solution)/shard_map/matmul_scatter/pallas_call | solution.py:286
  933.9 36.1 %all-to-all-done.9 = bf16[4,64,1536]{2,1,0:T(8,128)(2,1)} async-done(((bf16[4,64,1536]{2,1,0:T(8,128)(2,1)}), bf16[4,64,1536]{2,1,0:T(8,128)(2,1)}, u32[]{:S(2)}, u32[]{:S(2)}) %all-to-all-start.9) | async-done | bytes 786464 | tf_op jit(solution)/shard_map/all_to_all | solution.py:645
  977.9 7.9 fusion.199
  990.0 12.3 %all-to-all-done.5 = bf16[4,64,1536]{2,1,0:T(8,128)(2,1)} async-done(((bf16[4,64,1536]{2,1,0:T(8,128)(2,1)}), bf16[4,64,1536]{2,1,0:T(8,128)(2,1)}, u32[]{:S(2)}, u32[]{:S(2)}) %all-to-all-start.5) | async-done | bytes 786464 | tf_op jit(solution)/shard_map/all_to_all | solution.py:645
  1006.1 38.4 %total.1 = f32[4,2,8,6144]{3,2,1,0:T(8,128)S(1)} custom-call(f32[8,6144]{1,0:T(8,128)S(1)} %pad_maximum_fusion.8.x_ref), custom_call_target="tpu_custom_call" | custom-call | bytes 60000000 | tf_op jit(solution)/shard_map/total/pallas_call | solution.py:479
  1068.6 48.2 %collect.3 = (bf16[4,2,128,1536]{3,2,1,0:T(8,128)(2,1)S(1)}, bf16[4,2,192,2048]{3,2,1,0:T(8,128)(2,1)S(1)}, bf16[4,2,192,384]{3,2,1,0:T(8,128)(2,1)S(1)}) custom-call(bf16[128,1536]{1,0:T(8,128)(2,1)S(1)} %bitcast.579, bf16[192,2048]{1,0:T(8,128)(2,1)S(1)} %bitcast.577, bf16[192,384]{1,0:T(8,128)(2,1)S(1)} %bitcast.580), custom_call_target="tpu_custom_call" | custom-call | bytes 53084160 | tf_op jit(solution)/shard_map/collect/pallas_call | solution.py:391
  1120.6 12.2 %spread.7 = f32[384,8192]{1,0:T(8,128)} custom-call(bf16[4,2,192,2048]{3,2,1,0:T(8,128)(2,1)} %copy-done.2), custom_call_target="tpu_custom_call" | custom-call | bytes 18874368 | tf_op jit(solution)/shard_map/spread/pallas_call | solution.py:421
  1141.3 44.6 %collect.2 = (bf16[4,2,512,768]{3,2,1,0:T(8,128)(2,1)S(1)}, bf16[4,2,192,1152]{3,2,1,0:T(8,128)(2,1)S(1)}) custom-call(bf16[512,768]{1,0:T(8,128)(2,1)S(1)} %bitcast.576, bf16[192,1152]{1,0:T(8,128)(2,1)S(1)} %bitcast.578), custom_call_target="tpu_custom_call" | custom-call | bytes 49152000 | tf_op jit(solution)/shard_map/collect/pallas_call | solution.py:391
  1190.3 8.9 spread.6
  (586 shorter events, 469.4 us)
Async XLA Ops:
  7.2 93.5 %reduce-scatter.7.cloned.1.call-start = ((), (), s32[]{:S(2)}) async-start(), calls=%async_computation.18 | async-start | bytes 983040 | tf_op jit(solution)/shard_map/reduce_scatter | solution.py:779
  20.5 123.6 %all-gather.23.cloned.1.call-start = ((), (), s32[]{:S(2)}) async-start(), calls=%async_computation.28 | async-start | bytes 1966080 | tf_op jit(solution)/shard_map/all_gather | solution.py:655
  22.4 123.8 %all-gather.17.cloned.1.call-start = ((), (), s32[]{:S(2)}) async-start(), calls=%async_computation.25 | async-start | bytes 2211840 | tf_op jit(solution)/shard_map/all_gather | solution.py:655
  24.4 285.6 %all-gather.19.cloned.1.call-start = ((), (), s32[]{:S(2)}) async-start(), calls=%async_computation.26 | async-start | bytes 3932160 | tf_op jit(solution)/shard_map/all_gather | solution.py:655
  26.6 395.8 %all-gather.15.cloned.1.call-start = ((), (), s32[]{:S(2)}) async-start(), calls=%async_computation.19 | async-start | bytes 1769472 | tf_op jit(solution)/shard_map/all_gather | solution.py:798
  64.1 29.4 %all-to-all-start = ((bf16[4,64,1536]{2,1,0:T(8,128)(2,1)}), bf16[4,64,1536]{2,1,0:T(8,128)(2,1)}, u32[]{:S(2)}, u32[]{:S(2)}) async-start(bf16[4,64,1536]{2,1,0:T(8,128)(2,1)} %bitcast), calls=%async_computation | async-start | bytes 1572864 | tf_op jit(solution)/shard_map/all_to_all | solution.py:637
  68.5 392.6 %all-gather.21.cloned.1.call-start = ((), (), s32[]{:S(2)}) async-start(), calls=%async_computation.27 | async-start | bytes 3932160 | tf_op jit(solution)/shard_map/all_gather | solution.py:655
  93.5 44.1 %all-to-all-start.1 = ((bf16[4,64,1536]{2,1,0:T(8,128)(2,1)}), bf16[4,64,1536]{2,1,0:T(8,128)(2,1)S(1)}, u32[]{:S(2)}, u32[]{:S(2)}) async-start(bf16[4,64,1536]{2,1,0:T(8,128)(2,1)} %all-to-all-done), calls=%async_computation.1 | async-start | bytes 1572864 | tf_op jit(solution)/shard_map/all_to_all | solution.py:638
  99.5 95.3 %copy-start.70 = (f32[384]{0:T(512)}, f32[384]{0:T(512)S(1)}, u32[]{:S(2)}) copy-start(f32[384]{0:T(512)S(1)} %get-tuple-element.669) | copy-start | bytes 4612
  99.5 96.1 %copy-start.68 = (f32[384]{0:T(512)}, f32[384]{0:T(512)S(1)}, u32[]{:S(2)}) copy-start(f32[384]{0:T(512)S(1)} %get-tuple-element.670) | copy-start | bytes 4612
  100.6 95.5 %copy-start.52 = (f32[1024,32]{0,1:T(8,128)}, f32[1024,32]{0,1:T(8,128)S(1)}, u32[]{:S(2)}) copy-start(f32[1024,32]{0,1:T(8,128)S(1)} %get-tuple-element.651) | copy-start | bytes 393220
  137.6 42.2 %all-to-all-start.7 = ((bf16[4,64,1536]{2,1,0:T(8,128)(2,1)}), bf16[4,64,1536]{2,1,0:T(8,128)(2,1)S(1)}, u32[]{:S(2)}, u32[]{:S(2)}) async-start(bf16[4,64,1536]{2,1,0:T(8,128)(2,1)} %bitcast.63), calls=%async_computation.8 | async-start | bytes 1572864 | tf_op jit(solution)/shard_map/all_to_all | solution.py:637
  141.1 352.5 %all-gather.25.cloned.1.call-start = ((), (), s32[]{:S(2)}) async-start(), calls=%async_computation.29 | async-start | bytes 4718592 | tf_op jit(solution)/shard_map/all_gather | solution.py:659
  180.7 29.9 %all-to-all-start.2 = ((bf16[4,16,4,4096]{3,1,2,0:T(8,128)(2,1)}), bf16[4,16,4,4096]{3,1,2,0:T(8,128)(2,1)}, u32[]{:S(2)}, u32[]{:S(2)}) async-start(bf16[4,16,4,4096]{3,1,2,0:T(8,128)(2,1)} %copy.191), calls=%async_computation.3 | async-start | bytes 4194304 | tf_op jit(solution)/shard_map/all_to_all | solution.py:637
  210.6 91.3 %all-to-all-start.3 = ((bf16[4,16,4,4096]{3,1,2,0:T(8,128)(2,1)}), bf16[4,16,4,4096]{3,1,2,0:T(8,128)(2,1)}, u32[]{:S(2)}, u32[]{:S(2)}) async-start(bf16[4,16,4,4096]{3,1,2,0:T(8,128)(2,1)} %all-to-all-done.2), calls=%async_computation.4 | async-start | bytes 4194304 | tf_op jit(solution)/shard_map/all_to_all | solution.py:638
  301.9 155.5 %all-to-all-start.8 = ((bf16[4,64,1536]{2,1,0:T(8,128)(2,1)}), bf16[4,64,1536]{2,1,0:T(8,128)(2,1)}, u32[]{:S(2)}, u32[]{:S(2)}) async-start(bf16[4,64,1536]{2,1,0:T(8,128)(2,1)} %copy-done.38), calls=%async_computation.9 | async-start | bytes 1572864 | tf_op jit(solution)/shard_map/all_to_all | solution.py:638
  652.2 3.4 collective-permute-start.4
  657.9 13.9 %all-to-all-start.11 = ((bf16[4,192,384]{2,1,0:T(8,128)(2,1)}), bf16[4,192,384]{2,1,0:T(8,128)(2,1)}, u32[]{:S(2)}, u32[]{:S(2)}) async-start(bf16[4,192,384]{2,1,0:T(8,128)(2,1)} %bitcast.501), calls=%async_computation.16 | async-start | bytes 1179648 | tf_op jit(solution)/shard_map/all_to_all | solution.py:932
  662.0 402.7 %reduce-scatter.17.cloned.1.call-start = ((), (), s32[]{:S(2)}) async-start(), calls=%async_computation.24 | async-start | bytes 737280 | tf_op jit(solution)/shard_map/reduce_scatter | solution.py:933
  671.0 14.5 %collective-permute-start.2 = (bf16[4,128,1536]{2,1,0:T(8,128)(2,1)}, bf16[4,128,1536]{2,1,0:T(8,128)(2,1)}, u32[]{:S(2)}, u32[]{:S(2)}) collective-permute-start(bf16[4,128,1536]{2,1,0:T(8,128)(2,1)} %dynamic-slice_bitcast_fusion.3), channel_id=1, source_target_pairs={{0,4},{4,0},{1,5},{5,1},{2,6},{6,2},{3,7},{7,3},{8,12},{12,8},{9,1... | collective-permute-start | bytes 4718600 | tf_op jit(solution)/shard_map/ppermute | solution.py:674
  671.8 393.0 %reduce-scatter.13.cloned.1.call-start = ((), (), s32[]{:S(2)}) async-start(), calls=%async_computation.22 | async-start | bytes 1966080 | tf_op jit(solution)/shard_map/reduce_scatter | solution.py:666
  685.4 72.5 %collective-permute-start.3 = (bf16[4,192,2048]{2,1,0:T(8,128)(2,1)}, bf16[4,192,2048]{2,1,0:T(8,128)(2,1)}, u32[]{:S(2)}, u32[]{:S(2)}) collective-permute-start(bf16[4,192,2048]{2,1,0:T(8,128)(2,1)} %dynamic-slice_bitcast_fusion), channel_id=1, source_target_pairs={{0,4},{4,0},{1,5},{5,1},{2,6},{6,2},{3,7},{7,3},{8,12},{12,8},{9,1... | collective-permute-start | bytes 9437192 | tf_op jit(solution)/shard_map/ppermute | solution.py:674
  688.4 376.3 %reduce-scatter.15.cloned.1.call-start = ((), (), s32[]{:S(2)}) async-start(), calls=%async_computation.23 | async-start | bytes 3932160 | tf_op jit(solution)/shard_map/reduce_scatter | solution.py:666
  764.1 375.1 %reduce-scatter.11.cloned.1.call-start = ((), (), s32[]{:S(2)}) async-start(), calls=%async_computation.21 | async-start | bytes 2211840 | tf_op jit(solution)/shard_map/reduce_scatter | solution.py:666
  852.4 13.0 %collective-permute-start.1 = (bf16[4,192,1152]{2,1,0:T(8,128)(2,1)S(1)}, bf16[4,192,1152]{2,1,0:T(8,128)(2,1)S(1)}, u32[]{:S(2)}, u32[]{:S(2)}) collective-permute-start(bf16[4,192,1152]{2,1,0:T(8,128)(2,1)S(1)} %dynamic-slice_bitcast_fusion.2), channel_id=1, source_target_pairs={{0,4},{4,0},{1,5},{5,1},{2,6},{6,2},{3,7},{7,3},{8,12},{12,8},{9,1... | collective-permute-start | bytes 5308424 | tf_op jit(solution)/shard_map/ppermute | solution.py:674
  867.1 272.1 %reduce-scatter.9.cloned.1.call-start = ((), (), s32[]{:S(2)}) async-start(), calls=%async_computation.20 | async-start | bytes 3932160 | tf_op jit(solution)/shard_map/reduce_scatter | solution.py:666
  871.0 6.1 collective-permute-start
  924.2 51.9 %copy-start.31 = (f32[4,256,384]{2,1,0:T(8,128)S(1)}, f32[4,256,384]{2,1,0:T(8,128)}, u32[]{:S(2)}) copy-start(f32[4,256,384]{2,1,0:T(8,128)} %get-tuple-element.226) | copy-start | bytes 4718596
  924.2 45.8 %all-to-all-start.9 = ((bf16[4,64,1536]{2,1,0:T(8,128)(2,1)}), bf16[4,64,1536]{2,1,0:T(8,128)(2,1)}, u32[]{:S(2)}, u32[]{:S(2)}) async-start(bf16[4,64,1536]{2,1,0:T(8,128)(2,1)} %bitcast.611), calls=%async_computation.10 | async-start | bytes 1572864 | tf_op jit(solution)/shard_map/all_to_all | solution.py:645
  970.0 32.4 %all-to-all-start.5 = ((bf16[4,64,1536]{2,1,0:T(8,128)(2,1)}), bf16[4,64,1536]{2,1,0:T(8,128)(2,1)}, u32[]{:S(2)}, u32[]{:S(2)}) async-start(bf16[4,64,1536]{2,1,0:T(8,128)(2,1)} %bitcast.604), calls=%async_computation.6 | async-start | bytes 1572864 | tf_op jit(solution)/shard_map/all_to_all | solution.py:645
  1002.4 46.5 %all-to-all-start.10 = ((bf16[4,64,1536]{2,1,0:T(8,128)(2,1)}), bf16[4,64,1536]{2,1,0:T(8,128)(2,1)S(1)}, u32[]{:S(2)}, u32[]{:S(2)}) async-start(bf16[4,64,1536]{2,1,0:T(8,128)(2,1)} %all-to-all-done.9), calls=%async_computation.11 | async-start | bytes 1572864 | tf_op jit(solution)/shard_map/all_to_all | solution.py:646
  1048.8 15.9 %all-to-all-start.6 = ((bf16[4,64,1536]{2,1,0:T(8,128)(2,1)}), bf16[4,64,1536]{2,1,0:T(8,128)(2,1)S(1)}, u32[]{:S(2)}, u32[]{:S(2)}) async-start(bf16[4,64,1536]{2,1,0:T(8,128)(2,1)} %all-to-all-done.5), calls=%async_computation.7 | async-start | bytes 1572864 | tf_op jit(solution)/shard_map/all_to_all | solution.py:646
  (89 other events, 608.8 us)
Sparse Core Ops, SparseCore 0:
  20.6 32.8 reduce-scatter.6
  55.6 35.5 all-gather.22
  93.4 52.7 all-gather.16
  148.2 60.7 all-gather.18
  211.0 7.8 all-gather.14
  220.9 106.1 all-gather.20
  328.7 11.7 all-gather.24
  671.9 23.1 reduce-scatter.16
  697.4 33.7 reduce-scatter.12
  764.2 61.7 reduce-scatter.14
  867.2 39.9 reduce-scatter.10
  910.0 73.7 reduce-scatter.8

commit v3 on v2

--- a/solution.py
+++ b/solution.py
@@ -52,13 +52,75 @@
 def multiply(left, weight_ref, columns, turned):
     if turned:
         return lax.dot_general(
-            left, weight_ref[columns, :], (((1,), (1,)), ((), ())),
+            left, weight_ref[columns, 0 : left.shape[1]], (((1,), (1,)), ((), ())),
             preferred_element_type=jnp.float32,
         )
     return jnp.dot(left, weight_ref[:, columns], preferred_element_type=jnp.float32)
 
 
-def gather_kernel(turned, halved, keep, *refs):
+class Aside:
+    def __init__(self, operands, outs, scratch, steps):
+        self.operands, self.outs, self.scratch, self.steps = operands, outs, scratch, steps
+
+    def in_specs(self):
+        return [pl.BlockSpec(memory_space=pl.ANY)] * len(self.operands)
+
+    def out_specs(self):
+        return [pl.BlockSpec(memory_space=pltpu.VMEM)] * len(self.outs)
+
+    def scratch_shapes(self):
+        return [
+            *[pltpu.VMEM(x.shape, x.dtype) for x in self.operands],
+            pltpu.SemaphoreType.DMA((len(self.operands),)),
+            *self.scratch,
+        ]
+
+    def split(self, refs, ins, outs, scratch):
+        count, given = len(self.operands), len(self.outs)
+        own, refs = list(refs[:ins]), refs[ins:]
+        sources, refs = refs[:count], refs[count:]
+        own, refs = own + list(refs[:outs]), refs[outs:]
+        self.out_refs, refs = refs[:given], refs[given:]
+        own, refs = own + list(refs[:scratch]), refs[scratch:]
+        self.in_refs, (sem, *self.scratch_refs) = refs[:count], refs[count:]
+        self.loads = [
+            pltpu.make_async_copy(source, target, sem.at[i])
+            for i, (source, target) in enumerate(zip(sources, self.in_refs))
+        ]
+        return own
+
+    def load(self):
+        for copy in self.loads:
+            copy.start()
+
+    def step(self, index):
+        if index == 0:
+            for copy in self.loads:
+                copy.wait()
+        self.steps(index, self.in_refs, self.out_refs, self.scratch_refs)
+
+
+class Nothing:
+    def __init__(self):
+        self.operands, self.outs = [], []
+
+    def in_specs(self):
+        return []
+
+    out_specs = scratch_shapes = in_specs
+
+    def split(self, refs, ins, outs, scratch):
+        return list(refs)
+
+    def load(self):
+        pass
+
+    def step(self, index):
+        pass
+
+
+def gather_kernel(turned, halved, early, aside, *refs):
+    refs = aside.split(refs, 2, 3 if halved else 2, 7)
     x_ref, w_ref, all_ref = refs[:3]
     refs = refs[3:]
     if halved:
@@ -109,9 +171,12 @@
             swaps.append(send(w_ref.at[z], wbuf.at[places_of[z]], sems, 6 + z, {"core": 1 - core}))
         for copy in swaps:
             copy.start()
+    aside.load()
     mine.wait()
     for copy in weights:
         copy.wait()
+    for step in range(early):
+        aside.step(step)
     first[0].wait_recv()
     on_a = pass_on(4, across, 0, {"tp": along})
     on_a.start()
@@ -120,6 +185,8 @@
     on_b.start()
     for copy in swaps:
         copy.wait()
+    for step in range(early, 3):
+        aside.step(step)
 
     tile = tile_of(ybuf.shape[-1])
     outs = []
@@ -146,10 +213,9 @@
     compute(along, 2)
     on_a.wait_recv()
     on_b.wait_recv()
-    if keep:
-        copy = pltpu.make_async_copy(xbuf, all_ref, load.at[0])
-        copy.start()
-        outs.append(copy)
+    copy = pltpu.make_async_copy(xbuf, all_ref, load.at[0])
+    copy.start()
+    outs.append(copy)
     compute(far, 3)
     for copy in first + [on_a, on_b]:
         copy.wait_send()
@@ -157,24 +223,27 @@
         copy.wait()
 
 
-def gather_matmul(ident, x, w, turned=False, halved=False, out=jnp.float32):
+def gather_matmul(
+    ident, x, w, turned=False, halved=False, width=None, aside=None, early=3, out=jnp.float32
+):
     rows, depth = x.shape
     if halved:
-        planes, part, width = w.shape
-        whole = (planes * 2 * part, width)
+        planes, part, columns = w.shape
+        whole = (planes * 2 * part, columns)
     else:
         whole = w.shape
-    width = whole[0] if turned else whole[1]
+    width = width or (whole[0] if turned else whole[1])
+    aside = aside or Nothing()
     shapes = [jax.ShapeDtypeStruct((4, rows, depth), x.dtype)]
     if halved:
         shapes.append(jax.ShapeDtypeStruct(whole, w.dtype))
     shapes.append(jax.ShapeDtypeStruct((4, rows, width), out))
     hbm = pl.BlockSpec(memory_space=pl.ANY)
     got = pl.pallas_call(
-        functools.partial(gather_kernel, turned, halved, True),
-        out_shape=shapes,
-        in_specs=[hbm, hbm],
-        out_specs=[hbm] * len(shapes),
+        functools.partial(gather_kernel, turned, halved, early, aside),
+        out_shape=shapes + aside.outs,
+        in_specs=[hbm, hbm] + aside.in_specs(),
+        out_specs=[hbm] * len(shapes) + aside.out_specs(),
         scratch_shapes=[
             pltpu.VMEM((4, rows, depth), x.dtype),
             pltpu.VMEM(whole, w.dtype),
@@ -183,6 +252,7 @@
             pltpu.SemaphoreType.DMA((5,)),
             pltpu.SemaphoreType.DMA((10,)),
             pltpu.SemaphoreType.DMA((10,)),
+            *aside.scratch_shapes(),
         ],
         compiler_params=pltpu.CompilerParams(
             collective_id=ident, has_side_effects=True, vmem_limit_bytes=VMEM_BYTES
@@ -193,11 +263,19 @@
             transcendentals=0,
         ),
         name="gather_matmul",
-    )(x, w)
-    return [got[0].reshape(4 * rows, depth), *got[1:-1], got[-1].reshape(4 * rows, width)]
-
-
-def scatter_kernel(turned, x_ref, w_ref, out_ref, sums, far_out, near_out, relay, land, s0, s1):
+    )(x, w, *aside.operands)
+    last = len(shapes) - 1
+    return [
+        got[0].reshape(4 * rows, depth),
+        got[1] if halved else w,
+        got[last].reshape(4 * rows, width),
+        *got[last + 1 :],
+    ]
+
+
+def scatter_kernel(turned, aside, *refs):
+    refs = aside.split(refs, 2, 1, 7)
+    x_ref, w_ref, out_ref, sums, far_out, near_out, relay, land, s0, s1 = refs
     me, across, along, far = neighbours()
     sems = (s0, s1)
     rows, width = out_ref.shape
@@ -205,6 +283,7 @@
     top, low = pl.ds(0, half), pl.ds(half, half)
     tile = tile_of(width)
     to_across, to_along = {"tp": across}, {"tp": along}
+    aside.load()
     greet([to_across, to_along])
 
     def tiles(body):
@@ -241,6 +320,7 @@
 
     along_b = send(near_out.at[1, low], land.at[1, low], sems, 3, to_along)
     along_b.start()
+    aside.step(0)
     far_b.wait_recv()
 
     @tiles
@@ -261,6 +341,8 @@
 
     along_a = send(near_out.at[1, top], land.at[1, top], sems, 5, to_along)
     along_a.start()
+    aside.step(1)
+    aside.step(2)
 
     @tiles
     def _(columns):
@@ -279,15 +361,16 @@
         copy.wait_send()
 
 
-def matmul_scatter(ident, x, w, turned=False):
+def matmul_scatter(ident, x, w, turned=False, aside=None):
+    aside = aside or Nothing()
     rows, depth = x.shape[0] // 4, x.shape[1]
     width = w.shape[0] if turned else w.shape[1]
     vmem = pl.BlockSpec(memory_space=pltpu.VMEM)
     return pl.pallas_call(
-        functools.partial(scatter_kernel, turned),
-        out_shape=jax.ShapeDtypeStruct((rows, width), jnp.float32),
-        in_specs=[vmem, vmem],
-        out_specs=vmem,
+        functools.partial(scatter_kernel, turned, aside),
+        out_shape=[jax.ShapeDtypeStruct((rows, width), jnp.float32)] + aside.outs,
+        in_specs=[vmem, vmem] + aside.in_specs(),
+        out_specs=[vmem] + aside.out_specs(),
         scratch_shapes=[
             pltpu.VMEM((2, rows // 2, width), jnp.float32),
             pltpu.VMEM((rows, width), jnp.bfloat16),
@@ -296,6 +379,7 @@
             pltpu.VMEM((2, rows, width), jnp.bfloat16),
             pltpu.SemaphoreType.DMA((6,)),
             pltpu.SemaphoreType.DMA((6,)),
+            *aside.scratch_shapes(),
         ],
         compiler_params=pltpu.CompilerParams(
             collective_id=ident, has_side_effects=True, vmem_limit_bytes=VMEM_BYTES
@@ -306,106 +390,181 @@
             transcendentals=0,
         ),
         name="matmul_scatter",
-    )(x.reshape(4, rows, depth), w)
-
-
-def collect_kernel(count, *refs):
-    ins, outs = refs[:count], refs[count : 2 * count]
-    load, s0, s1 = refs[2 * count :]
-    sems = (s0, s1)
-    me, across, along, far = neighbours()
-    core = lax.axis_index("core")
-    to_across, to_along, to_core = {"tp": across}, {"tp": along}, {"core": 1 - core}
-    local = [
-        pltpu.make_async_copy(ins[i], outs[i].at[me, core], load.at[i]) for i in range(count)
-    ]
-    for copy in local:
-        copy.start()
-    greet([to_across, to_along, to_core])
-
-    def half(i, part):
-        rows = ins[i].shape[0] // 2
+    )(x.reshape(4, rows, depth), w, *aside.operands)
+
+
+class Gathering:
+    def __init__(self, ins, outs, load, sems):
+        self.ins, self.outs, self.sems = ins, outs, sems
+        self.me, self.across, self.along, self.far = neighbours()
+        self.core = lax.axis_index("core")
+        self.to_across, self.to_along = {"tp": self.across}, {"tp": self.along}
+        self.to_core = {"core": 1 - self.core}
+        self.local = [
+            pltpu.make_async_copy(x, outs[i].at[self.me, self.core], load.at[i])
+            for i, x in enumerate(ins)
+        ]
+        for copy in self.local:
+            copy.start()
+
+    def half(self, i, part):
+        rows = self.ins[i].shape[0] // 2
         return pl.ds(part * rows, rows)
 
-    def first(i, part, index, place):
-        return send(
-            ins[i].at[half(i, part)],
-            outs[i].at[me, core, half(i, part)],
-            sems,
-            10 * i + index,
-            place,
-        )
-
-    def relay(i, owner, part, index, place):
-        block = outs[i].at[owner, core, half(i, part)]
-        return send(block, block, sems, 10 * i + index, place)
-
-    def hand(i, owner, index):
-        block = outs[i].at[owner, core]
-        return send(block, block, sems, 10 * i + index, to_core)
-
-    begun = []
-    for i in range(count):
-        begun.append(
-            [
-                first(i, 0, 0, to_across),
-                first(i, 1, 1, to_along),
-                first(i, 1, 2, to_across),
-                first(i, 0, 3, to_along),
-                send(ins[i], outs[i].at[me, core], sems, 10 * i + 6, to_core),
+    def first(self, i, part, index, place):
+        rows = self.half(i, part)
+        target = self.outs[i].at[self.me, self.core, rows]
+        return send(self.ins[i].at[rows], target, self.sems, 10 * i + index, place)
+
+    def pass_on(self, i, owner, part, index, place):
+        block = self.outs[i].at[owner, self.core, self.half(i, part)]
+        return send(block, block, self.sems, 10 * i + index, place)
+
+    def to_sibling(self, i, owner, index):
+        block = self.outs[i].at[owner, self.core]
+        return send(block, block, self.sems, 10 * i + index, self.to_core)
+
+    def begin(self):
+        self.begun = []
+        for i, x in enumerate(self.ins):
+            target = self.outs[i].at[self.me, self.core]
+            copies = [
+                self.first(i, 0, 0, self.to_across),
+                self.first(i, 1, 1, self.to_along),
+                self.first(i, 1, 2, self.to_across),
+                self.first(i, 0, 3, self.to_along),
+                send(x, target, self.sems, 10 * i + 6, self.to_core),
             ]
-        )
-        for copy in begun[i]:
+            for copy in copies:
+                copy.start()
+            self.begun.append(copies)
+
+    def relay(self):
+        for i, copies in enumerate(self.begun):
+            copies[0].wait_recv()
+            copies.append(self.pass_on(i, self.across, 0, 4, self.to_along))
+            copies[5].start()
+            copies[1].wait_recv()
+            copies.append(self.pass_on(i, self.along, 1, 5, self.to_across))
+            copies[6].start()
+
+    def hand(self):
+        for i, copies in enumerate(self.begun):
+            copies[2].wait_recv()
+            copies.append(self.to_sibling(i, self.across, 7))
+            copies[7].start()
+            copies[3].wait_recv()
+            copies.append(self.to_sibling(i, self.along, 8))
+            copies[8].start()
+            copies[5].wait_recv()
+            copies[6].wait_recv()
+            copies.append(self.to_sibling(i, self.far, 9))
+            copies[9].start()
+
+    def end(self):
+        for copies, local in zip(self.begun, self.local):
+            for copy in copies[4:5] + copies[7:]:
+                copy.wait_recv()
+            for copy in copies:
+                copy.wait_send()
+            local.wait()
+
+
+class Returning:
+    def __init__(self, back, home, stage, load, sems, base):
+        self.back, self.home, self.stage, self.load = back, home, stage, load
+        self.sems, self.base = sems, base
+        self.me, *self.peers = neighbours()
+        self.plane, self.others = planes_after()
+        self.stay = pltpu.make_async_copy(back.at[self.plane], stage.at[self.plane], load)
+        self.keep = pltpu.make_async_copy(stage.at[self.me], home.at[self.me], load)
+
+    def begin(self):
+        self.stay.start()
+        self.out = [
+            send(
+                self.back.at[p], self.stage.at[self.plane], self.sems, self.base + k, {"seq": p}
+            )
+            for k, p in enumerate(self.others)
+        ]
+        for copy in self.out:
             copy.start()
-    for i in range(count):
-        begun[i][0].wait_recv()
-        on_a = relay(i, across, 0, 4, to_along)
-        on_a.start()
-        begun[i][1].wait_recv()
-        on_b = relay(i, along, 1, 5, to_across)
-        on_b.start()
-        begun[i] += [on_a, on_b]
-    for i in range(count):
-        begun[i][2].wait_recv()
-        hands = [hand(i, across, 7)]
-        hands[0].start()
-        begun[i][3].wait_recv()
-        hands.append(hand(i, along, 8))
-        hands[1].start()
-        begun[i][5].wait_recv()
-        begun[i][6].wait_recv()
-        hands.append(hand(i, far, 9))
-        hands[2].start()
-        begun[i] += hands
-    for i in range(count):
-        for copy in begun[i][4:5] + begun[i][7:]:
+
+    def turn(self):
+        for copy in self.out:
             copy.wait_recv()
-        for copy in begun[i]:
+        self.stay.wait()
+        self.last = [
+            send(
+                self.stage.at[p], self.home.at[self.me], self.sems, self.base + 3 + k, {"tp": p}
+            )
+            for k, p in enumerate(self.peers)
+        ]
+        for copy in self.last:
+            copy.start()
+        self.keep.start()
+
+    def end(self):
+        for copy in self.last:
+            copy.wait_recv()
+        self.keep.wait()
+        for copy in self.out + self.last:
             copy.wait_send()
-        local[i].wait()
-
-
-def collect(ident, pieces):
+
+
+def collect_kernel(count, aside, *refs):
+    refs = aside.split(refs, count + 1, count + 1, 6)
+    ins, outs = refs[:count], refs[count + 1 : 2 * count + 1]
+    back, home = refs[count], refs[2 * count + 1]
+    stage, load, s0, s1, r0, r1 = refs[2 * count + 2 :]
+    gathering = Gathering(ins, outs, load, (s0, s1))
+    returning = Returning(back, home, stage, load.at[count], (r0, r1), 0)
+    greet_all()
+    gathering.begin()
+    returning.begin()
+    aside.load()
+    aside.step(0)
+    gathering.relay()
+    returning.turn()
+    aside.step(1)
+    gathering.hand()
+    aside.step(2)
+    returning.end()
+    gathering.end()
+
+
+def collect(ident, pieces, back, aside=None):
+    aside = aside or Nothing()
     hbm = pl.BlockSpec(memory_space=pl.ANY)
     count = len(pieces)
-    return pl.pallas_call(
-        functools.partial(collect_kernel, count),
-        out_shape=[jax.ShapeDtypeStruct((4, 2) + p.shape, p.dtype) for p in pieces],
-        in_specs=[hbm] * count,
-        out_specs=[hbm] * count,
+    tall, wide = back.shape
+    got = pl.pallas_call(
+        functools.partial(collect_kernel, count, aside),
+        out_shape=[
+            *[jax.ShapeDtypeStruct((4, 2) + p.shape, p.dtype) for p in pieces],
+            jax.ShapeDtypeStruct((4, tall // 4, wide), back.dtype),
+            *aside.outs,
+        ],
+        in_specs=[hbm] * (count + 1) + aside.in_specs(),
+        out_specs=[hbm] * (count + 1) + aside.out_specs(),
         scratch_shapes=[
-            pltpu.SemaphoreType.DMA((count,)),
+            pltpu.VMEM((4, tall // 4, wide), back.dtype),
+            pltpu.SemaphoreType.DMA((count + 1,)),
             pltpu.SemaphoreType.DMA((10 * count,)),
             pltpu.SemaphoreType.DMA((10 * count,)),
+            pltpu.SemaphoreType.DMA((6,)),
+            pltpu.SemaphoreType.DMA((6,)),
+            *aside.scratch_shapes(),
         ],
         compiler_params=pltpu.CompilerParams(
-            collective_id=ident, has_side_effects=True, vmem_limit_bytes=4 * 1024 * 1024
+            collective_id=ident, has_side_effects=True, vmem_limit_bytes=VMEM_BYTES
         ),
         cost_estimate=pl.CostEstimate(
             flops=0, bytes_accessed=80 * sum(p.size for p in pieces), transcendentals=0
         ),
         name="collect",
-    )(*pieces)
+    )(*pieces, back.reshape(4, tall // 4, wide), *aside.operands)
+    return got[:count], got[count].reshape(tall, wide), got[count + 1 :]
 
 
 def spread_kernel(in_ref, out_ref):
@@ -431,67 +590,528 @@
     )(blocks)
 
 
-def total_kernel(x_ref, out_ref, land, s0, s1):
+def planes_after():
+    plane = lax.axis_index("seq")
+    return plane, [lax.rem(plane + k, 4) for k in (1, 2, 3)]
+
+
+def greet_all():
+    _, across, along, far = neighbours()
+    _, others = planes_after()
+    greet(
+        [{"tp": p} for p in (across, along, far)]
+        + [{"core": 1 - lax.axis_index("core")}]
+        + [{"seq": p} for p in others]
+    )
+
+
+def arrive_kernel(
+    tok_ref, cap_ref, cot_ref, msg_ref, w_ref, in_ref, caps_ref, cots_ref, msgs_ref, mod_ref,
+    stage, wbuf, part, land, load, s0, s1,
+):
     sems = (s0, s1)
     me, across, along, far = neighbours()
-    core, plane = lax.axis_index("core"), lax.axis_index("seq")
+    core = lax.axis_index("core")
+    plane, others = planes_after()
     peers = [across, along, far]
-    others = [lax.rem(plane + k, 4) for k in (1, 2, 3)]
-    greet(
-        [{"tp": p} for p in peers] + [{"core": 1 - core}] + [{"seq": p} for p in others]
-    )
+    quarter = mod_ref.shape[1] // 4
+    depth = msgs_ref.shape[-1]
+    columns = pl.ds(pl.multiple_of(me * quarter, quarter), quarter)
+    weights = pltpu.make_async_copy(w_ref.at[:, columns], wbuf, load.at[0])
+    weights.start()
+    mine = pltpu.make_async_copy(tok_ref.at[me], stage.at[me], load.at[1])
+    mine.start()
+    msgs_ref[me, core] = msg_ref[:, pl.ds(pl.multiple_of(plane * depth, depth), depth)]
+    greet_all()
+    here = msgs_ref.at[me, core]
+    first = [send(here, here, sems, k, {"tp": p}) for k, p in enumerate(peers)]
+    for copy in first:
+        copy.start()
+    spread_out = [
+        send(tok_ref.at[p], stage.at[me], sems, 3 + k, {"tp": p}) for k, p in enumerate(peers)
+    ]
+    for copy in spread_out:
+        copy.start()
+    captions = [
+        send(cap_ref.at[:, p], caps_ref.at[me], sems, 16 + k, {"tp": p})
+        for k, p in enumerate(peers)
+    ]
+    captions += [
+        send(cot_ref.at[p], cots_ref.at[me], sems, 19 + k, {"tp": p}) for k, p in enumerate(peers)
+    ]
+    for copy in captions:
+        copy.start()
+    own_caps = pltpu.make_async_copy(cap_ref.at[:, me], caps_ref.at[me], load.at[3])
+    own_caps.start()
+    own_cots = pltpu.make_async_copy(cot_ref.at[me], cots_ref.at[me], load.at[4])
+    own_cots.start()
+    for copy in first:
+        copy.wait_recv()
+    here = msgs_ref.at[:, core]
+    swap = send(here, here, sems, 6, {"core": 1 - core})
+    swap.start()
+    weights.wait()
+    conditions = msgs_ref[:, core].reshape(4 * 8, depth).astype(wbuf.dtype)
+    tile = 512
+    for step in range(quarter // tile):
+        at = pl.ds(step * tile, tile)
+        part[:, :, at] = jnp.dot(
+            conditions, wbuf[:, at], preferred_element_type=jnp.float32
+        ).reshape(4, 8, tile)
+    second = [
+        send(part.at[p], land.at[k], sems, 7 + k, {"seq": p}) for k, p in enumerate(others)
+    ]
+    for copy in second:
+        copy.start()
+    mine.wait()
+    for copy in spread_out:
+        copy.wait_recv()
+    third = [
+        send(stage.at[p], in_ref.at[plane], sems, 10 + k, {"seq": p})
+        for k, p in enumerate(others)
+    ]
+    for copy in third:
+        copy.start()
+    stay = pltpu.make_async_copy(stage.at[plane], in_ref.at[plane], load.at[2])
+    stay.start()
+    for copy in second:
+        copy.wait_recv()
+    mod_ref[:, columns] = (part[plane] + land[0]) + (land[1] + land[2])
+    here = mod_ref.at[:, columns]
+    fourth = [send(here, here, sems, 13 + k, {"tp": p}) for k, p in enumerate(peers)]
+    for copy in fourth:
+        copy.start()
+    swap.wait_recv()
+    for copy in fourth + third + captions:
+        copy.wait_recv()
+    stay.wait()
+    own_caps.wait()
+    own_cots.wait()
+    for copy in first + spread_out + captions + [swap] + second + third + fourth:
+        copy.wait_send()
+
+
+def arrive(ident, tokens, captions, cotangent, message, w_mod):
+    rows, width = tokens.shape
+    docs, caps, ctx = captions.shape
+    depth, wide = w_mod.shape
+    vmem, hbm = pl.BlockSpec(memory_space=pltpu.VMEM), pl.BlockSpec(memory_space=pl.ANY)
+    return pl.pallas_call(
+        arrive_kernel,
+        out_shape=[
+            jax.ShapeDtypeStruct((4, rows // 4, width), tokens.dtype),
+            jax.ShapeDtypeStruct((4, docs, caps // 4, ctx), captions.dtype),
+            jax.ShapeDtypeStruct((4, rows // 4, width), cotangent.dtype),
+            jax.ShapeDtypeStruct((4, 2, 8, depth), jnp.float32),
+            jax.ShapeDtypeStruct((8, wide), jnp.float32),
+        ],
+        in_specs=[hbm, hbm, hbm, vmem, hbm],
+        out_specs=[hbm, hbm, hbm, vmem, vmem],
+        scratch_shapes=[
+            pltpu.VMEM((4, rows // 4, width), tokens.dtype),
+            pltpu.VMEM((depth, wide // 4), w_mod.dtype),
+            pltpu.VMEM((4, 8, wide // 4), jnp.float32),
+            pltpu.VMEM((3, 8, wide // 4), jnp.float32),
+            pltpu.SemaphoreType.DMA((5,)),
+            pltpu.SemaphoreType.DMA((22,)),
+            pltpu.SemaphoreType.DMA((22,)),
+        ],
+        compiler_params=pltpu.CompilerParams(
+            collective_id=ident, has_side_effects=True, vmem_limit_bytes=16 * 1024 * 1024
+        ),
+        cost_estimate=pl.CostEstimate(flops=0, bytes_accessed=90_000_000, transcendentals=0),
+        name="arrive",
+    )(
+        tokens.reshape(4, rows // 4, width),
+        captions.reshape(docs, 4, caps // 4, ctx),
+        cotangent.reshape(4, rows // 4, width),
+        message,
+        w_mod,
+    )
+
+
+def finale_kernel(count, *refs):
+    ins, (back_ref, x_ref) = refs[:count], refs[count : count + 2]
+    outs, (home_ref, out_ref) = refs[count + 2 : 2 * count + 2], refs[2 * count + 2 : 2 * count + 4]
+    stage, land, load, c0, c1, s0, s1 = refs[2 * count + 4 :]
+    sems = (s0, s1)
+    me, across, along, far = neighbours()
+    core = lax.axis_index("core")
+    plane, others = planes_after()
+    peers = [across, along, far]
     quarter = x_ref.shape[1] // 4
+    gathering = Gathering(ins, outs, load, (c0, c1))
 
     def columns(t):
         return pl.ds(pl.multiple_of(t * quarter, quarter), quarter)
 
+    returning = Returning(back_ref, home_ref, stage, load.at[count], sems, 10)
+    greet_all()
     first = [
         send(x_ref.at[:, columns(p)], land.at[k], sems, k, {"tp": p}) for k, p in enumerate(peers)
     ]
     for copy in first:
         copy.start()
+    returning.begin()
+    gathering.begin()
     for copy in first:
         copy.wait_recv()
     out_ref[plane, core, :, columns(me)] = (x_ref[:, columns(me)] + land[0]) + (land[1] + land[2])
     here = out_ref.at[plane, core, :, columns(me)]
-    swap = send(here, here, sems, 3, {"core": 1 - core})
-    swap.start()
-    swap.wait_recv()
-    here = out_ref.at[plane, :, :, columns(me)]
-    second = [send(here, here, sems, 4 + k, {"seq": p}) for k, p in enumerate(others)]
+    second = [send(here, here, sems, 3 + k, {"seq": p}) for k, p in enumerate(others)]
     for copy in second:
         copy.start()
     for copy in second:
         copy.wait_recv()
-    here = out_ref.at[:, :, :, columns(me)]
-    third = [send(here, here, sems, 7 + k, {"tp": p}) for k, p in enumerate(peers)]
+    here = out_ref.at[:, core, :, columns(me)]
+    third = [send(here, here, sems, 6 + k, {"tp": p}) for k, p in enumerate(peers)]
     for copy in third:
         copy.start()
+    returning.turn()
+    gathering.relay()
     for copy in third:
         copy.wait_recv()
-    for copy in first + [swap] + second + third:
+    here = out_ref.at[:, core]
+    swap = send(here, here, sems, 9, {"core": 1 - core})
+    swap.start()
+    gathering.hand()
+    swap.wait_recv()
+    returning.end()
+    gathering.end()
+    for copy in first + second + third + [swap]:
         copy.wait_send()
 
 
-def total(ident, x):
-    vmem = pl.BlockSpec(memory_space=pltpu.VMEM)
+def finale(ident, pieces, back, x):
+    hbm, vmem = pl.BlockSpec(memory_space=pl.ANY), pl.BlockSpec(memory_space=pltpu.VMEM)
+    count = len(pieces)
     rows, width = x.shape
-    return pl.pallas_call(
-        total_kernel,
-        out_shape=jax.ShapeDtypeStruct((4, 2, rows, width), jnp.float32),
-        in_specs=[vmem],
-        out_specs=vmem,
+    tall, wide = back.shape
+    got = pl.pallas_call(
+        functools.partial(finale_kernel, count),
+        out_shape=[
+            *[jax.ShapeDtypeStruct((4, 2) + p.shape, p.dtype) for p in pieces],
+            jax.ShapeDtypeStruct((4, tall // 4, wide), back.dtype),
+            jax.ShapeDtypeStruct((4, 2, rows, width), jnp.float32),
+        ],
+        in_specs=[hbm] * (count + 1) + [vmem],
+        out_specs=[hbm] * (count + 1) + [vmem],
         scratch_shapes=[
+            pltpu.VMEM((4, tall // 4, wide), back.dtype),
             pltpu.VMEM((3, rows, width // 4), jnp.float32),
-            pltpu.SemaphoreType.DMA((10,)),
-            pltpu.SemaphoreType.DMA((10,)),
+            pltpu.SemaphoreType.DMA((count + 1,)),
+            pltpu.SemaphoreType.DMA((10 * count,)),
+            pltpu.SemaphoreType.DMA((10 * count,)),
+            pltpu.SemaphoreType.DMA((16,)),
+            pltpu.SemaphoreType.DMA((16,)),
         ],
         compiler_params=pltpu.CompilerParams(
             collective_id=ident, has_side_effects=True, vmem_limit_bytes=16 * 1024 * 1024
         ),
-        cost_estimate=pl.CostEstimate(flops=0, bytes_accessed=60_000_000, transcendentals=0),
-        name="total",
-    )(x)
+        cost_estimate=pl.CostEstimate(flops=0, bytes_accessed=120_000_000, transcendentals=0),
+        name="finale",
+    )(*pieces, back.reshape(4, tall // 4, wide), x)
+    return got[:count], got[count].reshape(tall, wide), got[count + 1]
+
+
+def lanes_of(rows):
+    return lax.broadcasted_iota(jnp.int32, (rows, 128), 1)
+
+
+def pair_norm(values):
+    lane = lanes_of(values.shape[0])
+    square = values * values
+    low = jnp.sum(jnp.where(lane < HDIM, square, 0.0), axis=-1, keepdims=True)
+    high = jnp.sum(jnp.where(lane < HDIM, 0.0, square), axis=-1, keepdims=True)
+    inverse = jnp.where(lane < HDIM, lax.rsqrt(low / HDIM + eps), lax.rsqrt(high / HDIM + eps))
+    return values * inverse, inverse
+
+
+def pair_back(grads, normed, inverse):
+    lane = lanes_of(grads.shape[0])
+    inner = grads * normed
+    low = jnp.sum(jnp.where(lane < HDIM, inner, 0.0), axis=-1, keepdims=True)
+    high = jnp.sum(jnp.where(lane < HDIM, 0.0, inner), axis=-1, keepdims=True)
+    return inverse * (grads - normed * (jnp.where(lane < HDIM, low, high) / HDIM))
+
+
+def pair_turn(values, cosine, sine):
+    lane = lanes_of(values.shape[0])
+    partner = jnp.where(
+        lane % HDIM < HDIM // 2, pltpu.roll(values, 96, 1), pltpu.roll(values, 32, 1)
+    )
+    return values * cosine + partner * sine
+
+
+def store_heads(target, strip, pair, spare):
+    lane = lanes_of(pair.shape[0])
+    first = jnp.where(lane < HDIM, pair, spare)
+    second = jnp.where(lane < HDIM, pltpu.roll(pair, HDIM, 1), spare)
+    target[strip, 0:128] = first.astype(target.dtype)
+    target[strip, 128:256] = second.astype(target.dtype)
+
+
+def join_heads(first, second):
+    lane = lanes_of(first.shape[0])
+    return jnp.where(lane < HDIM, first, pltpu.roll(second, HDIM, 1))
+
+
+def ones_beside(rows):
+    lane = lanes_of(rows)
+    return jnp.where((lane == HDIM) | (lane == HDIM + 1), 1.0, 0.0)
+
+
+def not_turned(left, right):
+    return lax.dot_general(
+        left, right, (((1,), (1,)), ((), ())), preferred_element_type=jnp.float32
+    )
+
+
+STRIP = 256
+SPARE = 128.0
+
+
+def strips(rows, body):
+    @pl.loop(0, rows // STRIP)
+    def _(step):
+        body(pl.ds(pl.multiple_of(step * STRIP, STRIP), STRIP))
+
+
+def weigh(qa_ref, ka_ref, va_ref, ov_ref):
+    for head in range(2):
+        at = pl.ds(head * 128, 128)
+
+        def body(strip):
+            scores = not_turned(qa_ref[strip, at], ka_ref[:, at])
+            weights = jnp.exp(scores).astype(jnp.bfloat16)
+            ov_ref[strip, at] = jnp.dot(
+                weights, va_ref[:, at], preferred_element_type=jnp.float32
+            )
+
+        strips(qa_ref.shape[0], body)
+
+
+def own_kernel(
+    q_ref, k_ref, v_ref, gq_ref, gk_ref, cos_ref, sin_ref, sq_ref, sk_ref,
+    qa_ref, ka_ref, va_ref, ov_ref,
+):
+    def prepare(strip):
+        cosine, sine = cos_ref[strip, :], sin_ref[strip, :]
+        query = pair_turn(pair_norm(q_ref[strip, :])[0] * gq_ref[...], cosine, sine)
+        store_heads(qa_ref, strip, query * HDIM**-0.5, sq_ref[strip, :])
+        keys = pair_turn(pair_norm(k_ref[strip, :])[0] * gk_ref[...], cosine, sine)
+        store_heads(ka_ref, strip, keys, sk_ref[strip, :])
+        store_heads(va_ref, strip, v_ref[strip, :], ones_beside(STRIP))
+
+    strips(q_ref.shape[0], prepare)
+    weigh(qa_ref, ka_ref, va_ref, ov_ref)
+
+
+def cross_kernel(
+    qa_ref, k_ref, v_ref, gk_ref, sq_ref, sk_ref, own_ref, gate_ref,
+    ka_ref, va_ref, ov_ref, mix_ref, qx_ref,
+):
+    def prepare(strip):
+        keys = pair_norm(k_ref[strip, :])[0] * gk_ref[...]
+        store_heads(ka_ref, strip, keys, sk_ref[strip, :])
+        store_heads(va_ref, strip, v_ref[strip, :], ones_beside(STRIP))
+
+    strips(k_ref.shape[0], prepare)
+
+    def requery(strip):
+        lane = lanes_of(STRIP)
+        for head in range(2):
+            at = pl.ds(head * 128, 128)
+            qx_ref[strip, at] = jnp.where(
+                lane < HDIM, qa_ref[strip, at].astype(jnp.float32), sq_ref[strip, :]
+            ).astype(qx_ref.dtype)
+
+    strips(qa_ref.shape[0], requery)
+    weigh(qx_ref, ka_ref, va_ref, ov_ref)
+
+    def mix(strip):
+        parts = []
+        for head in range(2):
+            at = pl.ds(head * 128, 128)
+            own, cross = own_ref[strip, at], ov_ref[strip, at]
+            parts.append((own / own[:, 64:65], cross / cross[:, 64:65]))
+        own = join_heads(parts[0][0], parts[1][0])
+        cross = join_heads(parts[0][1], parts[1][1])
+        mix_ref[strip, :] = (own + gate_ref[...] * cross).astype(mix_ref.dtype)
+
+    strips(qa_ref.shape[0], mix)
+
+
+def back_kernel(own, *refs):
+    g_ref, gate_ref, ov_ref, qa_ref, sq_ref, ka_ref, va_ref, k_ref, gk_ref = refs[:9]
+    refs = refs[9:]
+    if own:
+        q_ref, gq_ref, cos_ref, sin_ref, more_ref = refs[:5]
+        refs = refs[5:]
+    dq_ref, dk_ref, dv_ref, sum_ref, qx, doa, dqt, dqh, dkh, dvh = refs
+    rows, count = qa_ref.shape[0], ka_ref.shape[0]
+    sum_ref[...] = jnp.zeros_like(sum_ref)
+    for head in range(2):
+        at = pl.ds(head * 128, 128)
+
+        def prepare(strip):
+            lane = lanes_of(STRIP)
+            plain = g_ref[strip, :]
+            grads = plain * gate_ref[...]
+            if head == 1:
+                plain = pltpu.roll(plain, HDIM, 1)
+                grads = pltpu.roll(grads, HDIM, 1)
+            both = ov_ref[strip, at]
+            inverse = 1.0 / both[:, 64:65]
+            out = jnp.where(lane < HDIM, both * inverse, 0.0)
+            if not own:
+                sum_ref[0, head : head + 1, :] += jnp.sum(plain * out, axis=0, keepdims=True)
+            scaled = (grads * inverse).astype(jnp.bfloat16).astype(jnp.float32)
+            delta = jnp.sum(scaled * out, axis=-1, keepdims=True)
+            high = delta.astype(jnp.bfloat16).astype(jnp.float32)
+            doa[strip, :] = jnp.where(
+                lane < HDIM,
+                scaled,
+                jnp.where(lane == HDIM, -high, jnp.where(lane == HDIM + 1, high - delta, 0.0)),
+            ).astype(doa.dtype)
+            qx[strip, :] = jnp.where(
+                lane < HDIM, qa_ref[strip, at].astype(jnp.float32), sq_ref[strip, :]
+            ).astype(qx.dtype)
+
+        strips(rows, prepare)
+        dqt[...] = jnp.zeros_like(dqt)
+
+        def block(strip):
+            keys, values = ka_ref[strip, at], va_ref[strip, at]
+            weights = jnp.exp(not_turned(keys, qx[...]))
+            grads = (weights * not_turned(values, doa[...])).astype(jnp.bfloat16)
+            dvh[head, strip, :] = jnp.dot(
+                weights.astype(jnp.bfloat16), doa[...], preferred_element_type=jnp.float32
+            )
+            dkh[head, strip, :] = jnp.dot(grads, qx[...], preferred_element_type=jnp.float32)
+            dqt[...] += lax.dot_general(
+                keys, grads, (((0,), (0,)), ((), ())), preferred_element_type=jnp.float32
+            )
+
+        strips(count, block)
+        dqh[head] = dqt[...].T * HDIM**-0.5
+
+    def add_up(row, values):
+        sum_ref[0, row : row + 1, :] += jnp.sum(values, axis=0, keepdims=True)
+
+    def finish(strip):
+        grads = join_heads(dkh[0, strip, :], dkh[1, strip, :])
+        if own:
+            grads = pair_turn(grads, cos_ref[strip, :], -sin_ref[strip, :])
+        normed, inverse = pair_norm(k_ref[strip, :])
+        add_up(2, grads * normed)
+        dk_ref[strip, :] = pair_back(grads * gk_ref[...], normed, inverse).astype(dk_ref.dtype)
+        dv_ref[strip, :] = join_heads(dvh[0, strip, :], dvh[1, strip, :]).astype(dv_ref.dtype)
+
+    strips(count, finish)
+
+    def finish_query(strip):
+        grads = join_heads(dqh[0, strip, :], dqh[1, strip, :])
+        if own:
+            grads = pair_turn(grads + more_ref[strip, :], cos_ref[strip, :], -sin_ref[strip, :])
+            normed, inverse = pair_norm(q_ref[strip, :])
+            add_up(3, grads * normed)
+            grads = pair_back(grads * gq_ref[...], normed, inverse)
+        dq_ref[strip, :] = grads.astype(dq_ref.dtype)
+
+    strips(rows, finish_query)
+
+
+def view(ref, index, width=128, offset=0):
+    return ref.at[:, pl.ds((offset + index) * width, width)]
+
+
+def attend_own(projected, gain_q, gain_k, cosine, sine, spare_q, spare_k):
+    rows, width = projected.shape[0], projected.shape[1] // 3
+    count = width // 128
+    bf, f32 = jnp.bfloat16, jnp.float32
+
+    def steps(i, ins, outs, scratch):
+        raw, gain_q, gain_k, *tables = ins
+        own_kernel(
+            view(raw, i), view(raw, i, offset=count), view(raw, i, offset=2 * count),
+            view(gain_q, i), view(gain_k, i), *tables, *[view(out, i, 256) for out in outs],
+        )
+
+    return Aside(
+        [projected, gain_q, gain_k, cosine, sine, spare_q, spare_k],
+        [jax.ShapeDtypeStruct((rows, 2 * width), d) for d in (bf, bf, bf, f32)],
+        [],
+        steps,
+    )
+
+
+def attend_cross(qa, cap_proj, gain, spare_q, spare_k, own, gate):
+    rows, count = qa.shape[0], qa.shape[1] // 256
+    caps, width = cap_proj.shape[0], cap_proj.shape[1] // 2
+    bf, f32 = jnp.bfloat16, jnp.float32
+
+    def steps(i, ins, outs, scratch):
+        qa, raw, gain, spare_q, spare_k, own, gate = ins
+        ka, va, ov, mix = outs
+        cross_kernel(
+            view(qa, i, 256), view(raw, i), view(raw, i, offset=count), view(gain, i),
+            spare_q, spare_k, view(own, i, 256), view(gate, i),
+            view(ka, i, 256), view(va, i, 256), view(ov, i, 256), view(mix, i), *scratch,
+        )
+
+    return Aside(
+        [qa, cap_proj, gain, spare_q, spare_k, own, gate],
+        [
+            jax.ShapeDtypeStruct((caps, 2 * width), bf),
+            jax.ShapeDtypeStruct((caps, 2 * width), bf),
+            jax.ShapeDtypeStruct((rows, 2 * width), f32),
+            jax.ShapeDtypeStruct((rows, width), bf),
+        ],
+        [pltpu.VMEM((rows, 256), bf)],
+        steps,
+    )
+
+
+def attend_back(grads, gate, ov, qa, spare_q, ka, va, raw, gain_k, rest=None):
+    rows, width = grads.shape
+    caps, count = ka.shape[0], width // 128
+    bf, f32 = jnp.bfloat16, jnp.float32
+    own = rest is not None
+
+    def steps(i, ins, outs, scratch):
+        grads, gate, ov, qa, spare_q, ka, va, raw, gain_k, *rest = ins
+        dq, dk, dv, sums = outs
+        operands = [
+            view(grads, i), view(gate, i), view(ov, i, 256), view(qa, i, 256), spare_q,
+            view(ka, i, 256), view(va, i, 256), view(raw, i, offset=count if own else 0),
+            view(gain_k, i),
+        ]
+        if own:
+            gain_q, cosine, sine, more = rest
+            operands += [view(raw, i), view(gain_q, i), cosine, sine, view(more, i)]
+        back_kernel(
+            own, *operands, view(dq, i), view(dk, i), view(dv, i), sums.at[pl.ds(i, 1)], *scratch
+        )
+
+    return Aside(
+        [grads, gate, ov, qa, spare_q, ka, va, raw, gain_k, *(rest or ())],
+        [
+            jax.ShapeDtypeStruct((rows, width), bf if own else f32),
+            jax.ShapeDtypeStruct((caps, width), bf),
+            jax.ShapeDtypeStruct((caps, width), bf),
+            jax.ShapeDtypeStruct((count, 8, 128), f32),
+        ],
+        [
+            pltpu.VMEM((rows, 128), bf),
+            pltpu.VMEM((rows, 128), bf),
+            pltpu.VMEM((128, rows), f32),
+            pltpu.VMEM((2, rows, 128), f32),
+            pltpu.VMEM((2, caps, 128), f32),
+            pltpu.VMEM((2, caps, 128), f32),
+        ],
+        steps,
+    )
 
 
 def row_stats(values):
@@ -543,6 +1163,23 @@
     return (segment, (within // stride).astype(jnp.float32), (within % stride).astype(jnp.float32))
 
 
+def turn_tables(row_pos, col_pos):
+    quarter = HDIM // 4
+    freqs = 10000.0 ** (-jnp.arange(quarter, dtype=jnp.float32) / quarter)
+    angles = jnp.concatenate([row_pos[:, None] * freqs, col_pos[:, None] * freqs], axis=1)
+    cosine, sine = jnp.cos(angles), jnp.sin(angles)
+    return jnp.tile(cosine, (1, 4)), jnp.concatenate([-sine, sine, -sine, sine], axis=1)
+
+
+def spare_columns(labels, height):
+    lane = jnp.arange(128)[None, :] - HDIM
+    at_label = (lane >= 0) & (lane <= DOCS) & (lane == labels[:, None])
+    last = lane == DOCS + 1
+    if height:
+        return jnp.where(at_label, height, jnp.where(last, -height, 0.0)).astype(jnp.float32)
+    return (at_label | last).astype(jnp.float32)
+
+
 def by_head(values):
     return values.reshape(values.shape[0], -1, 1, HDIM).transpose(1, 0, 2, 3)
 
@@ -660,10 +1297,13 @@
     return whole.reshape(-1, halves.shape[-1])
 
 
-def scatter_rows(term):
+def swap_rows(term):
     cores, planes = lax.axis_size("core"), lax.axis_size("seq")
-    shaped = term.astype(jnp.bfloat16).reshape(planes, cores, -1, term.shape[-1])
-    return lax.psum_scatter(swap_halves(shaped), "seq", scatter_dimension=0, tiled=False)
+    return swap_halves(term.astype(jnp.bfloat16).reshape(planes, cores, -1, term.shape[-1]))
+
+
+def scatter_planes(term):
+    return lax.psum_scatter(term, "seq", scatter_dimension=0, tiled=False)
 
 
 def swap_halves(shaped):
@@ -680,27 +1320,25 @@
     return lax.all_gather(values, "tp", axis=0, tiled=True)
 
 
-def plane_multiply(ident, x, weight, turned=False, halved=False):
+def plane_multiply(ident, x, weight, turned=False, halved=False, width=None, **more):
     if fast():
-        got = gather_matmul(ident, x, weight, turned, halved)
-        return got[0], got[1] if halved else weight, got[-1]
+        return gather_matmul(ident, x, weight, turned, halved, width, **more)
     whole = join_cores(weight) if halved else weight
     x = plane_gather(x)
-    return x, whole, contract_right(x, whole) if turned else matmul(x, whole)
-
-
-def multiply_plane(ident, x, weight, turned=False):
+    return x, whole, contract_right(x, whole) if turned else matmul(x, whole[:, :width])
+
+
+def multiply_plane(ident, x, weight, turned=False, **more):
     if fast():
-        return matmul_scatter(ident, x, weight, turned)
+        return matmul_scatter(ident, x, weight, turned, **more)
+    weight = weight[:, : x.shape[1]] if turned else weight
     term = contract_right(x, weight) if turned else matmul(x, weight)
     return lax.psum_scatter(
         term.astype(jnp.bfloat16), "tp", scatter_dimension=0, tiled=True
-    ).astype(jnp.float32)
-
-
-def collect_plane(ident, pieces):
-    if fast():
-        return collect(ident, pieces)
+    ).astype(jnp.float32), None
+
+
+def collect_plane(pieces):
     return [
         lax.all_gather(p, ("tp", "core"), axis=0, tiled=False).reshape(
             (lax.axis_size("tp"), lax.axis_size("core")) + p.shape
@@ -721,12 +1359,33 @@
     )
 
 
-def total_plane(ident, x):
+def arrive_plane(ident, tokens, captions, cotangent, message, w_mod):
     if fast():
-        return total(ident, x)
-    return lax.all_gather(lax.psum(x, "tp"), ("seq", "core"), axis=0, tiled=False).reshape(
-        (lax.axis_size("seq"), lax.axis_size("core")) + x.shape
-    )
+        return arrive(ident, tokens, captions, cotangent, message, w_mod)
+    ways = lax.axis_size("tp")
+    docs, caps, ctx = captions.shape
+    captions = captions.reshape(docs, ways, caps // ways, ctx).transpose(1, 0, 2, 3)
+    captions = lax.all_to_all(captions, "tp", 0, 0, tiled=True)
+    cotangent = lax.all_to_all(
+        cotangent.reshape(ways, -1, cotangent.shape[1]), "tp", 0, 0, tiled=True
+    )
+    planes, cores = lax.axis_size("seq"), lax.axis_size("core")
+    depth = w_mod.shape[0]
+    part = lax.dynamic_slice_in_dim(message, lax.axis_index("seq") * depth, depth, 1)
+    messages = lax.all_gather(part, ("tp", "core"), axis=0, tiled=False)
+    terms = matmul(messages.reshape(-1, depth).astype(w_mod.dtype), w_mod)
+    terms = lax.psum_scatter(
+        terms.reshape(planes, cores, 8, -1), "seq", scatter_dimension=0, tiled=False
+    )
+    messages = messages.reshape(lax.axis_size("tp"), cores, 8, depth)
+    return to_plane(tokens), captions, cotangent, messages, pick(terms, lax.axis_index("core"), 0)
+
+
+def finale_plane(ident, pieces, back, x):
+    if fast():
+        return finale(ident, pieces, back, x)
+    totals = lax.all_gather(lax.psum(x, "tp"), ("seq", "core"), axis=0, tiled=False)
+    return collect_plane(pieces), from_plane(back), totals
 
 
 def shards(
@@ -763,21 +1422,27 @@
     ctx = caption.shape[3]
     my_group = me_z * cores + me_c
 
-    numbers = jnp.concatenate([lengths[0], group_bucket, null_mask[0]])
-    numbers = lax.all_gather(numbers, ("tp", "core"), axis=0, tiled=False).reshape(groups, -1)
+    condition = jax.nn.silu(step_embed[0].astype(jnp.float32)).astype(jnp.bfloat16)
+    numbers = jnp.concatenate([lengths[0], group_bucket, null_mask[0]]).astype(jnp.float32)
+    mod_rows = w_mod.shape[0]
+    numbers = jnp.tile(jnp.pad(numbers, (0, mod_rows - numbers.shape[0])), planes)
+    message = jnp.concatenate(
+        [condition.astype(jnp.float32), numbers[None], jnp.zeros((3, numbers.shape[0]))], axis=0
+    )
+    arrived, captions, cotangents, messages, mod_doc = arrive_plane(
+        13, tokens, caption[0], cotangent, message, w_mod
+    )
+    captions = lax.all_to_all(captions, "seq", 0, 0, tiled=True)
+    messages = messages.reshape(groups, 8, mod_rows)
+    cond_mine = messages[:, :DOCS].reshape(groups * DOCS, mod_rows)
+    mod_doc = mod_doc[:DOCS] + b_mod
+
+    numbers = messages[:, DOCS, : 2 * DOCS + 1].astype(jnp.int32)
     counts = jnp.sum(numbers[:, :DOCS], axis=1).astype(jnp.float32)
     mine = pick(numbers, my_group, 0)
     doc_lengths, bucket, nulls = mine[:DOCS], mine[DOCS], mine[DOCS + 1 :]
     bucket_count = jnp.sum(jnp.where(numbers[:, DOCS] == bucket, counts, 0.0))
     scale_loss = jnp.sum(counts) / (RES * bucket_count)
-
-    steps = lax.all_gather(step_embed[0], ("tp", "core"), axis=0, tiled=True)
-    condition = jax.nn.silu(steps.astype(jnp.float32)).astype(jnp.bfloat16)
-    mod_rows = w_mod.shape[0]
-    cond_mine = lax.dynamic_slice_in_dim(condition, me_z * mod_rows, mod_rows, 1)
-    mod_all = matmul(cond_mine, w_mod).reshape(planes, cores * DOCS, -1)
-    mod_plane = lax.psum_scatter(mod_all, "seq", scatter_dimension=0, tiled=False)
-    mod_doc = pick(mod_plane.reshape(cores, DOCS, -1), me_c, 0) + b_mod
 
     def columns_of(weight, parts):
         share = weight.shape[0] // cores
@@ -790,20 +1455,19 @@
             axis=1,
         )
 
-    half_qkv = gather_planes(columns_of(w_qkv, 3))
-    half_capkv = gather_planes(columns_of(w_capkv, 2))
-    out_part = gather_planes(columns_of(w_out, 1))
-    out_part = lax.all_to_all(out_part, "tp", 0, 0, tiled=True)
-    out_part = out_part.transpose(1, 0, 2).reshape(local // cores, width)
-    full_out = lax.all_gather(out_part, "core", axis=0, tiled=True)
-    half_gateup = gather_planes(columns_of(w_gateup, 2 * planes))
+    half_qkv = gather_planes(
+        jnp.concatenate([columns_of(w_qkv, 3), columns_of(w_out, 1)], axis=1)
+    )
     share = w_down.shape[0] // groups
-    half_down = gather_planes(
-        lax.dynamic_slice_in_dim(w_down, (me_t * cores + me_c) * share, share, 0)
-    )
-    full_down = join_cores(half_down)
-
-    inputs = to_plane(tokens).astype(jnp.float32)
+    later = (
+        columns_of(w_capkv, 2),
+        lax.dynamic_slice_in_dim(w_down, (me_t * cores + me_c) * share, share, 0),
+        columns_of(w_gateup, 2 * planes),
+    )
+    arrived, *later = lax.optimization_barrier((arrived, *later))
+    half_capkv, half_down, half_gateup = [gather_planes(part) for part in later]
+
+    inputs = arrived.reshape(tokens.shape).astype(jnp.float32)
     row = jnp.arange(rows, dtype=jnp.int32)
     spread = (row // piece) * rows + row % piece
     positions = spread + me_t * piece
@@ -820,35 +1484,69 @@
 
     normed1, inverse1 = row_stats(inputs)
     hidden1 = (normed1 * gain_attn * (1.0 + scale_a)).astype(jnp.bfloat16)
-    hidden1, full_qkv, projected = plane_multiply(1, hidden1, half_qkv, halved=True)
-    query_raw, key_raw, value_raw = jnp.split(projected, 3, axis=1)
-    query_norm, query_inv = head_stats(query_raw)
-    key_norm, key_inv = head_stats(key_raw)
-    my_gain_query = pick(gain_query.reshape(tp, local), me_t, 0)
-    my_gain_key = pick(gain_key.reshape(tp, local), me_t, 0)
-    my_gain_capkey = pick(gain_capkey.reshape(tp, local), me_t, 0)
-    query = rotary(query_norm * my_gain_query, row_pos, col_pos, 1.0).astype(jnp.bfloat16)
-    keys = rotary(key_norm * my_gain_key, row_pos, col_pos, 1.0).astype(jnp.bfloat16)
-    values = value_raw.astype(jnp.bfloat16)
-
-    captions = to_plane(caption[0].transpose(1, 0, 2)).transpose(1, 0, 2)
+    hidden1, full_qkv, projected = plane_multiply(
+        1, hidden1, half_qkv, halved=True, width=3 * local
+    )
+    cotangents, projected = lax.optimization_barrier((cotangents, projected))
+    cotangents = lax.all_to_all(cotangents, "seq", 0, 0, tiled=True).reshape(tokens.shape)
+    full_out = full_qkv[:, 3 * local :].reshape(tp, local, local)
+    full_out = lax.all_to_all(full_out, "tp", 0, 0, tiled=True)
+    full_out = full_out.transpose(1, 0, 2).reshape(local, width)
+    my_gain_query = pick(gain_query.reshape(tp, 1, local), me_t, 0)
+    my_gain_key = pick(gain_key.reshape(tp, 1, local), me_t, 0)
+    my_gain_capkey = pick(gain_capkey.reshape(tp, 1, local), me_t, 0)
+    gate_tanh = pick(jnp.tanh(gate_head).reshape(tp, local_heads), me_t, 0)
+    head_gate = jnp.repeat(gate_tanh, HDIM)[None, :]
+    own_aside = {}
+    if fast():
+        cosine, sine = turn_tables(row_pos, col_pos)
+        own_spare = spare_columns(all_segment, SPARE)
+        own_aside["aside"] = attend_own(
+            projected, my_gain_query, my_gain_key, cosine, sine,
+            own_spare, spare_columns(all_segment, 0),
+        )
+
+    captions = captions.transpose(1, 0, 2, 3).reshape(caption.shape[1:])
     capmix = jnp.where(nulls[:, None, None] > 0, null_embed[None, None, :], captions)
     cap_flat = capmix.reshape(DOCS * cap_dev, ctx)
-    cap_flat, full_capkv, cap_proj = plane_multiply(2, cap_flat, half_capkv, halved=True)
+    cap_flat, full_capkv, cap_proj, *own_wides = plane_multiply(
+        2, cap_flat, half_capkv, halved=True, **own_aside
+    )
     cap_document = jnp.tile(jnp.repeat(jnp.arange(DOCS, dtype=jnp.int32), cap_dev), tp)
-    capkey_raw, capval_raw = jnp.split(cap_proj, 2, axis=1)
-    capkey_norm, capkey_inv = head_stats(capkey_raw)
-    capkeys = (capkey_norm * my_gain_capkey).astype(jnp.bfloat16)
-    capvals = capval_raw.astype(jnp.bfloat16)
-
-    self_allowed = all_segment[:, None] == all_segment[None, :]
-    cross_allowed = all_document[:, None] == cap_document[None, :]
-    own_out, own_log = attend_forward(query, keys, values, self_allowed)
-    cross_out, cross_log = attend_forward(query, capkeys, capvals, cross_allowed)
-    gate_tanh = pick(jnp.tanh(gate_head).reshape(tp, local_heads), me_t, 0)
-    head_gate = jnp.repeat(gate_tanh, HDIM)[None, :]
-    mixed_attn = (own_out + head_gate * cross_out).astype(jnp.bfloat16)
-    attn_out = multiply_plane(3, mixed_attn, full_out)
+    grad_res0 = cotangents.astype(jnp.float32) * (is_valid * scale_loss)[:, None]
+    grad_down = (tanh_f * grad_res0).astype(jnp.bfloat16)
+    if fast():
+        wide_query, wide_keys, wide_values, own_wide = own_wides
+        cross_spare = spare_columns(all_document, SPARE)
+        cross_aside = attend_cross(
+            wide_query, cap_proj, my_gain_capkey, cross_spare,
+            spare_columns(cap_document, 0), own_wide, head_gate,
+        )
+        grad_down, full_down, grad_ffn, wide_capkeys, wide_capvals, cross_wide, mixed_attn = (
+            plane_multiply(
+                6, grad_down, half_down, turned=True, halved=True, aside=cross_aside, early=1
+            )
+        )
+    else:
+        grad_down, full_down, grad_ffn = plane_multiply(
+            6, grad_down, half_down, turned=True, halved=True
+        )
+        query_raw, key_raw, value_raw = jnp.split(projected, 3, axis=1)
+        query_norm, query_inv = head_stats(query_raw)
+        key_norm, key_inv = head_stats(key_raw)
+        capkey_raw, capval_raw = jnp.split(cap_proj, 2, axis=1)
+        capkey_norm, capkey_inv = head_stats(capkey_raw)
+        query = rotary(query_norm * my_gain_query, row_pos, col_pos, 1.0).astype(jnp.bfloat16)
+        keys = rotary(key_norm * my_gain_key, row_pos, col_pos, 1.0).astype(jnp.bfloat16)
+        values = value_raw.astype(jnp.bfloat16)
+        capkeys = (capkey_norm * my_gain_capkey).astype(jnp.bfloat16)
+        capvals = capval_raw.astype(jnp.bfloat16)
+        self_allowed = all_segment[:, None] == all_segment[None, :]
+        cross_allowed = all_document[:, None] == cap_document[None, :]
+        own_out, own_log = attend_forward(query, keys, values, self_allowed)
+        cross_out, cross_log = attend_forward(query, capkeys, capvals, cross_allowed)
+        mixed_attn = (own_out + head_gate * cross_out).astype(jnp.bfloat16)
+    attn_out, *_ = multiply_plane(3, mixed_attn, full_out)
     residual = inputs + tanh_a * attn_out
     normed2, inverse2 = row_stats(residual)
     hidden2 = (normed2 * gain_ffn * (1.0 + scale_f)).astype(jnp.bfloat16)
@@ -857,17 +1555,16 @@
     sig_gate = jax.nn.sigmoid(gate_part)
     silu_gate = gate_part * sig_gate
     hidden_ffn = (silu_gate * up_part).astype(jnp.bfloat16)
-    down_out = multiply_plane(5, hidden_ffn, full_down)
-    result = from_plane((residual + tanh_f * down_out).astype(jnp.bfloat16))
-
-    grad_res0 = to_plane(cotangent).astype(jnp.float32) * (is_valid * scale_loss)[:, None]
-    grad_down = (tanh_f * grad_res0).astype(jnp.bfloat16)
-    grad_down, _, grad_ffn = plane_multiply(6, grad_down, full_down, turned=True)
-    grad_gate_f = grad_res0 * down_out * (1.0 - tanh_f * tanh_f)
     grad_gate_part = grad_ffn * up_part * sig_gate * (1.0 + gate_part * (1.0 - sig_gate))
     grad_up_part = grad_ffn * silu_gate
     grad_gateup = jnp.concatenate([grad_gate_part, grad_up_part], axis=1).astype(jnp.bfloat16)
-    grad_hidden2 = multiply_plane(7, grad_gateup, full_gateup, turned=True)
+    term_down = swap_rows(contract_rows(hidden_ffn, grad_down))
+    term_gateup = swap_rows(contract_rows(hidden2, grad_gateup))
+    grad_gateup, term_down, term_gateup = lax.optimization_barrier(
+        (grad_gateup, term_down, term_gateup)
+    )
+    term_down, term_gateup = scatter_planes(term_down), scatter_planes(term_gateup)
+    grad_hidden2, *_ = multiply_plane(7, grad_gateup, full_gateup, turned=True)
     gain_ffn_term = jnp.sum(grad_hidden2 * normed2 * (1.0 + scale_f), axis=0)
     grad_scale_f = grad_hidden2 * normed2 * gain_ffn
     grad_residual = grad_res0 + norm_back(
@@ -876,34 +1573,80 @@
     grad_attn = (tanh_a * grad_residual).astype(jnp.bfloat16)
     grad_attn, _, grad_mix = plane_multiply(8, grad_attn, full_out, turned=True)
     grad_gate_a = grad_residual * attn_out * (1.0 - tanh_a * tanh_a)
-    grad_own = grad_mix.astype(jnp.bfloat16)
-    grad_cross = (head_gate * grad_mix).astype(jnp.bfloat16)
-    gate_head_term = jnp.sum(
-        (grad_mix * cross_out).reshape(-1, local_heads, HDIM), axis=(0, 2)
-    ) * (1.0 - gate_tanh * gate_tanh)
-    query_own, grad_keys, grad_values = attend_backward(
-        query, keys, values, self_allowed, own_log, grad_own
-    )
-    query_cross, grad_capkeys, grad_capvals = attend_backward(
-        query, capkeys, capvals, cross_allowed, cross_log, grad_cross
-    )
-    grad_query = rotary(query_own + query_cross, row_pos, col_pos, -1.0)
-    gain_query_term = jnp.sum(grad_query * query_norm, axis=0)
-    grad_query_raw = head_back(grad_query * my_gain_query, query_norm, query_inv)
-    grad_key = rotary(grad_keys, row_pos, col_pos, -1.0)
-    gain_key_term = jnp.sum(grad_key * key_norm, axis=0)
-    grad_key_raw = head_back(grad_key * my_gain_key, key_norm, key_inv)
-    grad_projected = jnp.concatenate([grad_query_raw, grad_key_raw, grad_values], axis=1).astype(
-        jnp.bfloat16
-    )
-    grad_hidden1 = multiply_plane(9, grad_projected, full_qkv, turned=True)
+    term_out = contract_rows(mixed_attn, grad_attn).astype(jnp.bfloat16)
+    term_out = swap_halves(term_out.reshape(1, cores, -1, width))[0]
+    term_out = term_out.reshape(term_out.shape[0], tp, -1).transpose(1, 0, 2)
+    term_out = lax.all_to_all(term_out, "tp", 0, 0, tiled=True)
+    grad_mix, term_out, term_down, term_gateup = lax.optimization_barrier(
+        (grad_mix, term_out, term_down, term_gateup)
+    )
+    term_out = scatter_planes(term_out)
+    if fast():
+        cross_aside = attend_back(
+            grad_mix, head_gate, cross_wide, wide_query, cross_spare,
+            wide_capkeys, wide_capvals, cap_proj, my_gain_capkey,
+        )
+        down_out, query_cross, grad_capkey_raw, grad_capvals, cross_sums = multiply_plane(
+            5, hidden_ffn, full_down, aside=cross_aside
+        )
+        gate_head_term = jnp.sum(cross_sums[:, :2], axis=-1).reshape(-1)
+        gain_capkey_term = cross_sums[:, 2].reshape(-1)
+        grad_cap_proj = jnp.concatenate([grad_capkey_raw, grad_capvals], axis=1)
+        term_capkv = swap_rows(contract_rows(cap_flat, grad_cap_proj))
+        query_cross, term_capkv = lax.optimization_barrier((query_cross, term_capkv))
+        term_capkv = scatter_planes(term_capkv)
+        own_aside = attend_back(
+            grad_mix, jnp.ones_like(head_gate), own_wide, wide_query, own_spare,
+            wide_keys, wide_values, projected, my_gain_key,
+            (my_gain_query, cosine, sine, query_cross),
+        )
+        result = (residual + tanh_f * down_out).astype(jnp.bfloat16)
+        (all_down, all_gateup, all_out), result, (*grad_projected, own_sums) = collect(
+            10, [term_down, term_gateup, term_out], result, own_aside
+        )
+        gain_key_term, gain_query_term = own_sums[:, 2].reshape(-1), own_sums[:, 3].reshape(-1)
+        grad_projected = jnp.concatenate(grad_projected, axis=1)
+    else:
+        down_out, _ = multiply_plane(5, hidden_ffn, full_down)
+        result = from_plane((residual + tanh_f * down_out).astype(jnp.bfloat16))
+        all_down, all_gateup, all_out = collect_plane([term_down, term_gateup, term_out])
+        grad_own = grad_mix.astype(jnp.bfloat16)
+        grad_cross = (head_gate * grad_mix).astype(jnp.bfloat16)
+        gate_head_term = jnp.sum(
+            (grad_mix * cross_out).reshape(-1, local_heads, HDIM), axis=(0, 2)
+        )
+        query_own, grad_keys, grad_values = attend_backward(
+            query, keys, values, self_allowed, own_log, grad_own
+        )
+        query_cross, grad_capkeys, grad_capvals = attend_backward(
+            query, capkeys, capvals, cross_allowed, cross_log, grad_cross
+        )
+        grad_query = rotary(query_own + query_cross, row_pos, col_pos, -1.0)
+        gain_query_term = jnp.sum(grad_query * query_norm, axis=0)
+        grad_query_raw = head_back(grad_query * my_gain_query, query_norm, query_inv)
+        grad_key = rotary(grad_keys, row_pos, col_pos, -1.0)
+        gain_key_term = jnp.sum(grad_key * key_norm, axis=0)
+        grad_key_raw = head_back(grad_key * my_gain_key, key_norm, key_inv)
+        grad_projected = jnp.concatenate(
+            [grad_query_raw, grad_key_raw, grad_values], axis=1
+        ).astype(jnp.bfloat16)
+        gain_capkey_term = jnp.sum(grad_capkeys * capkey_norm, axis=0)
+        grad_capkey_raw = head_back(grad_capkeys * my_gain_capkey, capkey_norm, capkey_inv)
+        grad_cap_proj = jnp.concatenate([grad_capkey_raw, grad_capvals], axis=1).astype(
+            jnp.bfloat16
+        )
+        term_capkv = scatter_planes(swap_rows(contract_rows(cap_flat, grad_cap_proj)))
+    grad_gate_f = grad_res0 * down_out * (1.0 - tanh_f * tanh_f)
+    gate_head_term = gate_head_term * (1.0 - gate_tanh * gate_tanh)
+    term_qkv = swap_rows(contract_rows(hidden1, grad_projected))
+    grad_projected, term_qkv = lax.optimization_barrier((grad_projected, term_qkv))
+    term_qkv = scatter_planes(term_qkv)
+    grad_hidden1, *_ = multiply_plane(9, grad_projected, full_qkv, turned=True)
     gain_attn_term = jnp.sum(grad_hidden1 * normed1 * (1.0 + scale_a), axis=0)
     grad_scale_a = grad_hidden1 * normed1 * gain_attn
-    input_grad = from_plane(
-        (
-            grad_residual + norm_back(grad_hidden1 * gain_attn * (1.0 + scale_a), normed1, inverse1)
-        ).astype(jnp.bfloat16)
-    )
+    input_grad = (
+        grad_residual + norm_back(grad_hidden1 * gain_attn * (1.0 + scale_a), normed1, inverse1)
+    ).astype(jnp.bfloat16)
 
     grad_mod_tok = jnp.concatenate([grad_scale_a, grad_gate_a, grad_scale_f, grad_gate_f], axis=1)
     grad_mod_doc = lax.dot_general(
@@ -913,9 +1656,6 @@
         precision=lax.Precision.HIGHEST,
         preferred_element_type=jnp.float32,
     )
-    gain_capkey_term = jnp.sum(grad_capkeys * capkey_norm, axis=0)
-    grad_capkey_raw = head_back(grad_capkeys * my_gain_capkey, capkey_norm, capkey_inv)
-    grad_cap_proj = jnp.concatenate([grad_capkey_raw, grad_capvals], axis=1).astype(jnp.bfloat16)
     null_rows = nulls[cap_document] > 0
     null_sum = jnp.sum(
         jnp.where(null_rows[:, None], grad_cap_proj.astype(jnp.float32), 0.0), axis=0
@@ -924,22 +1664,9 @@
         full_capkv.astype(jnp.float32), null_sum, precision=lax.Precision.HIGHEST
     )
 
-    term_down = scatter_rows(contract_rows(hidden_ffn, grad_down))
-    term_gateup = scatter_rows(contract_rows(hidden2, grad_gateup))
-    term_out = contract_rows(mixed_attn, grad_attn).astype(jnp.bfloat16)
-    term_out = swap_halves(term_out.reshape(1, cores, -1, width))[0]
-    term_out = term_out.reshape(term_out.shape[0], tp, -1).transpose(1, 0, 2)
-    term_out = lax.all_to_all(term_out, "tp", 0, 0, tiled=True)
-    term_out = lax.psum_scatter(term_out, "seq", scatter_dimension=0, tiled=False)
-    term_capkv = scatter_rows(contract_rows(cap_flat, grad_cap_proj))
-    term_qkv = scatter_rows(contract_rows(hidden1, grad_projected))
-    all_down, all_gateup, all_out = collect_plane(10, [term_down, term_gateup, term_out])
-    all_capkv, all_qkv = collect_plane(11, [term_capkv, term_qkv])
     sum_down = all_down.reshape(w_down.shape).astype(jnp.float32)
     sum_gateup = spread_parts(all_gateup, 2 * planes)
     sum_out = spread_parts(all_out, 1)
-    sum_capkv = spread_parts(all_capkv, 2)
-    sum_qkv = spread_parts(all_qkv, 3)
 
     def at_mine(part):
         whole = jnp.zeros((tp,) + part.shape, jnp.float32)
@@ -959,12 +1686,18 @@
     small_rows = 8 - DOCS
     small_size = small.shape[0]
     small = jnp.pad(small, (0, small_rows * 4 * width - small_size))
-    totals = total_plane(
-        12, jnp.concatenate([grad_mod_doc, small.reshape(small_rows, 4 * width)], axis=0)
-    ).reshape(groups, 8, 4 * width)
+    (all_capkv, all_qkv), input_grad, totals = finale_plane(
+        12,
+        [term_capkv, term_qkv],
+        input_grad,
+        jnp.concatenate([grad_mod_doc, small.reshape(small_rows, 4 * width)], axis=0),
+    )
+    totals = totals.reshape(groups, 8, 4 * width)
+    sum_capkv = spread_parts(all_capkv, 2)
+    sum_qkv = spread_parts(all_qkv, 3)
     grad_mod_docs = totals[:, :DOCS].reshape(groups * DOCS, 4 * width)
     sum_mod = lax.dot_general(
-        cond_mine.astype(jnp.float32),
+        cond_mine,
         grad_mod_docs,
         (((0,), (0,)), ((), ())),
         precision=lax.Precision.HIGHEST,

time: 1230 us -> 943 us (0.77)
  matrix products: 212 us -> 54.4 us
  Pallas kernels: 488 us -> 554 us
  blocking collectives: 54.7 us -> 13.2 us
  local copies, waits for them, and re-layouts: 113 us -> 74 us
  waiting for transfers between devices: 159 us -> 120 us
  other arithmetic: 117 us -> 79.8 us
  starting transfers between devices: 52.1 us -> 20 us
    dot_general x86 -> x1, matrix products: 163 us -> 8.41 us  [shards(): lax.dot_general(cond_mine, grad_mod_docs, (((0,), (0,)), ((), ())), preci...]
    all_to_all x11 -> x3, waiting for transfers between devices: 156 us -> 78.7 us  [the longest x1 44.3 us: shards(): captions = lax.all_to_all(captions, 'seq', 0, 0, tiled=True)]
    pallas_call x12, Pallas kernels: 458 us -> 524 us  [the longest x5 202 us: gather_matmul(): pl.pallas_call(functools.partial(gather_kernel, turned, halved, early, as...]
    all_gather x2 -> x0, blocking collectives: 35.3 us -> none  [the longest x1 24.5 us: gather_planes(): return lax.all_gather(part, 'seq', axis=0, tiled=False)]
    reduce_scatter x6 -> x5, waiting for transfers between devices: 0.04 us -> 31 us  [scatter_planes(): return lax.psum_scatter(term, 'seq', scatter_dimension=0, tiled=False)]
    all_to_all x11 -> x3, starting transfers between devices: 49.9 us -> 19 us  [the longest x1 11.2 us: shards(): captions = lax.all_to_all(captions, 'seq', 0, 0, tiled=True)]
    reduce_sum x20 -> x1, other arithmetic: 15.9 us -> 0.79 us  [shards(): gate_head_term = jnp.sum(cross_sums[:, :2], axis=-1).reshape(-1)]
    convert_element_type x15 -> x7, other arithmetic: 19.7 us -> 6.02 us  [the longest x1 2.58 us: shards(): hidden2 = (normed2 * gain_ffn * (1.0 + scale_f)).astype(jnp.bfloat16)]
  transfers between devices with their start and end apart: 28 -> 17, of which waited for: 9 -> 8; matrix products, arithmetic and copies ran while one was open for 31% -> 13% of each run, Pallas kernels for 25% -> 36%
where the time goes in v3:
time: 943 us; the launch traced here: 932 us
  Pallas kernels  554 us (59%)
  waiting for transfers between devices  120 us (13%)
  other arithmetic  79.8 us (8%)
  local copies, waits for them, and re-layouts  74 us (8%)
  matrix products  54.4 us (6%)
  starting transfers between devices  20 us (2%)
  between operations  17.6 us (2%)
  blocking collectives  13.2 us (1%)
    pallas_call x5, Pallas kernels, gather_matmul(): pl.pallas_call(functools.partial(gather_kernel, turned, halved, early, as...  202 us
    pallas_call x4, Pallas kernels, matmul_scatter(): pl.pallas_call(functools.partial(scatter_kernel, turned, aside), out_shap...  144 us
    pallas_call x1, Pallas kernels, finale(): pl.pallas_call(functools.partial(finale_kernel, count), out_shape=[*[jax....  65.4 us
    pallas_call x1, Pallas kernels, collect(): pl.pallas_call(functools.partial(collect_kernel, count, aside), out_shape...  61.8 us
    pallas_call x1, Pallas kernels, arrive(): pl.pallas_call(arrive_kernel, out_shape=[jax.ShapeDtypeStruct((4, rows //...  50.6 us
    all_to_all x1, waiting for transfers between devices, shards(): captions = lax.all_to_all(captions, 'seq', 0, 0, tiled=True)  44.3 us
    unnamed x121, local copies, waits for them, and re-layouts  40.9 us
    dot_general x5, matrix products, contract_rows(): lax.dot_general(left, right, (((0,), (0,)), ((), ())), preferred_element_...  31.2 us
  transfers between devices with their start and end apart: 17, of which 8 were waited for; matrix products, arithmetic and copies ran while one was open for 13% of the time, Pallas kernels for 36%

profile of v3, /device:TPU:0, one launch (start us, length us, event | category | flops | bytes accessed | tf_op | source)
XLA Modules:
  0.0 932.5 jit_solution(16605738259205007004)
XLA Ops:
  17.1 50.6 %arrive.1 = (bf16[4,64,1536]{2,1,0:T(8,128)(2,1)S(1)}, bf16[4,4,16,4096]{3,2,1,0:T(8,128)(2,1)S(1)}, bf16[4,64,1536]{2,1,0:T(8,128)(2,1)}, f32[4,2,8,256]{3,2,1,0:T(8,128)S(1)}, f32[8,6144]{1,0:T(8,128)S(1)}) custom-call(bf16[4,64,1536]{2,1,0:T(8,128)(2,1)S(1)} %bitcast.206, bf16[4,4,16,4096]{3,2,1,0:T(8,128)(2,1)S(1)} %bitcast.202, ...), custom_call_target="tpu_custom_call" | custom-call | bytes 90000000 | tf_op jit(solution)/shard_map/arrive/pallas_call | solution.py:699
  86.0 11.2 %all-to-all-start.1 = ((bf16[4,4,16,4096]{3,2,1,0:T(8,128)(2,1)}), bf16[4,4,16,4096]{3,2,1,0:T(8,128)(2,1)S(1)}, u32[]{:S(2)}, u32[]{:S(2)}) async-start(bf16[4,4,16,4096]{3,2,1,0:T(8,128)(2,1)} %copy-done.8), calls=%async_computation.1 | async-start | bytes 4194304 | tf_op jit(solution)/shard_map/all_to_all | solution.py:1435
  115.0 30.9 %gather_matmul.5 = (bf16[4,256,1536]{2,1,0:T(8,128)(2,1)}, bf16[1536,1536]{1,0:T(8,128)(2,1)}, f32[4,256,1152]{2,1,0:T(8,128)}) custom-call(bf16[256,1536]{1,0:T(8,128)(2,1)} %fusion.27.refs_0_, bf16[4,192,1536]{2,1,0:T(8,128)(2,1)} %bitcast.260), custom_call_target="tpu_custom_call" | custom-call | flops 3623878656 | bytes 90000000 | tf_op jit(solution)/shard_map/gather_matmul/pallas_call | solution.py:242
  148.3 44.3 %all-to-all-done.1 = bf16[4,4,16,4096]{3,2,1,0:T(8,128)(2,1)S(1)} async-done(((bf16[4,4,16,4096]{3,2,1,0:T(8,128)(2,1)}), bf16[4,4,16,4096]{3,2,1,0:T(8,128)(2,1)S(1)}, u32[]{:S(2)}, u32[]{:S(2)}) %all-to-all-start.1) | async-done | bytes 2097184 | tf_op jit(solution)/shard_map/all_to_all | solution.py:1435
  204.8 4.7 all-to-all-done.2
  219.0 29.7 %all-to-all-done = bf16[4,64,1536]{2,1,0:T(8,128)(2,1)S(1)} async-done(((bf16[4,64,1536]{2,1,0:T(8,128)(2,1)}), bf16[4,64,1536]{2,1,0:T(8,128)(2,1)S(1)}, u32[]{:S(2)}, u32[]{:S(2)}) %all-to-all-start) | async-done | bytes 786464 | tf_op jit(solution)/shard_map/all_to_all | solution.py:1491
  251.2 77.4 %gather_matmul.6 = (bf16[4,256,4096]{2,1,0:T(8,128)(2,1)}, bf16[4096,768]{1,0:T(8,128)(2,1)}, f32[4,256,768]{2,1,0:T(8,128)}, bf16[1024,768]{1,0:T(8,128)(2,1)},...) custom-call(bf16[256,4096]{1,0:T(8,128)(2,1)} %bitcast_select_fusion.refs_0_, ...), custom_call_target="tpu_custom_call" | custom-call | flops 6442450944 | bytes 90000000 | tf_op jit(solution)/shard_map/gather_matmul/pallas_call | solution.py:242
  328.7 33.6 %gather_matmul.7 = (bf16[4,256,1536]{2,1,0:T(8,128)(2,1)}, bf16[1024,1536]{1,0:T(8,128)(2,1)}, f32[4,256,1024]{2,1,0:T(8,128)}, bf16[1024,768]{1,0:T(8,128)(2,1)...) custom-call(bf16[256,1536]{1,0:T(8,128)(2,1)} %fusion.20.refs_0_, ...), custom_call_target="tpu_custom_call" | custom-call | flops 3221225472 | bytes 90000000 | tf_op jit(solution)/shard_map/gather_matmul/pallas_call | solution.py:242
  362.2 30.9 %matmul_scatter.4 = f32[256,1536]{1,0:T(8,128)} custom-call(bf16[4,256,384]{2,1,0:T(8,128)(2,1)} %bitcast.267, bf16[384,1536]{1,0:T(8,128)(2,1)} %bitcast.233), custom_call_target="tpu_custom_call" | custom-call | flops 1207959552 | bytes 90000000 | tf_op jit(solution)/shard_map/matmul_scatter/pallas_call | solution.py:369
  398.1 31.1 %gather_matmul.8 = (bf16[4,256,1536]{2,1,0:T(8,128)(2,1)}, bf16[1536,2048]{1,0:T(8,128)(2,1)}, f32[4,256,2048]{2,1,0:T(8,128)}) custom-call(bf16[256,1536]{1,0:T(8,128)(2,1)} %multiply_convert_fusion.2.refs_0_, bf16[4,192,2048]{2,1,0:T(8,128)(2,1)} %bitcast.258), custom_call_target="tpu_custom_call" | custom-call | flops 6442450944 | bytes 90000000 | tf_op jit(solution)/shard_map/gather_matmul/pallas_call | solution.py:242
  429.2 6.3 fusion.12
  435.6 7.4 convolution_convert_fusion.1
  454.8 4.9 pad_maximum_fusion
  462.7 6.1 fusion.9
  469.4 35.7 %matmul_scatter.5 = f32[256,1536]{1,0:T(8,128)} custom-call(bf16[4,256,2048]{2,1,0:T(8,128)(2,1)} %bitcast.223, bf16[1536,2048]{1,0:T(8,128)(2,1)} %get-tuple-element.99.refs_1_), custom_call_target="tpu_custom_call" | custom-call | flops 6442450944 | bytes 90000000 | tf_op jit(solution)/shard_map/matmul_scatter/pallas_call | solution.py:369
  516.2 29.5 %gather_matmul.9 = (bf16[4,256,1536]{2,1,0:T(8,128)(2,1)}, f32[4,256,384]{2,1,0:T(8,128)}) custom-call(bf16[256,1536]{1,0:T(8,128)(2,1)} %multiply_convert_fusion.1.refs_0_, bf16[384,1536]{1,0:T(8,128)(2,1)} %bitcast.234), custom_call_target="tpu_custom_call" | custom-call | flops 1207959552 | bytes 90000000 | tf_op jit(solution)/shard_map/gather_matmul/pallas_call | solution.py:242
  555.7 13.2 %all_to_all.20 = bf16[4,192,384]{2,1,0:T(8,128)(2,1)} all-to-all(bf16[4,192,384]{2,1,0:T(8,128)(2,1)S(1)} %bitcast.231), channel_id=1, replica_groups=mesh['tp'=4,'core'=2,'seq'=4] {'tp'}, dimensions={0} | all-to-all | bytes 1179648 | tf_op jit(solution)/shard_map/all_to_all | solution.py:1579
  569.0 42.4 %matmul_scatter.6 = (f32[256,1536]{1,0:T(8,128)}, f32[1024,384]{1,0:T(8,128)}, bf16[1024,384]{1,0:T(8,128)(2,1)}, bf16[1024,384]{1,0:T(8,128)(2,1)}, f32[3,8,128]{2,1,0:T(8,128)}) custom-call(bf16[4,256,1024]{2,1,0:T(8,128)(2,1)} %bitcast.211, bf16[1024,1536]{1,0:T(8,128)(2,1)} %get-tuple-element.107.refs_1_, f32[1024,384]{1,0:T(8,128)} %bitcast.218, ...), custom_call_target="tpu_custom_call" | custom-call | flops 3221225472 | bytes 90000000 | tf_op jit(solution)/shard_map/matmul_scatter/pallas_call | solution.py:369
  612.9 11.5 %convolution_convert_fusion.2 = bf16[4096,768]{1,0:T(8,128)(2,1)S(1)} fusion(bf16[1024,4096]{1,0:T(8,128)(2,1)} %bitcast.262, bf16[1024,768]{1,0:T(8,128)(2,1)S(1)} %constant_dynamic-update-slice_fusion), kind=kOutput, calls=%fused_computation.3 | convolution fusion | flops 6445596672 | bytes 16252928 | tf_op jit(solution)/shard_map/dot_general | solution.py:1262
  638.5 10.8 %reduce-scatter.10.cloned.1.call-done = bf16[1,192,384]{2,1,0:T(8,128)(2,1)} async-done(((bf16[4,192,384]{2,1,0:T(8,128)(2,1)}), bf16[1,192,384]{2,1,0:T(8,128)(2,1)}) %reduce-scatter.10.cloned.1.call-update) | async-done | bytes 147472 | tf_op jit(solution)/shard_map/reduce_scatter | solution.py:1306
  649.8 61.8 %collect.1 = (bf16[4,2,128,1536]{3,2,1,0:T(8,128)(2,1)}, bf16[4,2,192,2048]{3,2,1,0:T(8,128)(2,1)}, bf16[4,2,192,384]{3,2,1,0:T(8,128)(2,1)}, bf16[4,64,1536]{2,...) custom-call(bf16[128,1536]{1,0:T(8,128)(2,1)} %bitcast.240, ...), custom_call_target="tpu_custom_call" | custom-call | bytes 53084160 | tf_op jit(solution)/shard_map/collect/pallas_call | solution.py:541
  714.2 4.5 convolution_convert_fusion
  730.1 7.7 fusion.71
  741.4 12.2 %spread.7 = f32[384,8192]{1,0:T(8,128)} custom-call(bf16[4,2,192,2048]{3,2,1,0:T(8,128)(2,1)} %get-tuple-element.135.in_ref), custom_call_target="tpu_custom_call" | custom-call | bytes 18874368 | tf_op jit(solution)/shard_map/spread/pallas_call | solution.py:580
  753.6 5.5 bitcast_convert_fusion
  759.1 34.6 %matmul_scatter.7 = f32[256,1536]{1,0:T(8,128)} custom-call(bf16[4,256,1152]{2,1,0:T(8,128)(2,1)} %bitcast.241, bf16[1536,1536]{1,0:T(8,128)(2,1)} %get-tuple-element.92.refs_1_), custom_call_target="tpu_custom_call" | custom-call | flops 3623878656 | bytes 90000000 | tf_op jit(solution)/shard_map/matmul_scatter/pallas_call | solution.py:369
  797.6 4.4 fusion
  804.2 20.2 %reduce-scatter.12.cloned.1.call-done = bf16[1,512,768]{2,1,0:T(8,128)(2,1)} async-done(((bf16[4,512,768]{2,1,0:T(8,128)(2,1)}), bf16[1,512,768]{2,1,0:T(8,128)(2,1)}) %reduce-scatter.12.cloned.1.call-update) | async-done | bytes 786448 | tf_op jit(solution)/shard_map/reduce_scatter | solution.py:1306
  826.5 65.4 %finale.1 = (bf16[4,2,512,768]{3,2,1,0:T(8,128)(2,1)S(1)}, bf16[4,2,192,1152]{3,2,1,0:T(8,128)(2,1)S(1)}, bf16[4,64,1536]{2,1,0:T(8,128)(2,1)S(1)}, f32[4,2,8,6144]{3,2,1,0:T(8,128)S(1)}) custom-call(bf16[512,768]{1,0:T(8,128)(2,1)S(1)} %bitcast.204, bf16[192,1152]{1,0:T(8,128)(2,1)S(1)} %bitcast.208, bf16[4,64,1536]{2,1,0:T(8,128)(2,1)S(1)} %bitcast.201, ...), custom_call_target="tpu_custom_call" | custom-call | bytes 120000000 | tf_op jit(solution)/shard_map/finale/pallas_call | solution.py:790
  900.1 6.1 spread.4
  906.1 8.9 spread.6
  915.1 8.4 convolution_bitcast_fusion
  (287 shorter events, 162.8 us)
Async XLA Ops:
  7.2 77.2 %copy-start = (bf16[1024,1536]{1,0:T(8,128)(2,1)S(1)}, bf16[1024,1536]{1,0:T(8,128)(2,1)}, u32[]{:S(2)}) copy-start(bf16[1024,1536]{1,0:T(8,128)(2,1)} %param.32) | copy-start | bytes 9437188
  7.2 107.7 %all-gather.9.cloned.1.call-start = ((), (), s32[]{:S(2)}) async-start(), calls=%async_computation.14 | async-start | bytes 2949120 | tf_op jit(solution)/shard_map/all_gather | solution.py:1292
  10.4 240.8 %all-gather.13.cloned.1.call-start = ((), (), s32[]{:S(2)}) async-start(), calls=%async_computation.16 | async-start | bytes 3932160 | tf_op jit(solution)/shard_map/all_gather | solution.py:1292
  85.2 243.4 %all-gather.11.cloned.1.call-start = ((), (), s32[]{:S(2)}) async-start(), calls=%async_computation.15 | async-start | bytes 1966080 | tf_op jit(solution)/shard_map/all_gather | solution.py:1292
  86.0 13.3 %copy-start.3 = (bf16[4,64,1536]{2,1,0:T(8,128)(2,1)S(1)}, bf16[4,64,1536]{2,1,0:T(8,128)(2,1)}, u32[]{:S(2)}) copy-start(bf16[4,64,1536]{2,1,0:T(8,128)(2,1)} %copy-done.2) | copy-start | bytes 2359300
  86.0 106.6 %all-to-all-start.1 = ((bf16[4,4,16,4096]{3,2,1,0:T(8,128)(2,1)}), bf16[4,4,16,4096]{3,2,1,0:T(8,128)(2,1)S(1)}, u32[]{:S(2)}, u32[]{:S(2)}) async-start(bf16[4,4,16,4096]{3,2,1,0:T(8,128)(2,1)} %copy-done.8), calls=%async_computation.1 | async-start | bytes 4194304 | tf_op jit(solution)/shard_map/all_to_all | solution.py:1435
  97.2 300.8 %all-gather.15.cloned.1.call-start = ((), (), s32[]{:S(2)}) async-start(), calls=%async_computation.17 | async-start | bytes 3932160 | tf_op jit(solution)/shard_map/all_gather | solution.py:1292
  99.5 8.8 copy-start.39
  145.9 51.1 %copy-start.47 = (f32[24]{0:T(128)S(1)}, f32[24]{0:T(128)}, u32[]{:S(2)}) copy-start(f32[24]{0:T(128)} %param.40) | copy-start | bytes 292
  192.6 10.8 %copy-start.19 = (bf16[4,4,16,4096]{3,2,1,0:T(8,128)(2,1)}, bf16[4,4,16,4096]{3,2,1,0:T(8,128)(2,1)S(1)}, u32[]{:S(2)}) copy-start(bf16[4,4,16,4096]{3,2,1,0:T(8,128)(2,1)S(1)} %all-to-all-done.1) | copy-start | bytes 6291460
  192.6 16.9 %all-to-all-start.2 = ((bf16[4,384,384]{2,1,0:T(8,128)(2,1)}), bf16[4,384,384]{2,1,0:T(8,128)(2,1)}, u32[]{:S(2)}, u32[]{:S(2)}) async-start(bf16[4,384,384]{2,1,0:T(8,128)(2,1)} %bitcast.220), calls=%async_computation.2 | async-start | bytes 2359296 | tf_op jit(solution)/shard_map/all_to_all | solution.py:1493
  209.5 39.1 %all-to-all-start = ((bf16[4,64,1536]{2,1,0:T(8,128)(2,1)}), bf16[4,64,1536]{2,1,0:T(8,128)(2,1)S(1)}, u32[]{:S(2)}, u32[]{:S(2)}) async-start(bf16[4,64,1536]{2,1,0:T(8,128)(2,1)} %get-tuple-element.83), calls=%async_computation | async-start | bytes 1572864 | tf_op jit(solution)/shard_map/all_to_all | solution.py:1491
  213.0 356.0 %reduce-scatter.6.cloned.1.call-start = ((), (), s32[]{:S(2)}) async-start(), calls=%async_computation.9 | async-start | bytes 1966080 | tf_op jit(solution)/shard_map/reduce_scatter | solution.py:1306
  429.2 6.3 copy-start.50
  435.5 7.4 copy-start.20
  435.5 7.4 copy-start.21
  435.5 11.6 %copy-start.18 = (bf16[1024,1024]{1,0:T(8,128)(2,1)}, bf16[1024,1024]{1,0:T(8,128)(2,1)S(1)}, u32[]{:S(2)}) copy-start(bf16[1024,1024]{1,0:T(8,128)(2,1)S(1)} %get-tuple-element.152) | copy-start | bytes 6291460
  447.1 15.5 %collective-permute-start.1 = (bf16[4,192,2048]{2,1,0:T(8,128)(2,1)}, bf16[4,192,2048]{2,1,0:T(8,128)(2,1)}, u32[]{:S(2)}, u32[]{:S(2)}) collective-permute-start(bf16[4,192,2048]{2,1,0:T(8,128)(2,1)} %dynamic-slice_bitcast_fusion.1), channel_id=1, source_target_pairs={{0,4},{4,0},{1,5},{5,1},{2,6},{6,2},{3,7},{7,3},{8,12},{12,8},{9,1... | collective-permute-start | bytes 9437192 | tf_op jit(solution)/shard_map/ppermute | solution.py:1314
  454.3 5.4 collective-permute-start
  468.8 100.2 %reduce-scatter.8.cloned.1.call-start = ((), (), s32[]{:S(2)}) async-start(), calls=%async_computation.10 | async-start | bytes 3932160 | tf_op jit(solution)/shard_map/reduce_scatter | solution.py:1306
  469.4 179.9 %reduce-scatter.10.cloned.1.call-start = ((), (), s32[]{:S(2)}) async-start(), calls=%async_computation.11 | async-start | bytes 737280 | tf_op jit(solution)/shard_map/reduce_scatter | solution.py:1306
  549.3 2.1 collective-permute-start.2
  612.9 11.5 %copy-start.28 = (bf16[1024,768]{1,0:T(8,128)(2,1)}, bf16[1024,768]{1,0:T(8,128)(2,1)S(1)}, u32[]{:S(2)}) copy-start(bf16[1024,768]{1,0:T(8,128)(2,1)S(1)} %constant_dynamic-update-slice_fusion) | copy-start | bytes 4718596
  628.1 6.0 collective-permute-start.3
  628.1 176.1 %reduce-scatter.14.cloned.1.call-start = ((), (), s32[]{:S(2)}) async-start(), calls=%async_computation.13 | async-start | bytes 2211840 | tf_op jit(solution)/shard_map/reduce_scatter | solution.py:1306
  628.1 5.9 copy-start.26
  713.4 5.4 copy-start.36
  718.9 3.8 collective-permute-start.4
  724.3 5.4 copy-start.29
  724.4 100.0 %reduce-scatter.12.cloned.1.call-start = ((), (), s32[]{:S(2)}) async-start(), calls=%async_computation.12 | async-start | bytes 3932160 | tf_op jit(solution)/shard_map/reduce_scatter | solution.py:1306
  915.1 8.4 copy-start.32
  915.1 10.7 %copy-start.1 = (bf16[1024,1536]{1,0:T(8,128)(2,1)S(1)}, bf16[1024,1536]{1,0:T(8,128)(2,1)}, u32[]{:S(2)}) copy-start(bf16[1024,1536]{1,0:T(8,128)(2,1)} %param.32) | copy-start | bytes 9437188
  (36 other events, 93.4 us)
Sparse Core Ops, SparseCore 0:
  10.5 73.8 all-gather.8
  86.5 109.2 all-gather.12
  197.4 50.9 all-gather.10
  250.4 62.6 all-gather.14
  468.9 34.0 reduce-scatter.5
  505.8 59.2 reduce-scatter.7
  628.2 21.0 reduce-scatter.9
  724.5 37.4 reduce-scatter.13
  765.0 59.3 reduce-scatter.11

commit v4 on v3

--- a/solution.py
+++ b/solution.py
@@ -58,75 +58,151 @@
     return jnp.dot(left, weight_ref[:, columns], preferred_element_type=jnp.float32)
 
 
+def bind(refs, counts, *riders):
+    refs, own = list(refs), []
+    for kind in range(3):
+        own += refs[: counts[kind]]
+        refs = refs[counts[kind] :]
+        for rider in riders:
+            count = rider.counts[kind]
+            rider.refs[kind] = refs[:count]
+            refs = refs[count:]
+    return own
+
+
 class Aside:
     def __init__(self, operands, outs, scratch, steps):
-        self.operands, self.outs, self.scratch, self.steps = operands, outs, scratch, steps
-
-    def in_specs(self):
-        return [pl.BlockSpec(memory_space=pl.ANY)] * len(self.operands)
-
-    def out_specs(self):
-        return [pl.BlockSpec(memory_space=pltpu.VMEM)] * len(self.outs)
-
-    def scratch_shapes(self):
-        return [
-            *[pltpu.VMEM(x.shape, x.dtype) for x in self.operands],
-            pltpu.SemaphoreType.DMA((len(self.operands),)),
-            *self.scratch,
+        self.operands, self.outs, self.steps = operands, outs, steps
+        self.in_specs = [pl.BlockSpec(memory_space=pl.ANY)] * len(operands)
+        self.out_specs = [pl.BlockSpec(memory_space=pltpu.VMEM)] * len(outs)
+        self.scratch = [
+            *[pltpu.VMEM(x.shape, x.dtype) for x in operands],
+            pltpu.SemaphoreType.DMA((max(len(operands), 1),)),
+            *scratch,
         ]
-
-    def split(self, refs, ins, outs, scratch):
-        count, given = len(self.operands), len(self.outs)
-        own, refs = list(refs[:ins]), refs[ins:]
-        sources, refs = refs[:count], refs[count:]
-        own, refs = own + list(refs[:outs]), refs[outs:]
-        self.out_refs, refs = refs[:given], refs[given:]
-        own, refs = own + list(refs[:scratch]), refs[scratch:]
-        self.in_refs, (sem, *self.scratch_refs) = refs[:count], refs[count:]
+        self.counts = (len(operands), len(outs), len(self.scratch))
+        self.refs = [None] * 3
+
+    def load(self):
+        count = len(self.operands)
+        sem = self.refs[2][count]
         self.loads = [
-            pltpu.make_async_copy(source, target, sem.at[i])
-            for i, (source, target) in enumerate(zip(sources, self.in_refs))
+            pltpu.make_async_copy(self.refs[0][i], self.refs[2][i], sem.at[i])
+            for i in range(count)
         ]
-        return own
-
-    def load(self):
         for copy in self.loads:
             copy.start()
 
     def step(self, index):
+        count = len(self.operands)
         if index == 0:
             for copy in self.loads:
                 copy.wait()
-        self.steps(index, self.in_refs, self.out_refs, self.scratch_refs)
-
-
-class Nothing:
-    def __init__(self):
-        self.operands, self.outs = [], []
-
-    def in_specs(self):
-        return []
-
-    out_specs = scratch_shapes = in_specs
-
-    def split(self, refs, ins, outs, scratch):
-        return list(refs)
+        if self.steps:
+            self.steps(index, self.refs[2][:count], self.refs[1], self.refs[2][count + 1 :])
+
+
+def nothing():
+    return Aside([], [], [], None)
+
+
+class Finish:
+    def __init__(self, operands, outs, work):
+        self.operands, self.outs, self.work = operands, outs, work
+        hbm = pl.BlockSpec(memory_space=pl.ANY)
+        self.in_specs, self.out_specs = [hbm] * len(operands), [hbm] * len(outs)
+        self.scratch = [
+            *[pltpu.VMEM(x.shape, x.dtype) for x in operands],
+            *[pltpu.VMEM(x.shape, x.dtype) for x in outs],
+            pltpu.SemaphoreType.DMA((max(len(operands), 1),)),
+            pltpu.SemaphoreType.DMA((4 * max(len(outs), 1),)),
+        ]
+        self.counts = (len(operands), len(outs), len(self.scratch))
+        self.refs = [None] * 3
 
     def load(self):
-        pass
-
-    def step(self, index):
-        pass
-
-
-def gather_kernel(turned, halved, early, aside, *refs):
-    refs = aside.split(refs, 2, 3 if halved else 2, 7)
-    x_ref, w_ref, all_ref = refs[:3]
-    refs = refs[3:]
+        count = len(self.operands)
+        self.ins, self.made = self.refs[2][:count], self.refs[2][count:-2]
+        sem = self.refs[2][-2]
+        self.loads = [
+            pltpu.make_async_copy(self.refs[0][i], self.ins[i], sem.at[i]) for i in range(count)
+        ]
+        for copy in self.loads:
+            copy.start()
+        self.copies = []
+
+    def run(self, index, owner, product):
+        if not self.work:
+            return
+        if index == 0:
+            for copy in self.loads:
+                copy.wait()
+        made = [ref.at[owner] for ref in self.made]
+        self.work(product, [ref.at[owner] for ref in self.ins], made)
+        for i, ref in enumerate(made):
+            copy = pltpu.make_async_copy(
+                ref, self.refs[1][i].at[owner], self.refs[2][-1].at[4 * i + index]
+            )
+            copy.start()
+            self.copies.append(copy)
+
+    def end(self):
+        for copy in self.copies:
+            copy.wait()
+
+
+class Trade:
+    def __init__(self, *items):
+        self.items = items
+        hbm = pl.BlockSpec(memory_space=pl.ANY)
+        self.operands = [item[0] for item in items]
+        self.outs = [jax.ShapeDtypeStruct(item[2], item[0].dtype) for item in items]
+        self.in_specs = self.out_specs = [hbm] * len(items)
+        count = max(len(items), 1)
+        self.scratch = [pltpu.SemaphoreType.DMA((n,)) for n in (count, 3 * count, 3 * count)]
+        self.counts = (len(items), len(items), 3)
+        self.refs = [None] * 3
+
+    def begin(self):
+        local, *sems = self.refs[2]
+        self.copies, self.local = [], []
+        for i, (_, axis, _, source, target) in enumerate(self.items):
+            from_ref, to_ref = self.refs[0][i], self.refs[1][i]
+            if axis == "tp":
+                here, *others = neighbours()
+            else:
+                here, others = planes_after()
+            self.local.append(
+                pltpu.make_async_copy(source(from_ref, here), target(to_ref, here), local.at[i])
+            )
+            self.copies += [
+                send(source(from_ref, p), target(to_ref, here), sems, 3 * i + k, {axis: p})
+                for k, p in enumerate(others)
+            ]
+        for copy in self.local + self.copies:
+            copy.start()
+
+    def end(self):
+        for copy in self.local + self.copies:
+            copy.wait()
+
+
+def block_of(ref, place):
+    return ref.at[place]
+
+
+def swap_blocks(x, axis):
+    return (x, axis, x.shape, block_of, block_of)
+
+
+def gather_kernel(turned, halved, early, aside, trade, finish, keep, *refs):
+    refs = bind(refs, (2, 1 + halved + keep, 7), aside, trade, finish)
+    x_ref, w_ref, all_ref, *refs = refs
     if halved:
-        full_ref, refs = refs[0], refs[1:]
-    y_ref, xbuf, wbuf, ybuf, load, done = refs[:6]
-    sems = refs[6:8]
+        full_ref, *refs = refs
+    if keep:
+        y_ref, *refs = refs
+    xbuf, wbuf, ybuf, load, done, *sems = refs
     me, across, along, far = neighbours()
     rows = x_ref.shape[0]
     half = rows // 2
@@ -149,7 +225,10 @@
         weights = [pltpu.make_async_copy(w_ref, wbuf, load.at[1])]
     for copy in weights:
         copy.start()
-    greet(places)
+    if trade.items:
+        greet_all()
+    else:
+        greet(places)
 
     def block(owner, part):
         return xbuf.at[owner, pl.ds(part * half, half)]
@@ -171,7 +250,9 @@
             swaps.append(send(w_ref.at[z], wbuf.at[places_of[z]], sems, 6 + z, {"core": 1 - core}))
         for copy in swaps:
             copy.start()
+    trade.begin()
     aside.load()
+    finish.load()
     mine.wait()
     for copy in weights:
         copy.wait()
@@ -202,9 +283,11 @@
                 ybuf.dtype
             )
 
-        copy = pltpu.make_async_copy(ybuf.at[index], y_ref.at[owner], done.at[index])
-        copy.start()
-        outs.append(copy)
+        if keep:
+            copy = pltpu.make_async_copy(ybuf.at[index], y_ref.at[owner], done.at[index])
+            copy.start()
+            outs.append(copy)
+        finish.run(index, owner, ybuf.at[index])
 
     compute(me, 0)
     first[2].wait_recv()
@@ -221,10 +304,13 @@
         copy.wait_send()
     for copy in outs:
         copy.wait()
+    finish.end()
+    trade.end()
 
 
 def gather_matmul(
-    ident, x, w, turned=False, halved=False, width=None, aside=None, early=3, out=jnp.float32
+    ident, x, w, turned=False, halved=False, width=None, aside=None, early=3, trade=(),
+    finish=None, keep=True,
 ):
     rows, depth = x.shape
     if halved:
@@ -233,26 +319,27 @@
     else:
         whole = w.shape
     width = width or (whole[0] if turned else whole[1])
-    aside = aside or Nothing()
+    riders = [aside or nothing(), Trade(*trade), finish or Finish([], [], None)]
     shapes = [jax.ShapeDtypeStruct((4, rows, depth), x.dtype)]
     if halved:
         shapes.append(jax.ShapeDtypeStruct(whole, w.dtype))
-    shapes.append(jax.ShapeDtypeStruct((4, rows, width), out))
+    if keep:
+        shapes.append(jax.ShapeDtypeStruct((4, rows, width), jnp.float32))
     hbm = pl.BlockSpec(memory_space=pl.ANY)
     got = pl.pallas_call(
-        functools.partial(gather_kernel, turned, halved, early, aside),
-        out_shape=shapes + aside.outs,
-        in_specs=[hbm, hbm] + aside.in_specs(),
-        out_specs=[hbm] * len(shapes) + aside.out_specs(),
+        functools.partial(gather_kernel, turned, halved, early, *riders, keep),
+        out_shape=shapes + [y for rider in riders for y in rider.outs],
+        in_specs=[hbm, hbm] + [y for rider in riders for y in rider.in_specs],
+        out_specs=[hbm] * len(shapes) + [y for rider in riders for y in rider.out_specs],
         scratch_shapes=[
             pltpu.VMEM((4, rows, depth), x.dtype),
             pltpu.VMEM(whole, w.dtype),
-            pltpu.VMEM((4, rows, width), out),
+            pltpu.VMEM((4, rows, width), jnp.float32),
             pltpu.SemaphoreType.DMA((6,)),
             pltpu.SemaphoreType.DMA((5,)),
             pltpu.SemaphoreType.DMA((10,)),
             pltpu.SemaphoreType.DMA((10,)),
-            *aside.scratch_shapes(),
+            *[y for rider in riders for y in rider.scratch],
         ],
         compiler_params=pltpu.CompilerParams(
             collective_id=ident, has_side_effects=True, vmem_limit_bytes=VMEM_BYTES
@@ -263,19 +350,57 @@
             transcendentals=0,
         ),
         name="gather_matmul",
-    )(x, w, *aside.operands)
-    last = len(shapes) - 1
+    )(x, w, *[y for rider in riders for y in rider.operands])
     return [
         got[0].reshape(4 * rows, depth),
         got[1] if halved else w,
-        got[last].reshape(4 * rows, width),
-        *got[last + 1 :],
+        *[part.reshape(4 * rows, width) for part in got[1 + halved : len(shapes)]],
+        *got[len(shapes) :],
     ]
 
 
-def scatter_kernel(turned, aside, *refs):
-    refs = aside.split(refs, 2, 1, 7)
-    x_ref, w_ref, out_ref, sums, far_out, near_out, relay, land, s0, s1 = refs
+def head_finish(rows, width, gain):
+    def work(product, ins, outs):
+        (gain_ref,), (out_ref,) = ins, outs
+        size = width // 2
+        for at in range(0, size, 128):
+            keys = pair_norm(product[:, at : at + 128])[0] * gain_ref[:, at : at + 128]
+            out_ref[:, at : at + 128] = keys.astype(out_ref.dtype)
+        out_ref[:, size:] = product[:, size:].astype(out_ref.dtype)
+
+    gains = jnp.broadcast_to(gain[None], (4, 1, width // 2))
+    return Finish([gains], [jax.ShapeDtypeStruct((4, rows, width), jnp.bfloat16)], work)
+
+
+def swiglu_finish(grads):
+    rows, size = grads.shape[0] // 4, grads.shape[1]
+
+    def work(product, ins, outs):
+        (grad_ref,), (ffn_ref, back_ref) = ins, outs
+
+        @pl.loop(0, rows // 32)
+        def _(step):
+            strip = pl.ds(pl.multiple_of(step * 32, 32), 32)
+            for at in range(0, size, 256):
+                lanes, ups = pl.ds(at, 256), pl.ds(size + at, 256)
+                gate, up, grad = product[strip, lanes], product[strip, ups], grad_ref[strip, lanes]
+                sig = 1.0 / (1.0 + jnp.exp(-gate))
+                silu = gate * sig
+                ffn_ref[strip, lanes] = (silu * up).astype(ffn_ref.dtype)
+                back = grad * up * sig * (1.0 + gate * (1.0 - sig))
+                back_ref[strip, lanes] = back.astype(back_ref.dtype)
+                back_ref[strip, ups] = (grad * silu).astype(back_ref.dtype)
+
+    return Finish(
+        [grads.reshape(4, rows, size)],
+        [jax.ShapeDtypeStruct((4, rows, n), jnp.bfloat16) for n in (size, 2 * size)],
+        work,
+    )
+
+
+def scatter_kernel(turned, aside, trade, *refs):
+    refs = bind(refs, (2, 1, 10), aside, trade)
+    x_hbm, w_hbm, out_ref, sums, far_out, near_out, relay, land, s0, s1, x_ref, w_ref, load = refs
     me, across, along, far = neighbours()
     sems = (s0, s1)
     rows, width = out_ref.shape
@@ -283,25 +408,43 @@
     top, low = pl.ds(0, half), pl.ds(half, half)
     tile = tile_of(width)
     to_across, to_along = {"tp": across}, {"tp": along}
+    weights = pltpu.make_async_copy(w_hbm, w_ref, load.at[4])
+    weights.start()
+    blocks = {}
+    for k, owner in enumerate((far, across, along, me)):
+        blocks[k] = pltpu.make_async_copy(x_hbm.at[owner], x_ref.at[owner], load.at[k])
+        blocks[k].start()
     aside.load()
-    greet([to_across, to_along])
+    if trade.items:
+        greet_all()
+    else:
+        greet([to_across, to_along])
 
     def tiles(body):
         @pl.loop(0, width // tile)
         def _(step):
             body(pl.ds(pl.multiple_of(step * tile, tile), tile))
 
-    def product(owner, columns):
-        return multiply(x_ref[owner], w_ref, columns, turned)
+    def product(owner, columns, part=slice(None)):
+        return multiply(x_ref[owner, part], w_ref, columns, turned)
+
+    weights.wait()
+    blocks[0].wait()
 
     @tiles
     def _(columns):
-        far_out[:, columns] = product(far, columns).astype(far_out.dtype)
+        far_out[top, columns] = product(far, columns, top).astype(far_out.dtype)
 
     far_a = send(far_out.at[top], relay.at[0], sems, 0, to_across)
+    far_a.start()
+
+    @tiles
+    def _(columns):
+        far_out[low, columns] = product(far, columns, low).astype(far_out.dtype)
+
     far_b = send(far_out.at[low], relay.at[1], sems, 1, to_along)
-    far_a.start()
     far_b.start()
+    blocks[1].wait()
 
     @tiles
     def _(columns):
@@ -311,6 +454,7 @@
 
     across_a = send(near_out.at[0, top], land.at[0, top], sems, 2, to_across)
     across_a.start()
+    blocks[2].wait()
 
     @tiles
     def _(columns):
@@ -320,6 +464,7 @@
 
     along_b = send(near_out.at[1, low], land.at[1, low], sems, 3, to_along)
     along_b.start()
+    trade.begin()
     aside.step(0)
     far_b.wait_recv()
 
@@ -343,6 +488,7 @@
     along_a.start()
     aside.step(1)
     aside.step(2)
+    blocks[3].wait()
 
     @tiles
     def _(columns):
@@ -359,18 +505,19 @@
 
     for copy in (far_a, far_b, across_a, along_b, across_b, along_a):
         copy.wait_send()
-
-
-def matmul_scatter(ident, x, w, turned=False, aside=None):
-    aside = aside or Nothing()
+    trade.end()
+
+
+def matmul_scatter(ident, x, w, turned=False, aside=None, trade=()):
+    aside, trade = aside or nothing(), Trade(*trade)
     rows, depth = x.shape[0] // 4, x.shape[1]
     width = w.shape[0] if turned else w.shape[1]
     vmem = pl.BlockSpec(memory_space=pltpu.VMEM)
     return pl.pallas_call(
-        functools.partial(scatter_kernel, turned, aside),
-        out_shape=[jax.ShapeDtypeStruct((rows, width), jnp.float32)] + aside.outs,
-        in_specs=[vmem, vmem] + aside.in_specs(),
-        out_specs=[vmem] + aside.out_specs(),
+        functools.partial(scatter_kernel, turned, aside, trade),
+        out_shape=[jax.ShapeDtypeStruct((rows, width), jnp.float32)] + aside.outs + trade.outs,
+        in_specs=[pl.BlockSpec(memory_space=pl.ANY)] * 2 + aside.in_specs + trade.in_specs,
+        out_specs=[vmem] + aside.out_specs + trade.out_specs,
         scratch_shapes=[
             pltpu.VMEM((2, rows // 2, width), jnp.float32),
             pltpu.VMEM((rows, width), jnp.bfloat16),
@@ -379,7 +526,11 @@
             pltpu.VMEM((2, rows, width), jnp.bfloat16),
             pltpu.SemaphoreType.DMA((6,)),
             pltpu.SemaphoreType.DMA((6,)),
-            *aside.scratch_shapes(),
+            pltpu.VMEM((4, rows, depth), x.dtype),
+            pltpu.VMEM(w.shape, w.dtype),
+            pltpu.SemaphoreType.DMA((5,)),
+            *aside.scratch,
+            *trade.scratch,
         ],
         compiler_params=pltpu.CompilerParams(
             collective_id=ident, has_side_effects=True, vmem_limit_bytes=VMEM_BYTES
@@ -390,7 +541,7 @@
             transcendentals=0,
         ),
         name="matmul_scatter",
-    )(x.reshape(4, rows, depth), w, *aside.operands)
+    )(x.reshape(4, rows, depth), w, *aside.operands, *trade.operands)
 
 
 class Gathering:
@@ -512,49 +663,160 @@
             copy.wait_send()
 
 
-def collect_kernel(count, aside, *refs):
-    refs = aside.split(refs, count + 1, count + 1, 6)
-    ins, outs = refs[:count], refs[count + 1 : 2 * count + 1]
-    back, home = refs[count], refs[2 * count + 1]
-    stage, load, s0, s1, r0, r1 = refs[2 * count + 2 :]
-    gathering = Gathering(ins, outs, load, (s0, s1))
-    returning = Returning(back, home, stage, load.at[count], (r0, r1), 0)
-    greet_all()
+class Home:
+    def __init__(self, backs):
+        self.outs, self.operands, self.scratch = [], [], []
+        for back in backs:
+            tall, wide = back.shape
+            blocks = (4, tall // 4, wide)
+            self.operands.append(back.reshape(blocks))
+            self.outs.append(jax.ShapeDtypeStruct(blocks, back.dtype))
+            self.scratch += [
+                pltpu.VMEM(blocks, back.dtype),
+                *[pltpu.SemaphoreType.DMA((n,)) for n in (1, 6, 6)],
+            ]
+        self.in_specs = self.out_specs = [pl.BlockSpec(memory_space=pl.ANY)] * len(self.outs)
+        self.counts = (len(self.operands), len(self.outs), len(self.scratch))
+        self.refs = [None] * 3
+
+    def begin(self):
+        self.ways = []
+        for i, (back, home) in enumerate(zip(*self.refs[:2])):
+            stage, load, *sems = self.refs[2][4 * i : 4 * i + 4]
+            self.ways.append(Returning(back, home, stage, load.at[0], sems, 0))
+        for way in self.ways:
+            way.begin()
+
+    def turn(self):
+        for way in self.ways:
+            way.turn()
+
+    def end(self):
+        for way in self.ways:
+            way.end()
+
+
+class Total:
+    def __init__(self, x):
+        vmem = pl.BlockSpec(memory_space=pltpu.VMEM)
+        self.outs, self.operands, self.scratch = [], [], []
+        if x is not None:
+            rows, width = x.shape
+            self.operands = [x]
+            self.outs = [jax.ShapeDtypeStruct((4, 2, rows, width), jnp.float32)]
+            self.scratch = [
+                pltpu.VMEM((3, rows, width // 4), jnp.float32),
+                *[pltpu.SemaphoreType.DMA((10,))] * 2,
+            ]
+        self.in_specs = self.out_specs = [vmem] * len(self.outs)
+        self.counts = (len(self.operands), len(self.outs), len(self.scratch))
+        self.refs = [None] * 3
+
+    def begin(self):
+        if not self.operands:
+            return
+        (x_ref,), (out_ref,), (land, *sems) = self.refs
+        me, *peers = neighbours()
+        core = lax.axis_index("core")
+        plane, others = planes_after()
+        quarter = x_ref.shape[1] // 4
+
+        def columns(t):
+            return pl.ds(pl.multiple_of(t * quarter, quarter), quarter)
+
+        self.first = [
+            send(x_ref.at[:, columns(p)], land.at[k], sems, k, {"tp": p})
+            for k, p in enumerate(peers)
+        ]
+        for copy in self.first:
+            copy.start()
+
+    def go_on(self):
+        if not self.operands:
+            return
+        (x_ref,), (out_ref,), (land, *sems) = self.refs
+        me, *peers = neighbours()
+        core = lax.axis_index("core")
+        plane, others = planes_after()
+        quarter = x_ref.shape[1] // 4
+
+        def columns(t):
+            return pl.ds(pl.multiple_of(t * quarter, quarter), quarter)
+
+        for copy in self.first:
+            copy.wait_recv()
+        mine = (x_ref[:, columns(me)] + land[0]) + (land[1] + land[2])
+        out_ref[plane, core, :, columns(me)] = mine
+        here = out_ref.at[plane, core, :, columns(me)]
+        second = [send(here, here, sems, 3 + k, {"seq": p}) for k, p in enumerate(others)]
+        for copy in second:
+            copy.start()
+        for copy in second:
+            copy.wait_recv()
+        here = out_ref.at[:, core, :, columns(me)]
+        self.third = [send(here, here, sems, 6 + k, {"tp": p}) for k, p in enumerate(peers)]
+        for copy in self.third:
+            copy.start()
+        self.copies = self.first + second + self.third
+
+    def end(self):
+        if not self.operands:
+            return
+        (_,), (out_ref,), (_, *sems) = self.refs
+        core = lax.axis_index("core")
+        for copy in self.third:
+            copy.wait_recv()
+        here = out_ref.at[:, core]
+        swap = send(here, here, sems, 9, {"core": 1 - core})
+        swap.start()
+        swap.wait_recv()
+        for copy in self.copies + [swap]:
+            copy.wait_send()
+
+
+def collect_kernel(count, aside, trade, home, total, *refs):
+    refs = bind(refs, (count, count, 3), aside, trade, home, total)
+    load, *sems = refs[2 * count :]
+    gathering = Gathering(refs[:count], refs[count : 2 * count], load, sems)
+    if trade.items or home.operands or total.operands:
+        greet_all()
+    else:
+        greet([gathering.to_across, gathering.to_along, gathering.to_core])
+    total.begin()
     gathering.begin()
-    returning.begin()
+    total.go_on()
+    trade.begin()
+    home.begin()
     aside.load()
     aside.step(0)
     gathering.relay()
-    returning.turn()
     aside.step(1)
+    home.turn()
     gathering.hand()
     aside.step(2)
-    returning.end()
+    trade.end()
+    total.end()
+    home.end()
     gathering.end()
 
 
-def collect(ident, pieces, back, aside=None):
-    aside = aside or Nothing()
+def collect(ident, pieces, aside=None, trade=(), backs=(), sums=None):
+    riders = [aside or nothing(), Trade(*trade), Home(backs), Total(sums)]
     hbm = pl.BlockSpec(memory_space=pl.ANY)
     count = len(pieces)
-    tall, wide = back.shape
     got = pl.pallas_call(
-        functools.partial(collect_kernel, count, aside),
+        functools.partial(collect_kernel, count, *riders),
         out_shape=[
             *[jax.ShapeDtypeStruct((4, 2) + p.shape, p.dtype) for p in pieces],
-            jax.ShapeDtypeStruct((4, tall // 4, wide), back.dtype),
-            *aside.outs,
+            *[x for rider in riders for x in rider.outs],
         ],
-        in_specs=[hbm] * (count + 1) + aside.in_specs(),
-        out_specs=[hbm] * (count + 1) + aside.out_specs(),
+        in_specs=[hbm] * count + [x for rider in riders for x in rider.in_specs],
+        out_specs=[hbm] * count + [x for rider in riders for x in rider.out_specs],
         scratch_shapes=[
-            pltpu.VMEM((4, tall // 4, wide), back.dtype),
-            pltpu.SemaphoreType.DMA((count + 1,)),
+            pltpu.SemaphoreType.DMA((count,)),
             pltpu.SemaphoreType.DMA((10 * count,)),
             pltpu.SemaphoreType.DMA((10 * count,)),
-            pltpu.SemaphoreType.DMA((6,)),
-            pltpu.SemaphoreType.DMA((6,)),
-            *aside.scratch_shapes(),
+            *[x for rider in riders for x in rider.scratch],
         ],
         compiler_params=pltpu.CompilerParams(
             collective_id=ident, has_side_effects=True, vmem_limit_bytes=VMEM_BYTES
@@ -563,26 +825,30 @@
             flops=0, bytes_accessed=80 * sum(p.size for p in pieces), transcendentals=0
         ),
         name="collect",
-    )(*pieces, back.reshape(4, tall // 4, wide), *aside.operands)
-    return got[:count], got[count].reshape(tall, wide), got[count + 1 :]
-
-
-def spread_kernel(in_ref, out_ref):
-    width = in_ref.shape[-1]
-    for t in range(4):
-        out_ref[:, pl.ds(t * width, width)] = in_ref[t, 0].astype(jnp.float32)
+    )(*pieces, *[x for rider in riders for x in rider.operands])
+    return got[:count], got[count:]
+
+
+def spread_kernel(parts, in_ref, out_ref):
+    size = in_ref.shape[-1] // parts
+    for q in range(parts):
+        for t in range(4):
+            out_ref[:, pl.ds((q * 4 + t) * size, size)] = in_ref[
+                t, 0, :, pl.ds(q * size, size)
+            ].astype(jnp.float32)
 
 
 def spread(blocks, parts):
     _, cores, rows, width = blocks.shape
-    width = width // parts
-    cut = 1 if rows <= 256 else rows // 256
+    cut = 2
+    tall = rows // cut
     return pl.pallas_call(
-        spread_kernel,
-        grid=(cores, cut, parts),
-        out_shape=jax.ShapeDtypeStruct((cores * rows, parts * 4 * width), jnp.float32),
-        in_specs=[pl.BlockSpec((4, 1, rows // cut, width), lambda c, k, q: (0, c, k, q))],
-        out_specs=pl.BlockSpec((rows // cut, 4 * width), lambda c, k, q: (c * cut + k, q)),
+        functools.partial(spread_kernel, parts),
+        grid=(cores, cut),
+        out_shape=jax.ShapeDtypeStruct((cores * rows, 4 * width), jnp.float32),
+        in_specs=[pl.BlockSpec((4, 1, tall, width), lambda c, k: (0, c, k, 0))],
+        out_specs=pl.BlockSpec((tall, 4 * width), lambda c, k: (c * cut + k, 0)),
+        compiler_params=pltpu.CompilerParams(vmem_limit_bytes=32 * 1024 * 1024),
         cost_estimate=pl.CostEstimate(
             flops=0, bytes_accessed=6 * blocks.size, transcendentals=0
         ),
@@ -606,8 +872,9 @@
 
 
 def arrive_kernel(
-    tok_ref, cap_ref, cot_ref, msg_ref, w_ref, in_ref, caps_ref, cots_ref, msgs_ref, mod_ref,
-    stage, wbuf, part, land, load, s0, s1,
+    tok_ref, cot_ref, msg_ref, w_ref, qkv_ref, wout_ref, down_ref, gateup_ref,
+    in_ref, cots_ref, msgs_ref, mod_ref, qkv_cut, down_cut, gateup_cut,
+    stage, wbuf, part, land, qkv_buf, down_buf, gateup_buf, load, cuts, s0, s1,
 ):
     sems = (s0, s1)
     me, across, along, far = neighbours()
@@ -619,6 +886,34 @@
     columns = pl.ds(pl.multiple_of(me * quarter, quarter), quarter)
     weights = pltpu.make_async_copy(w_ref.at[:, columns], wbuf, load.at[0])
     weights.start()
+    cutting = []
+
+    def cut(source, target, parts, at):
+        rows, size = target.shape[0], source.shape[1] // (parts * 4)
+        for q in range(parts):
+            lanes = pl.ds(pl.multiple_of((q * 4 + me) * size, size), size)
+            cutting.append(
+                pltpu.make_async_copy(
+                    source.at[pl.ds(pl.multiple_of(core * rows, rows), rows), lanes],
+                    target.at[:, pl.ds(at + q * size, size)],
+                    cuts.at[len(cutting)],
+                )
+            )
+
+    cut(qkv_ref, qkv_buf, 3, 0)
+    cut(wout_ref, qkv_buf, 1, qkv_ref.shape[1] // 4)
+    cut(gateup_ref, gateup_buf, 8, 0)
+    share = down_cut.shape[0]
+    rows = pl.ds(pl.multiple_of((me * 2 + core) * share, share), share)
+    cutting.append(pltpu.make_async_copy(down_ref.at[rows], down_buf, cuts.at[len(cutting)]))
+    for copy in cutting:
+        copy.start()
+    keeping = [
+        pltpu.make_async_copy(source, target, cuts.at[13 + k])
+        for k, (source, target) in enumerate(
+            zip((qkv_buf, down_buf, gateup_buf), (qkv_cut, down_cut, gateup_cut))
+        )
+    ]
     mine = pltpu.make_async_copy(tok_ref.at[me], stage.at[me], load.at[1])
     mine.start()
     msgs_ref[me, core] = msg_ref[:, pl.ds(pl.multiple_of(plane * depth, depth), depth)]
@@ -632,18 +927,12 @@
     ]
     for copy in spread_out:
         copy.start()
-    captions = [
-        send(cap_ref.at[:, p], caps_ref.at[me], sems, 16 + k, {"tp": p})
-        for k, p in enumerate(peers)
+    cotangents = [
+        send(cot_ref.at[p], cots_ref.at[me], sems, 16 + k, {"tp": p}) for k, p in enumerate(peers)
     ]
-    captions += [
-        send(cot_ref.at[p], cots_ref.at[me], sems, 19 + k, {"tp": p}) for k, p in enumerate(peers)
-    ]
-    for copy in captions:
+    for copy in cotangents:
         copy.start()
-    own_caps = pltpu.make_async_copy(cap_ref.at[:, me], caps_ref.at[me], load.at[3])
-    own_caps.start()
-    own_cots = pltpu.make_async_copy(cot_ref.at[me], cots_ref.at[me], load.at[4])
+    own_cots = pltpu.make_async_copy(cot_ref.at[me], cots_ref.at[me], load.at[3])
     own_cots.start()
     for copy in first:
         copy.wait_recv()
@@ -653,6 +942,10 @@
     weights.wait()
     conditions = msgs_ref[:, core].reshape(4 * 8, depth).astype(wbuf.dtype)
     tile = 512
+    for copy in cutting:
+        copy.wait()
+    for copy in keeping:
+        copy.start()
     for step in range(quarter // tile):
         at = pl.ds(step * tile, tile)
         part[:, :, at] = jnp.dot(
@@ -682,136 +975,62 @@
     for copy in fourth:
         copy.start()
     swap.wait_recv()
-    for copy in fourth + third + captions:
+    for copy in fourth + third + cotangents:
         copy.wait_recv()
     stay.wait()
-    own_caps.wait()
     own_cots.wait()
-    for copy in first + spread_out + captions + [swap] + second + third + fourth:
+    for copy in keeping:
+        copy.wait()
+    for copy in first + spread_out + cotangents + [swap] + second + third + fourth:
         copy.wait_send()
 
 
-def arrive(ident, tokens, captions, cotangent, message, w_mod):
+def arrive(ident, tokens, cotangent, message, w_mod, w_qkv, w_out, w_down, w_gateup):
     rows, width = tokens.shape
-    docs, caps, ctx = captions.shape
+    share, kind = w_qkv.shape[0] // 2, w_qkv.dtype
     depth, wide = w_mod.shape
     vmem, hbm = pl.BlockSpec(memory_space=pltpu.VMEM), pl.BlockSpec(memory_space=pl.ANY)
     return pl.pallas_call(
         arrive_kernel,
         out_shape=[
             jax.ShapeDtypeStruct((4, rows // 4, width), tokens.dtype),
-            jax.ShapeDtypeStruct((4, docs, caps // 4, ctx), captions.dtype),
             jax.ShapeDtypeStruct((4, rows // 4, width), cotangent.dtype),
             jax.ShapeDtypeStruct((4, 2, 8, depth), jnp.float32),
             jax.ShapeDtypeStruct((8, wide), jnp.float32),
+            jax.ShapeDtypeStruct((share, (w_qkv.shape[1] + w_out.shape[1]) // 4), kind),
+            jax.ShapeDtypeStruct((w_down.shape[0] // 8, w_down.shape[1]), kind),
+            jax.ShapeDtypeStruct((share, w_gateup.shape[1] // 4), kind),
         ],
-        in_specs=[hbm, hbm, hbm, vmem, hbm],
-        out_specs=[hbm, hbm, hbm, vmem, vmem],
+        in_specs=[hbm, hbm, vmem] + [hbm] * 5,
+        out_specs=[hbm, hbm, vmem, vmem, hbm, hbm, hbm],
         scratch_shapes=[
             pltpu.VMEM((4, rows // 4, width), tokens.dtype),
             pltpu.VMEM((depth, wide // 4), w_mod.dtype),
             pltpu.VMEM((4, 8, wide // 4), jnp.float32),
             pltpu.VMEM((3, 8, wide // 4), jnp.float32),
-            pltpu.SemaphoreType.DMA((5,)),
-            pltpu.SemaphoreType.DMA((22,)),
-            pltpu.SemaphoreType.DMA((22,)),
+            pltpu.VMEM((share, (w_qkv.shape[1] + w_out.shape[1]) // 4), kind),
+            pltpu.VMEM((w_down.shape[0] // 8, w_down.shape[1]), kind),
+            pltpu.VMEM((share, w_gateup.shape[1] // 4), kind),
+            pltpu.SemaphoreType.DMA((4,)),
+            pltpu.SemaphoreType.DMA((16,)),
+            pltpu.SemaphoreType.DMA((19,)),
+            pltpu.SemaphoreType.DMA((19,)),
         ],
         compiler_params=pltpu.CompilerParams(
-            collective_id=ident, has_side_effects=True, vmem_limit_bytes=16 * 1024 * 1024
+            collective_id=ident, has_side_effects=True, vmem_limit_bytes=VMEM_BYTES
         ),
         cost_estimate=pl.CostEstimate(flops=0, bytes_accessed=90_000_000, transcendentals=0),
         name="arrive",
     )(
         tokens.reshape(4, rows // 4, width),
-        captions.reshape(docs, 4, caps // 4, ctx),
         cotangent.reshape(4, rows // 4, width),
         message,
         w_mod,
-    )
-
-
-def finale_kernel(count, *refs):
-    ins, (back_ref, x_ref) = refs[:count], refs[count : count + 2]
-    outs, (home_ref, out_ref) = refs[count + 2 : 2 * count + 2], refs[2 * count + 2 : 2 * count + 4]
-    stage, land, load, c0, c1, s0, s1 = refs[2 * count + 4 :]
-    sems = (s0, s1)
-    me, across, along, far = neighbours()
-    core = lax.axis_index("core")
-    plane, others = planes_after()
-    peers = [across, along, far]
-    quarter = x_ref.shape[1] // 4
-    gathering = Gathering(ins, outs, load, (c0, c1))
-
-    def columns(t):
-        return pl.ds(pl.multiple_of(t * quarter, quarter), quarter)
-
-    returning = Returning(back_ref, home_ref, stage, load.at[count], sems, 10)
-    greet_all()
-    first = [
-        send(x_ref.at[:, columns(p)], land.at[k], sems, k, {"tp": p}) for k, p in enumerate(peers)
-    ]
-    for copy in first:
-        copy.start()
-    returning.begin()
-    gathering.begin()
-    for copy in first:
-        copy.wait_recv()
-    out_ref[plane, core, :, columns(me)] = (x_ref[:, columns(me)] + land[0]) + (land[1] + land[2])
-    here = out_ref.at[plane, core, :, columns(me)]
-    second = [send(here, here, sems, 3 + k, {"seq": p}) for k, p in enumerate(others)]
-    for copy in second:
-        copy.start()
-    for copy in second:
-        copy.wait_recv()
-    here = out_ref.at[:, core, :, columns(me)]
-    third = [send(here, here, sems, 6 + k, {"tp": p}) for k, p in enumerate(peers)]
-    for copy in third:
-        copy.start()
-    returning.turn()
-    gathering.relay()
-    for copy in third:
-        copy.wait_recv()
-    here = out_ref.at[:, core]
-    swap = send(here, here, sems, 9, {"core": 1 - core})
-    swap.start()
-    gathering.hand()
-    swap.wait_recv()
-    returning.end()
-    gathering.end()
-    for copy in first + second + third + [swap]:
-        copy.wait_send()
-
-
-def finale(ident, pieces, back, x):
-    hbm, vmem = pl.BlockSpec(memory_space=pl.ANY), pl.BlockSpec(memory_space=pltpu.VMEM)
-    count = len(pieces)
-    rows, width = x.shape
-    tall, wide = back.shape
-    got = pl.pallas_call(
-        functools.partial(finale_kernel, count),
-        out_shape=[
-            *[jax.ShapeDtypeStruct((4, 2) + p.shape, p.dtype) for p in pieces],
-            jax.ShapeDtypeStruct((4, tall // 4, wide), back.dtype),
-            jax.ShapeDtypeStruct((4, 2, rows, width), jnp.float32),
-        ],
-        in_specs=[hbm] * (count + 1) + [vmem],
-        out_specs=[hbm] * (count + 1) + [vmem],
-        scratch_shapes=[
-            pltpu.VMEM((4, tall // 4, wide), back.dtype),
-            pltpu.VMEM((3, rows, width // 4), jnp.float32),
-            pltpu.SemaphoreType.DMA((count + 1,)),
-            pltpu.SemaphoreType.DMA((10 * count,)),
-            pltpu.SemaphoreType.DMA((10 * count,)),
-            pltpu.SemaphoreType.DMA((16,)),
-            pltpu.SemaphoreType.DMA((16,)),
-        ],
-        compiler_params=pltpu.CompilerParams(
-            collective_id=ident, has_side_effects=True, vmem_limit_bytes=16 * 1024 * 1024
-        ),
-        cost_estimate=pl.CostEstimate(flops=0, bytes_accessed=120_000_000, transcendentals=0),
-        name="finale",
-    )(*pieces, back.reshape(4, tall // 4, wide), x)
-    return got[:count], got[count].reshape(tall, wide), got[count + 1]
+        w_qkv,
+        w_out,
+        w_down,
+        w_gateup,
+    )
 
 
 def lanes_of(rows):
@@ -908,13 +1127,12 @@
 
 
 def cross_kernel(
-    qa_ref, k_ref, v_ref, gk_ref, sq_ref, sk_ref, own_ref, gate_ref,
+    qa_ref, k_ref, v_ref, sq_ref, sk_ref, own_ref, gate_ref,
     ka_ref, va_ref, ov_ref, mix_ref, qx_ref,
 ):
     def prepare(strip):
-        keys = pair_norm(k_ref[strip, :])[0] * gk_ref[...]
-        store_heads(ka_ref, strip, keys, sk_ref[strip, :])
-        store_heads(va_ref, strip, v_ref[strip, :], ones_beside(STRIP))
+        store_heads(ka_ref, strip, k_ref[strip, :].astype(jnp.float32), sk_ref[strip, :])
+        store_heads(va_ref, strip, v_ref[strip, :].astype(jnp.float32), ones_beside(STRIP))
 
     strips(k_ref.shape[0], prepare)
 
@@ -943,11 +1161,11 @@
 
 
 def back_kernel(own, *refs):
-    g_ref, gate_ref, ov_ref, qa_ref, sq_ref, ka_ref, va_ref, k_ref, gk_ref = refs[:9]
-    refs = refs[9:]
+    g_ref, gate_ref, ov_ref, qa_ref, sq_ref, ka_ref, va_ref = refs[:7]
+    refs = refs[7:]
     if own:
-        q_ref, gq_ref, cos_ref, sin_ref, more_ref = refs[:5]
-        refs = refs[5:]
+        k_ref, gk_ref, q_ref, gq_ref, cos_ref, sin_ref, more_ref = refs[:7]
+        refs = refs[7:]
     dq_ref, dk_ref, dv_ref, sum_ref, qx, doa, dqt, dqh, dkh, dvh = refs
     rows, count = qa_ref.shape[0], ka_ref.shape[0]
     sum_ref[...] = jnp.zeros_like(sum_ref)
@@ -1003,9 +1221,10 @@
         grads = join_heads(dkh[0, strip, :], dkh[1, strip, :])
         if own:
             grads = pair_turn(grads, cos_ref[strip, :], -sin_ref[strip, :])
-        normed, inverse = pair_norm(k_ref[strip, :])
-        add_up(2, grads * normed)
-        dk_ref[strip, :] = pair_back(grads * gk_ref[...], normed, inverse).astype(dk_ref.dtype)
+            normed, inverse = pair_norm(k_ref[strip, :])
+            add_up(2, grads * normed)
+            grads = pair_back(grads * gk_ref[...], normed, inverse)
+        dk_ref[strip, :] = grads.astype(dk_ref.dtype)
         dv_ref[strip, :] = join_heads(dvh[0, strip, :], dvh[1, strip, :]).astype(dv_ref.dtype)
 
     strips(count, finish)
@@ -1026,45 +1245,32 @@
     return ref.at[:, pl.ds((offset + index) * width, width)]
 
 
-def attend_own(projected, gain_q, gain_k, cosine, sine, spare_q, spare_k):
+def attend(
+    projected, heads, gain_q, gain_k, gate, cosine, sine, own_q, own_k, cross_q, cross_k
+):
     rows, width = projected.shape[0], projected.shape[1] // 3
-    count = width // 128
+    caps, count = heads.shape[0], width // 128
     bf, f32 = jnp.bfloat16, jnp.float32
 
     def steps(i, ins, outs, scratch):
-        raw, gain_q, gain_k, *tables = ins
+        raw, heads, gain_q, gain_k, gate, cosine, sine, own_q, own_k, cross_q, cross_k = ins
+        qa, ka, va, own, cka, cva, cross, mix = outs
         own_kernel(
             view(raw, i), view(raw, i, offset=count), view(raw, i, offset=2 * count),
-            view(gain_q, i), view(gain_k, i), *tables, *[view(out, i, 256) for out in outs],
+            view(gain_q, i), view(gain_k, i), cosine, sine, own_q, own_k,
+            view(qa, i, 256), view(ka, i, 256), view(va, i, 256), view(own, i, 256),
+        )
+        cross_kernel(
+            view(qa, i, 256), view(heads, i), view(heads, i, offset=count), cross_q, cross_k,
+            view(own, i, 256), view(gate, i), view(cka, i, 256), view(cva, i, 256),
+            view(cross, i, 256), view(mix, i), *scratch,
         )
 
     return Aside(
-        [projected, gain_q, gain_k, cosine, sine, spare_q, spare_k],
-        [jax.ShapeDtypeStruct((rows, 2 * width), d) for d in (bf, bf, bf, f32)],
-        [],
-        steps,
-    )
-
-
-def attend_cross(qa, cap_proj, gain, spare_q, spare_k, own, gate):
-    rows, count = qa.shape[0], qa.shape[1] // 256
-    caps, width = cap_proj.shape[0], cap_proj.shape[1] // 2
-    bf, f32 = jnp.bfloat16, jnp.float32
-
-    def steps(i, ins, outs, scratch):
-        qa, raw, gain, spare_q, spare_k, own, gate = ins
-        ka, va, ov, mix = outs
-        cross_kernel(
-            view(qa, i, 256), view(raw, i), view(raw, i, offset=count), view(gain, i),
-            spare_q, spare_k, view(own, i, 256), view(gate, i),
-            view(ka, i, 256), view(va, i, 256), view(ov, i, 256), view(mix, i), *scratch,
-        )
-
-    return Aside(
-        [qa, cap_proj, gain, spare_q, spare_k, own, gate],
+        [projected, heads, gain_q, gain_k, gate, cosine, sine, own_q, own_k, cross_q, cross_k],
         [
-            jax.ShapeDtypeStruct((caps, 2 * width), bf),
-            jax.ShapeDtypeStruct((caps, 2 * width), bf),
+            *[jax.ShapeDtypeStruct((rows, 2 * width), d) for d in (bf, bf, bf, f32)],
+            *[jax.ShapeDtypeStruct((caps, 2 * width), bf)] * 2,
             jax.ShapeDtypeStruct((rows, 2 * width), f32),
             jax.ShapeDtypeStruct((rows, width), bf),
         ],
@@ -1073,29 +1279,68 @@
     )
 
 
-def attend_back(grads, gate, ov, qa, spare_q, ka, va, raw, gain_k, rest=None):
+def cap_back_kernel(g_ref, k_ref, gain_ref, out_ref, sum_ref):
+    sum_ref[...] = jnp.zeros_like(sum_ref)
+
+    def body(strip):
+        for at in range(0, k_ref.shape[1], 128):
+            lanes = pl.ds(at, 128)
+            grads = g_ref[strip, lanes].astype(jnp.float32)
+            normed, inverse = pair_norm(k_ref[strip, lanes])
+            sum_ref[0:1, lanes] += jnp.sum(grads * normed, axis=0, keepdims=True)
+            out_ref[strip, lanes] = pair_back(
+                grads * gain_ref[:, lanes], normed, inverse
+            ).astype(out_ref.dtype)
+        values = pl.ds(k_ref.shape[1], k_ref.shape[1])
+        out_ref[strip, values] = g_ref[strip, values]
+
+    strips(g_ref.shape[0], body)
+
+
+def cap_back(grads, cap_proj, gain):
+    rows, width = grads.shape
+    whole = pl.BlockSpec((rows, width), lambda i: (0, 0))
+    part = pl.BlockSpec((rows, width // 2), lambda i: (0, 0))
+    return pl.pallas_call(
+        cap_back_kernel,
+        grid=(1,),
+        out_shape=[
+            jax.ShapeDtypeStruct((rows, width), jnp.bfloat16),
+            jax.ShapeDtypeStruct((8, width // 2), jnp.float32),
+        ],
+        in_specs=[whole, part, pl.BlockSpec((1, width // 2), lambda i: (0, 0))],
+        out_specs=[whole, pl.BlockSpec((8, width // 2), lambda i: (0, 0))],
+        compiler_params=pltpu.CompilerParams(vmem_limit_bytes=32 * 1024 * 1024),
+        cost_estimate=pl.CostEstimate(
+            flops=0, bytes_accessed=6 * grads.size, transcendentals=0
+        ),
+        name="cap_back",
+    )(grads, cap_proj, gain)
+
+
+def attend_back(grads, gate, ov, qa, spare_q, ka, va, rest=None):
     rows, width = grads.shape
     caps, count = ka.shape[0], width // 128
     bf, f32 = jnp.bfloat16, jnp.float32
     own = rest is not None
 
     def steps(i, ins, outs, scratch):
-        grads, gate, ov, qa, spare_q, ka, va, raw, gain_k, *rest = ins
+        grads, gate, ov, qa, spare_q, ka, va, *rest = ins
         dq, dk, dv, sums = outs
         operands = [
             view(grads, i), view(gate, i), view(ov, i, 256), view(qa, i, 256), spare_q,
-            view(ka, i, 256), view(va, i, 256), view(raw, i, offset=count if own else 0),
-            view(gain_k, i),
+            view(ka, i, 256), view(va, i, 256),
         ]
         if own:
-            gain_q, cosine, sine, more = rest
+            raw, gain_k, gain_q, cosine, sine, more = rest
+            operands += [view(raw, i, offset=count), view(gain_k, i)]
             operands += [view(raw, i), view(gain_q, i), cosine, sine, view(more, i)]
         back_kernel(
             own, *operands, view(dq, i), view(dk, i), view(dv, i), sums.at[pl.ds(i, 1)], *scratch
         )
 
     return Aside(
-        [grads, gate, ov, qa, spare_q, ka, va, raw, gain_k, *(rest or ())],
+        [grads, gate, ov, qa, spare_q, ka, va, *(rest or ())],
         [
             jax.ShapeDtypeStruct((rows, width), bf if own else f32),
             jax.ShapeDtypeStruct((caps, width), bf),
@@ -1359,13 +1604,10 @@
     )
 
 
-def arrive_plane(ident, tokens, captions, cotangent, message, w_mod):
+def arrive_plane(ident, tokens, cotangent, message, w_mod, *weights):
     if fast():
-        return arrive(ident, tokens, captions, cotangent, message, w_mod)
+        return arrive(ident, tokens, cotangent, message, w_mod, *weights)
     ways = lax.axis_size("tp")
-    docs, caps, ctx = captions.shape
-    captions = captions.reshape(docs, ways, caps // ways, ctx).transpose(1, 0, 2, 3)
-    captions = lax.all_to_all(captions, "tp", 0, 0, tiled=True)
     cotangent = lax.all_to_all(
         cotangent.reshape(ways, -1, cotangent.shape[1]), "tp", 0, 0, tiled=True
     )
@@ -1378,14 +1620,32 @@
         terms.reshape(planes, cores, 8, -1), "seq", scatter_dimension=0, tiled=False
     )
     messages = messages.reshape(lax.axis_size("tp"), cores, 8, depth)
-    return to_plane(tokens), captions, cotangent, messages, pick(terms, lax.axis_index("core"), 0)
-
-
-def finale_plane(ident, pieces, back, x):
-    if fast():
-        return finale(ident, pieces, back, x)
-    totals = lax.all_gather(lax.psum(x, "tp"), ("seq", "core"), axis=0, tiled=False)
-    return collect_plane(pieces), from_plane(back), totals
+    w_qkv, w_out, w_down, w_gateup = weights
+    share = w_down.shape[0] // (ways * cores)
+    block = lax.axis_index("tp") * cores + lax.axis_index("core")
+    return (
+        to_plane(tokens),
+        cotangent,
+        messages,
+        pick(terms, lax.axis_index("core"), 0),
+        jnp.concatenate([columns_of(w_qkv, 3), columns_of(w_out, 1)], axis=1),
+        lax.dynamic_slice_in_dim(w_down, block * share, share, 0),
+        columns_of(w_gateup, 2 * planes),
+    )
+
+
+def columns_of(weight, parts):
+    tp, cores = lax.axis_size("tp"), lax.axis_size("core")
+    me_t, me_c = lax.axis_index("tp"), lax.axis_index("core")
+    share = weight.shape[0] // cores
+    size = weight.shape[1] // (parts * tp)
+    return jnp.concatenate(
+        [
+            lax.dynamic_slice(weight, (me_c * share, (q * tp + me_t) * size), (share, size))
+            for q in range(parts)
+        ],
+        axis=1,
+    )
 
 
 def shards(
@@ -1429,10 +1689,9 @@
     message = jnp.concatenate(
         [condition.astype(jnp.float32), numbers[None], jnp.zeros((3, numbers.shape[0]))], axis=0
     )
-    arrived, captions, cotangents, messages, mod_doc = arrive_plane(
-        13, tokens, caption[0], cotangent, message, w_mod
-    )
-    captions = lax.all_to_all(captions, "seq", 0, 0, tiled=True)
+    arrived, cotangents, messages, mod_doc, *cuts = arrive_plane(
+        13, tokens, cotangent, message, w_mod, w_qkv, w_out, w_down, w_gateup
+    )
     messages = messages.reshape(groups, 8, mod_rows)
     cond_mine = messages[:, :DOCS].reshape(groups * DOCS, mod_rows)
     mod_doc = mod_doc[:DOCS] + b_mod
@@ -1440,32 +1699,30 @@
     numbers = messages[:, DOCS, : 2 * DOCS + 1].astype(jnp.int32)
     counts = jnp.sum(numbers[:, :DOCS], axis=1).astype(jnp.float32)
     mine = pick(numbers, my_group, 0)
-    doc_lengths, bucket, nulls = mine[:DOCS], mine[DOCS], mine[DOCS + 1 :]
+    doc_lengths, bucket = mine[:DOCS], mine[DOCS]
     bucket_count = jnp.sum(jnp.where(numbers[:, DOCS] == bucket, counts, 0.0))
     scale_loss = jnp.sum(counts) / (RES * bucket_count)
 
-    def columns_of(weight, parts):
-        share = weight.shape[0] // cores
-        size = weight.shape[1] // (parts * tp)
-        return jnp.concatenate(
-            [
-                lax.dynamic_slice(weight, (me_c * share, (q * tp + me_t) * size), (share, size))
-                for q in range(parts)
-            ],
-            axis=1,
-        )
-
-    half_qkv = gather_planes(
-        jnp.concatenate([columns_of(w_qkv, 3), columns_of(w_out, 1)], axis=1)
-    )
-    share = w_down.shape[0] // groups
-    later = (
-        columns_of(w_capkv, 2),
-        lax.dynamic_slice_in_dim(w_down, (me_t * cores + me_c) * share, share, 0),
-        columns_of(w_gateup, 2 * planes),
-    )
-    arrived, *later = lax.optimization_barrier((arrived, *later))
-    half_capkv, half_down, half_gateup = [gather_planes(part) for part in later]
+    half_capkv = gather_planes(columns_of(w_capkv, 2))
+    half_qkv, half_down, half_gateup = [gather_planes(part) for part in cuts]
+
+    capmix = jnp.where(null_mask[0][:, None, None] > 0, null_embed[None, None, :], caption[0])
+    my_gain_capkey = pick(gain_capkey.reshape(tp, 1, local), me_t, 0)
+    cap_flat = capmix.reshape(DOCS * cap_dev, ctx)
+    if fast():
+        cap_flat, full_capkv, cap_proj, cotangents, heads = gather_matmul(
+            2, cap_flat, half_capkv, halved=True, trade=[swap_blocks(cotangents, "seq")],
+            finish=head_finish(DOCS * cap_dev, 2 * local, my_gain_capkey),
+        )
+    else:
+        cap_flat, full_capkv, cap_proj = plane_multiply(2, cap_flat, half_capkv, halved=True)
+        capkey_raw, capval_raw = jnp.split(cap_proj, 2, axis=1)
+        capkey_norm, capkey_inv = head_stats(capkey_raw)
+        heads = jnp.concatenate([capkey_norm * my_gain_capkey, capval_raw], axis=1)
+        heads = heads.astype(jnp.bfloat16)
+        cotangents = lax.all_to_all(cotangents, "seq", 0, 0, tiled=True)
+    cotangents = cotangents.reshape(tokens.shape)
+    cap_document = jnp.tile(jnp.repeat(jnp.arange(DOCS, dtype=jnp.int32), cap_dev), planes)
 
     inputs = arrived.reshape(tokens.shape).astype(jnp.float32)
     row = jnp.arange(rows, dtype=jnp.int32)
@@ -1484,49 +1741,50 @@
 
     normed1, inverse1 = row_stats(inputs)
     hidden1 = (normed1 * gain_attn * (1.0 + scale_a)).astype(jnp.bfloat16)
-    hidden1, full_qkv, projected = plane_multiply(
-        1, hidden1, half_qkv, halved=True, width=3 * local
-    )
-    cotangents, projected = lax.optimization_barrier((cotangents, projected))
-    cotangents = lax.all_to_all(cotangents, "seq", 0, 0, tiled=True).reshape(tokens.shape)
-    full_out = full_qkv[:, 3 * local :].reshape(tp, local, local)
-    full_out = lax.all_to_all(full_out, "tp", 0, 0, tiled=True)
-    full_out = full_out.transpose(1, 0, 2).reshape(local, width)
+    hidden1, heads = lax.optimization_barrier((hidden1, heads))
+    heads = heads.reshape(planes, DOCS * cap_dev, 2 * local)
+    if fast():
+        hidden1, full_qkv, projected, heads = gather_matmul(
+            1, hidden1, half_qkv, halved=True, width=3 * local,
+            trade=[swap_blocks(heads, "seq")],
+        )
+    else:
+        hidden1, full_qkv, projected = plane_multiply(
+            1, hidden1, half_qkv, halved=True, width=3 * local
+        )
+        heads = lax.all_to_all(heads, "seq", 0, 0, tiled=True)
+        full_out = full_qkv[:, 3 * local :].reshape(tp, local, local)
+        full_out = lax.all_to_all(full_out, "tp", 0, 0, tiled=True)
+        full_out = full_out.transpose(1, 0, 2).reshape(local, width)
+    heads = heads.reshape(-1, 2 * local)
     my_gain_query = pick(gain_query.reshape(tp, 1, local), me_t, 0)
     my_gain_key = pick(gain_key.reshape(tp, 1, local), me_t, 0)
-    my_gain_capkey = pick(gain_capkey.reshape(tp, 1, local), me_t, 0)
     gate_tanh = pick(jnp.tanh(gate_head).reshape(tp, local_heads), me_t, 0)
     head_gate = jnp.repeat(gate_tanh, HDIM)[None, :]
-    own_aside = {}
+    grad_res0 = cotangents.astype(jnp.float32) * (is_valid * scale_loss)[:, None]
+    grad_down = (tanh_f * grad_res0).astype(jnp.bfloat16)
     if fast():
         cosine, sine = turn_tables(row_pos, col_pos)
         own_spare = spare_columns(all_segment, SPARE)
-        own_aside["aside"] = attend_own(
-            projected, my_gain_query, my_gain_key, cosine, sine,
+        cross_spare = spare_columns(all_document, SPARE)
+        aside = attend(
+            projected, heads, my_gain_query, my_gain_key, head_gate, cosine, sine,
             own_spare, spare_columns(all_segment, 0),
-        )
-
-    captions = captions.transpose(1, 0, 2, 3).reshape(caption.shape[1:])
-    capmix = jnp.where(nulls[:, None, None] > 0, null_embed[None, None, :], captions)
-    cap_flat = capmix.reshape(DOCS * cap_dev, ctx)
-    cap_flat, full_capkv, cap_proj, *own_wides = plane_multiply(
-        2, cap_flat, half_capkv, halved=True, **own_aside
-    )
-    cap_document = jnp.tile(jnp.repeat(jnp.arange(DOCS, dtype=jnp.int32), cap_dev), tp)
-    grad_res0 = cotangents.astype(jnp.float32) * (is_valid * scale_loss)[:, None]
-    grad_down = (tanh_f * grad_res0).astype(jnp.bfloat16)
-    if fast():
-        wide_query, wide_keys, wide_values, own_wide = own_wides
-        cross_spare = spare_columns(all_document, SPARE)
-        cross_aside = attend_cross(
-            wide_query, cap_proj, my_gain_capkey, cross_spare,
-            spare_columns(cap_document, 0), own_wide, head_gate,
-        )
-        grad_down, full_down, grad_ffn, wide_capkeys, wide_capvals, cross_wide, mixed_attn = (
-            plane_multiply(
-                6, grad_down, half_down, turned=True, halved=True, aside=cross_aside, early=1
-            )
-        )
+            cross_spare, spare_columns(cap_document, 0),
+        )
+        out_rows = (
+            full_qkv,
+            "tp",
+            (local, width),
+            lambda ref, p: ref.at[pl.ds(p * local, local), pl.ds(3 * local, local)],
+            lambda ref, p: ref.at[:, pl.ds(pl.multiple_of(p * local, local), local)],
+        )
+        grad_down, full_down, grad_ffn, *wides, full_out = gather_matmul(
+            6, grad_down, half_down, turned=True, halved=True, aside=aside, early=1,
+            trade=[out_rows],
+        )
+        wide_query, wide_keys, wide_values, own_wide = wides[:4]
+        wide_capkeys, wide_capvals, cross_wide, mixed_attn = wides[4:]
     else:
         grad_down, full_down, grad_ffn = plane_multiply(
             6, grad_down, half_down, turned=True, halved=True
@@ -1534,13 +1792,10 @@
         query_raw, key_raw, value_raw = jnp.split(projected, 3, axis=1)
         query_norm, query_inv = head_stats(query_raw)
         key_norm, key_inv = head_stats(key_raw)
-        capkey_raw, capval_raw = jnp.split(cap_proj, 2, axis=1)
-        capkey_norm, capkey_inv = head_stats(capkey_raw)
         query = rotary(query_norm * my_gain_query, row_pos, col_pos, 1.0).astype(jnp.bfloat16)
         keys = rotary(key_norm * my_gain_key, row_pos, col_pos, 1.0).astype(jnp.bfloat16)
         values = value_raw.astype(jnp.bfloat16)
-        capkeys = (capkey_norm * my_gain_capkey).astype(jnp.bfloat16)
-        capvals = capval_raw.astype(jnp.bfloat16)
+        capkeys, capvals = jnp.split(heads, 2, axis=1)
         self_allowed = all_segment[:, None] == all_segment[None, :]
         cross_allowed = all_document[:, None] == cap_document[None, :]
         own_out, own_log = attend_forward(query, keys, values, self_allowed)
@@ -1550,14 +1805,21 @@
     residual = inputs + tanh_a * attn_out
     normed2, inverse2 = row_stats(residual)
     hidden2 = (normed2 * gain_ffn * (1.0 + scale_f)).astype(jnp.bfloat16)
-    hidden2, full_gateup, gate_up = plane_multiply(4, hidden2, half_gateup, halved=True)
-    gate_part, up_part = jnp.split(gate_up, 2, axis=1)
-    sig_gate = jax.nn.sigmoid(gate_part)
-    silu_gate = gate_part * sig_gate
-    hidden_ffn = (silu_gate * up_part).astype(jnp.bfloat16)
-    grad_gate_part = grad_ffn * up_part * sig_gate * (1.0 + gate_part * (1.0 - sig_gate))
-    grad_up_part = grad_ffn * silu_gate
-    grad_gateup = jnp.concatenate([grad_gate_part, grad_up_part], axis=1).astype(jnp.bfloat16)
+    if fast():
+        hidden2, full_gateup, hidden_ffn, grad_gateup = gather_matmul(
+            4, hidden2, half_gateup, halved=True, finish=swiglu_finish(grad_ffn), keep=False
+        )
+        hidden_ffn = hidden_ffn.reshape(grad_ffn.shape)
+        grad_gateup = grad_gateup.reshape(grad_ffn.shape[0], -1)
+    else:
+        hidden2, full_gateup, gate_up = plane_multiply(4, hidden2, half_gateup, halved=True)
+        gate_part, up_part = jnp.split(gate_up, 2, axis=1)
+        sig_gate = jax.nn.sigmoid(gate_part)
+        silu_gate = gate_part * sig_gate
+        hidden_ffn = (silu_gate * up_part).astype(jnp.bfloat16)
+        grad_gate_part = grad_ffn * up_part * sig_gate * (1.0 + gate_part * (1.0 - sig_gate))
+        grad_gateup = jnp.concatenate([grad_gate_part, grad_ffn * silu_gate], axis=1)
+        grad_gateup = grad_gateup.astype(jnp.bfloat16)
     term_down = swap_rows(contract_rows(hidden_ffn, grad_down))
     term_gateup = swap_rows(contract_rows(hidden2, grad_gateup))
     grad_gateup, term_down, term_gateup = lax.optimization_barrier(
@@ -1576,40 +1838,38 @@
     term_out = contract_rows(mixed_attn, grad_attn).astype(jnp.bfloat16)
     term_out = swap_halves(term_out.reshape(1, cores, -1, width))[0]
     term_out = term_out.reshape(term_out.shape[0], tp, -1).transpose(1, 0, 2)
-    term_out = lax.all_to_all(term_out, "tp", 0, 0, tiled=True)
-    grad_mix, term_out, term_down, term_gateup = lax.optimization_barrier(
-        (grad_mix, term_out, term_down, term_gateup)
-    )
-    term_out = scatter_planes(term_out)
     if fast():
         cross_aside = attend_back(
             grad_mix, head_gate, cross_wide, wide_query, cross_spare,
-            wide_capkeys, wide_capvals, cap_proj, my_gain_capkey,
-        )
-        down_out, query_cross, grad_capkey_raw, grad_capvals, cross_sums = multiply_plane(
-            5, hidden_ffn, full_down, aside=cross_aside
-        )
+            wide_capkeys, wide_capvals,
+        )
+        down_out, query_cross, grad_capkeys, grad_capvals, cross_sums, term_out = matmul_scatter(
+            5, hidden_ffn, full_down, aside=cross_aside, trade=[swap_blocks(term_out, "tp")]
+        )
+        grad_heads = jnp.concatenate([grad_capkeys, grad_capvals], axis=1)
+        grad_heads = grad_heads.reshape(planes, DOCS * cap_dev, 2 * local)
         gate_head_term = jnp.sum(cross_sums[:, :2], axis=-1).reshape(-1)
-        gain_capkey_term = cross_sums[:, 2].reshape(-1)
-        grad_cap_proj = jnp.concatenate([grad_capkey_raw, grad_capvals], axis=1)
-        term_capkv = swap_rows(contract_rows(cap_flat, grad_cap_proj))
-        query_cross, term_capkv = lax.optimization_barrier((query_cross, term_capkv))
-        term_capkv = scatter_planes(term_capkv)
         own_aside = attend_back(
             grad_mix, jnp.ones_like(head_gate), own_wide, wide_query, own_spare,
-            wide_keys, wide_values, projected, my_gain_key,
-            (my_gain_query, cosine, sine, query_cross),
+            wide_keys, wide_values,
+            (projected, my_gain_key, my_gain_query, cosine, sine, query_cross),
         )
         result = (residual + tanh_f * down_out).astype(jnp.bfloat16)
-        (all_down, all_gateup, all_out), result, (*grad_projected, own_sums) = collect(
-            10, [term_down, term_gateup, term_out], result, own_aside
-        )
+        (all_down, all_gateup), riders = collect(
+            10,
+            [term_down, term_gateup],
+            own_aside,
+            [swap_blocks(grad_heads, "seq"), swap_blocks(term_out, "seq")],
+        )
+        *grad_projected, own_sums, grad_heads, term_out = riders
+        term_out = jnp.sum(term_out.astype(jnp.float32), axis=0).astype(jnp.bfloat16)
         gain_key_term, gain_query_term = own_sums[:, 2].reshape(-1), own_sums[:, 3].reshape(-1)
         grad_projected = jnp.concatenate(grad_projected, axis=1)
     else:
         down_out, _ = multiply_plane(5, hidden_ffn, full_down)
         result = from_plane((residual + tanh_f * down_out).astype(jnp.bfloat16))
-        all_down, all_gateup, all_out = collect_plane([term_down, term_gateup, term_out])
+        all_down, all_gateup = collect_plane([term_down, term_gateup])
+        term_out = scatter_planes(lax.all_to_all(term_out, "tp", 0, 0, tiled=True))
         grad_own = grad_mix.astype(jnp.bfloat16)
         grad_cross = (head_gate * grad_mix).astype(jnp.bfloat16)
         gate_head_term = jnp.sum(
@@ -1630,17 +1890,28 @@
         grad_projected = jnp.concatenate(
             [grad_query_raw, grad_key_raw, grad_values], axis=1
         ).astype(jnp.bfloat16)
+        grad_heads = jnp.concatenate([grad_capkeys, grad_capvals], axis=1).astype(jnp.bfloat16)
+        grad_heads = grad_heads.reshape(planes, DOCS * cap_dev, 2 * local)
+        grad_heads = lax.all_to_all(grad_heads, "seq", 0, 0, tiled=True)
+    grad_gate_f = grad_res0 * down_out * (1.0 - tanh_f * tanh_f)
+    gate_head_term = gate_head_term * (1.0 - gate_tanh * gate_tanh)
+    grad_heads = grad_heads.reshape(-1, 2 * local)
+    if fast():
+        grad_cap_proj, capkey_sums = cap_back(grad_heads, cap_proj, my_gain_capkey)
+        gain_capkey_term = capkey_sums[0]
+    else:
+        grad_capkeys, grad_capvals = jnp.split(grad_heads.astype(jnp.float32), 2, axis=1)
         gain_capkey_term = jnp.sum(grad_capkeys * capkey_norm, axis=0)
         grad_capkey_raw = head_back(grad_capkeys * my_gain_capkey, capkey_norm, capkey_inv)
         grad_cap_proj = jnp.concatenate([grad_capkey_raw, grad_capvals], axis=1).astype(
             jnp.bfloat16
         )
-        term_capkv = scatter_planes(swap_rows(contract_rows(cap_flat, grad_cap_proj)))
-    grad_gate_f = grad_res0 * down_out * (1.0 - tanh_f * tanh_f)
-    gate_head_term = gate_head_term * (1.0 - gate_tanh * gate_tanh)
     term_qkv = swap_rows(contract_rows(hidden1, grad_projected))
-    grad_projected, term_qkv = lax.optimization_barrier((grad_projected, term_qkv))
+    cap_side, _ = lax.optimization_barrier((grad_cap_proj, term_qkv))
     term_qkv = scatter_planes(term_qkv)
+    term_capkv = swap_rows(contract_rows(cap_flat, cap_side))
+    grad_projected, _ = lax.optimization_barrier((grad_projected, term_capkv))
+    term_capkv = scatter_planes(term_capkv)
     grad_hidden1, *_ = multiply_plane(9, grad_projected, full_qkv, turned=True)
     gain_attn_term = jnp.sum(grad_hidden1 * normed1 * (1.0 + scale_a), axis=0)
     grad_scale_a = grad_hidden1 * normed1 * gain_attn
@@ -1656,17 +1927,17 @@
         precision=lax.Precision.HIGHEST,
         preferred_element_type=jnp.float32,
     )
-    null_rows = nulls[cap_document] > 0
+    plane_nulls = pick(numbers[:, DOCS + 1 :].reshape(tp, cores, DOCS), me_c, 1)
+    null_rows = jnp.repeat(plane_nulls.reshape(-1), cap_dev) > 0
+    grad_hidden1, null_rows, all_down, all_gateup = lax.optimization_barrier(
+        (grad_hidden1, null_rows, all_down, all_gateup)
+    )
     null_sum = jnp.sum(
         jnp.where(null_rows[:, None], grad_cap_proj.astype(jnp.float32), 0.0), axis=0
     )
     null_term = jnp.dot(
         full_capkv.astype(jnp.float32), null_sum, precision=lax.Precision.HIGHEST
     )
-
-    sum_down = all_down.reshape(w_down.shape).astype(jnp.float32)
-    sum_gateup = spread_parts(all_gateup, 2 * planes)
-    sum_out = spread_parts(all_out, 1)
 
     def at_mine(part):
         whole = jnp.zeros((tp,) + part.shape, jnp.float32)
@@ -1686,15 +1957,30 @@
     small_rows = 8 - DOCS
     small_size = small.shape[0]
     small = jnp.pad(small, (0, small_rows * 4 * width - small_size))
-    (all_capkv, all_qkv), input_grad, totals = finale_plane(
-        12,
-        [term_capkv, term_qkv],
-        input_grad,
-        jnp.concatenate([grad_mod_doc, small.reshape(small_rows, 4 * width)], axis=0),
-    )
+    sums = jnp.concatenate([grad_mod_doc, small.reshape(small_rows, 4 * width)], axis=0)
+    if fast():
+        (all_qkv, all_out), _ = collect(12, [term_qkv, term_out])
+    else:
+        all_qkv, all_out = collect_plane([term_qkv, term_out])
+    all_qkv, all_down, all_gateup = lax.optimization_barrier((all_qkv, all_down, all_gateup))
+    sum_down = all_down.reshape(w_down.shape).astype(jnp.float32)
+    sum_gateup = spread_parts(all_gateup, 2 * planes)
+    sum_out = spread_parts(all_out, 1)
+    sum_qkv = spread_parts(all_qkv, 3)
+    sum_qkv, sum_gateup, sum_down, sum_out, term_capkv = lax.optimization_barrier(
+        (sum_qkv, sum_gateup, sum_down, sum_out, term_capkv)
+    )
+    if fast():
+        (all_capkv,), (result, input_grad, totals) = collect(
+            14, [term_capkv], backs=[result, input_grad], sums=sums
+        )
+        result, input_grad = result.reshape(tokens.shape), input_grad.reshape(tokens.shape)
+    else:
+        (all_capkv,) = collect_plane([term_capkv])
+        input_grad = from_plane(input_grad)
+        totals = lax.all_gather(lax.psum(sums, "tp"), ("seq", "core"), axis=0, tiled=False)
     totals = totals.reshape(groups, 8, 4 * width)
     sum_capkv = spread_parts(all_capkv, 2)
-    sum_qkv = spread_parts(all_qkv, 3)
     grad_mod_docs = totals[:, :DOCS].reshape(groups * DOCS, 4 * width)
     sum_mod = lax.dot_general(
         cond_mine,

time: 943 us -> 794 us (0.84)
  waiting for transfers between devices: 120 us -> 29.5 us
  local copies, waits for them, and re-layouts: 74 us -> 33.3 us
  Pallas kernels: 554 us -> 588 us
  starting transfers between devices: 20 us -> 0.54 us
  other arithmetic: 79.8 us -> 64.9 us
  blocking collectives: 13.2 us -> 0 us
    all_to_all x3 -> x0, waiting for transfers between devices: 78.7 us -> none  [the longest x1 44.3 us: shards(): captions = lax.all_to_all(captions, 'seq', 0, 0, tiled=True)]
    pallas_call x15 -> x17, Pallas kernels: 503 us -> 543 us  [the longest x5 239 us: gather_matmul(): pl.pallas_call(functools.partial(gather_kernel, turned, halved, early, *r...]
    reduce_scatter x5 -> x4, waiting for transfers between devices: 31 us -> 0.01 us  [scatter_planes(): return lax.psum_scatter(term, 'seq', scatter_dimension=0, tiled=False)]
    unnamed x121 -> x96, local copies, waits for them, and re-layouts: 40.9 us -> 18.9 us
    all_to_all x3 -> x0, starting transfers between devices: 19 us -> none  [the longest x1 11.2 us: shards(): captions = lax.all_to_all(captions, 'seq', 0, 0, tiled=True)]
    all_gather x4, waiting for transfers between devices: 0.03 us -> 16.5 us  [gather_planes(): return lax.all_gather(part, 'seq', axis=0, tiled=False)]
    all_to_all x1 -> x0, blocking collectives: 13.2 us -> none  [shards(): term_out = lax.all_to_all(term_out, 'tp', 0, 0, tiled=True)]
  transfers between devices with their start and end apart: 17 -> 13, of which waited for: 8 -> 4; matrix products, arithmetic and copies ran while one was open for 13% -> 12% of each run, Pallas kernels for 36% -> 55%
where the time goes in v4:
time: 794 us; the launch traced here: 789 us
  Pallas kernels  588 us (74%)
  other arithmetic  64.9 us (8%)
  matrix products  54.6 us (7%)
  local copies, waits for them, and re-layouts  33.3 us (4%)
  waiting for transfers between devices  29.5 us (4%)
  between operations  17.9 us (2%)
    pallas_call x5, Pallas kernels, gather_matmul(): pl.pallas_call(functools.partial(gather_kernel, turned, halved, early, *r...  239 us
    pallas_call x4, Pallas kernels, matmul_scatter(): pl.pallas_call(functools.partial(scatter_kernel, turned, aside, trade), o...  146 us
    pallas_call x3, Pallas kernels, collect(): pl.pallas_call(functools.partial(collect_kernel, count, *riders), out_sha...  139 us
    pallas_call x1, Pallas kernels, arrive(): pl.pallas_call(arrive_kernel, out_shape=[jax.ShapeDtypeStruct((4, rows //...  45.3 us
    dot_general x5, matrix products, contract_rows(): lax.dot_general(left, right, (((0,), (0,)), ((), ())), preferred_element_...  32.7 us
    unnamed x96, local copies, waits for them, and re-layouts  18.9 us
    all_gather x4, waiting for transfers between devices, gather_planes(): return lax.all_gather(part, 'seq', axis=0, tiled=False)  16.5 us
    pallas_call x4, Pallas kernels, spread(): pl.pallas_call(functools.partial(spread_kernel, parts), grid=(cores, cut)...  16 us
  transfers between devices with their start and end apart: 13, of which 4 were waited for; matrix products, arithmetic and copies ran while one was open for 12% of the time, Pallas kernels for 55%

profile of v4, /device:TPU:0, one launch (start us, length us, event | category | flops | bytes accessed | tf_op | source)
XLA Modules:
  0.0 789.3 jit_solution(10553682745710857347)
XLA Ops:
  11.1 45.3 %arrive.1 = (bf16[4,64,1536]{2,1,0:T(8,128)(2,1)}, bf16[4,64,1536]{2,1,0:T(8,128)(2,1)}, f32[4,2,8,256]{3,2,1,0:T(8,128)}, f32[8,6144]{1,0:T(8,128)}, bf16[192,1...) custom-call(bf16[4,64,1536]{2,1,0:T(8,128)(2,1)} %bitcast.203, ...), custom_call_target="tpu_custom_call" | custom-call | bytes 90000000 | tf_op jit(solution)/shard_map/arrive/pallas_call | solution.py:993
  70.8 4.8 fusion.33
  77.2 16.4 %all-gather.9.cloned.1.call-done = bf16[2048,768]{1,0:T(8,128)(2,1)} async-done(((bf16[512,768]{1,0:T(8,128)(2,1)}), bf16[2048,768]{1,0:T(8,128)(2,1)}) %all-gather.9.cloned.1.call-update) | async-done | bytes 3145744 | tf_op jit(solution)/shard_map/all_gather | solution.py:1537
  94.3 75.7 %gather_matmul.5 = (bf16[4,256,4096]{2,1,0:T(8,128)(2,1)}, bf16[4096,768]{1,0:T(8,128)(2,1)}, f32[4,256,768]{2,1,0:T(8,128)}, bf16[4,64,1536]{2,1,0:T(8,128)(2,1)}, bf16[4,256,768]{2,1,0:T(8,128)(2,1)}) custom-call(bf16[256,4096]{1,0:T(8,128)(2,1)} %bitcast_select_fusion.refs_0_, bf16[4,512,768]{2,1,0:T(8,128)(2,1)} %bitcast.231, ...), custom_call_target="tpu_custom_call" | custom-call | flops 6442450944 | bytes 90000000 | tf_op jit(solution)/shard_map/gather_matmul/pallas_call | solution.py:329
  170.0 3.7 fusion.15
  173.7 42.7 %gather_matmul.6 = (bf16[4,256,1536]{2,1,0:T(8,128)(2,1)}, bf16[1536,1536]{1,0:T(8,128)(2,1)}, f32[4,256,1152]{2,1,0:T(8,128)}, bf16[4,256,768]{2,1,0:T(8,128)(2,1)}) custom-call(bf16[256,1536]{1,0:T(8,128)(2,1)} %get-tuple-element.95.refs_0_, bf16[4,192,1536]{2,1,0:T(8,128)(2,1)} %bitcast.232, bf16[4,256,768]{2,1,0:T(8,128)(2,1)} %get-tuple-element.97.refs_2_), custom_call_target="tpu_custom_call" | custom-call | flops 3623878656 | bytes 90000000 | tf_op jit(solution)/shard_map/gather_matmul/pallas_call | solution.py:329
  216.4 58.7 %gather_matmul.7 = (bf16[4,256,1536]{2,1,0:T(8,128)(2,1)}, bf16[1024,1536]{1,0:T(8,128)(2,1)}, f32[4,256,1024]{2,1,0:T(8,128)}, bf16[1024,768]{1,0:T(8,128)(2,1)...) custom-call(bf16[256,1536]{1,0:T(8,128)(2,1)} %get-tuple-element.179, ...), custom_call_target="tpu_custom_call" | custom-call | flops 3221225472 | bytes 90000000 | tf_op jit(solution)/shard_map/gather_matmul/pallas_call | solution.py:329
  275.2 31.7 %matmul_scatter.4 = f32[256,1536]{1,0:T(8,128)} custom-call(bf16[4,256,384]{2,1,0:T(8,128)(2,1)} %bitcast.233, bf16[384,1536]{1,0:T(8,128)(2,1)} %get-tuple-element.105.refs_1_), custom_call_target="tpu_custom_call" | custom-call | flops 1207959552 | bytes 90000000 | tf_op jit(solution)/shard_map/matmul_scatter/pallas_call | solution.py:516
  311.9 32.8 %gather_matmul.8 = (bf16[4,256,1536]{2,1,0:T(8,128)(2,1)}, bf16[1536,2048]{1,0:T(8,128)(2,1)}, bf16[4,256,1024]{2,1,0:T(8,128)(2,1)}, bf16[4,256,2048]{2,1,0:T(8,128)(2,1)}) custom-call(bf16[256,1536]{1,0:T(8,128)(2,1)} %multiply_convert_fusion.1.refs_0_, bf16[4,192,2048]{2,1,0:T(8,128)(2,1)} %bitcast.230, f32[4,256,1024]{2,1,0:T(8,128)} %get-tuple-element.107.refs_2_), custom_call_target="tpu_custom_call" | custom-call | flops 6442450944 | bytes 90000000 | tf_op jit(solution)/shard_map/gather_matmul/pallas_call | solution.py:329
  344.7 10.1 %bitcast_convert_fusion = bf16[1536,2048]{1,0:T(8,128)(2,1)S(1)} fusion(bf16[4,256,1536]{2,1,0:T(8,128)(2,1)} %get-tuple-element.111, bf16[4,256,2048]{2,1,0:T(8,128)(2,1)} %get-tuple-element.108), kind=kOutput, calls=%fused_computation | convolution fusion | flops 6445596672 | bytes 13631488 | tf_op jit(solution)/shard_map/dot_general | solution.py:1507
  360.7 3.8 bitcast_convert_fusion.1
  366.7 3.6 collective-permute-done
  373.3 6.1 fusion.9
  380.0 36.6 %matmul_scatter.5 = f32[256,1536]{1,0:T(8,128)} custom-call(bf16[4,256,2048]{2,1,0:T(8,128)(2,1)} %get-tuple-element.108, bf16[1536,2048]{1,0:T(8,128)(2,1)} %get-tuple-element.115.refs_1_), custom_call_target="tpu_custom_call" | custom-call | flops 6442450944 | bytes 90000000 | tf_op jit(solution)/shard_map/matmul_scatter/pallas_call | solution.py:516
  419.7 4.9 subtract_multiply_fusion
  428.4 29.4 %gather_matmul.9 = (bf16[4,256,1536]{2,1,0:T(8,128)(2,1)}, f32[4,256,384]{2,1,0:T(8,128)}) custom-call(bf16[256,1536]{1,0:T(8,128)(2,1)} %multiply_convert_fusion.refs_0_, bf16[384,1536]{1,0:T(8,128)(2,1)} %get-tuple-element.105.refs_1_), custom_call_target="tpu_custom_call" | custom-call | flops 1207959552 | bytes 90000000 | tf_op jit(solution)/shard_map/gather_matmul/pallas_call | solution.py:329
  457.8 3.3 convolution_convert_fusion.2
  464.4 42.7 %matmul_scatter.6 = (f32[256,1536]{1,0:T(8,128)}, f32[1024,384]{1,0:T(8,128)}, bf16[1024,384]{1,0:T(8,128)(2,1)}, bf16[1024,384]{1,0:T(8,128)(2,1)}, f32[3,8,128]{2,1,0:T(8,128)}, /*index=5*/bf16[4,192,384]{2,1,0:T(8,128)(2,1)}) custom-call(bf16[4,256,1024]{2,1,0:T(8,128)(2,1)} %get-tuple-element.109.refs_0_, bf16[1024,1536]{1,0:T(8,128)(2,1)} %get-tuple-element.121.refs_1_, ...), custom_call_target="tpu_custom_call" | custom-call | flops 3221225472 | bytes 90000000 | tf_op jit(solution)/shard_map/matmul_scatter/pallas_call | solution.py:516
  510.4 55.4 %collect.3 = (bf16[4,2,128,1536]{3,2,1,0:T(8,128)(2,1)}, bf16[4,2,192,2048]{3,2,1,0:T(8,128)(2,1)}, bf16[1024,384]{1,0:T(8,128)(2,1)}, bf16[1024,384]{1,0:T(8,12...) custom-call(bf16[128,1536]{1,0:T(8,128)(2,1)} %bitcast.211, ...), custom_call_target="tpu_custom_call" | custom-call | bytes 47185920 | tf_op jit(solution)/shard_map/collect/pallas_call | solution.py:807
  569.9 4.5 convolution_convert_fusion
  580.9 10.9 %convolution_convert_fusion.1 = bf16[4096,768]{1,0:T(8,128)(2,1)S(1)} fusion(bf16[1024,4096]{1,0:T(8,128)(2,1)} %bitcast.234, bf16[1024,768]{1,0:T(8,128)(2,1)S(1)} %get-tuple-element.139), kind=kOutput, calls=%fused_computation.3 | convolution fusion | flops 6445596672 | bytes 16252928 | tf_op jit(solution)/shard_map/dot_general | solution.py:1507
  592.1 5.6 collective-permute-done.4
  604.4 35.0 %matmul_scatter.7 = f32[256,1536]{1,0:T(8,128)} custom-call(bf16[4,256,1152]{2,1,0:T(8,128)(2,1)} %bitcast.212, bf16[1536,1536]{1,0:T(8,128)(2,1)} %get-tuple-element.103.refs_13_.refs_1_), custom_call_target="tpu_custom_call" | custom-call | flops 3623878656 | bytes 90000000 | tf_op jit(solution)/shard_map/matmul_scatter/pallas_call | solution.py:516
  643.2 7.9 fusion.66
  651.3 6.2 fusion.16
  660.6 23.7 %collect.4 = (bf16[4,2,192,1152]{3,2,1,0:T(8,128)(2,1)}, bf16[4,2,192,384]{3,2,1,0:T(8,128)(2,1)}) custom-call(bf16[192,1152]{1,0:T(8,128)(2,1)} %bitcast.209, bf16[192,384]{1,0:T(8,128)(2,1)} %reduce_sum.165.refs_1_), custom_call_target="tpu_custom_call" | custom-call | bytes 23592960 | tf_op jit(solution)/shard_map/collect/pallas_call | solution.py:807
  687.7 3.5 spread.4
  691.2 5.2 spread.5
  696.4 3.8 bitcast_convert_fusion.2
  700.2 59.9 %collect.5 = (bf16[4,2,512,768]{3,2,1,0:T(8,128)(2,1)}, bf16[4,64,1536]{2,1,0:T(8,128)(2,1)}, bf16[4,64,1536]{2,1,0:T(8,128)(2,1)}, f32[4,2,8,6144]{3,2,1,0:T(8,128)}) custom-call(bf16[512,768]{1,0:T(8,128)(2,1)} %bitcast.208, bf16[4,64,1536]{2,1,0:T(8,128)(2,1)} %bitcast.192, bf16[4,64,1536]{2,1,0:T(8,128)(2,1)} %bitcast.193, ...), custom_call_target="tpu_custom_call" | custom-call | bytes 31457280 | tf_op jit(solution)/shard_map/collect/pallas_call | solution.py:807
  767.6 5.3 spread.7
  772.9 7.0 convolution_bitcast_fusion
  (248 shorter events, 85.0 us)
Async XLA Ops:
  7.2 86.5 %all-gather.9.cloned.1.call-start = ((), (), s32[]{:S(2)}) async-start(), calls=%async_computation.8 | async-start | bytes 3932160 | tf_op jit(solution)/shard_map/all_gather | solution.py:1537
  9.4 164.3 %all-gather.11.cloned.1.call-start = ((), (), s32[]{:S(2)}) async-start(), calls=%async_computation.9 | async-start | bytes 2949120 | tf_op jit(solution)/shard_map/all_gather | solution.py:1537
  56.4 5.0 copy-start.32
  56.4 5.0 copy-start.33
  56.4 5.0 copy-start.34
  56.4 5.0 copy-start.5
  56.5 160.0 %all-gather.13.cloned.1.call-start = ((), (), s32[]{:S(2)}) async-start(), calls=%async_computation.10 | async-start | bytes 1966080 | tf_op jit(solution)/shard_map/all_gather | solution.py:1537
  57.2 254.7 %all-gather.15.cloned.1.call-start = ((), (), s32[]{:S(2)}) async-start(), calls=%async_computation.11 | async-start | bytes 3932160 | tf_op jit(solution)/shard_map/all_gather | solution.py:1537
  57.8 452.0 %reduce-scatter.5.cloned.1.call-start = ((), (), s32[]{:S(2)}) async-start(), calls=%async_computation.4 | async-start | bytes 1966080 | tf_op jit(solution)/shard_map/reduce_scatter | solution.py:1551
  64.5 6.2 copy-start.25
  64.5 6.2 copy-start.28
  70.7 4.8 copy-start.17
  94.3 75.7 %copy-start.27 = (f32[1536]{0:T(1024)S(1)}, f32[1536]{0:T(1024)}, u32[]{:S(2)}) copy-start(f32[1536]{0:T(1024)} %param.35) | copy-start | bytes 18436
  354.9 5.8 copy-start.37
  359.5 13.8 %collective-permute-start.1 = (bf16[4,192,2048]{2,1,0:T(8,128)(2,1)}, bf16[4,192,2048]{2,1,0:T(8,128)(2,1)}, u32[]{:S(2)}, u32[]{:S(2)}) collective-permute-start(bf16[4,192,2048]{2,1,0:T(8,128)(2,1)} %dynamic-slice_bitcast_fusion.1), channel_id=1, source_target_pairs={{0,4},{4,0},{1,5},{5,1},{2,6},{6,2},{3,7},{7,3},{8,12},{12,8},{9,1... | collective-permute-start | bytes 9437192 | tf_op jit(solution)/shard_map/ppermute | solution.py:1559
  366.7 3.6 collective-permute-start
  379.4 130.4 %reduce-scatter.7.cloned.1.call-start = ((), (), s32[]{:S(2)}) async-start(), calls=%async_computation.5 | async-start | bytes 3932160 | tf_op jit(solution)/shard_map/reduce_scatter | solution.py:1551
  380.0 280.6 %reduce-scatter.9.cloned.1.call-start = ((), (), s32[]{:S(2)}) async-start(), calls=%async_computation.6 | async-start | bytes 2211840 | tf_op jit(solution)/shard_map/reduce_scatter | solution.py:1551
  428.4 29.4 %copy-start.38 = (bf16[1024,384]{1,0:T(8,128)(2,1)S(1)}, bf16[1024,384]{1,0:T(8,128)(2,1)}, u32[]{:S(2)}) copy-start(bf16[1024,384]{1,0:T(8,128)(2,1)} %get-tuple-element.104) | copy-start | bytes 2359300
  461.2 2.1 collective-permute-start.2
  567.5 6.9 copy-start.24
  569.9 4.8 copy-start.3
  574.7 4.5 collective-permute-start.3
  580.8 119.3 %reduce-scatter.11.cloned.1.call-start = ((), (), s32[]{:S(2)}) async-start(), calls=%async_computation.7 | async-start | bytes 3932160 | tf_op jit(solution)/shard_map/reduce_scatter | solution.py:1551
  592.0 5.7 collective-permute-start.4
  643.2 8.0 %copy-start.7 = (bf16[4,64,1536]{2,1,0:T(8,128)(2,1)S(1)}, bf16[4,64,1536]{2,1,0:T(8,128)(2,1)}, u32[]{:S(2)}) copy-start(bf16[4,64,1536]{2,1,0:T(8,128)(2,1)} %get-tuple-element.90) | copy-start | bytes 2359300
  643.2 8.0 %copy-start.10 = (bf16[4,64,1536]{2,1,0:T(8,128)(2,1)S(1)}, bf16[4,64,1536]{2,1,0:T(8,128)(2,1)}, u32[]{:S(2)}) copy-start(bf16[4,64,1536]{2,1,0:T(8,128)(2,1)} %get-tuple-element.99) | copy-start | bytes 2359300
  651.3 6.2 copy-start.18
  651.3 6.2 copy-start.19
  685.7 5.5 slice-start
  691.2 5.2 copy-start.15
  772.9 7.0 copy-start.21
  (24 other events, 60.6 us)
Sparse Core Ops, SparseCore 0:
  10.2 83.4 all-gather.8
  95.3 58.4 all-gather.10
  155.3 58.7 all-gather.12
  215.6 62.4 all-gather.14
  379.5 33.8 reduce-scatter.4
  416.1 59.2 reduce-scatter.6
  581.0 36.8 reduce-scatter.8
  620.8 59.3 reduce-scatter.10

commit v5 on v4

--- a/solution.py
+++ b/solution.py
@@ -398,8 +398,16 @@
     )
 
 
-def scatter_kernel(turned, aside, trade, *refs):
-    refs = bind(refs, (2, 1, 10), aside, trade)
+def finished(aside, out_ref):
+    count = len(aside.operands)
+    for copy in aside.loads:
+        copy.wait()
+    if aside.steps:
+        aside.steps(out_ref, aside.refs[2][:count], aside.refs[1], aside.refs[2][count + 1 :])
+
+
+def scatter_kernel(turned, aside, trade, after, *refs):
+    refs = bind(refs, (2, 1, 10), aside, trade, after)
     x_hbm, w_hbm, out_ref, sums, far_out, near_out, relay, land, s0, s1, x_ref, w_ref, load = refs
     me, across, along, far = neighbours()
     sems = (s0, s1)
@@ -415,6 +423,7 @@
         blocks[k] = pltpu.make_async_copy(x_hbm.at[owner], x_ref.at[owner], load.at[k])
         blocks[k].start()
     aside.load()
+    after.load()
     if trade.items:
         greet_all()
     else:
@@ -503,21 +512,24 @@
             1, :, columns
         ].astype(jnp.float32)
 
+    finished(after, out_ref)
     for copy in (far_a, far_b, across_a, along_b, across_b, along_a):
         copy.wait_send()
     trade.end()
 
 
-def matmul_scatter(ident, x, w, turned=False, aside=None, trade=()):
-    aside, trade = aside or nothing(), Trade(*trade)
+def matmul_scatter(ident, x, w, turned=False, aside=None, trade=(), after=None):
+    riders = [aside or nothing(), Trade(*trade), after or nothing()]
     rows, depth = x.shape[0] // 4, x.shape[1]
     width = w.shape[0] if turned else w.shape[1]
     vmem = pl.BlockSpec(memory_space=pltpu.VMEM)
     return pl.pallas_call(
-        functools.partial(scatter_kernel, turned, aside, trade),
-        out_shape=[jax.ShapeDtypeStruct((rows, width), jnp.float32)] + aside.outs + trade.outs,
-        in_specs=[pl.BlockSpec(memory_space=pl.ANY)] * 2 + aside.in_specs + trade.in_specs,
-        out_specs=[vmem] + aside.out_specs + trade.out_specs,
+        functools.partial(scatter_kernel, turned, *riders),
+        out_shape=[jax.ShapeDtypeStruct((rows, width), jnp.float32)]
+        + [y for rider in riders for y in rider.outs],
+        in_specs=[pl.BlockSpec(memory_space=pl.ANY)] * 2
+        + [y for rider in riders for y in rider.in_specs],
+        out_specs=[vmem] + [y for rider in riders for y in rider.out_specs],
         scratch_shapes=[
             pltpu.VMEM((2, rows // 2, width), jnp.float32),
             pltpu.VMEM((rows, width), jnp.bfloat16),
@@ -529,8 +541,7 @@
             pltpu.VMEM((4, rows, depth), x.dtype),
             pltpu.VMEM(w.shape, w.dtype),
             pltpu.SemaphoreType.DMA((5,)),
-            *aside.scratch,
-            *trade.scratch,
+            *[y for rider in riders for y in rider.scratch],
         ],
         compiler_params=pltpu.CompilerParams(
             collective_id=ident, has_side_effects=True, vmem_limit_bytes=VMEM_BYTES
@@ -541,7 +552,104 @@
             transcendentals=0,
         ),
         name="matmul_scatter",
-    )(x.reshape(4, rows, depth), w, *aside.operands, *trade.operands)
+    )(x.reshape(4, rows, depth), w, *[y for rider in riders for y in rider.operands])
+
+
+def outer_kernel(count, *refs):
+    pairs, outs = refs[: 2 * count], refs[2 * count : 3 * count]
+    lefts, rights, owns, aways, lands = [
+        refs[(3 + k) * count : (4 + k) * count] for k in range(5)
+    ]
+    load, s0, s1 = refs[8 * count :]
+    core = lax.axis_index("core")
+    to_core = {"core": 1 - core}
+    loads = []
+    for i in range(count):
+        left, right = pairs[2 * i : 2 * i + 2]
+        blocks = outs[i].shape[0]
+        size = left.shape[1] // blocks
+        copies = [pltpu.make_async_copy(right, rights[i], load.at[5 * i])]
+        for z in range(blocks):
+            at = pl.ds(z * size, size)
+            copies.append(
+                pltpu.make_async_copy(left.at[:, at], lefts[i].at[:, at], load.at[5 * i + 1 + z])
+            )
+        for copy in copies:
+            copy.start()
+        loads.append(copies)
+    greet([to_core])
+    sent = []
+    for i in range(count):
+        blocks, rows, width = outs[i].shape
+        tile = tile_of(width)
+        loads[i][0].wait()
+        for z in range(blocks):
+            loads[i][1 + z].wait()
+            left = lefts[i][:, z * 2 * rows : (z + 1) * 2 * rows]
+
+            @pl.loop(0, width // tile)
+            def _(step):
+                columns = pl.ds(pl.multiple_of(step * tile, tile), tile)
+                product = lax.dot_general(
+                    left, rights[i][:, columns], (((0,), (0,)), ((), ())),
+                    preferred_element_type=jnp.float32,
+                )
+                first, second = product[:rows], product[rows:]
+                mine = jnp.where(core == 0, first, second)
+                away = jnp.where(core == 0, second, first)
+                owns[i][z, :, columns] = mine
+                aways[i][z, :, columns] = away.astype(aways[i].dtype)
+
+            copy = send(aways[i].at[z], lands[i].at[z], (s0, s1), 4 * i + z, to_core)
+            copy.start()
+            sent.append((i, z, copy))
+    for i, z, copy in sent:
+        copy.wait_recv()
+        tile = tile_of(outs[i].shape[-1])
+
+        @pl.loop(0, outs[i].shape[-1] // tile)
+        def _(step):
+            columns = pl.ds(pl.multiple_of(step * tile, tile), tile)
+            outs[i][z, :, columns] = (
+                owns[i][z, :, columns] + lands[i][z, :, columns].astype(jnp.float32)
+            ).astype(outs[i].dtype)
+
+    for _, _, copy in sent:
+        copy.wait_send()
+
+
+def outer(ident, *items):
+    bf, f32 = jnp.bfloat16, jnp.float32
+    shapes = [
+        (blocks, left.shape[1] // (2 * blocks), right.shape[1]) for left, right, blocks in items
+    ]
+    count = len(items)
+    hbm, vmem = pl.BlockSpec(memory_space=pl.ANY), pl.BlockSpec(memory_space=pltpu.VMEM)
+    return pl.pallas_call(
+        functools.partial(outer_kernel, count),
+        out_shape=[jax.ShapeDtypeStruct(shape, bf) for shape in shapes],
+        in_specs=[hbm] * (2 * count),
+        out_specs=[vmem] * count,
+        scratch_shapes=[
+            *[pltpu.VMEM(left.shape, bf) for left, _, _ in items],
+            *[pltpu.VMEM(right.shape, bf) for _, right, _ in items],
+            *[pltpu.VMEM(shape, f32) for shape in shapes],
+            *[pltpu.VMEM(shape, bf) for shape in shapes],
+            *[pltpu.VMEM(shape, bf) for shape in shapes],
+            pltpu.SemaphoreType.DMA((5 * count,)),
+            pltpu.SemaphoreType.DMA((4 * count,)),
+            pltpu.SemaphoreType.DMA((4 * count,)),
+        ],
+        compiler_params=pltpu.CompilerParams(
+            collective_id=ident, has_side_effects=True, vmem_limit_bytes=VMEM_BYTES
+        ),
+        cost_estimate=pl.CostEstimate(
+            flops=sum(2 * left.size * right.shape[1] for left, right, _ in items),
+            bytes_accessed=20_000_000,
+            transcendentals=0,
+        ),
+        name="outer",
+    )(*[x for left, right, _ in items for x in (left, right)])
 
 
 class Gathering:
@@ -1033,6 +1141,177 @@
     )
 
 
+def by_rows(rows, sums, body):
+    for ref in sums:
+        ref[...] = jnp.zeros_like(ref)
+
+    @pl.loop(0, rows // 32)
+    def _(step):
+        body(pl.ds(pl.multiple_of(step * 32, 32), 32))
+
+
+def chosen(mod_ref, document, part, width):
+    at = pl.ds(part * width, width)
+    found = mod_ref[DOCS - 1 : DOCS, at]
+    for d in range(DOCS - 1):
+        found = jnp.where(document == d, mod_ref[d : d + 1, at], found)
+    return found
+
+
+def tally(ref, row, values):
+    ref[row] += (values[:8] + values[8:16]) + (values[16:24] + values[24:])
+
+
+def tally_docs(ref, row, document, values):
+    for d in range(DOCS):
+        tally(ref, row + d, jnp.where(document == d, values, 0.0))
+
+
+def norm_of(values):
+    inverse = lax.rsqrt(jnp.mean(values * values, axis=-1, keepdims=True) + eps)
+    return values * inverse, inverse
+
+
+def settle(out_ref, sums):
+    out_ref[...] = jnp.sum(sums[...], axis=1)
+
+
+def after_attention(inputs, mod_doc, document, gain):
+    rows, width = inputs.shape
+
+    def work(attn_ref, ins, outs, scratch):
+        (x_ref, mod_ref, doc_ref, gain_ref), (residual_ref, hidden_ref) = ins, outs
+
+        def body(strip):
+            document = doc_ref[strip, 0:1]
+            gate = jnp.tanh(chosen(mod_ref, document, 1, width))
+            residual = x_ref[strip, :].astype(jnp.float32) + gate * attn_ref[strip, :]
+            residual_ref[strip, :] = residual
+            normed, _ = norm_of(residual)
+            scale = chosen(mod_ref, document, 2, width)
+            hidden_ref[strip, :] = (normed * gain_ref[...] * (1.0 + scale)).astype(
+                hidden_ref.dtype
+            )
+
+        by_rows(rows, [], body)
+
+    return Aside(
+        [inputs, mod_doc, document, gain],
+        [
+            jax.ShapeDtypeStruct((rows, width), jnp.float32),
+            jax.ShapeDtypeStruct((rows, width), jnp.bfloat16),
+        ],
+        [],
+        work,
+    )
+
+
+def after_ffn_back(residual, attn_out, cotangent, weight, mod_doc, document, gain):
+    rows, width = residual.shape
+
+    def work(back_ref, ins, outs, scratch):
+        res_ref, attn_ref, cot_ref, weight_ref, mod_ref, doc_ref, gain_ref = ins
+        grad_ref, attn_back_ref, sum_ref = outs
+        (sums,) = scratch
+
+        def body(strip):
+            document = doc_ref[strip, 0:1]
+            normed, inverse = norm_of(res_ref[strip, :])
+            scale = 1.0 + chosen(mod_ref, document, 2, width)
+            gain = gain_ref[...]
+            back = back_ref[strip, :]
+            both = back * normed
+            tally(sums, 8, both * scale)
+            tally_docs(sums, 0, document, both * gain)
+            inner = back * gain * scale
+            inner = inner - normed * jnp.mean(inner * normed, axis=-1, keepdims=True)
+            grads = cot_ref[strip, :].astype(jnp.float32) * weight_ref[strip, 0:1]
+            grads = grads + inverse * inner
+            grad_ref[strip, :] = grads
+            gate = jnp.tanh(chosen(mod_ref, document, 1, width))
+            attn_back_ref[strip, :] = (gate * grads).astype(attn_back_ref.dtype)
+            tally_docs(sums, 4, document, grads * attn_ref[strip, :] * (1.0 - gate * gate))
+
+        by_rows(rows, [sums], body)
+        settle(sum_ref, sums)
+
+    return Aside(
+        [residual, attn_out, cotangent, weight, mod_doc, document, gain],
+        [
+            jax.ShapeDtypeStruct((rows, width), jnp.float32),
+            jax.ShapeDtypeStruct((rows, width), jnp.bfloat16),
+            jax.ShapeDtypeStruct((16, width), jnp.float32),
+        ],
+        [pltpu.VMEM((16, 8, width), jnp.float32)],
+        work,
+    )
+
+
+def after_ffn(residual, cotangent, weight, mod_doc, document):
+    rows, width = residual.shape
+
+    def work(down_ref, ins, outs, scratch):
+        res_ref, cot_ref, weight_ref, mod_ref, doc_ref = ins
+        result_ref, sum_ref = outs
+        (sums,) = scratch
+
+        def body(strip):
+            document = doc_ref[strip, 0:1]
+            gate = jnp.tanh(chosen(mod_ref, document, 3, width))
+            down = down_ref[strip, :]
+            result_ref[strip, :] = (res_ref[strip, :] + gate * down).astype(result_ref.dtype)
+            grads = cot_ref[strip, :].astype(jnp.float32) * weight_ref[strip, 0:1]
+            tally_docs(sums, 0, document, grads * down * (1.0 - gate * gate))
+
+        by_rows(rows, [sums], body)
+        settle(sum_ref, sums)
+
+    return Aside(
+        [residual, cotangent, weight, mod_doc, document],
+        [
+            jax.ShapeDtypeStruct((rows, width), jnp.bfloat16),
+            jax.ShapeDtypeStruct((8, width), jnp.float32),
+        ],
+        [pltpu.VMEM((8, 8, width), jnp.float32)],
+        work,
+    )
+
+
+def after_input_back(inputs, grads, mod_doc, document, gain):
+    rows, width = inputs.shape
+
+    def work(back_ref, ins, outs, scratch):
+        x_ref, grad_ref, mod_ref, doc_ref, gain_ref = ins
+        out_ref, sum_ref = outs
+        (sums,) = scratch
+
+        def body(strip):
+            document = doc_ref[strip, 0:1]
+            normed, inverse = norm_of(x_ref[strip, :].astype(jnp.float32))
+            scale = 1.0 + chosen(mod_ref, document, 0, width)
+            gain = gain_ref[...]
+            back = back_ref[strip, :]
+            both = back * normed
+            tally(sums, 4, both * scale)
+            tally_docs(sums, 0, document, both * gain)
+            inner = back * gain * scale
+            inner = inner - normed * jnp.mean(inner * normed, axis=-1, keepdims=True)
+            out_ref[strip, :] = (grad_ref[strip, :] + inverse * inner).astype(out_ref.dtype)
+
+        by_rows(rows, [sums], body)
+        settle(sum_ref, sums)
+
+    return Aside(
+        [inputs, grads, mod_doc, document, gain],
+        [
+            jax.ShapeDtypeStruct((rows, width), jnp.bfloat16),
+            jax.ShapeDtypeStruct((8, width), jnp.float32),
+        ],
+        [pltpu.VMEM((8, 8, width), jnp.float32)],
+        work,
+    )
+
+
 def lanes_of(rows):
     return lax.broadcasted_iota(jnp.int32, (rows, 128), 1)
 
@@ -1326,7 +1605,12 @@
 
     def steps(i, ins, outs, scratch):
         grads, gate, ov, qa, spare_q, ka, va, *rest = ins
-        dq, dk, dv, sums = outs
+        if own:
+            all_out, sums = outs
+            dq, dk, dv = [view(all_out, i, offset=k * count) for k in range(3)]
+        else:
+            dq, all_out, sums = outs
+            dq, dk, dv = view(dq, i), view(all_out, i), view(all_out, i, offset=count)
         operands = [
             view(grads, i), view(gate, i), view(ov, i, 256), view(qa, i, 256), spare_q,
             view(ka, i, 256), view(va, i, 256),
@@ -1335,16 +1619,19 @@
             raw, gain_k, gain_q, cosine, sine, more = rest
             operands += [view(raw, i, offset=count), view(gain_k, i)]
             operands += [view(raw, i), view(gain_q, i), cosine, sine, view(more, i)]
-        back_kernel(
-            own, *operands, view(dq, i), view(dk, i), view(dv, i), sums.at[pl.ds(i, 1)], *scratch
-        )
+        back_kernel(own, *operands, dq, dk, dv, sums.at[pl.ds(i, 1)], *scratch)
 
     return Aside(
         [grads, gate, ov, qa, spare_q, ka, va, *(rest or ())],
         [
-            jax.ShapeDtypeStruct((rows, width), bf if own else f32),
-            jax.ShapeDtypeStruct((caps, width), bf),
-            jax.ShapeDtypeStruct((caps, width), bf),
+            *(
+                [jax.ShapeDtypeStruct((rows, 3 * width), bf)]
+                if own
+                else [
+                    jax.ShapeDtypeStruct((rows, width), f32),
+                    jax.ShapeDtypeStruct((caps, 2 * width), bf),
+                ]
+            ),
             jax.ShapeDtypeStruct((count, 8, 128), f32),
         ],
         [
@@ -1542,9 +1829,15 @@
     return whole.reshape(-1, halves.shape[-1])
 
 
-def swap_rows(term):
-    cores, planes = lax.axis_size("core"), lax.axis_size("seq")
-    return swap_halves(term.astype(jnp.bfloat16).reshape(planes, cores, -1, term.shape[-1]))
+def outer_plane(ident, *items):
+    if fast():
+        return outer(ident, *items)
+    cores = lax.axis_size("core")
+    terms = [contract_rows(left, right).astype(jnp.bfloat16) for left, right, _ in items]
+    return [
+        swap_halves(term.reshape(item[2], cores, -1, term.shape[-1]))
+        for term, item in zip(terms, items)
+    ]
 
 
 def scatter_planes(term):
@@ -1631,6 +1924,25 @@
         jnp.concatenate([columns_of(w_qkv, 3), columns_of(w_out, 1)], axis=1),
         lax.dynamic_slice_in_dim(w_down, block * share, share, 0),
         columns_of(w_gateup, 2 * planes),
+    )
+
+
+def three_parts(values):
+    parts = []
+    for _ in range(3):
+        part = lax.reduce_precision(values, 8, 7)
+        parts.append(part.astype(jnp.bfloat16))
+        values = values - part
+    return parts
+
+
+def by_document(doc_pick, values):
+    return lax.dot_general(
+        doc_pick,
+        values,
+        (((0,), (0,)), ((), ())),
+        precision=lax.Precision.HIGHEST,
+        preferred_element_type=jnp.float32,
     )
 
 
@@ -1694,7 +2006,8 @@
     )
     messages = messages.reshape(groups, 8, mod_rows)
     cond_mine = messages[:, :DOCS].reshape(groups * DOCS, mod_rows)
-    mod_doc = mod_doc[:DOCS] + b_mod
+    mod_rows_doc = mod_doc + b_mod
+    mod_doc = mod_rows_doc[:DOCS]
 
     numbers = messages[:, DOCS, : 2 * DOCS + 1].astype(jnp.int32)
     counts = jnp.sum(numbers[:, :DOCS], axis=1).astype(jnp.float32)
@@ -1801,10 +2114,19 @@
         own_out, own_log = attend_forward(query, keys, values, self_allowed)
         cross_out, cross_log = attend_forward(query, capkeys, capvals, cross_allowed)
         mixed_attn = (own_out + head_gate * cross_out).astype(jnp.bfloat16)
-    attn_out, *_ = multiply_plane(3, mixed_attn, full_out)
-    residual = inputs + tanh_a * attn_out
-    normed2, inverse2 = row_stats(residual)
-    hidden2 = (normed2 * gain_ffn * (1.0 + scale_f)).astype(jnp.bfloat16)
+    token_rows = arrived.reshape(tokens.shape)
+    doc_column = jnp.broadcast_to(document.astype(jnp.float32)[:, None], (rows, 128))
+    weight_column = jnp.broadcast_to((is_valid * scale_loss)[:, None], (rows, 128))
+    if fast():
+        attn_out, residual, hidden2 = matmul_scatter(
+            3, mixed_attn, full_out,
+            after=after_attention(token_rows, mod_rows_doc, doc_column, gain_ffn[None]),
+        )
+    else:
+        attn_out, *_ = multiply_plane(3, mixed_attn, full_out)
+        residual = inputs + tanh_a * attn_out
+        normed2, inverse2 = row_stats(residual)
+        hidden2 = (normed2 * gain_ffn * (1.0 + scale_f)).astype(jnp.bfloat16)
     if fast():
         hidden2, full_gateup, hidden_ffn, grad_gateup = gather_matmul(
             4, hidden2, half_gateup, halved=True, finish=swiglu_finish(grad_ffn), keep=False
@@ -1820,33 +2142,50 @@
         grad_gate_part = grad_ffn * up_part * sig_gate * (1.0 + gate_part * (1.0 - sig_gate))
         grad_gateup = jnp.concatenate([grad_gate_part, grad_ffn * silu_gate], axis=1)
         grad_gateup = grad_gateup.astype(jnp.bfloat16)
-    term_down = swap_rows(contract_rows(hidden_ffn, grad_down))
-    term_gateup = swap_rows(contract_rows(hidden2, grad_gateup))
+    term_gateup, term_down = outer_plane(
+        15, (hidden2, grad_gateup, planes), (hidden_ffn, grad_down, planes)
+    )
     grad_gateup, term_down, term_gateup = lax.optimization_barrier(
         (grad_gateup, term_down, term_gateup)
     )
     term_down, term_gateup = scatter_planes(term_down), scatter_planes(term_gateup)
-    grad_hidden2, *_ = multiply_plane(7, grad_gateup, full_gateup, turned=True)
-    gain_ffn_term = jnp.sum(grad_hidden2 * normed2 * (1.0 + scale_f), axis=0)
-    grad_scale_f = grad_hidden2 * normed2 * gain_ffn
-    grad_residual = grad_res0 + norm_back(
-        grad_hidden2 * gain_ffn * (1.0 + scale_f), normed2, inverse2
-    )
-    grad_attn = (tanh_a * grad_residual).astype(jnp.bfloat16)
+    if fast():
+        _, grad_residual, grad_attn, ffn_sums = matmul_scatter(
+            7, grad_gateup, full_gateup, turned=True,
+            after=after_ffn_back(
+                residual, attn_out, cotangents, weight_column, mod_rows_doc, doc_column,
+                gain_ffn[None],
+            ),
+        )
+        doc_scale_f, doc_gate_a, gain_ffn_term = ffn_sums[:4], ffn_sums[4:8], ffn_sums[8]
+    else:
+        grad_hidden2, *_ = multiply_plane(7, grad_gateup, full_gateup, turned=True)
+        gain_ffn_term = jnp.sum(grad_hidden2 * normed2 * (1.0 + scale_f), axis=0)
+        doc_scale_f = by_document(doc_pick, grad_hidden2 * normed2 * gain_ffn)
+        grad_residual = grad_res0 + norm_back(
+            grad_hidden2 * gain_ffn * (1.0 + scale_f), normed2, inverse2
+        )
+        grad_attn = (tanh_a * grad_residual).astype(jnp.bfloat16)
+        doc_gate_a = by_document(doc_pick, grad_residual * attn_out * (1.0 - tanh_a * tanh_a))
     grad_attn, _, grad_mix = plane_multiply(8, grad_attn, full_out, turned=True)
-    grad_gate_a = grad_residual * attn_out * (1.0 - tanh_a * tanh_a)
-    term_out = contract_rows(mixed_attn, grad_attn).astype(jnp.bfloat16)
-    term_out = swap_halves(term_out.reshape(1, cores, -1, width))[0]
-    term_out = term_out.reshape(term_out.shape[0], tp, -1).transpose(1, 0, 2)
+    term_out = outer_plane(16, (mixed_attn, grad_attn, 1))[0][0]
     if fast():
         cross_aside = attend_back(
             grad_mix, head_gate, cross_wide, wide_query, cross_spare,
             wide_capkeys, wide_capvals,
         )
-        down_out, query_cross, grad_capkeys, grad_capvals, cross_sums, term_out = matmul_scatter(
-            5, hidden_ffn, full_down, aside=cross_aside, trade=[swap_blocks(term_out, "tp")]
-        )
-        grad_heads = jnp.concatenate([grad_capkeys, grad_capvals], axis=1)
+        out_columns = (
+            term_out,
+            "tp",
+            (tp, term_out.shape[0], local),
+            lambda ref, p: ref.at[:, pl.ds(pl.multiple_of(p * local, local), local)],
+            block_of,
+        )
+        _, query_cross, grad_heads, cross_sums, term_out, result, gate_sums = matmul_scatter(
+            5, hidden_ffn, full_down, aside=cross_aside, trade=[out_columns],
+            after=after_ffn(residual, cotangents, weight_column, mod_rows_doc, doc_column),
+        )
+        doc_gate_f = gate_sums[:DOCS]
         grad_heads = grad_heads.reshape(planes, DOCS * cap_dev, 2 * local)
         gate_head_term = jnp.sum(cross_sums[:, :2], axis=-1).reshape(-1)
         own_aside = attend_back(
@@ -1854,21 +2193,20 @@
             wide_keys, wide_values,
             (projected, my_gain_key, my_gain_query, cosine, sine, query_cross),
         )
-        result = (residual + tanh_f * down_out).astype(jnp.bfloat16)
         (all_down, all_gateup), riders = collect(
             10,
             [term_down, term_gateup],
             own_aside,
             [swap_blocks(grad_heads, "seq"), swap_blocks(term_out, "seq")],
         )
-        *grad_projected, own_sums, grad_heads, term_out = riders
+        grad_projected, own_sums, grad_heads, term_out = riders
         term_out = jnp.sum(term_out.astype(jnp.float32), axis=0).astype(jnp.bfloat16)
         gain_key_term, gain_query_term = own_sums[:, 2].reshape(-1), own_sums[:, 3].reshape(-1)
-        grad_projected = jnp.concatenate(grad_projected, axis=1)
     else:
         down_out, _ = multiply_plane(5, hidden_ffn, full_down)
         result = from_plane((residual + tanh_f * down_out).astype(jnp.bfloat16))
         all_down, all_gateup = collect_plane([term_down, term_gateup])
+        term_out = term_out.reshape(term_out.shape[0], tp, -1).transpose(1, 0, 2)
         term_out = scatter_planes(lax.all_to_all(term_out, "tp", 0, 0, tiled=True))
         grad_own = grad_mix.astype(jnp.bfloat16)
         grad_cross = (head_gate * grad_mix).astype(jnp.bfloat16)
@@ -1893,7 +2231,7 @@
         grad_heads = jnp.concatenate([grad_capkeys, grad_capvals], axis=1).astype(jnp.bfloat16)
         grad_heads = grad_heads.reshape(planes, DOCS * cap_dev, 2 * local)
         grad_heads = lax.all_to_all(grad_heads, "seq", 0, 0, tiled=True)
-    grad_gate_f = grad_res0 * down_out * (1.0 - tanh_f * tanh_f)
+        doc_gate_f = by_document(doc_pick, grad_res0 * down_out * (1.0 - tanh_f * tanh_f))
     gate_head_term = gate_head_term * (1.0 - gate_tanh * gate_tanh)
     grad_heads = grad_heads.reshape(-1, 2 * local)
     if fast():
@@ -1906,38 +2244,39 @@
         grad_cap_proj = jnp.concatenate([grad_capkey_raw, grad_capvals], axis=1).astype(
             jnp.bfloat16
         )
-    term_qkv = swap_rows(contract_rows(hidden1, grad_projected))
+    (term_qkv,) = outer_plane(17, (hidden1, grad_projected, planes))
     cap_side, _ = lax.optimization_barrier((grad_cap_proj, term_qkv))
     term_qkv = scatter_planes(term_qkv)
-    term_capkv = swap_rows(contract_rows(cap_flat, cap_side))
+    (term_capkv,) = outer_plane(18, (cap_flat, cap_side, planes))
     grad_projected, _ = lax.optimization_barrier((grad_projected, term_capkv))
     term_capkv = scatter_planes(term_capkv)
-    grad_hidden1, *_ = multiply_plane(9, grad_projected, full_qkv, turned=True)
-    gain_attn_term = jnp.sum(grad_hidden1 * normed1 * (1.0 + scale_a), axis=0)
-    grad_scale_a = grad_hidden1 * normed1 * gain_attn
-    input_grad = (
-        grad_residual + norm_back(grad_hidden1 * gain_attn * (1.0 + scale_a), normed1, inverse1)
-    ).astype(jnp.bfloat16)
-
-    grad_mod_tok = jnp.concatenate([grad_scale_a, grad_gate_a, grad_scale_f, grad_gate_f], axis=1)
-    grad_mod_doc = lax.dot_general(
-        doc_pick,
-        grad_mod_tok,
-        (((0,), (0,)), ((), ())),
-        precision=lax.Precision.HIGHEST,
-        preferred_element_type=jnp.float32,
-    )
+    if fast():
+        _, input_grad, input_sums = matmul_scatter(
+            9, grad_projected, full_qkv, turned=True,
+            after=after_input_back(
+                token_rows, grad_residual, mod_rows_doc, doc_column, gain_attn[None]
+            ),
+        )
+        doc_scale_a, gain_attn_term = input_sums[:4], input_sums[4]
+    else:
+        grad_hidden1, *_ = multiply_plane(9, grad_projected, full_qkv, turned=True)
+        gain_attn_term = jnp.sum(grad_hidden1 * normed1 * (1.0 + scale_a), axis=0)
+        doc_scale_a = by_document(doc_pick, grad_hidden1 * normed1 * gain_attn)
+        input_grad = (
+            grad_residual + norm_back(grad_hidden1 * gain_attn * (1.0 + scale_a), normed1, inverse1)
+        ).astype(jnp.bfloat16)
+    grad_mod_doc = jnp.concatenate([doc_scale_a, doc_gate_a, doc_scale_f, doc_gate_f], axis=1)
+
     plane_nulls = pick(numbers[:, DOCS + 1 :].reshape(tp, cores, DOCS), me_c, 1)
     null_rows = jnp.repeat(plane_nulls.reshape(-1), cap_dev) > 0
-    grad_hidden1, null_rows, all_down, all_gateup = lax.optimization_barrier(
-        (grad_hidden1, null_rows, all_down, all_gateup)
+    grad_mod_doc, null_rows, all_down, all_gateup = lax.optimization_barrier(
+        (grad_mod_doc, null_rows, all_down, all_gateup)
     )
     null_sum = jnp.sum(
         jnp.where(null_rows[:, None], grad_cap_proj.astype(jnp.float32), 0.0), axis=0
     )
-    null_term = jnp.dot(
-        full_capkv.astype(jnp.float32), null_sum, precision=lax.Precision.HIGHEST
-    )
+    null_parts = jnp.stack(three_parts(null_sum), axis=1)
+    null_term = jnp.sum(matmul(full_capkv, null_parts), axis=1)
 
     def at_mine(part):
         whole = jnp.zeros((tp,) + part.shape, jnp.float32)
@@ -1982,12 +2321,9 @@
     totals = totals.reshape(groups, 8, 4 * width)
     sum_capkv = spread_parts(all_capkv, 2)
     grad_mod_docs = totals[:, :DOCS].reshape(groups * DOCS, 4 * width)
-    sum_mod = lax.dot_general(
-        cond_mine,
-        grad_mod_docs,
-        (((0,), (0,)), ((), ())),
-        precision=lax.Precision.HIGHEST,
-        preferred_element_type=jnp.float32,
+    sum_mod = contract_rows(
+        jnp.concatenate([cond_mine.astype(jnp.bfloat16)] * 3, axis=0),
+        jnp.concatenate(three_parts(grad_mod_docs), axis=0),
     )
     sum_bias = jnp.sum(grad_mod_docs, axis=0)
     small = jnp.sum(totals[:, DOCS:], axis=0).reshape(-1)[:small_size]

time: 794 us -> 768 us (0.967)
  Pallas kernels: 588 us -> 665 us
  matrix products: 54.6 us -> 13.1 us
  other arithmetic: 64.9 us -> 23.8 us
  waiting for transfers between devices: 29.5 us -> 17.1 us
    pallas_call x4 -> x8, Pallas kernels: 146 us -> 220 us  [the longest x4 163 us: matmul_scatter(): pl.pallas_call(functools.partial(scatter_kernel, turned, *riders), out_sh...]
    dot_general x5 -> x1, matrix products: 32.7 us -> 3.71 us  [contract_rows(): lax.dot_general(left, right, (((0,), (0,)), ((), ())), preferred_element_...]
    convert_element_type x7 -> x3, other arithmetic: 18.6 us -> 0.19 us  [the longest x2 0.19 us: three_parts(): parts.append(part.astype(jnp.bfloat16))]
    dot_general x3 -> x1, matrix products: 17.1 us -> 4.59 us  [matmul(): return jnp.dot(left, right, preferred_element_type=jnp.float32)]
    ppermute x5 -> x0, waiting for transfers between devices: 11.3 us -> none  [swap_halves(): other = lax.ppermute(pick(shaped, (me_c + step) % cores, 1), 'core', ring)]
    mul x2 -> x0, other arithmetic: 11.1 us -> none  [the longest x1 6.22 us: shards(): grad_gate_f = grad_res0 * down_out * (1.0 - tanh_f * tanh_f)]
    unnamed x96 -> x68, local copies, waits for them, and re-layouts: 18.9 us -> 10.9 us
  transfers between devices with their start and end apart: 13 -> 8, of which waited for: 4 -> 1; matrix products, arithmetic and copies ran while one was open for 12% -> 5% of each run, Pallas kernels for 55% -> 62%
where the time goes in v5:
time: 768 us; the launch traced here: 763 us
  Pallas kernels  665 us (87%)
  local copies, waits for them, and re-layouts  26.6 us (3%)
  other arithmetic  23.8 us (3%)
  between operations  17.7 us (2%)
  waiting for transfers between devices  17.1 us (2%)
  matrix products  13.1 us (2%)
    pallas_call x5, Pallas kernels, gather_matmul(): pl.pallas_call(functools.partial(gather_kernel, turned, halved, early, *r...  241 us
    pallas_call x4, Pallas kernels, matmul_scatter(): pl.pallas_call(functools.partial(scatter_kernel, turned, *riders), out_sh...  163 us
    pallas_call x3, Pallas kernels, collect(): pl.pallas_call(functools.partial(collect_kernel, count, *riders), out_sha...  140 us
    pallas_call x4, Pallas kernels, outer(): pl.pallas_call(functools.partial(outer_kernel, count), out_shape=[jax.Sha...  57.4 us
    pallas_call x1, Pallas kernels, arrive(): pl.pallas_call(arrive_kernel, out_shape=[jax.ShapeDtypeStruct((4, rows //...  45.3 us
    pallas_call x4, Pallas kernels, spread(): pl.pallas_call(functools.partial(spread_kernel, parts), grid=(cores, cut)...  16 us
  transfers between devices with their start and end apart: 8, of which 1 were waited for; matrix products, arithmetic and copies ran while one was open for 5% of the time, Pallas kernels for 62%

profile of v5, /device:TPU:0, one launch (start us, length us, event | category | flops | bytes accessed | tf_op | source)
XLA Modules:
  0.0 763.4 jit_solution(14444746833516512842)
XLA Ops:
  11.1 45.3 %arrive.1 = (bf16[4,64,1536]{2,1,0:T(8,128)(2,1)}, bf16[4,64,1536]{2,1,0:T(8,128)(2,1)}, f32[4,2,8,256]{3,2,1,0:T(8,128)}, f32[8,6144]{1,0:T(8,128)}, bf16[192,1...) custom-call(bf16[4,64,1536]{2,1,0:T(8,128)(2,1)} %bitcast.110, ...), custom_call_target="tpu_custom_call" | custom-call | bytes 90000000 | tf_op jit(solution)/shard_map/arrive/pallas_call | solution.py:1101
  72.0 4.8 fusion.13
  76.8 1.7 bitcast_select_fusion.refs_0_
  78.5 15.2 %all-gather.9.cloned.1.call-done = bf16[2048,768]{1,0:T(8,128)(2,1)} async-done(((bf16[512,768]{1,0:T(8,128)(2,1)}), bf16[2048,768]{1,0:T(8,128)(2,1)}) %all-gather.9.cloned.1.call-update) | async-done | bytes 3145744 | tf_op jit(solution)/shard_map/all_gather | solution.py:1824
  94.3 75.6 %gather_matmul.5 = (bf16[4,256,4096]{2,1,0:T(8,128)(2,1)}, bf16[4096,768]{1,0:T(8,128)(2,1)}, f32[4,256,768]{2,1,0:T(8,128)}, bf16[4,64,1536]{2,1,0:T(8,128)(2,1)}, bf16[4,256,768]{2,1,0:T(8,128)(2,1)}) custom-call(bf16[256,4096]{1,0:T(8,128)(2,1)} %bitcast_select_fusion.refs_0_, bf16[4,512,768]{2,1,0:T(8,128)(2,1)} %bitcast.139, ...), custom_call_target="tpu_custom_call" | custom-call | flops 6442450944 | bytes 90000000 | tf_op jit(solution)/shard_map/gather_matmul/pallas_call | solution.py:329
  169.9 3.7 fusion.1
  173.6 42.7 %gather_matmul.6 = (bf16[4,256,1536]{2,1,0:T(8,128)(2,1)}, bf16[1536,1536]{1,0:T(8,128)(2,1)}, f32[4,256,1152]{2,1,0:T(8,128)}, bf16[4,256,768]{2,1,0:T(8,128)(2,1)}) custom-call(bf16[256,1536]{1,0:T(8,128)(2,1)} %get-tuple-element.104.refs_0_, bf16[4,192,1536]{2,1,0:T(8,128)(2,1)} %bitcast.141, bf16[4,256,768]{2,1,0:T(8,128)(2,1)} %get-tuple-element.106.refs_2_), custom_call_target="tpu_custom_call" | custom-call | flops 3623878656 | bytes 90000000 | tf_op jit(solution)/shard_map/gather_matmul/pallas_call | solution.py:329
  216.4 59.2 %gather_matmul.7 = (bf16[4,256,1536]{2,1,0:T(8,128)(2,1)}, bf16[1024,1536]{1,0:T(8,128)(2,1)}, f32[4,256,1024]{2,1,0:T(8,128)}, bf16[1024,768]{1,0:T(8,128)(2,1)...) custom-call(bf16[256,1536]{1,0:T(8,128)(2,1)} %get-tuple-element.186, ...), custom_call_target="tpu_custom_call" | custom-call | flops 3221225472 | bytes 90000000 | tf_op jit(solution)/shard_map/gather_matmul/pallas_call | solution.py:329
  276.4 34.8 %matmul_scatter.4 = (f32[256,1536]{1,0:T(8,128)}, f32[256,1536]{1,0:T(8,128)}, bf16[256,1536]{1,0:T(8,128)(2,1)}) custom-call(bf16[4,256,384]{2,1,0:T(8,128)(2,1)} %bitcast.118, bf16[384,1536]{1,0:T(8,128)(2,1)} %get-tuple-element.114.refs_1_, bf16[256,1536]{1,0:T(8,128)(2,1)} %bitcast.101, f32[8,6144]{1,0:T(8,128)} %copy-done.10, ...), custom_call_target="tpu_custom_call" | custom-call | flops 1207959552 | bytes 90000000 | tf_op jit(solution)/shard_map/matmul_scatter/pallas_call | solution.py:526
  311.2 33.0 %gather_matmul.8 = (bf16[4,256,1536]{2,1,0:T(8,128)(2,1)}, bf16[1536,2048]{1,0:T(8,128)(2,1)}, bf16[4,256,1024]{2,1,0:T(8,128)(2,1)}, bf16[4,256,2048]{2,1,0:T(8,128)(2,1)}) custom-call(bf16[256,1536]{1,0:T(8,128)(2,1)} %get-tuple-element.115.refs_0_, bf16[4,192,2048]{2,1,0:T(8,128)(2,1)} %bitcast.138, f32[4,256,1024]{2,1,0:T(8,128)} %get-tuple-element.117.refs_2_), custom_call_target="tpu_custom_call" | custom-call | flops 6442450944 | bytes 90000000 | tf_op jit(solution)/shard_map/gather_matmul/pallas_call | solution.py:329
  344.2 21.7 %outer.4 = (bf16[4,192,2048]{2,1,0:T(8,128)(2,1)}, bf16[4,128,1536]{2,1,0:T(8,128)(2,1)}) custom-call(bf16[1024,1536]{1,0:T(8,128)(2,1)} %bitcast.146, bf16[1024,2048]{1,0:T(8,128)(2,1)} %bitcast.144, bf16[1024,1024]{1,0:T(8,128)(2,1)} %bitcast.105, bf16[1024,1536]{1,0:T(8,128)(2,1)} %bitcast.140), custom_call_target="tpu_custom_call" | custom-call | flops 9663676416 | bytes 20000000 | tf_op jit(solution)/shard_map/outer/pallas_call | solution.py:628
  367.3 43.0 %matmul_scatter.5 = (f32[256,1536]{1,0:T(8,128)}, f32[256,1536]{1,0:T(8,128)}, bf16[256,1536]{1,0:T(8,128)(2,1)}, f32[16,1536]{1,0:T(8,128)}) custom-call(bf16[4,256,2048]{2,1,0:T(8,128)(2,1)} %get-tuple-element.118, bf16[1536,2048]{1,0:T(8,128)(2,1)} %get-tuple-element.127.refs_1_, f32[256,1536]{1,0:T(8,128)} %get-tuple-element.128.refs_2_.refs_10_, ...), custom_call_target="tpu_custom_call" | custom-call | flops 6442450944 | bytes 90000000 | tf_op jit(solution)/shard_map/matmul_scatter/pallas_call | solution.py:526
  410.4 30.4 %gather_matmul.9 = (bf16[4,256,1536]{2,1,0:T(8,128)(2,1)}, f32[4,256,384]{2,1,0:T(8,128)}) custom-call(bf16[256,1536]{1,0:T(8,128)(2,1)} %get-tuple-element.130.refs_0_, bf16[384,1536]{1,0:T(8,128)(2,1)} %get-tuple-element.114.refs_1_), custom_call_target="tpu_custom_call" | custom-call | flops 1207959552 | bytes 90000000 | tf_op jit(solution)/shard_map/gather_matmul/pallas_call | solution.py:329
  440.8 6.6 outer.5
  447.4 46.0 %matmul_scatter.6 = (f32[256,1536]{1,0:T(8,128)}, f32[1024,384]{1,0:T(8,128)}, bf16[1024,768]{1,0:T(8,128)(2,1)}, f32[3,8,128]{2,1,0:T(8,128)}, bf16[4,192,384]{...) custom-call(bf16[4,256,1024]{2,1,0:T(8,128)(2,1)} %get-tuple-element.120.refs_0_, ...), custom_call_target="tpu_custom_call" | custom-call | flops 3221225472 | bytes 90000000 | tf_op jit(solution)/shard_map/matmul_scatter/pallas_call | solution.py:526
  494.0 55.3 %collect.3 = (bf16[4,2,128,1536]{3,2,1,0:T(8,128)(2,1)}, bf16[4,2,192,2048]{3,2,1,0:T(8,128)(2,1)}, bf16[1024,1152]{1,0:T(8,128)(2,1)}, f32[3,8,128]{2,1,0:T(8,1...) custom-call(bf16[128,1536]{1,0:T(8,128)(2,1)} %bitcast.121, bf16[192,2048]{1,0:T(8,128)(2,1)} %bitcast.112, ...), custom_call_target="tpu_custom_call" | custom-call | bytes 47185920 | tf_op jit(solution)/shard_map/collect/pallas_call | solution.py:915
  549.3 12.6 %outer.6 = bf16[4,192,1152]{2,1,0:T(8,128)(2,1)} custom-call(bf16[1024,1536]{1,0:T(8,128)(2,1)} %bitcast.145, bf16[1024,1152]{1,0:T(8,128)(2,1)} %get-tuple-element.152.refs_1_), custom_call_target="tpu_custom_call" | custom-call | flops 3623878656 | bytes 20000000 | tf_op jit(solution)/shard_map/outer/pallas_call | solution.py:628
  563.4 2.8 cap_back.1
  567.3 16.6 %outer.7 = bf16[4,512,768]{2,1,0:T(8,128)(2,1)} custom-call(bf16[1024,4096]{1,0:T(8,128)(2,1)} %bitcast.143, bf16[1024,768]{1,0:T(8,128)(2,1)} %copy-done.3), custom_call_target="tpu_custom_call" | custom-call | flops 6442450944 | bytes 20000000 | tf_op jit(solution)/shard_map/outer/pallas_call | solution.py:628
  586.8 38.8 %matmul_scatter.7 = (f32[256,1536]{1,0:T(8,128)}, bf16[256,1536]{1,0:T(8,128)(2,1)}, f32[8,1536]{1,0:T(8,128)}) custom-call(bf16[4,256,1152]{2,1,0:T(8,128)(2,1)} %bitcast.142, bf16[1536,1536]{1,0:T(8,128)(2,1)} %get-tuple-element.112.refs_13_.refs_1_, bf16[256,1536]{1,0:T(8,128)(2,1)} %bitcast.102, f32[256,1536]{1,0:T(8,128)} %get-tuple-element.153.refs_3_, ...), custom_call_target="tpu_custom_call" | custom-call | flops 3623878656 | bytes 90000000 | tf_op jit(solution)/shard_map/matmul_scatter/pallas_call | solution.py:526
  628.7 4.6 convolution_reduce_fusion
  634.9 24.0 %collect.4 = (bf16[4,2,192,1152]{3,2,1,0:T(8,128)(2,1)}, bf16[4,2,192,384]{3,2,1,0:T(8,128)(2,1)}) custom-call(bf16[192,1152]{1,0:T(8,128)(2,1)} %bitcast.119, bf16[192,384]{1,0:T(8,128)(2,1)} %reduce_sum.129.refs_1_), custom_call_target="tpu_custom_call" | custom-call | bytes 23592960 | tf_op jit(solution)/shard_map/collect/pallas_call | solution.py:915
  658.9 2.0 copy-done.1
  660.9 3.7 spread.4
  665.1 5.2 spread.5
  670.2 2.0 spread.6
  673.0 3.8 bitcast_convert_fusion
  676.7 60.5 %collect.5 = (bf16[4,2,512,768]{3,2,1,0:T(8,128)(2,1)}, bf16[4,64,1536]{2,1,0:T(8,128)(2,1)}, bf16[4,64,1536]{2,1,0:T(8,128)(2,1)}, f32[4,2,8,6144]{3,2,1,0:T(8,128)}) custom-call(bf16[512,768]{1,0:T(8,128)(2,1)} %bitcast.116, bf16[4,64,1536]{2,1,0:T(8,128)(2,1)} %bitcast.115, bf16[4,64,1536]{2,1,0:T(8,128)(2,1)} %bitcast.117, ...), custom_call_target="tpu_custom_call" | custom-call | bytes 31457280 | tf_op jit(solution)/shard_map/collect/pallas_call | solution.py:915
  737.2 3.0 slice_reduce_fusion
  742.0 2.8 copy-done
  744.8 5.1 spread.7
  750.4 3.7 fusion.4
  (198 shorter events, 35.6 us)
Async XLA Ops:
  7.2 3.0 copy-start.26
  7.2 3.0 copy-start.25
  7.2 3.1 copy-start.20
  7.2 86.5 %all-gather.9.cloned.1.call-start = ((), (), s32[]{:S(2)}) async-start(), calls=%async_computation.8 | async-start | bytes 3932160 | tf_op jit(solution)/shard_map/all_gather | solution.py:1824
  9.4 164.2 %all-gather.11.cloned.1.call-start = ((), (), s32[]{:S(2)}) async-start(), calls=%async_computation.9 | async-start | bytes 2949120 | tf_op jit(solution)/shard_map/all_gather | solution.py:1824
  11.1 52.0 %copy-start.21 = (f32[1536]{0:T(1024)S(1)}, f32[1536]{0:T(1024)}, u32[]{:S(2)}) copy-start(f32[1536]{0:T(1024)} %param.39) | copy-start | bytes 18436
  56.4 6.7 copy-start.8
  56.4 7.0 copy-start.22
  56.4 7.0 copy-start.23
  56.4 7.0 copy-start.27
  56.4 160.0 %all-gather.13.cloned.1.call-start = ((), (), s32[]{:S(2)}) async-start(), calls=%async_computation.10 | async-start | bytes 1966080 | tf_op jit(solution)/shard_map/all_gather | solution.py:1824
  57.2 254.1 %all-gather.15.cloned.1.call-start = ((), (), s32[]{:S(2)}) async-start(), calls=%async_computation.11 | async-start | bytes 3932160 | tf_op jit(solution)/shard_map/all_gather | solution.py:1824
  57.8 435.7 %reduce-scatter.5.cloned.1.call-start = ((), (), s32[]{:S(2)}) async-start(), calls=%async_computation.4 | async-start | bytes 1966080 | tf_op jit(solution)/shard_map/reduce_scatter | solution.py:1844
  66.0 5.3 copy-start.24
  66.0 5.9 copy-start.14
  66.0 5.9 copy-start.17
  71.9 4.9 copy-start.10
  71.9 4.9 copy-start.9
  72.0 4.9 copy-start.19
  94.3 75.6 %copy-start.15 = (f32[1536]{0:T(1024)S(1)}, f32[1536]{0:T(1024)}, u32[]{:S(2)}) copy-start(f32[1536]{0:T(1024)} %param.35) | copy-start | bytes 18436
  365.9 127.5 %reduce-scatter.7.cloned.1.call-start = ((), (), s32[]{:S(2)}) async-start(), calls=%async_computation.5 | async-start | bytes 3932160 | tf_op jit(solution)/shard_map/reduce_scatter | solution.py:1844
  366.5 268.4 %reduce-scatter.9.cloned.1.call-start = ((), (), s32[]{:S(2)}) async-start(), calls=%async_computation.6 | async-start | bytes 2211840 | tf_op jit(solution)/shard_map/reduce_scatter | solution.py:1844
  549.3 12.7 %copy-start.2 = (f32[4,256,768]{2,1,0:T(8,128)S(1)}, f32[4,256,768]{2,1,0:T(8,128)}, u32[]{:S(2)}) copy-start(f32[4,256,768]{2,1,0:T(8,128)} %get-tuple-element.149) | copy-start | bytes 9437188
  561.9 114.8 %reduce-scatter.11.cloned.1.call-start = ((), (), s32[]{:S(2)}) async-start(), calls=%async_computation.7 | async-start | bytes 3932160 | tf_op jit(solution)/shard_map/reduce_scatter | solution.py:1844
  583.9 2.8 copy-start.16
  586.8 40.6 %copy-start.4 = (bf16[1024,768]{1,0:T(8,128)(2,1)S(1)}, bf16[1024,768]{1,0:T(8,128)(2,1)}, u32[]{:S(2)}) copy-start(bf16[1024,768]{1,0:T(8,128)(2,1)} %copy-done.3) | copy-start | bytes 4718596
  628.7 4.7 copy-start.13
  634.2 30.4 %slice-start = ((s8[6291456]{0:T(1024)(128)(4,1)}), s8[2097152]{0:T(1024)(128)(4,1)S(1)}, s32[]{:S(2)}) async-start(s8[6291456]{0:T(1024)(128)(4,1)} %bitcast.90), calls=%async_computation.12 | async-start | bytes 4194304
  660.9 4.2 slice-start.1
  665.1 5.2 copy-start.6
  742.0 2.8 copy-start
  750.4 3.7 copy-start.12
  (6 other events, 10.5 us)
Sparse Core Ops, SparseCore 0:
  10.2 83.4 all-gather.8
  95.3 58.4 all-gather.10
  155.3 58.8 all-gather.12
  215.6 62.3 all-gather.14
  366.1 33.9 reduce-scatter.4
  402.2 59.2 reduce-scatter.6
  562.0 37.0 reduce-scatter.8
  601.5 59.3 reduce-scatter.10

commit v6 on v5

--- a/solution.py
+++ b/solution.py
@@ -406,8 +406,8 @@
         aside.steps(out_ref, aside.refs[2][:count], aside.refs[1], aside.refs[2][count + 1 :])
 
 
-def scatter_kernel(turned, aside, trade, after, *refs):
-    refs = bind(refs, (2, 1, 10), aside, trade, after)
+def scatter_kernel(turned, aside, after, trade, *refs):
+    refs = bind(refs, (2, 1, 10), aside, after, trade)
     x_hbm, w_hbm, out_ref, sums, far_out, near_out, relay, land, s0, s1, x_ref, w_ref, load = refs
     me, across, along, far = neighbours()
     sems = (s0, s1)
@@ -519,7 +519,7 @@
 
 
 def matmul_scatter(ident, x, w, turned=False, aside=None, trade=(), after=None):
-    riders = [aside or nothing(), Trade(*trade), after or nothing()]
+    riders = [aside or nothing(), after or nothing(), Trade(*trade)]
     rows, depth = x.shape[0] // 4, x.shape[1]
     width = w.shape[0] if turned else w.shape[1]
     vmem = pl.BlockSpec(memory_space=pltpu.VMEM)
@@ -581,7 +581,7 @@
     sent = []
     for i in range(count):
         blocks, rows, width = outs[i].shape
-        tile = tile_of(width)
+        tile = width
         loads[i][0].wait()
         for z in range(blocks):
             loads[i][1 + z].wait()
@@ -2181,7 +2181,7 @@
             lambda ref, p: ref.at[:, pl.ds(pl.multiple_of(p * local, local), local)],
             block_of,
         )
-        _, query_cross, grad_heads, cross_sums, term_out, result, gate_sums = matmul_scatter(
+        _, query_cross, grad_heads, cross_sums, result, gate_sums, term_out = matmul_scatter(
             5, hidden_ffn, full_down, aside=cross_aside, trade=[out_columns],
             after=after_ffn(residual, cotangents, weight_column, mod_rows_doc, doc_column),
         )
@@ -2197,10 +2197,9 @@
             10,
             [term_down, term_gateup],
             own_aside,
-            [swap_blocks(grad_heads, "seq"), swap_blocks(term_out, "seq")],
-        )
-        grad_projected, own_sums, grad_heads, term_out = riders
-        term_out = jnp.sum(term_out.astype(jnp.float32), axis=0).astype(jnp.bfloat16)
+            [swap_blocks(grad_heads, "seq")],
+        )
+        grad_projected, own_sums, grad_heads = riders
         gain_key_term, gain_query_term = own_sums[:, 2].reshape(-1), own_sums[:, 3].reshape(-1)
     else:
         down_out, _ = multiply_plane(5, hidden_ffn, full_down)
@@ -2251,13 +2250,14 @@
     grad_projected, _ = lax.optimization_barrier((grad_projected, term_capkv))
     term_capkv = scatter_planes(term_capkv)
     if fast():
-        _, input_grad, input_sums = matmul_scatter(
-            9, grad_projected, full_qkv, turned=True,
+        _, input_grad, input_sums, term_out = matmul_scatter(
+            9, grad_projected, full_qkv, turned=True, trade=[swap_blocks(term_out, "seq")],
             after=after_input_back(
                 token_rows, grad_residual, mod_rows_doc, doc_column, gain_attn[None]
             ),
         )
         doc_scale_a, gain_attn_term = input_sums[:4], input_sums[4]
+        term_out = jnp.sum(term_out.astype(jnp.float32), axis=0).astype(jnp.bfloat16)
     else:
         grad_hidden1, *_ = multiply_plane(9, grad_projected, full_qkv, turned=True)
         gain_attn_term = jnp.sum(grad_hidden1 * normed1 * (1.0 + scale_a), axis=0)

time: 768 us -> 761 us (level)
  Pallas kernels: 665 us -> 657 us
  transfers between devices with their start and end apart: 8 -> 8, of which waited for: 1 -> 1; matrix products, arithmetic and copies ran while one was open for 5% -> 5% of each run, Pallas kernels for 62% -> 63%
where the time goes in v6:
time: 761 us; the launch traced here: 756 us
  Pallas kernels  657 us (86%)
  local copies, waits for them, and re-layouts  26.9 us (4%)
  other arithmetic  23.8 us (3%)
  between operations  17.7 us (2%)
  waiting for transfers between devices  17.2 us (2%)
  matrix products  13.1 us (2%)
    pallas_call x5, Pallas kernels, gather_matmul(): pl.pallas_call(functools.partial(gather_kernel, turned, halved, early, *r...  241 us
    pallas_call x4, Pallas kernels, matmul_scatter(): pl.pallas_call(functools.partial(scatter_kernel, turned, *riders), out_sh...  163 us
    pallas_call x3, Pallas kernels, collect(): pl.pallas_call(functools.partial(collect_kernel, count, *riders), out_sha...  139 us
    pallas_call x4, Pallas kernels, outer(): pl.pallas_call(functools.partial(outer_kernel, count), out_shape=[jax.Sha...  49.8 us
    pallas_call x1, Pallas kernels, arrive(): pl.pallas_call(arrive_kernel, out_shape=[jax.ShapeDtypeStruct((4, rows //...  45.3 us
    pallas_call x4, Pallas kernels, spread(): pl.pallas_call(functools.partial(spread_kernel, parts), grid=(cores, cut)...  16.1 us
    all_gather x4, waiting for transfers between devices, gather_planes(): return lax.all_gather(part, 'seq', axis=0, tiled=False)  15.3 us
  transfers between devices with their start and end apart: 8, of which 1 were waited for; matrix products, arithmetic and copies ran while one was open for 5% of the time, Pallas kernels for 63%

profile of v6, /device:TPU:0, one launch (start us, length us, event | category | flops | bytes accessed | tf_op | source)
XLA Modules:
  0.0 756.3 jit_solution(12445060190712384364)
XLA Ops:
  11.1 45.3 %arrive.1 = (bf16[4,64,1536]{2,1,0:T(8,128)(2,1)}, bf16[4,64,1536]{2,1,0:T(8,128)(2,1)}, f32[4,2,8,256]{3,2,1,0:T(8,128)}, f32[8,6144]{1,0:T(8,128)}, bf16[192,1...) custom-call(bf16[4,64,1536]{2,1,0:T(8,128)(2,1)} %bitcast.110, ...), custom_call_target="tpu_custom_call" | custom-call | bytes 90000000 | tf_op jit(solution)/shard_map/arrive/pallas_call | solution.py:1101
  72.0 4.7 fusion.13
  76.7 1.7 bitcast_select_fusion.refs_0_
  78.4 15.3 %all-gather.9.cloned.1.call-done = bf16[2048,768]{1,0:T(8,128)(2,1)} async-done(((bf16[512,768]{1,0:T(8,128)(2,1)}), bf16[2048,768]{1,0:T(8,128)(2,1)}) %all-gather.9.cloned.1.call-update) | async-done | bytes 3145744 | tf_op jit(solution)/shard_map/all_gather | solution.py:1824
  94.3 75.6 %gather_matmul.5 = (bf16[4,256,4096]{2,1,0:T(8,128)(2,1)}, bf16[4096,768]{1,0:T(8,128)(2,1)}, f32[4,256,768]{2,1,0:T(8,128)}, bf16[4,64,1536]{2,1,0:T(8,128)(2,1)}, bf16[4,256,768]{2,1,0:T(8,128)(2,1)}) custom-call(bf16[256,4096]{1,0:T(8,128)(2,1)} %bitcast_select_fusion.refs_0_, bf16[4,512,768]{2,1,0:T(8,128)(2,1)} %bitcast.139, ...), custom_call_target="tpu_custom_call" | custom-call | flops 6442450944 | bytes 90000000 | tf_op jit(solution)/shard_map/gather_matmul/pallas_call | solution.py:329
  169.9 3.7 fusion.1
  173.6 42.7 %gather_matmul.6 = (bf16[4,256,1536]{2,1,0:T(8,128)(2,1)}, bf16[1536,1536]{1,0:T(8,128)(2,1)}, f32[4,256,1152]{2,1,0:T(8,128)}, bf16[4,256,768]{2,1,0:T(8,128)(2,1)}) custom-call(bf16[256,1536]{1,0:T(8,128)(2,1)} %get-tuple-element.104.refs_0_, bf16[4,192,1536]{2,1,0:T(8,128)(2,1)} %bitcast.141, bf16[4,256,768]{2,1,0:T(8,128)(2,1)} %get-tuple-element.106.refs_2_), custom_call_target="tpu_custom_call" | custom-call | flops 3623878656 | bytes 90000000 | tf_op jit(solution)/shard_map/gather_matmul/pallas_call | solution.py:329
  216.4 58.8 %gather_matmul.7 = (bf16[4,256,1536]{2,1,0:T(8,128)(2,1)}, bf16[1024,1536]{1,0:T(8,128)(2,1)}, f32[4,256,1024]{2,1,0:T(8,128)}, bf16[1024,768]{1,0:T(8,128)(2,1)...) custom-call(bf16[256,1536]{1,0:T(8,128)(2,1)} %get-tuple-element.186, ...), custom_call_target="tpu_custom_call" | custom-call | flops 3221225472 | bytes 90000000 | tf_op jit(solution)/shard_map/gather_matmul/pallas_call | solution.py:329
  276.0 34.8 %matmul_scatter.4 = (f32[256,1536]{1,0:T(8,128)}, f32[256,1536]{1,0:T(8,128)}, bf16[256,1536]{1,0:T(8,128)(2,1)}) custom-call(bf16[4,256,384]{2,1,0:T(8,128)(2,1)} %bitcast.118, bf16[384,1536]{1,0:T(8,128)(2,1)} %get-tuple-element.114.refs_1_, bf16[256,1536]{1,0:T(8,128)(2,1)} %bitcast.101, f32[8,6144]{1,0:T(8,128)} %copy-done.10, ...), custom_call_target="tpu_custom_call" | custom-call | flops 1207959552 | bytes 90000000 | tf_op jit(solution)/shard_map/matmul_scatter/pallas_call | solution.py:526
  310.9 33.2 %gather_matmul.8 = (bf16[4,256,1536]{2,1,0:T(8,128)(2,1)}, bf16[1536,2048]{1,0:T(8,128)(2,1)}, bf16[4,256,1024]{2,1,0:T(8,128)(2,1)}, bf16[4,256,2048]{2,1,0:T(8,128)(2,1)}) custom-call(bf16[256,1536]{1,0:T(8,128)(2,1)} %get-tuple-element.115.refs_0_, bf16[4,192,2048]{2,1,0:T(8,128)(2,1)} %bitcast.138, f32[4,256,1024]{2,1,0:T(8,128)} %get-tuple-element.117.refs_2_), custom_call_target="tpu_custom_call" | custom-call | flops 6442450944 | bytes 90000000 | tf_op jit(solution)/shard_map/gather_matmul/pallas_call | solution.py:329
  344.1 17.5 %outer.4 = (bf16[4,192,2048]{2,1,0:T(8,128)(2,1)}, bf16[4,128,1536]{2,1,0:T(8,128)(2,1)}) custom-call(bf16[1024,1536]{1,0:T(8,128)(2,1)} %bitcast.146, bf16[1024,2048]{1,0:T(8,128)(2,1)} %bitcast.144, bf16[1024,1024]{1,0:T(8,128)(2,1)} %bitcast.105, bf16[1024,1536]{1,0:T(8,128)(2,1)} %bitcast.140), custom_call_target="tpu_custom_call" | custom-call | flops 9663676416 | bytes 20000000 | tf_op jit(solution)/shard_map/outer/pallas_call | solution.py:628
  363.0 43.0 %matmul_scatter.5 = (f32[256,1536]{1,0:T(8,128)}, f32[256,1536]{1,0:T(8,128)}, bf16[256,1536]{1,0:T(8,128)(2,1)}, f32[16,1536]{1,0:T(8,128)}) custom-call(bf16[4,256,2048]{2,1,0:T(8,128)(2,1)} %get-tuple-element.118, bf16[1536,2048]{1,0:T(8,128)(2,1)} %get-tuple-element.127.refs_1_, f32[256,1536]{1,0:T(8,128)} %get-tuple-element.128.refs_2_.refs_9_, ...), custom_call_target="tpu_custom_call" | custom-call | flops 6442450944 | bytes 90000000 | tf_op jit(solution)/shard_map/matmul_scatter/pallas_call | solution.py:526
  406.0 30.4 %gather_matmul.9 = (bf16[4,256,1536]{2,1,0:T(8,128)(2,1)}, f32[4,256,384]{2,1,0:T(8,128)}) custom-call(bf16[256,1536]{1,0:T(8,128)(2,1)} %get-tuple-element.130.refs_0_, bf16[384,1536]{1,0:T(8,128)(2,1)} %get-tuple-element.114.refs_1_), custom_call_target="tpu_custom_call" | custom-call | flops 1207959552 | bytes 90000000 | tf_op jit(solution)/shard_map/gather_matmul/pallas_call | solution.py:329
  436.4 6.1 outer.5
  442.6 46.0 %matmul_scatter.6 = (f32[256,1536]{1,0:T(8,128)}, f32[1024,384]{1,0:T(8,128)}, bf16[1024,768]{1,0:T(8,128)(2,1)}, f32[3,8,128]{2,1,0:T(8,128)}, bf16[256,1536]{1...) custom-call(bf16[4,256,1024]{2,1,0:T(8,128)(2,1)} %get-tuple-element.120.refs_0_, ...), custom_call_target="tpu_custom_call" | custom-call | flops 3221225472 | bytes 90000000 | tf_op jit(solution)/shard_map/matmul_scatter/pallas_call | solution.py:526
  489.3 55.3 %collect.3 = (bf16[4,2,128,1536]{3,2,1,0:T(8,128)(2,1)}, bf16[4,2,192,2048]{3,2,1,0:T(8,128)(2,1)}, bf16[1024,1152]{1,0:T(8,128)(2,1)}, f32[3,8,128]{2,1,0:T(8,128)}, bf16[4,256,768]{2,1,0:T(8,128)(2,1)}) custom-call(bf16[128,1536]{1,0:T(8,128)(2,1)} %bitcast.121, bf16[192,2048]{1,0:T(8,128)(2,1)} %bitcast.112, f32[1024,384]{1,0:T(8,128)} %bitcast.97, ...), custom_call_target="tpu_custom_call" | custom-call | bytes 47185920 | tf_op jit(solution)/shard_map/collect/pallas_call | solution.py:915
  544.5 10.5 %outer.6 = bf16[4,192,1152]{2,1,0:T(8,128)(2,1)} custom-call(bf16[1024,1536]{1,0:T(8,128)(2,1)} %bitcast.145, bf16[1024,1152]{1,0:T(8,128)(2,1)} %get-tuple-element.149.refs_1_), custom_call_target="tpu_custom_call" | custom-call | flops 3623878656 | bytes 20000000 | tf_op jit(solution)/shard_map/outer/pallas_call | solution.py:628
  556.5 2.8 cap_back.1
  560.4 15.7 %outer.7 = bf16[4,512,768]{2,1,0:T(8,128)(2,1)} custom-call(bf16[1024,4096]{1,0:T(8,128)(2,1)} %bitcast.143, bf16[1024,768]{1,0:T(8,128)(2,1)} %copy-done.3), custom_call_target="tpu_custom_call" | custom-call | flops 6442450944 | bytes 20000000 | tf_op jit(solution)/shard_map/outer/pallas_call | solution.py:628
  579.0 39.3 %matmul_scatter.7 = (f32[256,1536]{1,0:T(8,128)}, bf16[256,1536]{1,0:T(8,128)(2,1)}, f32[8,1536]{1,0:T(8,128)}, bf16[4,192,384]{2,1,0:T(8,128)(2,1)}) custom-call(bf16[4,256,1152]{2,1,0:T(8,128)(2,1)} %bitcast.142, bf16[1536,1536]{1,0:T(8,128)(2,1)} %get-tuple-element.112.refs_13_.refs_1_, bf16[256,1536]{1,0:T(8,128)(2,1)} %bitcast.102, ...), custom_call_target="tpu_custom_call" | custom-call | flops 3623878656 | bytes 90000000 | tf_op jit(solution)/shard_map/matmul_scatter/pallas_call | solution.py:526
  621.4 4.7 convolution_reduce_fusion
  627.7 23.6 %collect.4 = (bf16[4,2,192,1152]{3,2,1,0:T(8,128)(2,1)}, bf16[4,2,192,384]{3,2,1,0:T(8,128)(2,1)}) custom-call(bf16[192,1152]{1,0:T(8,128)(2,1)} %bitcast.119, bf16[192,384]{1,0:T(8,128)(2,1)} %reduce_sum.129.refs_1_), custom_call_target="tpu_custom_call" | custom-call | bytes 23592960 | tf_op jit(solution)/shard_map/collect/pallas_call | solution.py:915
  651.3 2.0 copy-done.1
  653.3 3.8 spread.4
  657.9 5.2 spread.5
  663.0 2.0 spread.6
  665.8 3.8 bitcast_convert_fusion
  669.6 60.6 %collect.5 = (bf16[4,2,512,768]{3,2,1,0:T(8,128)(2,1)}, bf16[4,64,1536]{2,1,0:T(8,128)(2,1)}, bf16[4,64,1536]{2,1,0:T(8,128)(2,1)}, f32[4,2,8,6144]{3,2,1,0:T(8,128)}) custom-call(bf16[512,768]{1,0:T(8,128)(2,1)} %bitcast.116, bf16[4,64,1536]{2,1,0:T(8,128)(2,1)} %bitcast.115, bf16[4,64,1536]{2,1,0:T(8,128)(2,1)} %bitcast.117, ...), custom_call_target="tpu_custom_call" | custom-call | bytes 31457280 | tf_op jit(solution)/shard_map/collect/pallas_call | solution.py:915
  730.2 3.0 slice_reduce_fusion
  734.9 2.8 copy-done
  737.7 5.1 spread.7
  743.3 3.7 fusion.4
  (198 shorter events, 36.0 us)
Async XLA Ops:
  7.2 3.0 copy-start.26
  7.2 3.0 copy-start.25
  7.2 3.1 copy-start.20
  7.2 86.5 %all-gather.9.cloned.1.call-start = ((), (), s32[]{:S(2)}) async-start(), calls=%async_computation.8 | async-start | bytes 3932160 | tf_op jit(solution)/shard_map/all_gather | solution.py:1824
  9.4 164.2 %all-gather.11.cloned.1.call-start = ((), (), s32[]{:S(2)}) async-start(), calls=%async_computation.9 | async-start | bytes 2949120 | tf_op jit(solution)/shard_map/all_gather | solution.py:1824
  11.1 52.0 %copy-start.21 = (f32[1536]{0:T(1024)S(1)}, f32[1536]{0:T(1024)}, u32[]{:S(2)}) copy-start(f32[1536]{0:T(1024)} %param.39) | copy-start | bytes 18436
  56.4 6.7 copy-start.8
  56.4 7.0 copy-start.22
  56.4 7.0 copy-start.23
  56.4 7.0 copy-start.27
  56.4 160.0 %all-gather.13.cloned.1.call-start = ((), (), s32[]{:S(2)}) async-start(), calls=%async_computation.10 | async-start | bytes 1966080 | tf_op jit(solution)/shard_map/all_gather | solution.py:1824
  57.2 253.7 %all-gather.15.cloned.1.call-start = ((), (), s32[]{:S(2)}) async-start(), calls=%async_computation.11 | async-start | bytes 3932160 | tf_op jit(solution)/shard_map/all_gather | solution.py:1824
  57.8 430.9 %reduce-scatter.5.cloned.1.call-start = ((), (), s32[]{:S(2)}) async-start(), calls=%async_computation.4 | async-start | bytes 1966080 | tf_op jit(solution)/shard_map/reduce_scatter | solution.py:1844
  66.0 5.3 copy-start.24
  66.0 5.9 copy-start.14
  66.0 5.9 copy-start.17
  71.9 4.8 copy-start.10
  71.9 4.8 copy-start.9
  72.0 4.7 copy-start.19
  94.3 75.6 %copy-start.15 = (f32[1536]{0:T(1024)S(1)}, f32[1536]{0:T(1024)}, u32[]{:S(2)}) copy-start(f32[1536]{0:T(1024)} %param.35) | copy-start | bytes 18436
  361.6 127.1 %reduce-scatter.7.cloned.1.call-start = ((), (), s32[]{:S(2)}) async-start(), calls=%async_computation.5 | async-start | bytes 3932160 | tf_op jit(solution)/shard_map/reduce_scatter | solution.py:1844
  362.2 265.5 %reduce-scatter.9.cloned.1.call-start = ((), (), s32[]{:S(2)}) async-start(), calls=%async_computation.6 | async-start | bytes 2211840 | tf_op jit(solution)/shard_map/reduce_scatter | solution.py:1844
  544.5 10.6 %copy-start.2 = (f32[4,256,768]{2,1,0:T(8,128)S(1)}, f32[4,256,768]{2,1,0:T(8,128)}, u32[]{:S(2)}) copy-start(f32[4,256,768]{2,1,0:T(8,128)} %get-tuple-element.146) | copy-start | bytes 9437188
  555.0 114.5 %reduce-scatter.11.cloned.1.call-start = ((), (), s32[]{:S(2)}) async-start(), calls=%async_computation.7 | async-start | bytes 3932160 | tf_op jit(solution)/shard_map/reduce_scatter | solution.py:1844
  576.2 2.8 copy-start.16
  579.0 41.1 %copy-start.4 = (bf16[1024,768]{1,0:T(8,128)(2,1)S(1)}, bf16[1024,768]{1,0:T(8,128)(2,1)}, u32[]{:S(2)}) copy-start(bf16[1024,768]{1,0:T(8,128)(2,1)} %copy-done.3) | copy-start | bytes 4718596
  621.4 4.8 copy-start.13
  627.0 30.1 %slice-start = ((s8[6291456]{0:T(1024)(128)(4,1)}), s8[2097152]{0:T(1024)(128)(4,1)S(1)}, s32[]{:S(2)}) async-start(s8[6291456]{0:T(1024)(128)(4,1)} %bitcast.90), calls=%async_computation.12 | async-start | bytes 4194304
  653.3 4.6 slice-start.1
  657.9 5.2 copy-start.6
  734.9 2.8 copy-start
  743.3 3.7 copy-start.12
  (6 other events, 10.5 us)
Sparse Core Ops, SparseCore 0:
  10.2 83.4 all-gather.8
  95.3 58.4 all-gather.10
  155.3 58.8 all-gather.12
  215.6 62.4 all-gather.14
  361.7 33.9 reduce-scatter.4
  397.8 59.2 reduce-scatter.6
  555.2 37.3 reduce-scatter.8
  595.0 60.6 reduce-scatter.10
